TPU v7x, 512 devices: a whole 4x8x8 slice. The times are simulated.
512 devices in a mesh: ctx: 32 (over y_hi, z), tp: 16 (over y_lo, x, core).
Axes of the slice: x: 4, y: 8 (y_hi: 4, y_lo: 2; y = y_hi * 2 + y_lo), z: 8, core: 2. Of those that a mesh axis runs over, the one named last changes fastest.
Arguments:
- tokens: bfloat16 [4096, 4096], P('ctx', 'tp'), may hold values from -6 to 6
- in_weight: bfloat16 [3, 4096, 4096], P(None, 'ctx', 'tp'), may hold values from -0.1875 to 0.1875
- out_weight: bfloat16 [4096, 4096], P('tp', 'ctx'), may hold values from -0.1875 to 0.1875
- mr_filter: float32 [256, 128], P('tp'), may hold values from -0.5 to 0.5
- cotangent: bfloat16 [4096, 4096], P('ctx', 'tp'), may hold values from -6 to 6
Outputs:
- mixed_out: bfloat16 [4096, 4096], P('ctx', 'tp')
- grad_tokens: bfloat16 [4096, 4096], P('ctx', 'tp')
All inputs are finite; a program needn't handle non-finite values.
Results may differ from a plain program's by a relative error of at most 0.03.
Values may be sent and summed in bfloat16 or wider, within the bound.
No kernel may reach another device: no remote copies, remote signals or barrier semaphores. Data moves between devices by JAX's collectives and lax.ppermute only.
A program may use at most 128 MiB of HBM per device.

v0:
```python
import jax
import jax.numpy as jnp
from jax import lax
from jax.sharding import PartitionSpec as P


def passed_along(value, axis, steps):
    count = lax.axis_size(axis)
    leading, last = (max(0, -steps), min(count, count - steps))
    return lax.ppermute(value, axis, [(source, source + steps) for source in range(leading, last)])


def banded_matrix(mr_filter, row_count, causal_side):
    tap_count = mr_filter.shape[1]
    shape_full = (row_count, row_count + tap_count - 1)
    target = lax.broadcasted_iota(jnp.int32, shape_full, 0)
    source = lax.broadcasted_iota(jnp.int32, shape_full, 1)
    tap_offset = target + tap_count - 1 - source if causal_side else source - target
    inside = (tap_offset >= 0) & (tap_offset < tap_count)
    entries = jnp.take(mr_filter, jnp.clip(tap_offset, 0, tap_count - 1), axis=1)
    return jnp.where(inside[None], entries, 0.0)


def apply_banded(banded, extended, row_count):
    group_count = banded.shape[0]
    source_count, chan_count = extended.shape
    grouped = extended.T.reshape(group_count, chan_count // group_count, source_count)
    result = jnp.einsum(
        "gts,gcs->gct",
        banded,
        grouped,
        precision=lax.Precision.HIGHEST,
        preferred_element_type=jnp.float32,
    )
    return result.reshape(chan_count, row_count).T


def streams_of(columns, weight_piece):
    return jnp.stack(
        [
            jnp.dot(columns, weight_piece[stream], preferred_element_type=jnp.float32)
            for stream in range(3)
        ],
        0,
    )


def back_terms(grad_projected, weight_piece):
    return lax.dot_general(
        grad_projected,
        weight_piece,
        (((0, 2), (0, 2)), ((), ())),
        preferred_element_type=jnp.float32,
    )


def local(tokens, in_weight, out_weight, mr_filter, cotangent):
    whole_tokens, whole_cotangent = (
        lax.all_gather(tokens, "tp", axis=1, tiled=True),
        lax.all_gather(cotangent, "tp", axis=1, tiled=True),
    )
    row_count = tokens.shape[0]
    tap_count = mr_filter.shape[1]
    full_input, full_output = (
        lax.all_gather(in_weight, "ctx", axis=1, tiled=True),
        lax.all_gather(out_weight, "ctx", axis=1, tiled=True),
    )
    projected = streams_of(whole_tokens, full_input)
    projected = projected.astype(jnp.bfloat16)
    query_part = projected[0].astype(jnp.float32)
    key_part = projected[1].astype(jnp.float32)
    value_part = projected[2].astype(jnp.float32)
    product = (key_part * value_part).astype(jnp.bfloat16)
    earlier = passed_along(product[row_count - (tap_count - 1) :], "ctx", 1)
    extended = jnp.concatenate([earlier, product], 0).astype(jnp.float32)
    mixed_conv = apply_banded(banded_matrix(mr_filter, row_count, True), extended, row_count)
    gating = (query_part * mixed_conv).astype(jnp.bfloat16)
    out_terms = jnp.dot(gating, full_output, preferred_element_type=jnp.float32)
    grad_gate = lax.dot_general(
        whole_cotangent, full_output, (((1,), (1,)), ((), ())), preferred_element_type=jnp.float32
    )
    grad_query = grad_gate * mixed_conv
    grad_mixed = (grad_gate * query_part).astype(jnp.bfloat16)
    later_rim = passed_along(grad_mixed[: tap_count - 1], "ctx", -1)
    extended_grad = jnp.concatenate([grad_mixed, later_rim], 0).astype(jnp.float32)
    grad_product = apply_banded(
        banded_matrix(mr_filter, row_count, False), extended_grad, row_count
    )
    grad_projected = jnp.stack(
        [grad_query, grad_product * value_part, grad_product * key_part], 0
    ).astype(jnp.bfloat16)
    in_terms = back_terms(grad_projected, full_input)
    mixed_out, grad_tokens = (
        lax.psum_scatter(
            out_terms.astype(jnp.bfloat16), "tp", scatter_dimension=1, tiled=True
        ).astype(jnp.float32),
        lax.psum_scatter(
            in_terms.astype(jnp.bfloat16), "tp", scatter_dimension=1, tiled=True
        ).astype(jnp.float32),
    )
    return (mixed_out.astype(jnp.bfloat16), grad_tokens.astype(jnp.bfloat16))


def solution(mesh):
    return jax.shard_map(
        local,
        mesh=mesh,
        in_specs=(
            P("ctx", "tp"),
            P(None, "ctx", "tp"),
            P("tp", "ctx"),
            P("tp", None),
            P("ctx", "tp"),
        ),
        out_specs=(P("ctx", "tp"), P("ctx", "tp")),
        check_vma=False,
    )
```

profile of v0, /device:TPU:1, one launch (start us, length us, event | category | flops | bytes accessed | tf_op | source)
XLA Modules:
  0.0 441.8 jit_solution(1172755258269071237)
XLA Ops:
  7.9 0.7 all-gather.7.cloned.1.call-update
  8.7 0.7 all-gather.9.cloned.1.call-update
  10.5 0.8 copy.16
  11.3 60.6 %gather_fusion = f32[32640,16]{1,0:T(8,128)} fusion(f32[16,128]{0,1:T(8,128)S(1)} %copy.16, s32[32768]{0:T(1024)S(1)} %pad_clamp_fusion.1), kind=kCustom, calls=%fused_computation.clone | custom fusion | bytes 4308480 | tf_op jit(solution)/shard_map/jit(_take)/gather | solution.py:20
  71.9 10.7 %copy.17 = f32[32640,16]{0,1:T(8,128)} copy(f32[32640,16]{1,0:T(8,128)} %gather_fusion) | data formatting | bytes 4177920 | tf_op jit(solution)/shard_map/jit(_take)/gather | solution.py:20
  82.6 4.8 %reshape.85 = f32[128,255,16]{1,0,2:T(8,128)S(1)} reshape(f32[32640,16]{0,1:T(8,128)} %copy.17) | data formatting | bytes 4177920 | tf_op jit(solution)/shard_map/jit(_take)/gather | solution.py:20
  87.6 87.1 %all-gather.7.cloned.1.call-done = bf16[3,4096,256]{2,1,0:T(8,128)(2,1)} async-done(((bf16[3,128,256]{2,1,0:T(8,128)(2,1)}), bf16[3,4096,256]{2,1,0:T(8,128)(2,1)}) %all-gather.7.cloned.1.call-update) | async-done | bytes 6291472 | tf_op jit(solution)/shard_map/all_gather | solution.py:65
  174.7 2.4 fusion.11
  177.2 2.0 multiply_convert_fusion.1
  179.2 3.3 collective-permute-start
  182.5 2.0 fusion.13
  184.7 1.3 fusion.5
  186.1 74.1 %all-gather.9.cloned.1.call-done = bf16[256,4096]{1,0:T(8,128)(2,1)} async-done(((bf16[256,128]{1,0:T(8,128)(2,1)}), bf16[256,4096]{1,0:T(8,128)(2,1)}) %all-gather.9.cloned.1.call-update) | async-done | bytes 2097168 | tf_op jit(solution)/shard_map/all_gather | solution.py:66
  260.2 3.0 convolution_convert_fusion
  263.7 60.6 %gather_fusion.1 = f32[32640,16]{1,0:T(8,128)} fusion(f32[16,128]{0,1:T(8,128)S(1)} %copy.16, s32[32768]{0:T(1024)S(1)} %pad_clamp_fusion), kind=kCustom, calls=%fused_computation.1.clone | custom fusion | bytes 4308480 | tf_op jit(solution)/shard_map/jit(_take)/gather | solution.py:20
  324.3 10.7 %copy.21 = f32[32640,16]{0,1:T(8,128)} copy(f32[32640,16]{1,0:T(8,128)} %gather_fusion.1) | data formatting | bytes 4177920 | tf_op jit(solution)/shard_map/jit(_take)/gather | solution.py:20
  335.0 6.3 %reshape.89 = f32[128,255,16]{1,0,2:T(8,128)} reshape(f32[32640,16]{0,1:T(8,128)} %copy.21) | data formatting | bytes 4177920 | tf_op jit(solution)/shard_map/jit(_take)/gather | solution.py:20
  341.3 2.1 fusion.37
  343.4 1.5 collective-permute-start.1
  345.0 3.6 collective-permute-done.1
  348.7 2.9 fusion.4
  351.8 6.0 %fusion = bf16[128,4096]{1,0:T(8,128)(2,1)} fusion(bf16[3,4096,256]{2,1,0:T(8,128)(2,1)} %all-gather.7.cloned.1.call-done, bf16[1,128,256]{2,1,0:T(8,128)(2,1)S(1)} %get-tuple-element.6, bf16[1,128,256]{2,1,0:T(8,128)(2,1)S(1)} %get-tuple-element.5, bf16[1,128,256]{2,1,0:T(8,128)(2,1)S(1)} %get-tuple-element.3), kind=kOutput, calls=%fused_computation.3 | convolution fusion | flops 806027264 | bytes 7536640 | tf_op jit(solution)/shard_map/dot_general | solution.py:49
  357.8 9.5 %reduce-scatter.3.cloned.1.call-done = bf16[128,256]{1,0:T(8,128)(2,1)} async-done(((bf16[128,4096]{1,0:T(8,128)(2,1)}), bf16[128,256]{1,0:T(8,128)(2,1)}) %reduce-scatter.3.cloned.1.call-update) | async-done | bytes 65552 | tf_op jit(solution)/shard_map/reduce_scatter | solution.py:94
  367.3 67.7 %reduce-scatter.5.cloned.1.call-done = bf16[128,256]{1,0:T(8,128)(2,1)} async-done(((bf16[128,4096]{1,0:T(8,128)(2,1)}), bf16[128,256]{1,0:T(8,128)(2,1)}) %reduce-scatter.5.cloned.1.call-update) | async-done | bytes 65552 | tf_op jit(solution)/shard_map/reduce_scatter | solution.py:97
  (34 shorter events, 3.1 us)
Async XLA Ops:
  7.2 80.4 %all-gather.5.cloned.1.call-start = ((), (), s32[]{:S(2)}) async-start(), calls=%async_computation.2 | async-start | bytes 1114112 | tf_op jit(solution)/shard_map/all_gather | solution.py:59
  7.9 166.8 %all-gather.7.cloned.1.call-start = ((), (), s32[]{:S(2)}) async-start(), calls=%async_computation.3 | async-start | bytes 6488064 | tf_op jit(solution)/shard_map/all_gather | solution.py:65
  8.6 251.6 %all-gather.9.cloned.1.call-start = ((), (), s32[]{:S(2)}) async-start(), calls=%async_computation.4 | async-start | bytes 2162688 | tf_op jit(solution)/shard_map/all_gather | solution.py:66
  9.4 331.9 %all-gather.11.cloned.1.call-start = ((), (), s32[]{:S(2)}) async-start(), calls=%async_computation.6 | async-start | bytes 1114112 | tf_op jit(solution)/shard_map/all_gather | solution.py:60
  10.0 357.4 %reduce-scatter.3.cloned.1.call-start = ((), (), s32[]{:S(2)}) async-start(), calls=%async_computation.5 | async-start | bytes 1114112 | tf_op jit(solution)/shard_map/reduce_scatter | solution.py:94
  174.7 2.4 copy-start.1
  179.2 5.3 %collective-permute-start = (bf16[127,256]{1,0:T(8,128)(2,1)S(1)}, bf16[127,256]{1,0:T(8,128)(2,1)S(1)}, u32[]{:S(2)}, u32[]{:S(2)}) collective-permute-start(bf16[127,256]{1,0:T(8,128)(2,1)S(1)} %slice.30), channel_id=1, source_target_pairs={{0,16},{16,32},{32,48},{48,64},{64,80},{80,96},{96,112},{112,128},... | collective-permute-start | bytes 195080 | tf_op jit(solution)/shard_map/ppermute | solution.py:10
  263.3 171.7 %reduce-scatter.5.cloned.1.call-start = ((), (), s32[]{:S(2)}) async-start(), calls=%async_computation.7 | async-start | bytes 1114112 | tf_op jit(solution)/shard_map/reduce_scatter | solution.py:97
  335.0 6.3 %copy-start = (bf16[256,4096]{1,0:T(8,128)(2,1)S(1)}, bf16[256,4096]{1,0:T(8,128)(2,1)}, u32[]{:S(2)}) copy-start(bf16[256,4096]{1,0:T(8,128)(2,1)} %all-gather.9.cloned.1.call-done) | copy-start | bytes 6291460
  343.4 5.2 %collective-permute-start.1 = (bf16[127,256]{1,0:T(8,128)(2,1)S(1)}, bf16[127,256]{1,0:T(8,128)(2,1)S(1)}, u32[]{:S(2)}, u32[]{:S(2)}) collective-permute-start(bf16[127,256]{1,0:T(8,128)(2,1)S(1)} %bitcast.86), channel_id=1, source_target_pairs={{16,0},{32,16},{48,32},{64,48},{80,64},{96,80},{112,96},{128,112},... | collective-permute-start | bytes 195080 | tf_op jit(solution)/shard_map/ppermute | solution.py:10
Sparse Core Ops, SparseCore 0:
  10.0 45.1 all-gather.4
  58.4 116.2 all-gather.6
  177.8 82.3 all-gather.8
  262.1 37.5 all-gather.10
  302.9 64.3 reduce-scatter.2
  370.8 64.1 reduce-scatter.4
where the time goes:
time: 444 us; the launch traced here: 442 us
  waiting for transfers between devices  245 us (55%)
  local copies, waits for them, and re-layouts  156 us (35%)
  matrix products  21.8 us (5%)
  between operations  14.3 us (3%)
  starting transfers between devices  4.96 us (1%)
    gather x6, local copies, waits for them, and re-layouts, banded_matrix(): jnp.take(mr_filter, jnp.clip(tap_offset, 0, tap_count - 1), axis=1)  154 us
    all_gather x1, waiting for transfers between devices, local(): lax.all_gather(in_weight, 'ctx', axis=1, tiled=True)  87.1 us
    all_gather x1, waiting for transfers between devices, local(): lax.all_gather(out_weight, 'ctx', axis=1, tiled=True)  74.1 us
    reduce_scatter x1, waiting for transfers between devices, local(): lax.psum_scatter(in_terms.astype(jnp.bfloat16), 'tp', scatter_dimension=1...  67.7 us
    reduce_scatter x1, waiting for transfers between devices, local(): lax.psum_scatter(out_terms.astype(jnp.bfloat16), 'tp', scatter_dimension=...  9.54 us
  transfers between devices with their start and end apart: 8, of which 5 were waited for; matrix products, arithmetic and copies ran while one was open for 40% of the time, Pallas kernels for 0%

commit v1 on v0

v1 whole, which is shorter than its diff:
```python
import functools

import jax
import jax.numpy as jnp
from jax import lax
from jax.experimental import pallas as pl
from jax.experimental.pallas import tpu as pltpu
from jax.sharding import Mesh, PartitionSpec as P

AXES = ("h", "l", "z", "ylo", "x", "core")
SIZES = (2, 2, 8, 2, 4, 2)
ROWS = 128
HALF = 128
TAPS = 128
GROUP = 16
GROUPS = HALF // GROUP
STREAMS = 4 * HALF
BACK = 3 * HALF


def bands_kernel(base_ref, band_ref):
    for row in range(base_ref.shape[0]):
        spread = jnp.broadcast_to(base_ref[row : row + 1, :], (ROWS, 2 * ROWS))
        band_ref[row] = pltpu.roll(spread, 0, 1, stride=1, stride_axis=0).astype(jnp.bfloat16)


def bands(filters):
    count = filters.shape[0]
    zeros = jnp.zeros((count, TAPS), filters.dtype)
    causal = jnp.concatenate([zeros[:, :1], filters[:, ::-1], zeros[:, 1:]], 1)
    anticausal = jnp.concatenate([filters, zeros], 1)
    return pl.pallas_call(
        bands_kernel,
        out_shape=jax.ShapeDtypeStruct((2 * count, ROWS, 2 * ROWS), jnp.bfloat16),
    )(jnp.concatenate([causal, anticausal], 0))


def forward_kernel(place_ref, own_ref, other_ref, weight_ref, streams_ref, gate_ref, product_ref, mixed_ref, total):
    step = pl.program_id(0)
    core = place_ref[0]

    @pl.when(step == 0)
    def _():
        total[...] = jnp.zeros_like(total)

    for values_ref, which in ((own_ref, core), (other_ref, 1 - core)):
        weight = weight_ref[pl.ds(2 * which, 2), 0].reshape(2 * ROWS, STREAMS)
        tokens = values_ref[0, :, 0, 0].reshape(2 * ROWS, 2 * HALF)
        cotangent = values_ref[0, :, 0, 1].reshape(2 * ROWS, 2 * HALF)
        total[:, :BACK] += jnp.dot(tokens, weight[:, :BACK], preferred_element_type=jnp.float32)
        total[:, BACK:] += jnp.dot(cotangent, weight[:, BACK:], preferred_element_type=jnp.float32)

    @pl.when(step == pl.num_programs(0) - 1)
    def _():
        streams = total[:, :BACK].astype(jnp.bfloat16)
        streams_ref[...] = streams
        grad_gate = total[:, BACK:]
        gate_ref[...] = grad_gate
        query, key, value = (streams[:, i * HALF : (i + 1) * HALF].astype(jnp.float32) for i in range(3))
        product_ref[...] = (key * value).astype(jnp.bfloat16)
        mixed_ref[...] = (grad_gate * query).astype(jnp.bfloat16)


def forward(place, own, other, weight):
    values = pl.BlockSpec((1, 2, 1, 2, ROWS, 2 * HALF), lambda j, p: (j // 2, 0, j % 2, 0, 0, 0))
    whole = lambda width: pl.BlockSpec((2 * ROWS, width), lambda j, p: (0, 0))
    shape = lambda width, kind: jax.ShapeDtypeStruct((2 * ROWS, width), kind)
    return pl.pallas_call(
        forward_kernel,
        out_shape=(
            shape(BACK, jnp.bfloat16),
            shape(HALF, jnp.float32),
            shape(HALF, jnp.bfloat16),
            shape(HALF, jnp.bfloat16),
        ),
        grid_spec=pltpu.PrefetchScalarGridSpec(
            num_scalar_prefetch=1,
            grid=(8,),
            in_specs=[
                values,
                values,
                pl.BlockSpec((4, 1, ROWS, STREAMS), lambda j, p: ((j // 2) % 2, (j % 2) * 2 + j // 4, 0, 0)),
            ],
            out_specs=[whole(BACK), whole(HALF), whole(HALF), whole(HALF)],
            scratch_shapes=[pltpu.VMEM((2 * ROWS, STREAMS), jnp.float32)],
        ),
        cost_estimate=pl.CostEstimate(flops=1 << 30, bytes_accessed=9 << 20, transcendentals=0),
    )(place, own, other, weight)


def pick(result, segment):
    rows = result.reshape(GROUPS, ROWS, 2 * HALF)[:, :, segment * HALF : (segment + 1) * HALF]
    group = lax.broadcasted_iota(jnp.int32, (ROWS, HALF), 1) // GROUP
    picked = rows[0]
    for g in range(1, GROUPS):
        picked = jnp.where(group == g, rows[g], picked)
    return picked


def middle_kernel(place_ref, band_ref, streams_ref, gate_ref, product_ref, mixed_ref, before_ref, after_ref, out_ref):
    position = place_ref[1]
    first = position == 0
    last = position == 15
    product = [product_ref[s * ROWS : (s + 1) * ROWS] for s in range(2)]
    mixed = [mixed_ref[s * ROWS : (s + 1) * ROWS] for s in range(2)]
    before = [before_ref[s * ROWS : (s + 1) * ROWS] for s in range(2)]
    after = [after_ref[s * ROWS : (s + 1) * ROWS] for s in range(2)]
    zero = jnp.zeros_like(before[0])
    earlier = [jnp.where(first, zero, before[0]), jnp.where(first, before[0], before[1])]
    later = [jnp.where(last, after[1], after[0]), jnp.where(last, zero, after[1])]
    causal = jnp.concatenate(
        [jnp.concatenate(earlier, 1), jnp.concatenate(product, 1)], 0
    )
    anticausal = jnp.concatenate(
        [jnp.concatenate(mixed, 1), jnp.concatenate(later, 1)], 0
    )
    count = GROUPS * ROWS
    conv = jnp.dot(
        band_ref[:GROUPS].reshape(count, 2 * ROWS), causal, preferred_element_type=jnp.float32
    )
    back = jnp.dot(
        band_ref[GROUPS:].reshape(count, 2 * ROWS), anticausal, preferred_element_type=jnp.float32
    )
    for s in range(2):
        rows = slice(s * ROWS, (s + 1) * ROWS)
        query, key, value = (
            streams_ref[rows, i * HALF : (i + 1) * HALF].astype(jnp.float32) for i in range(3)
        )
        mixed_conv = pick(conv, s)
        grad_product = pick(back, s)
        out_ref[rows, :HALF] = (gate_ref[rows] * mixed_conv).astype(jnp.bfloat16)
        out_ref[rows, HALF : 2 * HALF] = (grad_product * value).astype(jnp.bfloat16)
        out_ref[rows, 2 * HALF : 3 * HALF] = (grad_product * key).astype(jnp.bfloat16)
        out_ref[rows, 3 * HALF :] = (query * mixed_conv).astype(jnp.bfloat16)


def middle(place, band, streams, gate, product, mixed, before, after):
    smem = pl.BlockSpec(memory_space=pltpu.SMEM)
    vmem = pl.BlockSpec(memory_space=pltpu.VMEM)
    return pl.pallas_call(
        middle_kernel,
        out_shape=jax.ShapeDtypeStruct((2 * ROWS, STREAMS), jnp.bfloat16),
        in_specs=[smem] + [vmem] * 7,
        out_specs=vmem,
        compiler_params=pltpu.CompilerParams(vmem_limit_bytes=32 << 20),
        cost_estimate=pl.CostEstimate(flops=1 << 28, bytes_accessed=3 << 20, transcendentals=0),
    )(place, band, streams, gate, product, mixed, before, after)


def backward_kernel(which_ref, terms_ref, weight_ref, out_ref):
    weight = weight_ref[:, 0].reshape(2 * ROWS, STREAMS)
    contract = (((1,), (1,)), ((), ()))
    mixed = lax.dot_general(
        terms_ref[:, BACK:], weight[:, BACK:], contract, preferred_element_type=jnp.float32
    )
    grad = lax.dot_general(
        terms_ref[:, :BACK], weight[:, :BACK], contract, preferred_element_type=jnp.float32
    )
    out_ref[0, :, 0, 0] = mixed.astype(jnp.bfloat16).reshape(2, ROWS, 2 * HALF)
    out_ref[0, :, 0, 1] = grad.astype(jnp.bfloat16).reshape(2, ROWS, 2 * HALF)


def backward(which, terms, weight):
    return pl.pallas_call(
        backward_kernel,
        out_shape=jax.ShapeDtypeStruct((4, 2, 2, 2, ROWS, 2 * HALF), jnp.bfloat16),
        grid_spec=pltpu.PrefetchScalarGridSpec(
            num_scalar_prefetch=1,
            grid=(8,),
            in_specs=[
                pl.BlockSpec((2 * ROWS, STREAMS), lambda j, c: (0, 0)),
                pl.BlockSpec(
                    (2, 1, ROWS, STREAMS),
                    lambda j, c: (((j // 2) % 2) * 2 + c[0], (j % 2) * 2 + j // 4, 0, 0),
                ),
            ],
            out_specs=pl.BlockSpec((1, 2, 1, 2, ROWS, 2 * HALF), lambda j, c: (j // 2, 0, j % 2, 0, 0, 0)),
        ),
        cost_estimate=pl.CostEstimate(flops=1 << 29, bytes_accessed=4 << 20, transcendentals=0),
    )(which, terms, weight)


def swapped(value, axes):
    return lax.all_to_all(value, axes, 0, 0, tiled=True)


def gathered(value, axes, count):
    return swapped(jnp.broadcast_to(value[None], (count,) + value.shape), axes)


def local(tokens, in_weight, out_weight, mr_filter, cotangent):
    half, core = lax.axis_index("h"), lax.axis_index("core")
    position = lax.axis_index(("l", "z"))
    place = jnp.stack([core, position]).astype(jnp.int32)

    weight = jnp.concatenate([in_weight, out_weight.T[None]], 0)
    weight = weight.reshape(4, ROWS, 2, HALF).transpose(2, 1, 0, 3).reshape(2, 1, ROWS, STREAMS)
    weight = jnp.broadcast_to(weight, (2, 2, ROWS, STREAMS)).reshape(4, ROWS, STREAMS)
    weight = swapped(weight, ("h", "l"))
    values = jnp.stack([tokens, cotangent], 0)
    weight, values, mr_filter = lax.optimization_barrier((weight, values, mr_filter))
    weight = lax.all_gather(weight, "z", axis=0)

    filters = lax.dynamic_slice_in_dim(mr_filter, half * GROUPS, GROUPS, 0)
    band = bands(filters)

    values = gathered(values, ("h", "ylo"), 4)
    values = gathered(values, "x", 4).reshape(4, 2, 2, 2, ROWS, 2 * HALF)
    cross = [(0, 1), (1, 0)]
    other = lax.ppermute(values, "core", cross)

    streams, gate, product, mixed = forward(place, values, other, weight)
    ring = [(n, (n + 1) % 16) for n in range(16)]
    before = lax.ppermute(product, ("l", "z"), ring)
    after = lax.ppermute(mixed, ("l", "z"), [(b, a) for a, b in ring])
    terms = middle(place, band, streams, gate, product, mixed, before, after)

    far = backward((1 - core).reshape(1).astype(jnp.int32), terms, weight)
    near = backward(core.reshape(1).astype(jnp.int32), terms, weight)
    far = lax.ppermute(far, "core", cross)
    sums = (near.astype(jnp.float32) + far.astype(jnp.float32)).astype(jnp.bfloat16)
    sums = swapped(sums, "x").astype(jnp.float32).sum(0).astype(jnp.bfloat16)
    sums = swapped(sums.reshape(4, 2, ROWS, 2 * HALF), ("h", "ylo")).astype(jnp.float32).sum(0)
    sums = sums.astype(jnp.bfloat16)
    return sums[0], sums[1]


def solution(mesh):
    fine = Mesh(mesh.devices.reshape(SIZES), AXES)
    ctx, tp = AXES[:3], AXES[3:]
    return jax.shard_map(
        local,
        mesh=fine,
        in_specs=(P(ctx, tp), P(None, ctx, tp), P(tp, ctx), P(tp, None), P(ctx, tp)),
        out_specs=(P(ctx, tp), P(ctx, tp)),
        check_vma=False,
    )
```

time: 444 us -> 201 us (0.45)
  waiting for transfers between devices: 245 us -> 23.6 us
  local copies, waits for them, and re-layouts: 156 us -> 9.43 us
  blocking collectives: 0 us -> 94.3 us
  Pallas kernels: 0 us -> 25.2 us
  matrix products: 21.8 us -> 0 us
  starting transfers between devices: 4.96 us -> 25.8 us
    all_gather x4 -> x1, waiting for transfers between devices: 161 us -> 6.17 us  [local(): weight = lax.all_gather(weight, 'z', axis=0)]
    gather x6 -> x0, local copies, waits for them, and re-layouts: 154 us -> none  [banded_matrix(): jnp.take(mr_filter, jnp.clip(tap_offset, 0, tap_count - 1), axis=1)]
    all_to_all x0 -> x4, blocking collectives: none -> 94.3 us  [swapped(): return lax.all_to_all(value, axes, 0, 0, tiled=True)]
    reduce_scatter x2 -> x0, waiting for transfers between devices: 77.2 us -> none  [the longest x1 67.7 us: local(): lax.psum_scatter(in_terms.astype(jnp.bfloat16), 'tp', scatter_dimension=1...]
    pallas_call x0 -> x5, Pallas kernels: none -> 25.2 us  [the longest x2 13.4 us: backward(): pl.pallas_call(backward_kernel, out_shape=jax.ShapeDtypeStruct((4, 2, 2,...]
    dot_general x8 -> x0, matrix products: 21.8 us -> none  [the longest x3 6.5 us: streams_of(): jnp.dot(columns, weight_piece[stream], preferred_element_type=jnp.float32)]
    all_to_all x0 -> x1, waiting for transfers between devices: none -> 14.2 us  [swapped(): return lax.all_to_all(value, axes, 0, 0, tiled=True)]
    ppermute x2 -> x4, starting transfers between devices: 4.73 us -> 18.1 us  [the longest x1 9.24 us: local(): after = lax.ppermute(mixed, ('l', 'z'), [(b, a) for a, b in ring])]
  transfers between devices with their start and end apart: 8 -> 6, of which waited for: 5 -> 3; matrix products, arithmetic and copies ran while one was open for 40% -> 1% of each run, Pallas kernels for 0% -> 4%
where the time goes in v1:
time: 201 us; the launch traced here: 198 us
  blocking collectives  94.3 us (47%)
  starting transfers between devices  25.8 us (13%)
  Pallas kernels  25.2 us (13%)
  waiting for transfers between devices  23.6 us (12%)
  between operations  14.2 us (7%)
  local copies, waits for them, and re-layouts  9.43 us (5%)
  other arithmetic  4.93 us (2%)
    all_to_all x4, blocking collectives, swapped(): return lax.all_to_all(value, axes, 0, 0, tiled=True)  94.3 us
    all_to_all x1, waiting for transfers between devices, swapped(): return lax.all_to_all(value, axes, 0, 0, tiled=True)  14.2 us
    pallas_call x2, Pallas kernels, backward(): pl.pallas_call(backward_kernel, out_shape=jax.ShapeDtypeStruct((4, 2, 2,...  13.4 us
    ppermute x1, starting transfers between devices, local(): after = lax.ppermute(mixed, ('l', 'z'), [(b, a) for a, b in ring])  9.24 us
    pallas_call x1, Pallas kernels, forward(): pl.pallas_call(forward_kernel, out_shape=(shape(BACK, jnp.bfloat16), shap...  8.75 us
    all_to_all x1, starting transfers between devices, swapped(): return lax.all_to_all(value, axes, 0, 0, tiled=True)  7.64 us
    unnamed x25, local copies, waits for them, and re-layouts  7.4 us
    all_gather x1, waiting for transfers between devices, local(): weight = lax.all_gather(weight, 'z', axis=0)  6.17 us
  transfers between devices with their start and end apart: 6, of which 3 were waited for; matrix products, arithmetic and copies ran while one was open for 1% of the time, Pallas kernels for 4%

profile of v1, /device:TPU:1, one launch (start us, length us, event | category | flops | bytes accessed | tf_op | source)
XLA Modules:
  0.0 197.5 jit_solution(2885360136662097397)
XLA Ops:
  7.2 1.1 copy.15
  8.3 0.9 maximum_bitcast_fusion
  10.2 7.6 %all-to-all-start = ((bf16[4,128,512]{2,1,0:T(8,128)(2,1)}), bf16[4,128,512]{2,1,0:T(8,128)(2,1)S(1)}, u32[]{:S(2)}, u32[]{:S(2)}) async-start(bf16[4,128,512]{2,1,0:T(8,128)(2,1)} %bitcast.7), calls=%async_computation | async-start | bytes 1048576 | tf_op jit(solution)/shard_map/all_to_all | solution.py:184
  17.9 14.2 %all-to-all-done = bf16[4,128,512]{2,1,0:T(8,128)(2,1)S(1)} async-done(((bf16[4,128,512]{2,1,0:T(8,128)(2,1)}), bf16[4,128,512]{2,1,0:T(8,128)(2,1)S(1)}, u32[]{:S(2)}, u32[]{:S(2)}) %all-to-all-start) | async-done | bytes 524320 | tf_op jit(solution)/shard_map/all_to_all | solution.py:184
  32.1 0.8 copy-done.9
  33.0 17.9 %all_to_all.25 = bf16[4,2,128,256]{3,2,1,0:T(8,128)(2,1)S(1)} all-to-all(bf16[4,2,128,256]{3,2,1,0:T(8,128)(2,1)S(1)} %broadcast_in_dim.10), channel_id=1, replica_groups=mesh['h'=2,'l'=2,'z'=8,'ylo'=2,'x'=4,'core'=2] {'h','ylo'}, dimensions={0} | all-to-all | bytes 1048576 | tf_op jit(solution)/shard_map/all_to_all | solution.py:184
  51.1 28.7 %all_to_all.26 = bf16[4,4,2,128,256]{4,3,2,1,0:T(8,128)(2,1)S(1)} all-to-all(bf16[4,4,2,128,256]{4,3,2,1,0:T(8,128)(2,1)S(1)} %broadcast_in_dim.11), channel_id=1, replica_groups=mesh['h'=2,'l'=2,'z'=8,'ylo'=2,'x'=4,'core'=2] {'x'}, dimensions={0} | all-to-all | bytes 4194304 | tf_op jit(solution)/shard_map/all_to_all | solution.py:184
  79.8 4.4 %collective-permute-start = (bf16[4,2,2,2,128,256]{5,4,3,2,1,0:T(8,128)(2,1)S(1)}, bf16[4,2,2,2,128,256]{5,4,3,2,1,0:T(8,128)(2,1)}, u32[]{:S(2)}, u32[]{:S(2)}) collective-permute-start(bf16[4,2,2,2,128,256]{5,4,3,2,1,0:T(8,128)(2,1)S(1)} %bitcast.23), channel_id=1, source_target_pairs={{0,1},{1,0},{2,3},{3,2},{4,5},{5,4},{6,7},{7,6},{8,9},{9,8},{10,11... | collective-permute-start | bytes 6291464 | tf_op jit(solution)/shard_map/ppermute | solution.py:210
  84.9 3.2 %collective-permute-done.other_ref = bf16[4,2,2,2,128,256]{5,4,3,2,1,0:T(8,128)(2,1)} collective-permute-done((bf16[4,2,2,2,128,256]{5,4,3,2,1,0:T(8,128)(2,1)S(1)}, bf16[4,2,2,2,128,256]{5,4,3,2,1,0:T(8,128)(2,1)}, u32[]{:S(2)}, u32[]{:S(2)}) %collective-permute-start) | collective-permute-done | bytes 2097184 | tf_op jit(solution)/shard_map/ppermute | solution.py:210
  88.1 6.2 %all-gather.3.cloned.1.call-done = bf16[32,128,512]{2,1,0:T(8,128)(2,1)} async-done(((bf16[4,128,512]{2,1,0:T(8,128)(2,1)}), bf16[32,128,512]{2,1,0:T(8,128)(2,1)}) %all-gather.3.cloned.1.call-update) | async-done | bytes 4194320 | tf_op jit(solution)/shard_map/all_gather | solution.py:202
  94.3 8.8 %shard_map.69 = (bf16[256,384]{1,0:T(8,128)(2,1)}, f32[256,128]{1,0:T(8,128)}, bf16[256,128]{1,0:T(8,128)(2,1)}, bf16[256,128]{1,0:T(8,128)(2,1)}) custom-call(s32[2]{0:T(128)} %pad_add_fusion.place_ref, bf16[4,2,2,2,128,256]{5,4,3,2,1,0:T(8,128)(2,1)} %bitcast.24, bf16[4,2,2,2,128,256]{5,4,3,2,1,0:T(8,128)(2,1)} %collective-permute-done.other_ref, ...), custom_call_target="tpu_custom_call" | custom-call | flops 1073741824 | bytes 9437184 | tf_op jit(solution)/shard_map/pallas_call | solution.py:68
  103.1 1.9 collective-permute-start.1
  105.0 9.2 %collective-permute-start.2 = (bf16[256,128]{1,0:T(8,128)(2,1)}, bf16[256,128]{1,0:T(8,128)(2,1)S(1)}, u32[]{:S(2)}, u32[]{:S(2)}) collective-permute-start(bf16[256,128]{1,0:T(8,128)(2,1)} %get-tuple-element.15.mixed_ref), channel_id=1, source_target_pairs={{16,0},{32,16},{48,32},{64,48},{80,64},{96,80},{112,96},{128,112},... | collective-permute-start | bytes 196616 | tf_op jit(solution)/shard_map/ppermute | solution.py:215
  114.9 2.0 %shard_map.68.band_ref = bf16[16,128,256]{2,1,0:T(8,128)(2,1)} custom-call(f32[16,256]{1,0:T(8,128)} %select_maximum_fusion.base_ref), custom_call_target="tpu_custom_call" | custom-call | tf_op jit(solution)/shard_map/pallas_call | solution.py:32
  117.0 1.2 copy-done.1
  118.2 0.9 copy-done.3
  119.1 0.9 copy-done.4
  121.7 1.0 shard_map.70.terms_ref
  123.4 6.7 %shard_map.72 = bf16[4,2,2,2,128,256]{5,4,3,2,1,0:T(8,128)(2,1)} custom-call(s32[1]{0:T(128)} %bitcast.12.which_ref, bf16[256,512]{1,0:T(8,128)(2,1)} %copy-done.2, bf16[8,4,128,512]{3,2,1,0:T(8,128)(2,1)} %bitcast.21), custom_call_target="tpu_custom_call" | custom-call | flops 536870912 | bytes 4194304 | tf_op jit(solution)/shard_map/pallas_call | solution.py:164
  130.1 2.6 %collective-permute-start.3 = (bf16[4,2,2,2,128,256]{5,4,3,2,1,0:T(8,128)(2,1)}, bf16[4,2,2,2,128,256]{5,4,3,2,1,0:T(8,128)(2,1)S(1)}, u32[]{:S(2)}, u32[]{:S(2)}) collective-permute-start(bf16[4,2,2,2,128,256]{5,4,3,2,1,0:T(8,128)(2,1)} %shard_map.72), channel_id=1, source_target_pairs={{0,1},{1,0},{2,3},{3,2},{4,5},{5,4},{6,7},{7,6},{8,9},{9,8},{10,11... | collective-permute-start | bytes 6291464 | tf_op jit(solution)/shard_map/ppermute | solution.py:220
  132.7 6.7 %shard_map.71 = bf16[4,2,2,2,128,256]{5,4,3,2,1,0:T(8,128)(2,1)} custom-call(s32[1]{0:T(128)} %bitcast.which_ref, bf16[256,512]{1,0:T(8,128)(2,1)} %copy-done.2, bf16[8,4,128,512]{3,2,1,0:T(8,128)(2,1)} %bitcast.22), custom_call_target="tpu_custom_call" | custom-call | flops 536870912 | bytes 4194304 | tf_op jit(solution)/shard_map/pallas_call | solution.py:164
  139.4 2.3 %add_convert_fusion = bf16[4,2,2,2,128,256]{5,4,3,2,1,0:T(8,128)(2,1)S(1)} fusion(bf16[4,2,2,2,128,256]{5,4,3,2,1,0:T(8,128)(2,1)S(1)} %collective-permute-done.3, bf16[4,2,2,2,128,256]{5,4,3,2,1,0:T(8,128)(2,1)} %shard_map.71), kind=kLoop, calls=%fused_computation | loop fusion | flops 4194304 | bytes 6291456 | tf_op jit(solution)/shard_map/convert_element_type | solution.py:221
  141.8 28.7 %all_to_all.27 = bf16[4,2,2,2,128,256]{5,4,3,2,1,0:T(8,128)(2,1)S(1)} all-to-all(bf16[4,2,2,2,128,256]{5,4,3,2,1,0:T(8,128)(2,1)S(1)} %add_convert_fusion), channel_id=1, replica_groups=mesh['h'=2,'l'=2,'z'=8,'ylo'=2,'x'=4,'core'=2] {'x'}, dimensions={0} | all-to-all | bytes 4194304 | tf_op jit(solution)/shard_map/all_to_all | solution.py:184
  170.8 19.1 %all_to_all.28 = bf16[4,2,128,256]{3,2,1,0:T(8,128)(2,1)S(1)} all-to-all(bf16[4,2,128,256]{3,2,1,0:T(8,128)(2,1)S(1)} %bitcast.25), channel_id=1, replica_groups=mesh['h'=2,'l'=2,'z'=8,'ylo'=2,'x'=4,'core'=2] {'h','ylo'}, dimensions={0} | all-to-all | bytes 1048576 | tf_op jit(solution)/shard_map/all_to_all | solution.py:184
  (40 shorter events, 6.2 us)
Async XLA Ops:
  7.2 77.7 %copy-start = (f32[16,128]{1,0:T(8,128)S(1)}, f32[16,128]{1,0:T(8,128)}, u32[]{:S(2)}) copy-start(f32[16,128]{1,0:T(8,128)} %param.8) | copy-start | bytes 24580
  7.2 10.7 %copy-start.11 = (bf16[128,256]{1,0:T(8,128)(2,1)S(1)}, bf16[128,256]{1,0:T(8,128)(2,1)}, u32[]{:S(2)}) copy-start(bf16[128,256]{1,0:T(8,128)(2,1)} %param.5) | copy-start | bytes 196612
  7.2 10.7 %copy-start.10 = (bf16[128,256]{1,0:T(8,128)(2,1)S(1)}, bf16[128,256]{1,0:T(8,128)(2,1)}, u32[]{:S(2)}) copy-start(bf16[128,256]{1,0:T(8,128)(2,1)} %param.9) | copy-start | bytes 196612
  10.2 21.9 %all-to-all-start = ((bf16[4,128,512]{2,1,0:T(8,128)(2,1)}), bf16[4,128,512]{2,1,0:T(8,128)(2,1)S(1)}, u32[]{:S(2)}, u32[]{:S(2)}) async-start(bf16[4,128,512]{2,1,0:T(8,128)(2,1)} %bitcast.7), calls=%async_computation | async-start | bytes 1048576 | tf_op jit(solution)/shard_map/all_to_all | solution.py:184
  17.9 76.5 %all-gather.3.cloned.1.call-start = ((), (), s32[]{:S(2)}) async-start(), calls=%async_computation.5 | async-start | bytes 4718592 | tf_op jit(solution)/shard_map/all_gather | solution.py:202
  32.1 0.8 copy-start.9
  79.8 14.5 %copy-start.8 = (bf16[4,4,2,128,256]{4,3,2,1,0:T(8,128)(2,1)}, bf16[4,4,2,128,256]{4,3,2,1,0:T(8,128)(2,1)S(1)}, u32[]{:S(2)}) copy-start(bf16[4,4,2,128,256]{4,3,2,1,0:T(8,128)(2,1)S(1)} %all_to_all.26) | copy-start | bytes 6291460
  79.8 8.3 %collective-permute-start = (bf16[4,2,2,2,128,256]{5,4,3,2,1,0:T(8,128)(2,1)S(1)}, bf16[4,2,2,2,128,256]{5,4,3,2,1,0:T(8,128)(2,1)}, u32[]{:S(2)}, u32[]{:S(2)}) collective-permute-start(bf16[4,2,2,2,128,256]{5,4,3,2,1,0:T(8,128)(2,1)S(1)} %bitcast.23), channel_id=1, source_target_pairs={{0,1},{1,0},{2,3},{3,2},{4,5},{5,4},{6,7},{7,6},{8,9},{9,8},{10,11... | collective-permute-start | bytes 6291464 | tf_op jit(solution)/shard_map/ppermute | solution.py:210
  94.3 22.7 %copy-start.7 = (s32[2]{0:T(128)S(1)}, s32[2]{0:T(128)}, u32[]{:S(2)}) copy-start(s32[2]{0:T(128)} %pad_add_fusion.place_ref) | copy-start | bytes 28
  103.1 13.9 %collective-permute-start.1 = (bf16[256,128]{1,0:T(8,128)(2,1)}, bf16[256,128]{1,0:T(8,128)(2,1)S(1)}, u32[]{:S(2)}, u32[]{:S(2)}) collective-permute-start(bf16[256,128]{1,0:T(8,128)(2,1)} %get-tuple-element.14.product_ref), channel_id=1, source_target_pairs={{0,16},{16,32},{32,48},{48,64},{64,80},{80,96},{96,112},{112,128},... | collective-permute-start | bytes 196616 | tf_op jit(solution)/shard_map/ppermute | solution.py:214
  105.0 12.0 %collective-permute-start.2 = (bf16[256,128]{1,0:T(8,128)(2,1)}, bf16[256,128]{1,0:T(8,128)(2,1)S(1)}, u32[]{:S(2)}, u32[]{:S(2)}) collective-permute-start(bf16[256,128]{1,0:T(8,128)(2,1)} %get-tuple-element.15.mixed_ref), channel_id=1, source_target_pairs={{16,0},{32,16},{48,32},{64,48},{80,64},{96,80},{112,96},{128,112},... | collective-permute-start | bytes 196616 | tf_op jit(solution)/shard_map/ppermute | solution.py:215
  117.0 1.2 copy-start.1
  118.2 0.9 copy-start.3
  119.1 0.9 copy-start.4
  120.0 0.8 copy-start.5
  120.9 0.8 copy-start.6
  122.7 0.7 copy-start.2
  130.1 9.3 %collective-permute-start.3 = (bf16[4,2,2,2,128,256]{5,4,3,2,1,0:T(8,128)(2,1)}, bf16[4,2,2,2,128,256]{5,4,3,2,1,0:T(8,128)(2,1)S(1)}, u32[]{:S(2)}, u32[]{:S(2)}) collective-permute-start(bf16[4,2,2,2,128,256]{5,4,3,2,1,0:T(8,128)(2,1)} %shard_map.72), channel_id=1, source_target_pairs={{0,1},{1,0},{2,3},{3,2},{4,5},{5,4},{6,7},{7,6},{8,9},{9,8},{10,11... | collective-permute-start | bytes 6291464 | tf_op jit(solution)/shard_map/ppermute | solution.py:220
Sparse Core Ops, SparseCore 0:
  33.1 61.1 all-gather.2

commit v2 on v1

v2 whole, which is shorter than its diff:
```python
import jax
import jax.numpy as jnp
from jax import lax
from jax.experimental import pallas as pl
from jax.experimental.pallas import tpu as pltpu
from jax.sharding import Mesh, PartitionSpec as P

AXES = ("h", "l", "z", "ylo", "x", "core")
SIZES = (2, 2, 8, 2, 4, 2)
ROWS = 128
HALF = 128
TAPS = 128
GROUP = 16
GROUPS = HALF // GROUP
FEATURES = 256
STREAMS = 4 * HALF
BACK = 3 * HALF
BF16 = jnp.bfloat16
F32 = jnp.float32


def bands_kernel(base_ref, band_ref):
    for row in range(2 * GROUPS):
        spread = jnp.broadcast_to(base_ref[row : row + 1, :], (2 * ROWS, 2 * ROWS))
        rolled = pltpu.roll(spread, 0, 1, stride=1, stride_axis=0)
        band_ref[:, row * ROWS : (row + 1) * ROWS] = rolled[:, :ROWS].astype(BF16)


def bands(filters):
    zeros = jnp.zeros((GROUPS, TAPS), filters.dtype)
    causal = jnp.concatenate([zeros, filters], 1)
    anticausal = jnp.concatenate([filters[:, :1], zeros, filters[:, :0:-1]], 1)
    return pl.pallas_call(
        bands_kernel,
        out_shape=jax.ShapeDtypeStruct((2 * ROWS, 2 * GROUPS * ROWS), BF16),
    )(jnp.concatenate([causal, anticausal], 0))


def forward_kernel(place_ref, own_ref, other_ref, weight_ref, streams_ref, gate_ref, product_ref, mixed_ref, total):
    step = pl.program_id(0)
    core = place_ref[0]

    @pl.when(step == 0)
    def _():
        total[...] = jnp.zeros_like(total)

    tokens, cotangent, weight = [], [], []
    for values_ref, which in ((own_ref, core), (other_ref, 1 - core)):
        for y in range(2):
            tokens.append(values_ref[0, :, y, 0].reshape(2 * ROWS, FEATURES))
            cotangent.append(values_ref[0, :, y, 1].reshape(2 * ROWS, FEATURES))
            weight.append(weight_ref[pl.ds(2 * which, 2), y, 0].reshape(FEATURES, STREAMS))
    tokens, cotangent = jnp.concatenate(tokens, 1), jnp.concatenate(cotangent, 1)
    weight = jnp.concatenate(weight, 0)
    total[:, :BACK] += jnp.dot(tokens, weight[:, :BACK], preferred_element_type=F32)
    total[:, BACK:] += jnp.dot(cotangent, weight[:, BACK:], preferred_element_type=F32)

    @pl.when(step == pl.num_programs(0) - 1)
    def _():
        turned = total[...].T
        streams = turned[:BACK].astype(BF16)
        streams_ref[...] = streams
        grad_gate = turned[BACK:]
        gate_ref[...] = grad_gate
        query, key, value = (streams[i * HALF : (i + 1) * HALF].astype(F32) for i in range(3))
        product_ref[...] = (key * value).astype(BF16)
        mixed_ref[...] = (grad_gate * query).astype(BF16)


def forward(place, own, other, weight):
    values = pl.BlockSpec((1, 2, 2, 2, ROWS, FEATURES), lambda j, p: (j, 0, 0, 0, 0, 0))
    whole = lambda height: pl.BlockSpec((height, 2 * ROWS), lambda j, p: (0, 0))
    shape = lambda height, kind: jax.ShapeDtypeStruct((height, 2 * ROWS), kind)
    return pl.pallas_call(
        forward_kernel,
        out_shape=(shape(BACK, BF16), shape(HALF, F32), shape(HALF, BF16), shape(HALF, BF16)),
        grid_spec=pltpu.PrefetchScalarGridSpec(
            num_scalar_prefetch=1,
            grid=(4,),
            in_specs=[
                values,
                values,
                pl.BlockSpec((4, 2, 1, ROWS, STREAMS), lambda j, p: (j % 2, 0, j // 2, 0, 0)),
            ],
            out_specs=[whole(BACK), whole(HALF), whole(HALF), whole(HALF)],
            scratch_shapes=[pltpu.VMEM((2 * ROWS, STREAMS), F32)],
        ),
        compiler_params=pltpu.CompilerParams(vmem_limit_bytes=24 << 20),
        cost_estimate=pl.CostEstimate(flops=1 << 30, bytes_accessed=9 << 20, transcendentals=0),
    )(place, own, other, weight)


def filtered(left, right, band):
    segments = [
        jnp.concatenate([left[s], right[s]], 1) for s in range(2)
    ]
    result = jnp.dot(jnp.concatenate(segments, 0), band, preferred_element_type=F32)
    return [
        jnp.concatenate(
            [
                result[s * HALF + g * GROUP : s * HALF + (g + 1) * GROUP, g * ROWS : (g + 1) * ROWS]
                for g in range(GROUPS)
            ],
            0,
        )
        for s in range(2)
    ]


def middle(position, band_ref, streams_ref, gate_ref, product_ref, mixed_ref, before_ref, after_ref, terms_ref):
    first = position == 0
    last = position == 15
    lanes = [slice(s * ROWS, (s + 1) * ROWS) for s in range(2)]
    product, mixed, before, after = (
        [ref[:, lanes[s]] for s in range(2)] for ref in (product_ref, mixed_ref, before_ref, after_ref)
    )
    zero = jnp.zeros_like(before[0])
    earlier = [jnp.where(first, zero, before[0]), jnp.where(first, before[0], before[1])]
    later = [jnp.where(last, after[1], after[0]), jnp.where(last, zero, after[1])]
    conv = filtered(earlier, product, band_ref[:, : GROUPS * ROWS])
    back = filtered(mixed, later, band_ref[:, GROUPS * ROWS :])
    for s in range(2):
        query, key, value = (
            streams_ref[i * HALF : (i + 1) * HALF, lanes[s]].astype(F32) for i in range(3)
        )
        terms_ref[:HALF, lanes[s]] = (gate_ref[:, lanes[s]] * conv[s]).astype(BF16)
        terms_ref[HALF : 2 * HALF, lanes[s]] = (back[s] * value).astype(BF16)
        terms_ref[2 * HALF : BACK, lanes[s]] = (back[s] * key).astype(BF16)
        terms_ref[BACK:, lanes[s]] = (query * conv[s]).astype(BF16)


def halves(result):
    return result[:, :ROWS], result[:, ROWS:]


def mixed_far_kernel(
    place_ref, band_ref, streams_ref, gate_ref, product_ref, mixed_ref, before_ref, after_ref, weight_ref, terms_ref, out_ref
):
    @pl.when(pl.program_id(0) == 0)
    def _():
        middle(
            place_ref[1], band_ref, streams_ref, gate_ref, product_ref, mixed_ref, before_ref, after_ref, terms_ref
        )

    gating = terms_ref[BACK:]
    for y in range(2):
        weight = weight_ref[:, y, 0].reshape(FEATURES, HALF)
        for h, part in enumerate(halves(jnp.dot(weight, gating, preferred_element_type=F32))):
            out_ref[0, h, y] = part.astype(BF16)


def out_weight_spec(core):
    return pl.BlockSpec((2, 2, 1, ROWS, HALF), lambda j, p: ((j % 2) * 2 + core(p), 0, j // 2, 0, 3))


def in_weight_spec(core):
    return pl.BlockSpec((2, 2, 1, ROWS, BACK), lambda j, p: ((j % 2) * 2 + core(p), 0, j // 2, 0, 0))


MIXED_SHAPE = (4, 2, 2, FEATURES, ROWS)
MIXED_SPEC = pl.BlockSpec((1, 2, 2, FEATURES, ROWS), lambda j, p: (j, 0, 0, 0, 0))
GRAD_SHAPE = (2, 2, 4, FEATURES, ROWS)
GRAD_SPEC = pl.BlockSpec((2, 2, 1, FEATURES, ROWS), lambda j, p: (0, 0, j, 0, 0))
TERMS_SPEC = pl.BlockSpec((STREAMS, 2 * ROWS), lambda j, p: (0, 0))


def mixed_far(place, band, streams, gate, product, mixed, before, after, weight):
    flat = lambda value: pl.BlockSpec(value.shape, lambda j, p: (0, 0))
    operands = (band, streams, gate, product, mixed, before, after)
    return pl.pallas_call(
        mixed_far_kernel,
        out_shape=(
            jax.ShapeDtypeStruct((STREAMS, 2 * ROWS), BF16),
            jax.ShapeDtypeStruct(MIXED_SHAPE, BF16),
        ),
        grid_spec=pltpu.PrefetchScalarGridSpec(
            num_scalar_prefetch=1,
            grid=(4,),
            in_specs=[flat(value) for value in operands] + [out_weight_spec(lambda p: 1 - p[0])],
            out_specs=[TERMS_SPEC, MIXED_SPEC],
        ),
        compiler_params=pltpu.CompilerParams(vmem_limit_bytes=24 << 20),
        cost_estimate=pl.CostEstimate(flops=1 << 28, bytes_accessed=4 << 20, transcendentals=0),
    )(place, *operands, weight)


def mixed_near_kernel(place_ref, terms_ref, weight_ref, far_ref, out_ref):
    gating = terms_ref[BACK:]
    for y in range(2):
        weight = weight_ref[:, y, 0].reshape(FEATURES, HALF)
        for h, part in enumerate(halves(jnp.dot(weight, gating, preferred_element_type=F32))):
            out_ref[0, h, y] = (part + far_ref[0, h, y].astype(F32)).astype(BF16)


def mixed_near(place, terms, weight, far):
    return pl.pallas_call(
        mixed_near_kernel,
        out_shape=jax.ShapeDtypeStruct(MIXED_SHAPE, BF16),
        grid_spec=pltpu.PrefetchScalarGridSpec(
            num_scalar_prefetch=1,
            grid=(4,),
            in_specs=[TERMS_SPEC, out_weight_spec(lambda p: p[0]), MIXED_SPEC],
            out_specs=MIXED_SPEC,
        ),
        cost_estimate=pl.CostEstimate(flops=1 << 27, bytes_accessed=3 << 20, transcendentals=0),
    )(place, terms, weight, far)


def grad_far_kernel(place_ref, terms_ref, weight_ref, out_ref):
    for y in range(2):
        weight = weight_ref[:, y, 0].reshape(FEATURES, BACK)
        for h, part in enumerate(halves(jnp.dot(weight, terms_ref[:BACK], preferred_element_type=F32))):
            out_ref[h, y, 0] = part.astype(BF16)


def grad_near_kernel(place_ref, terms_ref, weight_ref, far_ref, out_ref):
    for y in range(2):
        weight = weight_ref[:, y, 0].reshape(FEATURES, BACK)
        for h, part in enumerate(halves(jnp.dot(weight, terms_ref[:BACK], preferred_element_type=F32))):
            out_ref[h, y, 0] = (part + far_ref[h, y, 0].astype(F32)).astype(BF16)


def grad_part(place, terms, weight, far=None):
    near = far is not None
    core = (lambda p: p[0]) if near else (lambda p: 1 - p[0])
    return pl.pallas_call(
        grad_near_kernel if near else grad_far_kernel,
        out_shape=jax.ShapeDtypeStruct(GRAD_SHAPE, BF16),
        grid_spec=pltpu.PrefetchScalarGridSpec(
            num_scalar_prefetch=1,
            grid=(4,),
            in_specs=[TERMS_SPEC, in_weight_spec(core)] + [GRAD_SPEC] * near,
            out_specs=GRAD_SPEC,
        ),
        cost_estimate=pl.CostEstimate(flops=1 << 28, bytes_accessed=4 << 20, transcendentals=0),
    )(place, terms, weight, *([far] if near else []))


def swapped(value, axes):
    return lax.all_to_all(value, axes, 0, 0, tiled=True)


def gathered(value, axes, count):
    return swapped(jnp.broadcast_to(value[None], (count,) + value.shape), axes)


def reduced(value, axes):
    return swapped(value, axes).astype(F32).sum(0).astype(BF16)


def local(tokens, in_weight, out_weight, mr_filter, cotangent):
    half, core = lax.axis_index("h"), lax.axis_index("core")
    position = lax.axis_index(("l", "z"))
    place = jnp.stack([core, position]).astype(jnp.int32)

    weight = jnp.concatenate([in_weight, out_weight.T[None]], 0)
    weight = weight.reshape(4, ROWS, 2, HALF).transpose(2, 1, 0, 3).reshape(2, 1, ROWS, STREAMS)
    weight = jnp.broadcast_to(weight, (2, 2, ROWS, STREAMS)).reshape(4, ROWS, STREAMS)
    weight = swapped(weight, ("h", "l"))
    values = jnp.stack([tokens, cotangent], 0)
    weight, values = lax.optimization_barrier((weight, values))
    weight = lax.all_gather(weight, "z", axis=0).reshape(8, 2, 2, ROWS, STREAMS)

    band = bands(lax.dynamic_slice_in_dim(mr_filter, half * GROUPS, GROUPS, 0))
    values = gathered(values, ("h", "ylo"), 4)
    values = gathered(values, "x", 4).reshape(4, 2, 2, 2, ROWS, FEATURES)
    values, band = lax.optimization_barrier((values, band))
    cross = [(0, 1), (1, 0)]
    other = lax.ppermute(values, "core", cross)

    streams, gate, product, mixed = forward(place, values, other, weight)
    ring = [(n, (n + 1) % 16) for n in range(16)]
    before = lax.ppermute(product, ("l", "z"), ring)
    after = lax.ppermute(mixed, ("l", "z"), [(b, a) for a, b in ring])

    terms, far_mixed = mixed_far(place, band, streams, gate, product, mixed, before, after, weight)
    far_mixed = lax.ppermute(far_mixed, "core", cross)
    far_grad = lax.ppermute(grad_part(place, terms, weight), "core", cross)
    mixed_sum = mixed_near(place, terms, weight, far_mixed)
    grad_sum = grad_part(place, terms, weight, far_grad)
    mixed_sum = reduced(mixed_sum, "x").reshape(4, FEATURES, ROWS)
    grad_sum = reduced(grad_sum.reshape(4, 4, FEATURES, ROWS), ("h", "ylo"))
    mixed_sum = reduced(mixed_sum, ("h", "ylo"))
    grad_sum = reduced(grad_sum, "x")
    return mixed_sum.T, grad_sum.T


def solution(mesh):
    fine = Mesh(mesh.devices.reshape(SIZES), AXES)
    ctx, tp = AXES[:3], AXES[3:]
    return jax.shard_map(
        local,
        mesh=fine,
        in_specs=(P(ctx, tp), P(None, ctx, tp), P(tp, ctx), P(tp, None), P(ctx, tp)),
        out_specs=(P(ctx, tp), P(ctx, tp)),
        check_vma=False,
    )
```

time: 201 us -> 214 us (1.065)
  blocking collectives: 94.3 us -> 17.9 us
  waiting for transfers between devices: 23.6 us -> 91.3 us
  starting transfers between devices: 25.8 us -> 50.6 us
    all_to_all x4 -> x1, blocking collectives: 94.3 us -> 17.9 us  [swapped(): return lax.all_to_all(value, axes, 0, 0, tiled=True)]
    all_to_all x1 -> x6, waiting for transfers between devices: 14.2 us -> 81.5 us  [swapped(): return lax.all_to_all(value, axes, 0, 0, tiled=True)]
    all_to_all x1 -> x6, starting transfers between devices: 7.64 us -> 28.4 us  [swapped(): return lax.all_to_all(value, axes, 0, 0, tiled=True)]
    ppermute x1 -> x2, starting transfers between devices: 2.55 us -> 5.04 us  [the longest x1 3.13 us: local(): far_mixed = lax.ppermute(far_mixed, 'core', cross)]
    convert_element_type x1 -> x0, other arithmetic: 2.34 us -> none  [local(): (near.astype(jnp.float32) + far.astype(jnp.float32)).astype(jnp.bfloat16)]
    pallas_call x5 -> x6, Pallas kernels: 25.2 us -> 23.6 us  [the longest x2 9.76 us: grad_part(): pl.pallas_call(grad_near_kernel if near else grad_far_kernel, out_shape=j...]
  transfers between devices with their start and end apart: 6 -> 12, of which waited for: 3 -> 10; matrix products, arithmetic and copies ran while one was open for 1% -> 2% of each run, Pallas kernels for 4% -> 8%
where the time goes in v2:
time: 214 us; the launch traced here: 212 us
  waiting for transfers between devices  91.3 us (43%)
  starting transfers between devices  50.6 us (24%)
  Pallas kernels  23.6 us (11%)
  blocking collectives  17.9 us (8%)
  between operations  14.2 us (7%)
  local copies, waits for them, and re-layouts  11 us (5%)
  other arithmetic  3.52 us (2%)
    all_to_all x6, waiting for transfers between devices, swapped(): return lax.all_to_all(value, axes, 0, 0, tiled=True)  81.5 us
    all_to_all x6, starting transfers between devices, swapped(): return lax.all_to_all(value, axes, 0, 0, tiled=True)  28.4 us
    all_to_all x1, blocking collectives, swapped(): return lax.all_to_all(value, axes, 0, 0, tiled=True)  17.9 us
    ppermute x1, starting transfers between devices, local(): after = lax.ppermute(mixed, ('l', 'z'), [(b, a) for a, b in ring])  10.8 us
    pallas_call x2, Pallas kernels, grad_part(): pl.pallas_call(grad_near_kernel if near else grad_far_kernel, out_shape=j...  9.76 us
    unnamed x25, local copies, waits for them, and re-layouts  8.25 us
    pallas_call x1, Pallas kernels, forward(): pl.pallas_call(forward_kernel, out_shape=(shape(BACK, BF16), shape(HALF,...  5.03 us
    pallas_call x1, Pallas kernels, mixed_near(): pl.pallas_call(mixed_near_kernel, out_shape=jax.ShapeDtypeStruct(MIXED_SH...  4.7 us
  transfers between devices with their start and end apart: 12, of which 10 were waited for; matrix products, arithmetic and copies ran while one was open for 2% of the time, Pallas kernels for 8%

profile of v2, /device:TPU:1, one launch (start us, length us, event | category | flops | bytes accessed | tf_op | source)
XLA Modules:
  0.0 212.2 jit_solution(7797758097224219194)
XLA Ops:
  10.2 7.6 %all-to-all-start = ((bf16[4,128,512]{2,1,0:T(8,128)(2,1)}), bf16[4,128,512]{2,1,0:T(8,128)(2,1)S(1)}, u32[]{:S(2)}, u32[]{:S(2)}) async-start(bf16[4,128,512]{2,1,0:T(8,128)(2,1)} %bitcast.7), calls=%async_computation | async-start | bytes 1048576 | tf_op jit(solution)/shard_map/all_to_all | solution.py:240
  17.9 14.2 %all-to-all-done = bf16[4,128,512]{2,1,0:T(8,128)(2,1)S(1)} async-done(((bf16[4,128,512]{2,1,0:T(8,128)(2,1)}), bf16[4,128,512]{2,1,0:T(8,128)(2,1)S(1)}, u32[]{:S(2)}, u32[]{:S(2)}) %all-to-all-start) | async-done | bytes 524320 | tf_op jit(solution)/shard_map/all_to_all | solution.py:240
  33.0 17.9 %all_to_all.35 = bf16[4,2,128,256]{3,2,1,0:T(8,128)(2,1)S(1)} all-to-all(bf16[4,2,128,256]{3,2,1,0:T(8,128)(2,1)S(1)} %broadcast_in_dim.12), channel_id=1, replica_groups=mesh['h'=2,'l'=2,'z'=8,'ylo'=2,'x'=4,'core'=2] {'h','ylo'}, dimensions={0} | all-to-all | bytes 1048576 | tf_op jit(solution)/shard_map/all_to_all | solution.py:240
  52.4 4.1 %all-to-all-start.2 = ((bf16[4,4,2,128,256]{4,3,2,1,0:T(8,128)(2,1)}), bf16[4,4,2,128,256]{4,3,2,1,0:T(8,128)(2,1)S(1)}, u32[]{:S(2)}, u32[]{:S(2)}) async-start(bf16[4,4,2,128,256]{4,3,2,1,0:T(8,128)(2,1)} %broadcast_in_dim.26), calls=%async_computation.2 | async-start | bytes 4194304 | tf_op jit(solution)/shard_map/all_to_all | solution.py:240
  59.5 21.8 %all-to-all-done.2 = bf16[4,4,2,128,256]{4,3,2,1,0:T(8,128)(2,1)S(1)} async-done(((bf16[4,4,2,128,256]{4,3,2,1,0:T(8,128)(2,1)}), bf16[4,4,2,128,256]{4,3,2,1,0:T(8,128)(2,1)S(1)}, u32[]{:S(2)}, u32[]{:S(2)}) %all-to-all-start.2) | async-done | bytes 2097184 | tf_op jit(solution)/shard_map/all_to_all | solution.py:240
  81.3 4.4 %collective-permute-start = (bf16[4,2,2,2,128,256]{5,4,3,2,1,0:T(8,128)(2,1)S(1)}, bf16[4,2,2,2,128,256]{5,4,3,2,1,0:T(8,128)(2,1)}, u32[]{:S(2)}, u32[]{:S(2)}) collective-permute-start(bf16[4,2,2,2,128,256]{5,4,3,2,1,0:T(8,128)(2,1)S(1)} %bitcast.24), channel_id=1, source_target_pairs={{0,1},{1,0},{2,3},{3,2},{4,5},{5,4},{6,7},{7,6},{8,9},{9,8},{10,11... | collective-permute-start | bytes 6291464 | tf_op jit(solution)/shard_map/ppermute | solution.py:269
  85.8 3.8 %collective-permute-done.other_ref = bf16[4,2,2,2,128,256]{5,4,3,2,1,0:T(8,128)(2,1)} collective-permute-done((bf16[4,2,2,2,128,256]{5,4,3,2,1,0:T(8,128)(2,1)S(1)}, bf16[4,2,2,2,128,256]{5,4,3,2,1,0:T(8,128)(2,1)}, u32[]{:S(2)}, u32[]{:S(2)}) %collective-permute-start) | collective-permute-done | bytes 2097184 | tf_op jit(solution)/shard_map/ppermute | solution.py:269
  89.6 4.6 %all-gather.3.cloned.1.call-done = bf16[32,128,512]{2,1,0:T(8,128)(2,1)} async-done(((bf16[4,128,512]{2,1,0:T(8,128)(2,1)}), bf16[32,128,512]{2,1,0:T(8,128)(2,1)}) %all-gather.3.cloned.1.call-update) | async-done | bytes 4194320 | tf_op jit(solution)/shard_map/all_gather | solution.py:262
  94.3 2.2 %copy-done.1 = bf16[32,128,512]{2,1,0:T(8,128)(2,1)S(1)} copy-done((bf16[32,128,512]{2,1,0:T(8,128)(2,1)S(1)}, bf16[32,128,512]{2,1,0:T(8,128)(2,1)}, u32[]{:S(2)}) %copy-start.1) | copy-done | bytes 4194328
  96.5 5.0 %shard_map.69 = (bf16[384,256]{1,0:T(8,128)(2,1)S(1)}, f32[128,256]{1,0:T(8,128)S(1)}, bf16[128,256]{1,0:T(8,128)(2,1)S(1)}, bf16[128,256]{1,0:T(8,128)(2,1)S(1)}) custom-call(s32[2]{0:T(128)S(1)} %pad_add_fusion.place_ref, bf16[4,2,2,2,128,256]{5,4,3,2,1,0:T(8,128)(2,1)S(1)} %bitcast.25, bf16[4,2,2,2,128,256]{5,4,3,2,1,0:T(8,128)(2,1)} %collective-permute-done.other_ref, ...), custom_call_target="tpu_custom_call" | custom-call | flops 1073741824 | bytes 9437184 | tf_op jit(solution)/shard_map/pallas_call | solution.py:74
  103.4 10.8 %collective-permute-start.2 = (bf16[128,256]{1,0:T(8,128)(2,1)S(1)}, bf16[128,256]{1,0:T(8,128)(2,1)S(1)}, u32[]{:S(2)}, u32[]{:S(2)}) collective-permute-start(bf16[128,256]{1,0:T(8,128)(2,1)S(1)} %get-tuple-element.19.mixed_ref), channel_id=1, source_target_pairs={{16,0},{32,16},{48,32},{64,48},{80,64},{96,80},{112,96},{128,112},... | collective-permute-start | bytes 196616 | tf_op jit(solution)/shard_map/ppermute | solution.py:274
  115.5 2.1 shard_map.70
  118.3 3.1 %collective-permute-start.3 = (bf16[4,2,2,256,128]{4,3,2,1,0:T(8,128)(2,1)S(1)}, bf16[4,2,2,256,128]{4,3,2,1,0:T(8,128)(2,1)S(1)}, u32[]{:S(2)}, u32[]{:S(2)}) collective-permute-start(bf16[4,2,2,256,128]{4,3,2,1,0:T(8,128)(2,1)S(1)} %get-tuple-element.21), channel_id=1, source_target_pairs={{0,1},{1,0},{2,3},{3,2},{4,5},{5,4},{6,7},{7,6},{8,9},{9,8},{10,11... | collective-permute-start | bytes 3145736 | tf_op jit(solution)/shard_map/ppermute | solution.py:277
  121.5 4.8 %shard_map.72 = bf16[2,2,4,256,128]{4,3,2,1,0:T(8,128)(2,1)} custom-call(s32[2]{0:T(128)} %copy-done.5, bf16[512,256]{1,0:T(8,128)(2,1)} %copy-done.4, bf16[8,2,2,128,512]{4,3,2,1,0:T(8,128)(2,1)} %bitcast.19), custom_call_target="tpu_custom_call" | custom-call | flops 268435456 | bytes 4194304 | tf_op jit(solution)/shard_map/pallas_call | solution.py:226
  129.2 4.7 %shard_map.71 = bf16[4,2,2,256,128]{4,3,2,1,0:T(8,128)(2,1)} custom-call(s32[2]{0:T(128)} %copy-done.5, bf16[512,256]{1,0:T(8,128)(2,1)} %copy-done.4, bf16[8,2,2,128,512]{4,3,2,1,0:T(8,128)(2,1)} %bitcast.20, bf16[4,2,2,256,128]{4,3,2,1,0:T(8,128)(2,1)} %copy-done.8), custom_call_target="tpu_custom_call" | custom-call | flops 134217728 | bytes 3145728 | tf_op jit(solution)/shard_map/pallas_call | solution.py:196
  133.9 3.5 %all-to-all-start.3 = ((bf16[4,2,2,256,128]{4,3,2,1,0:T(8,128)(2,1)}), bf16[4,2,2,256,128]{4,3,2,1,0:T(8,128)(2,1)S(1)}, u32[]{:S(2)}, u32[]{:S(2)}) async-start(bf16[4,2,2,256,128]{4,3,2,1,0:T(8,128)(2,1)} %shard_map.71), calls=%async_computation.3 | async-start | bytes 2097152 | tf_op jit(solution)/shard_map/all_to_all | solution.py:240
  138.4 5.0 %shard_map.73 = bf16[2,2,4,256,128]{4,3,2,1,0:T(8,128)(2,1)} custom-call(s32[2]{0:T(128)} %copy-done.5, bf16[512,256]{1,0:T(8,128)(2,1)} %copy-done.4, bf16[8,2,2,128,512]{4,3,2,1,0:T(8,128)(2,1)} %bitcast.21, bf16[2,2,4,256,128]{4,3,2,1,0:T(8,128)(2,1)} %copy-done.7), custom_call_target="tpu_custom_call" | custom-call | flops 268435456 | bytes 4194304 | tf_op jit(solution)/shard_map/pallas_call | solution.py:226
  143.3 8.7 %all-to-all-done.3 = bf16[4,2,2,256,128]{4,3,2,1,0:T(8,128)(2,1)S(1)} async-done(((bf16[4,2,2,256,128]{4,3,2,1,0:T(8,128)(2,1)}), bf16[4,2,2,256,128]{4,3,2,1,0:T(8,128)(2,1)S(1)}, u32[]{:S(2)}, u32[]{:S(2)}) %all-to-all-start.3) | async-done | bytes 1048608 | tf_op jit(solution)/shard_map/all_to_all | solution.py:240
  152.0 3.5 %all-to-all-start.5 = ((bf16[4,4,256,128]{3,2,1,0:T(8,128)(2,1)}), bf16[4,4,256,128]{3,2,1,0:T(8,128)(2,1)S(1)}, u32[]{:S(2)}, u32[]{:S(2)}) async-start(bf16[4,4,256,128]{3,2,1,0:T(8,128)(2,1)} %bitcast.26), calls=%async_computation.5 | async-start | bytes 2097152 | tf_op jit(solution)/shard_map/all_to_all | solution.py:240
  156.5 23.3 %all-to-all-done.5 = bf16[4,4,256,128]{3,2,1,0:T(8,128)(2,1)S(1)} async-done(((bf16[4,4,256,128]{3,2,1,0:T(8,128)(2,1)}), bf16[4,4,256,128]{3,2,1,0:T(8,128)(2,1)S(1)}, u32[]{:S(2)}, u32[]{:S(2)}) %all-to-all-start.5) | async-done | bytes 1048608 | tf_op jit(solution)/shard_map/all_to_all | solution.py:240
  179.8 6.3 %all-to-all-start.4 = ((bf16[4,256,128]{2,1,0:T(8,128)(2,1)}), bf16[4,256,128]{2,1,0:T(8,128)(2,1)S(1)}, u32[]{:S(2)}, u32[]{:S(2)}) async-start(bf16[4,256,128]{2,1,0:T(8,128)(2,1)} %bitcast.12), calls=%async_computation.4 | async-start | bytes 524288 | tf_op jit(solution)/shard_map/all_to_all | solution.py:240
  186.9 8.7 %all-to-all-done.4 = bf16[4,256,128]{2,1,0:T(8,128)(2,1)S(1)} async-done(((bf16[4,256,128]{2,1,0:T(8,128)(2,1)}), bf16[4,256,128]{2,1,0:T(8,128)(2,1)S(1)}, u32[]{:S(2)}, u32[]{:S(2)}) %all-to-all-start.4) | async-done | bytes 262176 | tf_op jit(solution)/shard_map/all_to_all | solution.py:240
  195.7 3.4 %all-to-all-start.6 = ((bf16[4,256,128]{2,1,0:T(8,128)(2,1)}), bf16[4,256,128]{2,1,0:T(8,128)(2,1)S(1)}, u32[]{:S(2)}, u32[]{:S(2)}) async-start(bf16[4,256,128]{2,1,0:T(8,128)(2,1)} %reduce_sum.50), calls=%async_computation.6 | async-start | bytes 524288 | tf_op jit(solution)/shard_map/all_to_all | solution.py:240
  199.9 4.7 %all-to-all-done.6 = bf16[4,256,128]{2,1,0:T(8,128)(2,1)S(1)} async-done(((bf16[4,256,128]{2,1,0:T(8,128)(2,1)}), bf16[4,256,128]{2,1,0:T(8,128)(2,1)S(1)}, u32[]{:S(2)}, u32[]{:S(2)}) %all-to-all-start.6) | async-done | bytes 262176 | tf_op jit(solution)/shard_map/all_to_all | solution.py:240
  (50 shorter events, 19.6 us)
Async XLA Ops:
  7.2 49.4 %copy-start = (f32[16,128]{1,0:T(8,128)S(1)}, f32[16,128]{1,0:T(8,128)}, u32[]{:S(2)}) copy-start(f32[16,128]{1,0:T(8,128)} %param.8) | copy-start | bytes 24580
  7.2 10.7 %copy-start.9 = (bf16[128,256]{1,0:T(8,128)(2,1)S(1)}, bf16[128,256]{1,0:T(8,128)(2,1)}, u32[]{:S(2)}) copy-start(bf16[128,256]{1,0:T(8,128)(2,1)} %param.9) | copy-start | bytes 196612
  7.2 10.7 %copy-start.10 = (bf16[128,256]{1,0:T(8,128)(2,1)S(1)}, bf16[128,256]{1,0:T(8,128)(2,1)}, u32[]{:S(2)}) copy-start(bf16[128,256]{1,0:T(8,128)(2,1)} %param.5) | copy-start | bytes 196612
  10.2 21.9 %all-to-all-start = ((bf16[4,128,512]{2,1,0:T(8,128)(2,1)}), bf16[4,128,512]{2,1,0:T(8,128)(2,1)S(1)}, u32[]{:S(2)}, u32[]{:S(2)}) async-start(bf16[4,128,512]{2,1,0:T(8,128)(2,1)} %bitcast.7), calls=%async_computation | async-start | bytes 1048576 | tf_op jit(solution)/shard_map/all_to_all | solution.py:240
  17.9 76.4 %all-gather.3.cloned.1.call-start = ((), (), s32[]{:S(2)}) async-start(), calls=%async_computation.7 | async-start | bytes 4718592 | tf_op jit(solution)/shard_map/all_gather | solution.py:262
  32.1 0.8 copy-start.6
  52.4 28.9 %all-to-all-start.2 = ((bf16[4,4,2,128,256]{4,3,2,1,0:T(8,128)(2,1)}), bf16[4,4,2,128,256]{4,3,2,1,0:T(8,128)(2,1)S(1)}, u32[]{:S(2)}, u32[]{:S(2)}) async-start(bf16[4,4,2,128,256]{4,3,2,1,0:T(8,128)(2,1)} %broadcast_in_dim.26), calls=%async_computation.2 | async-start | bytes 4194304 | tf_op jit(solution)/shard_map/all_to_all | solution.py:240
  81.3 8.3 %collective-permute-start = (bf16[4,2,2,2,128,256]{5,4,3,2,1,0:T(8,128)(2,1)S(1)}, bf16[4,2,2,2,128,256]{5,4,3,2,1,0:T(8,128)(2,1)}, u32[]{:S(2)}, u32[]{:S(2)}) collective-permute-start(bf16[4,2,2,2,128,256]{5,4,3,2,1,0:T(8,128)(2,1)S(1)} %bitcast.24), channel_id=1, source_target_pairs={{0,1},{1,0},{2,3},{3,2},{4,5},{5,4},{6,7},{7,6},{8,9},{9,8},{10,11... | collective-permute-start | bytes 6291464 | tf_op jit(solution)/shard_map/ppermute | solution.py:269
  85.8 29.7 %copy-start.5 = (s32[2]{0:T(128)}, s32[2]{0:T(128)S(1)}, u32[]{:S(2)}) copy-start(s32[2]{0:T(128)S(1)} %pad_add_fusion.place_ref) | copy-start | bytes 28
  94.3 2.2 %copy-start.1 = (bf16[32,128,512]{2,1,0:T(8,128)(2,1)S(1)}, bf16[32,128,512]{2,1,0:T(8,128)(2,1)}, u32[]{:S(2)}) copy-start(bf16[32,128,512]{2,1,0:T(8,128)(2,1)} %all-gather.3.cloned.1.call-done) | copy-start | bytes 12582916
  96.5 19.1 %copy-start.2 = (bf16[32,128,512]{2,1,0:T(8,128)(2,1)S(1)}, bf16[32,128,512]{2,1,0:T(8,128)(2,1)}, u32[]{:S(2)}) copy-start(bf16[32,128,512]{2,1,0:T(8,128)(2,1)} %all-gather.3.cloned.1.call-done) | copy-start | bytes 12582916
  96.5 19.1 %copy-start.3 = (bf16[256,2048]{1,0:T(8,128)(2,1)S(1)}, bf16[256,2048]{1,0:T(8,128)(2,1)}, u32[]{:S(2)}) copy-start(bf16[256,2048]{1,0:T(8,128)(2,1)} %shard_map.68.band_ref) | copy-start | bytes 3145732
  101.5 12.9 %collective-permute-start.1 = (bf16[128,256]{1,0:T(8,128)(2,1)S(1)}, bf16[128,256]{1,0:T(8,128)(2,1)S(1)}, u32[]{:S(2)}, u32[]{:S(2)}) collective-permute-start(bf16[128,256]{1,0:T(8,128)(2,1)S(1)} %get-tuple-element.18.product_ref), channel_id=1, source_target_pairs={{0,16},{16,32},{32,48},{48,64},{64,80},{80,96},{96,112},{112,128},... | collective-permute-start | bytes 196616 | tf_op jit(solution)/shard_map/ppermute | solution.py:273
  103.4 12.1 %collective-permute-start.2 = (bf16[128,256]{1,0:T(8,128)(2,1)S(1)}, bf16[128,256]{1,0:T(8,128)(2,1)S(1)}, u32[]{:S(2)}, u32[]{:S(2)}) collective-permute-start(bf16[128,256]{1,0:T(8,128)(2,1)S(1)} %get-tuple-element.19.mixed_ref), channel_id=1, source_target_pairs={{16,0},{32,16},{48,32},{64,48},{80,64},{96,80},{112,96},{128,112},... | collective-permute-start | bytes 196616 | tf_op jit(solution)/shard_map/ppermute | solution.py:274
  117.6 0.7 copy-start.4
  118.3 9.8 %collective-permute-start.3 = (bf16[4,2,2,256,128]{4,3,2,1,0:T(8,128)(2,1)S(1)}, bf16[4,2,2,256,128]{4,3,2,1,0:T(8,128)(2,1)S(1)}, u32[]{:S(2)}, u32[]{:S(2)}) collective-permute-start(bf16[4,2,2,256,128]{4,3,2,1,0:T(8,128)(2,1)S(1)} %get-tuple-element.21), channel_id=1, source_target_pairs={{0,1},{1,0},{2,3},{3,2},{4,5},{5,4},{6,7},{7,6},{8,9},{9,8},{10,11... | collective-permute-start | bytes 3145736 | tf_op jit(solution)/shard_map/ppermute | solution.py:277
  126.3 11.1 %collective-permute-start.4 = (bf16[2,2,4,256,128]{4,3,2,1,0:T(8,128)(2,1)}, bf16[2,2,4,256,128]{4,3,2,1,0:T(8,128)(2,1)S(1)}, u32[]{:S(2)}, u32[]{:S(2)}) collective-permute-start(bf16[2,2,4,256,128]{4,3,2,1,0:T(8,128)(2,1)} %shard_map.72), channel_id=1, source_target_pairs={{0,1},{1,0},{2,3},{3,2},{4,5},{5,4},{6,7},{7,6},{8,9},{9,8},{10,11... | collective-permute-start | bytes 3145736 | tf_op jit(solution)/shard_map/ppermute | solution.py:278
  128.2 1.0 copy-start.8
  133.9 18.2 %all-to-all-start.3 = ((bf16[4,2,2,256,128]{4,3,2,1,0:T(8,128)(2,1)}), bf16[4,2,2,256,128]{4,3,2,1,0:T(8,128)(2,1)S(1)}, u32[]{:S(2)}, u32[]{:S(2)}) async-start(bf16[4,2,2,256,128]{4,3,2,1,0:T(8,128)(2,1)} %shard_map.71), calls=%async_computation.3 | async-start | bytes 2097152 | tf_op jit(solution)/shard_map/all_to_all | solution.py:240
  137.4 1.0 copy-start.7
  152.0 27.8 %all-to-all-start.5 = ((bf16[4,4,256,128]{3,2,1,0:T(8,128)(2,1)}), bf16[4,4,256,128]{3,2,1,0:T(8,128)(2,1)S(1)}, u32[]{:S(2)}, u32[]{:S(2)}) async-start(bf16[4,4,256,128]{3,2,1,0:T(8,128)(2,1)} %bitcast.26), calls=%async_computation.5 | async-start | bytes 2097152 | tf_op jit(solution)/shard_map/all_to_all | solution.py:240
  179.8 15.9 %all-to-all-start.4 = ((bf16[4,256,128]{2,1,0:T(8,128)(2,1)}), bf16[4,256,128]{2,1,0:T(8,128)(2,1)S(1)}, u32[]{:S(2)}, u32[]{:S(2)}) async-start(bf16[4,256,128]{2,1,0:T(8,128)(2,1)} %bitcast.12), calls=%async_computation.4 | async-start | bytes 524288 | tf_op jit(solution)/shard_map/all_to_all | solution.py:240
  195.7 8.9 %all-to-all-start.6 = ((bf16[4,256,128]{2,1,0:T(8,128)(2,1)}), bf16[4,256,128]{2,1,0:T(8,128)(2,1)S(1)}, u32[]{:S(2)}, u32[]{:S(2)}) async-start(bf16[4,256,128]{2,1,0:T(8,128)(2,1)} %reduce_sum.50), calls=%async_computation.6 | async-start | bytes 524288 | tf_op jit(solution)/shard_map/all_to_all | solution.py:240
Sparse Core Ops, SparseCore 0:
  33.1 61.1 all-gather.2

commit v3 on v2

v3 whole, which is shorter than its diff:
```python
import jax
import jax.numpy as jnp
from jax import lax
from jax.experimental import pallas as pl
from jax.experimental.pallas import tpu as pltpu
from jax.sharding import Mesh, PartitionSpec as P

AXES = ("h", "l", "z", "ylo", "x", "core")
SIZES = (2, 2, 8, 2, 4, 2)
ROWS = 128
HALF = 128
TAPS = 128
GROUP = 16
GROUPS = HALF // GROUP
FEATURES = 256
STREAMS = 4 * HALF
BACK = 3 * HALF
BF16 = jnp.bfloat16
F32 = jnp.float32
VMEM_FORWARD = 56 << 20


def bands_kernel(base_ref, band_ref):
    for row in range(2 * GROUPS):
        spread = jnp.broadcast_to(base_ref[row : row + 1, :], (2 * ROWS, 2 * ROWS))
        rolled = pltpu.roll(spread, 0, 1, stride=1, stride_axis=0)
        band_ref[:, row * ROWS : (row + 1) * ROWS] = rolled[:, :ROWS].astype(BF16)


def bands(filters):
    zeros = jnp.zeros((GROUPS, TAPS), filters.dtype)
    causal = jnp.concatenate([zeros, filters], 1)
    anticausal = jnp.concatenate([filters[:, :1], zeros, filters[:, :0:-1]], 1)
    return pl.pallas_call(
        bands_kernel,
        out_shape=jax.ShapeDtypeStruct((2 * ROWS, 2 * GROUPS * ROWS), BF16),
    )(jnp.concatenate([causal, anticausal], 0))


def forward_kernel(place_ref, own_ref, other_ref, weight_ref, streams_ref, gate_ref, product_ref, mixed_ref, total):
    step = pl.program_id(0)
    core = place_ref[0]

    @pl.when(step == 0)
    def _():
        total[...] = jnp.zeros_like(total)

    tokens, cotangent, weight = [], [], []
    for values_ref, which in ((own_ref, core), (other_ref, 1 - core)):
        for y in range(2):
            tokens.append(values_ref[0, :, y, 0].reshape(2 * ROWS, FEATURES))
            cotangent.append(values_ref[0, :, y, 1].reshape(2 * ROWS, FEATURES))
            weight.append(weight_ref[pl.ds(2 * which, 2), 0, y, 0].reshape(FEATURES, STREAMS))
    tokens, cotangent = jnp.concatenate(tokens, 1), jnp.concatenate(cotangent, 1)
    weight = jnp.concatenate(weight, 0)
    total[:, :BACK] += jnp.dot(tokens, weight[:, :BACK], preferred_element_type=F32)
    total[:, BACK:] += jnp.dot(cotangent, weight[:, BACK:], preferred_element_type=F32)

    @pl.when(step == pl.num_programs(0) - 1)
    def _():
        turned = total[...].T
        streams = turned[:BACK].astype(BF16)
        streams_ref[...] = streams
        grad_gate = turned[BACK:]
        gate_ref[...] = grad_gate
        query, key, value = (streams[i * HALF : (i + 1) * HALF].astype(F32) for i in range(3))
        product_ref[...] = (key * value).astype(BF16)
        mixed_ref[...] = (grad_gate * query).astype(BF16)


def forward(place, own, other, weight):
    values = pl.BlockSpec((1, 2, 2, 2, ROWS, FEATURES), lambda j, p: (j, 0, 0, 0, 0, 0))
    whole = lambda height: pl.BlockSpec((height, 2 * ROWS), lambda j, p: (0, 0))
    shape = lambda height, kind: jax.ShapeDtypeStruct((height, 2 * ROWS), kind)
    return pl.pallas_call(
        forward_kernel,
        out_shape=(shape(BACK, BF16), shape(HALF, F32), shape(HALF, BF16), shape(HALF, BF16)),
        grid_spec=pltpu.PrefetchScalarGridSpec(
            num_scalar_prefetch=1,
            grid=(4,),
            in_specs=[
                values,
                values,
                pl.BlockSpec((4, 1, 2, 1, ROWS, STREAMS), lambda j, p: (j % 2, p[0], 0, j // 2, 0, 0)),
            ],
            out_specs=[whole(BACK), whole(HALF), whole(HALF), whole(HALF)],
            scratch_shapes=[pltpu.VMEM((2 * ROWS, STREAMS), F32)],
        ),
        compiler_params=pltpu.CompilerParams(vmem_limit_bytes=VMEM_FORWARD),
        cost_estimate=pl.CostEstimate(flops=1 << 30, bytes_accessed=9 << 20, transcendentals=0),
    )(place, own, other, weight)


def filtered(left, right, band):
    segments = [
        jnp.concatenate([left[s], right[s]], 1) for s in range(2)
    ]
    result = jnp.dot(jnp.concatenate(segments, 0), band, preferred_element_type=F32)
    return [
        jnp.concatenate(
            [
                result[s * HALF + g * GROUP : s * HALF + (g + 1) * GROUP, g * ROWS : (g + 1) * ROWS]
                for g in range(GROUPS)
            ],
            0,
        )
        for s in range(2)
    ]


def middle_kernel(
    place_ref, band_ref, streams_ref, gate_ref, product_ref, mixed_ref, before_ref, after_ref, terms_ref
):
    first = place_ref[1] == 0
    last = place_ref[1] == 15
    lanes = [slice(s * ROWS, (s + 1) * ROWS) for s in range(2)]
    product, mixed, before, after = (
        [ref[:, lanes[s]] for s in range(2)] for ref in (product_ref, mixed_ref, before_ref, after_ref)
    )
    zero = jnp.zeros_like(before[0])
    earlier = [jnp.where(first, zero, before[0]), jnp.where(first, before[0], before[1])]
    later = [jnp.where(last, after[1], after[0]), jnp.where(last, zero, after[1])]
    conv = filtered(earlier, product, band_ref[:, : GROUPS * ROWS])
    back = filtered(mixed, later, band_ref[:, GROUPS * ROWS :])
    for s in range(2):
        query, key, value = (
            streams_ref[i * HALF : (i + 1) * HALF, lanes[s]].astype(F32) for i in range(3)
        )
        terms_ref[:HALF, lanes[s]] = (gate_ref[:, lanes[s]] * conv[s]).astype(BF16)
        terms_ref[HALF : 2 * HALF, lanes[s]] = (back[s] * value).astype(BF16)
        terms_ref[2 * HALF : BACK, lanes[s]] = (back[s] * key).astype(BF16)
        terms_ref[BACK:, lanes[s]] = (query * conv[s]).astype(BF16)


TERMS_SPEC = pl.BlockSpec((STREAMS, 2 * ROWS), lambda j, p: (0, 0))


def middle(place, *operands):
    return pl.pallas_call(
        middle_kernel,
        out_shape=jax.ShapeDtypeStruct((STREAMS, 2 * ROWS), BF16),
        grid_spec=pltpu.PrefetchScalarGridSpec(
            num_scalar_prefetch=1,
            grid=(1,),
            in_specs=[pl.BlockSpec(value.shape, lambda j, p: (0, 0)) for value in operands],
            out_specs=TERMS_SPEC,
        ),
        cost_estimate=pl.CostEstimate(flops=1 << 28, bytes_accessed=3 << 20, transcendentals=0),
    )(place, *operands)


def backward_kernel(place_ref, own_ref, other_ref, weight_ref, *rest):
    *arrived, out_ref = rest
    core = place_ref[0]
    results = [0.0, 0.0]
    for terms_ref, which in ((own_ref, core), (other_ref, 1 - core)):
        weight = weight_ref[:, pl.ds(which, 1), 0, 0].reshape(FEATURES, STREAMS)
        results[0] += jnp.dot(weight[:, BACK:], terms_ref[BACK:], preferred_element_type=F32)
        results[1] += jnp.dot(weight[:, :BACK], terms_ref[:BACK], preferred_element_type=F32)
    for which in range(2):
        for h in range(2):
            part = results[which][:, h * ROWS : (h + 1) * ROWS]
            for ref in arrived:
                part += ref[h, 0, which].astype(F32)
            out_ref[h, 0, which] = part.astype(BF16)


def backward(steps, place, own, other, weight, arrived=()):
    spec = pl.BlockSpec((2, 1, 2, FEATURES, ROWS), lambda j, p: (0, j, 0, 0, 0))

    def weight_at(j, p):
        x = lax.rem(p[2] + steps, 4)
        return (lax.rem(x, 2) * 2 + p[0], 0, j, x // 2, 0, 0)

    return pl.pallas_call(
        backward_kernel,
        out_shape=jax.ShapeDtypeStruct((2, 2, 2, FEATURES, ROWS), BF16),
        grid_spec=pltpu.PrefetchScalarGridSpec(
            num_scalar_prefetch=1,
            grid=(2,),
            in_specs=[TERMS_SPEC, TERMS_SPEC, pl.BlockSpec((2, 2, 1, 1, ROWS, STREAMS), weight_at)]
            + [spec] * len(arrived),
            out_specs=spec,
        ),
        cost_estimate=pl.CostEstimate(flops=1 << 28, bytes_accessed=3 << 20, transcendentals=0),
    )(place, own, other, weight, *arrived)


def swapped(value, axes):
    return lax.all_to_all(value, axes, 0, 0, tiled=True)


def gathered(value, axes, count):
    return swapped(jnp.broadcast_to(value[None], (count,) + value.shape), axes)


def local(tokens, in_weight, out_weight, mr_filter, cotangent):
    half = lax.axis_index("h")
    position = lax.axis_index(("l", "z"))
    place = jnp.stack([lax.axis_index("core"), position, lax.axis_index("x")]).astype(jnp.int32)

    weight = jnp.concatenate([in_weight, out_weight.T[None]], 0)
    weight = weight.reshape(4, ROWS, 2, HALF).transpose(2, 1, 0, 3).reshape(2, 1, ROWS, STREAMS)
    weight = jnp.broadcast_to(weight, (2, 2, ROWS, STREAMS)).reshape(4, ROWS, STREAMS)
    weight = swapped(weight, ("h", "l"))
    values = jnp.stack([tokens, cotangent], 0)
    weight, values = lax.optimization_barrier((weight, values))
    weight = lax.all_gather(weight, ("z", "core"), axis=0).reshape(8, 2, 2, 2, ROWS, STREAMS)

    band = bands(lax.dynamic_slice_in_dim(mr_filter, half * GROUPS, GROUPS, 0))
    values = gathered(values, ("h", "ylo"), 4)
    values = gathered(values, "x", 4).reshape(4, 2, 2, 2, ROWS, FEATURES)
    values, band = lax.optimization_barrier((values, band))
    cross = [(0, 1), (1, 0)]
    other = lax.ppermute(values, "core", cross)

    streams, gate, product, mixed = forward(place, values, other, weight)
    ring = [(n, (n + 1) % 16) for n in range(16)]
    before = lax.ppermute(product, ("l", "z"), ring)
    after = lax.ppermute(mixed, ("l", "z"), [(b, a) for a, b in ring])

    terms = middle(place, band, streams, gate, product, mixed, before, after)
    other_terms = lax.ppermute(terms, "core", cross)
    arrived = []
    for steps in (2, 1, 3):
        part = backward(steps, place, terms, other_terms, weight)
        arrived.append(lax.ppermute(part, "x", [(n, (n + steps) % 4) for n in range(4)]))
    sums = backward(0, place, terms, other_terms, weight, arrived)
    sums = swapped(sums.reshape(4, 2, FEATURES, ROWS), ("h", "ylo")).astype(F32).sum(0).astype(BF16)
    return sums[0].T, sums[1].T


def solution(mesh):
    fine = Mesh(mesh.devices.reshape(SIZES), AXES)
    ctx, tp = AXES[:3], AXES[3:]
    return jax.shard_map(
        local,
        mesh=fine,
        in_specs=(P(ctx, tp), P(None, ctx, tp), P(tp, ctx), P(tp, None), P(ctx, tp)),
        out_specs=(P(ctx, tp), P(ctx, tp)),
        check_vma=False,
    )
```

time: 214 us -> 191 us (0.89)
  waiting for transfers between devices: 91.3 us -> 61.4 us
  blocking collectives: 17.9 us -> 35.4 us
  starting transfers between devices: 50.6 us -> 39.4 us
    all_to_all x6 -> x2, waiting for transfers between devices: 81.5 us -> 36 us  [swapped(): return lax.all_to_all(value, axes, 0, 0, tiled=True)]
    all_to_all x1 -> x2, blocking collectives: 17.9 us -> 35.4 us  [swapped(): return lax.all_to_all(value, axes, 0, 0, tiled=True)]
    all_to_all x6 -> x2, starting transfers between devices: 28.4 us -> 11.8 us  [swapped(): return lax.all_to_all(value, axes, 0, 0, tiled=True)]
    ppermute x2 -> x4, waiting for transfers between devices: 0.01 us -> 14.5 us  [the longest x3 13.1 us: local(): lax.ppermute(part, 'x', [(n, (n + steps) % 4) for n in range(4)])]
    ppermute x2 -> x4, starting transfers between devices: 5.04 us -> 12 us  [the longest x3 8.83 us: local(): lax.ppermute(part, 'x', [(n, (n + steps) % 4) for n in range(4)])]
    pallas_call x4 -> x5, Pallas kernels: 16.5 us -> 16.9 us  [the longest x4 13.7 us: backward(): pl.pallas_call(backward_kernel, out_shape=jax.ShapeDtypeStruct((2, 2, 2,...]
  transfers between devices with their start and end apart: 12 -> 10, of which waited for: 10 -> 9; matrix products, arithmetic and copies ran while one was open for 2% -> 2% of each run, Pallas kernels for 8% -> 5%
where the time goes in v3:
time: 191 us; the launch traced here: 188 us
  waiting for transfers between devices  61.4 us (32%)
  starting transfers between devices  39.4 us (21%)
  blocking collectives  35.4 us (19%)
  Pallas kernels  25.7 us (13%)
  between operations  14.2 us (7%)
  local copies, waits for them, and re-layouts  9.21 us (5%)
  other arithmetic  2.31 us (1%)
    all_to_all x2, waiting for transfers between devices, swapped(): return lax.all_to_all(value, axes, 0, 0, tiled=True)  36 us
    all_to_all x2, blocking collectives, swapped(): return lax.all_to_all(value, axes, 0, 0, tiled=True)  35.4 us
    pallas_call x4, Pallas kernels, backward(): pl.pallas_call(backward_kernel, out_shape=jax.ShapeDtypeStruct((2, 2, 2,...  13.7 us
    ppermute x3, waiting for transfers between devices, local(): lax.ppermute(part, 'x', [(n, (n + steps) % 4) for n in range(4)])  13.1 us
    all_to_all x2, starting transfers between devices, swapped(): return lax.all_to_all(value, axes, 0, 0, tiled=True)  11.8 us
    ppermute x1, starting transfers between devices, local(): after = lax.ppermute(mixed, ('l', 'z'), [(b, a) for a, b in ring])  9.32 us
    ppermute x3, starting transfers between devices, local(): lax.ppermute(part, 'x', [(n, (n + steps) % 4) for n in range(4)])  8.83 us
    pallas_call x1, Pallas kernels, forward(): pl.pallas_call(forward_kernel, out_shape=(shape(BACK, BF16), shape(HALF,...  6.69 us
  transfers between devices with their start and end apart: 10, of which 9 were waited for; matrix products, arithmetic and copies ran while one was open for 2% of the time, Pallas kernels for 5%

profile of v3, /device:TPU:1, one launch (start us, length us, event | category | flops | bytes accessed | tf_op | source)
XLA Modules:
  0.0 187.7 jit_solution(15446055825189133133)
XLA Ops:
  10.2 7.6 %all-to-all-start = ((bf16[4,128,512]{2,1,0:T(8,128)(2,1)}), bf16[4,128,512]{2,1,0:T(8,128)(2,1)S(1)}, u32[]{:S(2)}, u32[]{:S(2)}) async-start(bf16[4,128,512]{2,1,0:T(8,128)(2,1)} %bitcast.8), calls=%async_computation | async-start | bytes 1048576 | tf_op jit(solution)/shard_map/all_to_all | solution.py:190
  17.9 14.2 %all-to-all-done = bf16[4,128,512]{2,1,0:T(8,128)(2,1)S(1)} async-done(((bf16[4,128,512]{2,1,0:T(8,128)(2,1)}), bf16[4,128,512]{2,1,0:T(8,128)(2,1)S(1)}, u32[]{:S(2)}, u32[]{:S(2)}) %all-to-all-start) | async-done | bytes 524320 | tf_op jit(solution)/shard_map/all_to_all | solution.py:190
  33.0 17.9 %all_to_all.20 = bf16[4,2,128,256]{3,2,1,0:T(8,128)(2,1)S(1)} all-to-all(bf16[4,2,128,256]{3,2,1,0:T(8,128)(2,1)S(1)} %broadcast_in_dim.12), channel_id=1, replica_groups=mesh['h'=2,'l'=2,'z'=8,'ylo'=2,'x'=4,'core'=2] {'h','ylo'}, dimensions={0} | all-to-all | bytes 1048576 | tf_op jit(solution)/shard_map/all_to_all | solution.py:190
  50.9 1.6 broadcast_in_dim.26
  52.5 4.1 %all-to-all-start.2 = ((bf16[4,4,2,128,256]{4,3,2,1,0:T(8,128)(2,1)}), bf16[4,4,2,128,256]{4,3,2,1,0:T(8,128)(2,1)S(1)}, u32[]{:S(2)}, u32[]{:S(2)}) async-start(bf16[4,4,2,128,256]{4,3,2,1,0:T(8,128)(2,1)} %broadcast_in_dim.26), calls=%async_computation.2 | async-start | bytes 4194304 | tf_op jit(solution)/shard_map/all_to_all | solution.py:190
  57.5 2.1 %shard_map.68.band_ref = bf16[256,2048]{1,0:T(8,128)(2,1)} custom-call(f32[16,256]{1,0:T(8,128)} %select_maximum_fusion.base_ref), custom_call_target="tpu_custom_call" | custom-call | tf_op jit(solution)/shard_map/pallas_call | solution.py:34
  59.6 21.8 %all-to-all-done.2 = bf16[4,4,2,128,256]{4,3,2,1,0:T(8,128)(2,1)S(1)} async-done(((bf16[4,4,2,128,256]{4,3,2,1,0:T(8,128)(2,1)}), bf16[4,4,2,128,256]{4,3,2,1,0:T(8,128)(2,1)S(1)}, u32[]{:S(2)}, u32[]{:S(2)}) %all-to-all-start.2) | async-done | bytes 2097184 | tf_op jit(solution)/shard_map/all_to_all | solution.py:190
  81.4 4.4 %collective-permute-start = (bf16[4,2,2,2,128,256]{5,4,3,2,1,0:T(8,128)(2,1)S(1)}, bf16[4,2,2,2,128,256]{5,4,3,2,1,0:T(8,128)(2,1)}, u32[]{:S(2)}, u32[]{:S(2)}) collective-permute-start(bf16[4,2,2,2,128,256]{5,4,3,2,1,0:T(8,128)(2,1)S(1)} %bitcast.30), channel_id=1, source_target_pairs={{0,1},{1,0},{2,3},{3,2},{4,5},{5,4},{6,7},{7,6},{8,9},{9,8},{10,11... | collective-permute-start | bytes 6291464 | tf_op jit(solution)/shard_map/ppermute | solution.py:215
  86.5 3.3 %collective-permute-done.other_ref = bf16[4,2,2,2,128,256]{5,4,3,2,1,0:T(8,128)(2,1)} collective-permute-done((bf16[4,2,2,2,128,256]{5,4,3,2,1,0:T(8,128)(2,1)S(1)}, bf16[4,2,2,2,128,256]{5,4,3,2,1,0:T(8,128)(2,1)}, u32[]{:S(2)}, u32[]{:S(2)}) %collective-permute-start) | collective-permute-done | bytes 2097184 | tf_op jit(solution)/shard_map/ppermute | solution.py:215
  89.8 6.0 %all-gather.3.cloned.1.call-done = bf16[64,128,512]{2,1,0:T(8,128)(2,1)} async-done(((bf16[4,128,512]{2,1,0:T(8,128)(2,1)}), bf16[64,128,512]{2,1,0:T(8,128)(2,1)}) %all-gather.3.cloned.1.call-update) | async-done | bytes 8388624 | tf_op jit(solution)/shard_map/all_gather | solution.py:208
  95.8 6.7 %shard_map.69 = (bf16[384,256]{1,0:T(8,128)(2,1)}, f32[128,256]{1,0:T(8,128)}, bf16[128,256]{1,0:T(8,128)(2,1)}, bf16[128,256]{1,0:T(8,128)(2,1)}) custom-call(s32[3]{0:T(128)} %pad_add_fusion.place_ref, bf16[4,2,2,2,128,256]{5,4,3,2,1,0:T(8,128)(2,1)} %bitcast.31, bf16[4,2,2,2,128,256]{5,4,3,2,1,0:T(8,128)(2,1)} %collective-permute-done.other_ref, ...), custom_call_target="tpu_custom_call" | custom-call | flops 1073741824 | bytes 9437184 | tf_op jit(solution)/shard_map/pallas_call | solution.py:75
  102.5 1.9 %collective-permute-start.1 = (bf16[128,256]{1,0:T(8,128)(2,1)}, bf16[128,256]{1,0:T(8,128)(2,1)S(1)}, u32[]{:S(2)}, u32[]{:S(2)}) collective-permute-start(bf16[128,256]{1,0:T(8,128)(2,1)} %get-tuple-element.16.product_ref), channel_id=1, source_target_pairs={{0,16},{16,32},{32,48},{48,64},{64,80},{80,96},{96,112},{112,128},... | collective-permute-start | bytes 196616 | tf_op jit(solution)/shard_map/ppermute | solution.py:219
  104.4 9.3 %collective-permute-start.2 = (bf16[128,256]{1,0:T(8,128)(2,1)}, bf16[128,256]{1,0:T(8,128)(2,1)S(1)}, u32[]{:S(2)}, u32[]{:S(2)}) collective-permute-start(bf16[128,256]{1,0:T(8,128)(2,1)} %get-tuple-element.17.mixed_ref), channel_id=1, source_target_pairs={{16,0},{32,16},{48,32},{64,48},{80,64},{96,80},{112,96},{128,112},... | collective-permute-start | bytes 196616 | tf_op jit(solution)/shard_map/ppermute | solution.py:220
  116.0 3.2 %shard_map.70.own_ref = bf16[512,256]{1,0:T(8,128)(2,1)} custom-call(s32[3]{0:T(128)} %pad_add_fusion.place_ref, bf16[256,2048]{1,0:T(8,128)(2,1)} %shard_map.68.band_ref, bf16[384,256]{1,0:T(8,128)(2,1)} %get-tuple-element.14.streams_ref, f32[128,256]{1,0:T(8,128)} %get-tuple-element.15.gate_ref, bf16[128,256]{1,0:T(8,128)(2,1)} %get-tuple-element.16.product_ref, ...), custom_call_target="tpu_custom_call" | custom-call | flops 268435456 | bytes 3145728 | tf_op jit(solution)/shard_map/pallas_call | solution.py:139
  119.2 3.1 %collective-permute-start.3 = (bf16[512,256]{1,0:T(8,128)(2,1)}, bf16[512,256]{1,0:T(8,128)(2,1)S(1)}, u32[]{:S(2)}, u32[]{:S(2)}) collective-permute-start(bf16[512,256]{1,0:T(8,128)(2,1)} %shard_map.70.own_ref), channel_id=1, source_target_pairs={{0,1},{1,0},{2,3},{3,2},{4,5},{5,4},{6,7},{7,6},{8,9},{9,8},{10,11... | collective-permute-start | bytes 786440 | tf_op jit(solution)/shard_map/ppermute | solution.py:223
  124.4 3.4 %shard_map.71 = bf16[2,2,2,256,128]{4,3,2,1,0:T(8,128)(2,1)} custom-call(s32[3]{0:T(128)} %pad_add_fusion.place_ref, bf16[512,256]{1,0:T(8,128)(2,1)} %shard_map.70.own_ref, bf16[512,256]{1,0:T(8,128)(2,1)} %copy-done.2, bf16[8,2,2,2,128,512]{5,4,3,2,1,0:T(8,128)(2,1)} %bitcast.26), custom_call_target="tpu_custom_call" | custom-call | flops 268435456 | bytes 3145728 | tf_op jit(solution)/shard_map/pallas_call | solution.py:175
  127.8 2.4 %collective-permute-start.4 = (bf16[2,2,2,256,128]{4,3,2,1,0:T(8,128)(2,1)}, bf16[2,2,2,256,128]{4,3,2,1,0:T(8,128)(2,1)S(1)}, u32[]{:S(2)}, u32[]{:S(2)}) collective-permute-start(bf16[2,2,2,256,128]{4,3,2,1,0:T(8,128)(2,1)} %shard_map.71), channel_id=1, source_target_pairs={{0,4},{2,6},{4,0},{6,2},{1,5},{3,7},{5,1},{7,3},{8,12},{10,14},{12... | collective-permute-start | bytes 1572872 | tf_op jit(solution)/shard_map/ppermute | solution.py:227
  130.1 3.3 %shard_map.72 = bf16[2,2,2,256,128]{4,3,2,1,0:T(8,128)(2,1)} custom-call(s32[3]{0:T(128)} %pad_add_fusion.place_ref, bf16[512,256]{1,0:T(8,128)(2,1)} %shard_map.70.own_ref, bf16[512,256]{1,0:T(8,128)(2,1)} %copy-done.2, bf16[8,2,2,2,128,512]{5,4,3,2,1,0:T(8,128)(2,1)} %bitcast.27), custom_call_target="tpu_custom_call" | custom-call | flops 268435456 | bytes 3145728 | tf_op jit(solution)/shard_map/pallas_call | solution.py:175
  133.5 2.9 %collective-permute-start.5 = (bf16[2,2,2,256,128]{4,3,2,1,0:T(8,128)(2,1)}, bf16[2,2,2,256,128]{4,3,2,1,0:T(8,128)(2,1)S(1)}, u32[]{:S(2)}, u32[]{:S(2)}) collective-permute-start(bf16[2,2,2,256,128]{4,3,2,1,0:T(8,128)(2,1)} %shard_map.72), channel_id=1, source_target_pairs={{0,2},{2,4},{4,6},{6,0},{1,3},{3,5},{5,7},{7,1},{8,10},{10,12},{12... | collective-permute-start | bytes 1572872 | tf_op jit(solution)/shard_map/ppermute | solution.py:227
  136.4 3.3 %shard_map.73 = bf16[2,2,2,256,128]{4,3,2,1,0:T(8,128)(2,1)} custom-call(s32[3]{0:T(128)} %pad_add_fusion.place_ref, bf16[512,256]{1,0:T(8,128)(2,1)} %shard_map.70.own_ref, bf16[512,256]{1,0:T(8,128)(2,1)} %copy-done.2, bf16[8,2,2,2,128,512]{5,4,3,2,1,0:T(8,128)(2,1)} %bitcast.28), custom_call_target="tpu_custom_call" | custom-call | flops 268435456 | bytes 3145728 | tf_op jit(solution)/shard_map/pallas_call | solution.py:175
  139.7 3.6 %collective-permute-start.6 = (bf16[2,2,2,256,128]{4,3,2,1,0:T(8,128)(2,1)}, bf16[2,2,2,256,128]{4,3,2,1,0:T(8,128)(2,1)S(1)}, u32[]{:S(2)}, u32[]{:S(2)}) collective-permute-start(bf16[2,2,2,256,128]{4,3,2,1,0:T(8,128)(2,1)} %shard_map.73), channel_id=1, source_target_pairs={{0,6},{2,0},{4,2},{6,4},{1,7},{3,1},{5,3},{7,5},{8,14},{10,8},{12,... | collective-permute-start | bytes 1572872 | tf_op jit(solution)/shard_map/ppermute | solution.py:227
  144.5 11.9 %collective-permute-done.5.rest_1_ = bf16[2,2,2,256,128]{4,3,2,1,0:T(8,128)(2,1)S(1)} collective-permute-done((bf16[2,2,2,256,128]{4,3,2,1,0:T(8,128)(2,1)}, bf16[2,2,2,256,128]{4,3,2,1,0:T(8,128)(2,1)S(1)}, u32[]{:S(2)}, u32[]{:S(2)}) %collective-permute-start.5) | collective-permute-done | bytes 524320 | tf_op jit(solution)/shard_map/ppermute | solution.py:227
  158.0 3.6 %shard_map.74 = bf16[2,2,2,256,128]{4,3,2,1,0:T(8,128)(2,1)} custom-call(s32[3]{0:T(128)} %pad_add_fusion.place_ref, bf16[512,256]{1,0:T(8,128)(2,1)} %shard_map.70.own_ref, bf16[512,256]{1,0:T(8,128)(2,1)} %copy-done.2, bf16[8,2,2,2,128,512]{5,4,3,2,1,0:T(8,128)(2,1)} %bitcast.29, bf16[2,2,2,256,128]{4,3,2,1,0:T(8,128)(2,1)} %copy-done.4, ...), custom_call_target="tpu_custom_call" | custom-call | flops 268435456 | bytes 3145728 | tf_op jit(solution)/shard_map/pallas_call | solution.py:175
  161.7 17.6 %all_to_all.21 = bf16[4,2,256,128]{3,2,1,0:T(8,128)(2,1)S(1)} all-to-all(bf16[4,2,256,128]{3,2,1,0:T(8,128)(2,1)} %bitcast.32), channel_id=1, replica_groups=mesh['h'=2,'l'=2,'z'=8,'ylo'=2,'x'=4,'core'=2] {'h','ylo'}, dimensions={0} | all-to-all | bytes 1048576 | tf_op jit(solution)/shard_map/all_to_all | solution.py:190
  (46 shorter events, 14.1 us)
Async XLA Ops:
  7.2 49.5 %copy-start = (f32[16,128]{1,0:T(8,128)S(1)}, f32[16,128]{1,0:T(8,128)}, u32[]{:S(2)}) copy-start(f32[16,128]{1,0:T(8,128)} %param.8) | copy-start | bytes 24580
  7.2 10.7 %copy-start.9 = (bf16[128,256]{1,0:T(8,128)(2,1)S(1)}, bf16[128,256]{1,0:T(8,128)(2,1)}, u32[]{:S(2)}) copy-start(bf16[128,256]{1,0:T(8,128)(2,1)} %param.9) | copy-start | bytes 196612
  7.2 10.7 %copy-start.10 = (bf16[128,256]{1,0:T(8,128)(2,1)S(1)}, bf16[128,256]{1,0:T(8,128)(2,1)}, u32[]{:S(2)}) copy-start(bf16[128,256]{1,0:T(8,128)(2,1)} %param.5) | copy-start | bytes 196612
  10.2 21.9 %all-to-all-start = ((bf16[4,128,512]{2,1,0:T(8,128)(2,1)}), bf16[4,128,512]{2,1,0:T(8,128)(2,1)S(1)}, u32[]{:S(2)}, u32[]{:S(2)}) async-start(bf16[4,128,512]{2,1,0:T(8,128)(2,1)} %bitcast.8), calls=%async_computation | async-start | bytes 1048576 | tf_op jit(solution)/shard_map/all_to_all | solution.py:190
  17.9 77.9 %all-gather.3.cloned.1.call-start = ((), (), s32[]{:S(2)}) async-start(), calls=%async_computation.4 | async-start | bytes 8912896 | tf_op jit(solution)/shard_map/all_gather | solution.py:208
  32.1 0.8 copy-start.3
  52.5 28.9 %all-to-all-start.2 = ((bf16[4,4,2,128,256]{4,3,2,1,0:T(8,128)(2,1)}), bf16[4,4,2,128,256]{4,3,2,1,0:T(8,128)(2,1)S(1)}, u32[]{:S(2)}, u32[]{:S(2)}) async-start(bf16[4,4,2,128,256]{4,3,2,1,0:T(8,128)(2,1)} %broadcast_in_dim.26), calls=%async_computation.2 | async-start | bytes 4194304 | tf_op jit(solution)/shard_map/all_to_all | solution.py:190
  81.4 14.4 %copy-start.1 = (bf16[4,4,2,128,256]{4,3,2,1,0:T(8,128)(2,1)}, bf16[4,4,2,128,256]{4,3,2,1,0:T(8,128)(2,1)S(1)}, u32[]{:S(2)}) copy-start(bf16[4,4,2,128,256]{4,3,2,1,0:T(8,128)(2,1)S(1)} %all-to-all-done.2) | copy-start | bytes 6291460
  81.4 8.4 %collective-permute-start = (bf16[4,2,2,2,128,256]{5,4,3,2,1,0:T(8,128)(2,1)S(1)}, bf16[4,2,2,2,128,256]{5,4,3,2,1,0:T(8,128)(2,1)}, u32[]{:S(2)}, u32[]{:S(2)}) collective-permute-start(bf16[4,2,2,2,128,256]{5,4,3,2,1,0:T(8,128)(2,1)S(1)} %bitcast.30), channel_id=1, source_target_pairs={{0,1},{1,0},{2,3},{3,2},{4,5},{5,4},{6,7},{7,6},{8,9},{9,8},{10,11... | collective-permute-start | bytes 6291464 | tf_op jit(solution)/shard_map/ppermute | solution.py:215
  102.5 11.7 %collective-permute-start.1 = (bf16[128,256]{1,0:T(8,128)(2,1)}, bf16[128,256]{1,0:T(8,128)(2,1)S(1)}, u32[]{:S(2)}, u32[]{:S(2)}) collective-permute-start(bf16[128,256]{1,0:T(8,128)(2,1)} %get-tuple-element.16.product_ref), channel_id=1, source_target_pairs={{0,16},{16,32},{32,48},{48,64},{64,80},{80,96},{96,112},{112,128},... | collective-permute-start | bytes 196616 | tf_op jit(solution)/shard_map/ppermute | solution.py:219
  104.4 11.0 %collective-permute-start.2 = (bf16[128,256]{1,0:T(8,128)(2,1)}, bf16[128,256]{1,0:T(8,128)(2,1)S(1)}, u32[]{:S(2)}, u32[]{:S(2)}) collective-permute-start(bf16[128,256]{1,0:T(8,128)(2,1)} %get-tuple-element.17.mixed_ref), channel_id=1, source_target_pairs={{16,0},{32,16},{48,32},{64,48},{80,64},{96,80},{112,96},{128,112},... | collective-permute-start | bytes 196616 | tf_op jit(solution)/shard_map/ppermute | solution.py:220
  114.2 1.2 copy-start.7
  115.4 0.6 copy-start.8
  119.2 4.5 %collective-permute-start.3 = (bf16[512,256]{1,0:T(8,128)(2,1)}, bf16[512,256]{1,0:T(8,128)(2,1)S(1)}, u32[]{:S(2)}, u32[]{:S(2)}) collective-permute-start(bf16[512,256]{1,0:T(8,128)(2,1)} %shard_map.70.own_ref), channel_id=1, source_target_pairs={{0,1},{1,0},{2,3},{3,2},{4,5},{5,4},{6,7},{7,6},{8,9},{9,8},{10,11... | collective-permute-start | bytes 786440 | tf_op jit(solution)/shard_map/ppermute | solution.py:223
  123.7 0.7 copy-start.2
  127.8 16.8 %collective-permute-start.4 = (bf16[2,2,2,256,128]{4,3,2,1,0:T(8,128)(2,1)}, bf16[2,2,2,256,128]{4,3,2,1,0:T(8,128)(2,1)S(1)}, u32[]{:S(2)}, u32[]{:S(2)}) collective-permute-start(bf16[2,2,2,256,128]{4,3,2,1,0:T(8,128)(2,1)} %shard_map.71), channel_id=1, source_target_pairs={{0,4},{2,6},{4,0},{6,2},{1,5},{3,7},{5,1},{7,3},{8,12},{10,14},{12... | collective-permute-start | bytes 1572872 | tf_op jit(solution)/shard_map/ppermute | solution.py:227
  133.5 23.0 %collective-permute-start.5 = (bf16[2,2,2,256,128]{4,3,2,1,0:T(8,128)(2,1)}, bf16[2,2,2,256,128]{4,3,2,1,0:T(8,128)(2,1)S(1)}, u32[]{:S(2)}, u32[]{:S(2)}) collective-permute-start(bf16[2,2,2,256,128]{4,3,2,1,0:T(8,128)(2,1)} %shard_map.72), channel_id=1, source_target_pairs={{0,2},{2,4},{4,6},{6,0},{1,3},{3,5},{5,7},{7,1},{8,10},{10,12},{12... | collective-permute-start | bytes 1572872 | tf_op jit(solution)/shard_map/ppermute | solution.py:227
  139.7 16.7 %collective-permute-start.6 = (bf16[2,2,2,256,128]{4,3,2,1,0:T(8,128)(2,1)}, bf16[2,2,2,256,128]{4,3,2,1,0:T(8,128)(2,1)S(1)}, u32[]{:S(2)}, u32[]{:S(2)}) collective-permute-start(bf16[2,2,2,256,128]{4,3,2,1,0:T(8,128)(2,1)} %shard_map.73), channel_id=1, source_target_pairs={{0,6},{2,0},{4,2},{6,4},{1,7},{3,1},{5,3},{7,5},{8,14},{10,8},{12,... | collective-permute-start | bytes 1572872 | tf_op jit(solution)/shard_map/ppermute | solution.py:227
  144.5 11.9 %copy-start.4 = (bf16[2,2,2,256,128]{4,3,2,1,0:T(8,128)(2,1)}, bf16[2,2,2,256,128]{4,3,2,1,0:T(8,128)(2,1)S(1)}, u32[]{:S(2)}) copy-start(bf16[2,2,2,256,128]{4,3,2,1,0:T(8,128)(2,1)S(1)} %collective-permute-done.4.rest_0_) | copy-start | bytes 1572868
  156.4 0.8 copy-start.5
  157.2 0.8 copy-start.6
Sparse Core Ops, SparseCore 0:
  33.1 62.6 all-gather.2

commit v4 on v3

--- a/solution.py
+++ b/solution.py
@@ -194,6 +194,28 @@
     return swapped(jnp.broadcast_to(value[None], (count,) + value.shape), axes)
 
 
+def ring_gathered(piece):
+    z, core = lax.axis_index("z"), lax.axis_index("core")
+    away = 2 * core - 1
+    ring = [(2 * n + c, 2 * ((n + 1 - 2 * c) % 8) + c) for n in range(8) for c in range(2)]
+    cross = [(0, 1), (1, 0)]
+    current = gathered(piece, "core", 2)
+    whole = jnp.zeros((8,) + current.shape, current.dtype)
+    whole = lax.dynamic_update_slice_in_dim(whole, current[None], z, 0)
+    for step in range(1, 4):
+        current = lax.ppermute(current, ("z", "core"), ring)
+        passed = lax.ppermute(current, "core", cross)
+        whole = lax.dynamic_update_slice_in_dim(whole, current[None], (z + away * step) % 8, 0)
+        whole = lax.dynamic_update_slice_in_dim(whole, passed[None], (z - away * step) % 8, 0)
+    part = lax.dynamic_slice_in_dim(current, core, 1, 0)
+    part = lax.ppermute(part, ("z", "core"), ring)
+    passed = lax.ppermute(part, "core", cross)
+    zero = jnp.zeros_like(z)
+    at = lambda c: ((z + 4) % 8, c) + (zero,) * 3
+    whole = lax.dynamic_update_slice(whole, part[None], at(core))
+    return lax.dynamic_update_slice(whole, passed[None], at(1 - core))
+
+
 def local(tokens, in_weight, out_weight, mr_filter, cotangent):
     half = lax.axis_index("h")
     position = lax.axis_index(("l", "z"))
@@ -205,7 +227,7 @@
     weight = swapped(weight, ("h", "l"))
     values = jnp.stack([tokens, cotangent], 0)
     weight, values = lax.optimization_barrier((weight, values))
-    weight = lax.all_gather(weight, ("z", "core"), axis=0).reshape(8, 2, 2, 2, ROWS, STREAMS)
+    weight = ring_gathered(weight).reshape(8, 2, 2, 2, ROWS, STREAMS)
 
     band = bands(lax.dynamic_slice_in_dim(mr_filter, half * GROUPS, GROUPS, 0))
     values = gathered(values, ("h", "ylo"), 4)

time: 191 us -> 218 us (1.14)
  starting transfers between devices: 39.4 us -> 73.1 us
  local copies, waits for them, and re-layouts: 9.21 us -> 31.2 us
  between operations: 14.2 us -> 1.04 us
  blocking collectives: 35.4 us -> 23.9 us
  waiting for transfers between devices: 61.4 us -> 57.5 us
    ppermute x0 -> x8, starting transfers between devices: none -> 34.2 us  [the longest x3 20.7 us: ring_gathered(): current = lax.ppermute(current, ('z', 'core'), ring)]
    all_to_all x2 -> x3, waiting for transfers between devices: 36 us -> 14.4 us  [swapped(): return lax.all_to_all(value, axes, 0, 0, tiled=True)]
    ppermute x0 -> x8, waiting for transfers between devices: none -> 16.5 us  [the longest x3 13.6 us: ring_gathered(): current = lax.ppermute(current, ('z', 'core'), ring)]
    dynamic_update_slice x0 -> x9, local copies, waits for them, and re-layouts: none -> 15.2 us  [the longest x3 6.78 us: ring_gathered(): lax.dynamic_update_slice_in_dim(whole, current[None], (z + away * step) %...]
    all_to_all x2, blocking collectives: 35.4 us -> 23.9 us  [swapped(): return lax.all_to_all(value, axes, 0, 0, tiled=True)]
    all_gather x1 -> x0, waiting for transfers between devices: 6.02 us -> none  [local(): lax.all_gather(weight, ('z', 'core'), axis=0)]
    ppermute x3, waiting for transfers between devices: 13.1 us -> 19 us  [local(): lax.ppermute(part, 'x', [(n, (n + steps) % 4) for n in range(4)])]
    ppermute x1, waiting for transfers between devices: 0.43 us -> 6.28 us  [local(): before = lax.ppermute(product, ('l', 'z'), ring)]
  transfers between devices with their start and end apart: 10 -> 18, of which waited for: 9 -> 10; matrix products, arithmetic and copies ran while one was open for 2% -> 12% of each run, Pallas kernels for 5% -> 4%
where the time goes in v4:
time: 218 us; the launch traced here: 215 us
  starting transfers between devices  73.1 us (34%)
  waiting for transfers between devices  57.5 us (26%)
  local copies, waits for them, and re-layouts  31.2 us (14%)
  Pallas kernels  25.6 us (12%)
  blocking collectives  23.9 us (11%)
  other arithmetic  3.13 us (1%)
    all_to_all x2, blocking collectives, swapped(): return lax.all_to_all(value, axes, 0, 0, tiled=True)  23.9 us
    ppermute x3, starting transfers between devices, ring_gathered(): current = lax.ppermute(current, ('z', 'core'), ring)  20.7 us
    ppermute x3, waiting for transfers between devices, local(): lax.ppermute(part, 'x', [(n, (n + steps) % 4) for n in range(4)])  19 us
    all_to_all x3, starting transfers between devices, swapped(): return lax.all_to_all(value, axes, 0, 0, tiled=True)  15.2 us
    all_to_all x3, waiting for transfers between devices, swapped(): return lax.all_to_all(value, axes, 0, 0, tiled=True)  14.4 us
    pallas_call x4, Pallas kernels, backward(): pl.pallas_call(backward_kernel, out_shape=jax.ShapeDtypeStruct((2, 2, 2,...  13.6 us
    ppermute x3, waiting for transfers between devices, ring_gathered(): current = lax.ppermute(current, ('z', 'core'), ring)  13.6 us
    ppermute x1, starting transfers between devices, local(): after = lax.ppermute(mixed, ('l', 'z'), [(b, a) for a, b in ring])  8.77 us
  transfers between devices with their start and end apart: 18, of which 10 were waited for; matrix products, arithmetic and copies ran while one was open for 12% of the time, Pallas kernels for 4%

profile of v4, /device:TPU:1, one launch (start us, length us, event | category | flops | bytes accessed | tf_op | source)
XLA Modules:
  0.0 215.4 jit_solution(4369212514639641674)
XLA Ops:
  3.6 7.6 %all-to-all-start = ((bf16[4,128,512]{2,1,0:T(8,128)(2,1)}), bf16[4,128,512]{2,1,0:T(8,128)(2,1)S(1)}, u32[]{:S(2)}, u32[]{:S(2)}) async-start(bf16[4,128,512]{2,1,0:T(8,128)(2,1)} %bitcast.8), calls=%async_computation | async-start | bytes 1048576 | tf_op jit(solution)/shard_map/all_to_all | solution.py:190
  12.2 13.4 %all-to-all-done = bf16[4,128,512]{2,1,0:T(8,128)(2,1)S(1)} async-done(((bf16[4,128,512]{2,1,0:T(8,128)(2,1)}), bf16[4,128,512]{2,1,0:T(8,128)(2,1)S(1)}, u32[]{:S(2)}, u32[]{:S(2)}) %all-to-all-start) | async-done | bytes 524320 | tf_op jit(solution)/shard_map/all_to_all | solution.py:190
  25.6 6.5 %all_to_all.25 = bf16[2,4,128,512]{3,2,1,0:T(8,128)(2,1)S(1)} all-to-all(bf16[2,4,128,512]{3,2,1,0:T(8,128)(2,1)S(1)} %broadcast_in_dim.65), channel_id=1, replica_groups=mesh['h'=2,'l'=2,'z'=8,'ylo'=2,'x'=4,'core'=2] {'core'}, dimensions={0} | all-to-all | bytes 2097152 | tf_op jit(solution)/shard_map/all_to_all | solution.py:190
  32.1 10.4 %collective-permute-start.1 = (bf16[2,4,128,512]{3,2,1,0:T(8,128)(2,1)S(1)}, bf16[2,4,128,512]{3,2,1,0:T(8,128)(2,1)}, u32[]{:S(2)}, u32[]{:S(2)}) collective-permute-start(bf16[2,4,128,512]{3,2,1,0:T(8,128)(2,1)S(1)} %all_to_all.25), channel_id=1, source_target_pairs={{0,16},{1,113},{16,32},{17,1},{32,48},{33,17},{48,64},{49,33},{64,... | collective-permute-start | bytes 3145736 | tf_op jit(solution)/shard_map/ppermute | solution.py:206
  43.4 3.5 %all-to-all-start.1 = ((bf16[4,2,128,256]{3,2,1,0:T(8,128)(2,1)}), bf16[4,2,128,256]{3,2,1,0:T(8,128)(2,1)S(1)}, u32[]{:S(2)}, u32[]{:S(2)}) async-start(bf16[4,2,128,256]{3,2,1,0:T(8,128)(2,1)} %broadcast_in_dim.61), calls=%async_computation.1 | async-start | bytes 1048576 | tf_op jit(solution)/shard_map/all_to_all | solution.py:190
  46.9 7.3 %collective-permute-done.1 = bf16[2,4,128,512]{3,2,1,0:T(8,128)(2,1)} collective-permute-done((bf16[2,4,128,512]{3,2,1,0:T(8,128)(2,1)S(1)}, bf16[2,4,128,512]{3,2,1,0:T(8,128)(2,1)}, u32[]{:S(2)}, u32[]{:S(2)}) %collective-permute-start.1) | collective-permute-done | bytes 1048608 | tf_op jit(solution)/shard_map/ppermute | solution.py:206
  54.2 5.1 %collective-permute-start.3 = (bf16[2,4,128,512]{3,2,1,0:T(8,128)(2,1)}, bf16[2,4,128,512]{3,2,1,0:T(8,128)(2,1)}, u32[]{:S(2)}, u32[]{:S(2)}) collective-permute-start(bf16[2,4,128,512]{3,2,1,0:T(8,128)(2,1)} %collective-permute-done.1), channel_id=1, source_target_pairs={{0,16},{1,113},{16,32},{17,1},{32,48},{33,17},{48,64},{49,33},{64,... | collective-permute-start | bytes 3145736 | tf_op jit(solution)/shard_map/ppermute | solution.py:206
  61.1 4.0 %all-to-all-start.2 = ((bf16[4,4,2,128,256]{4,3,2,1,0:T(8,128)(2,1)}), bf16[4,4,2,128,256]{4,3,2,1,0:T(8,128)(2,1)S(1)}, u32[]{:S(2)}, u32[]{:S(2)}) async-start(bf16[4,4,2,128,256]{4,3,2,1,0:T(8,128)(2,1)} %broadcast_in_dim.62), calls=%async_computation.2 | async-start | bytes 4194304 | tf_op jit(solution)/shard_map/all_to_all | solution.py:190
  65.1 6.3 %collective-permute-done.3 = bf16[2,4,128,512]{3,2,1,0:T(8,128)(2,1)} collective-permute-done((bf16[2,4,128,512]{3,2,1,0:T(8,128)(2,1)}, bf16[2,4,128,512]{3,2,1,0:T(8,128)(2,1)}, u32[]{:S(2)}, u32[]{:S(2)}) %collective-permute-start.3) | collective-permute-done | bytes 1048608 | tf_op jit(solution)/shard_map/ppermute | solution.py:206
  71.4 5.2 %collective-permute-start.5 = (bf16[2,4,128,512]{3,2,1,0:T(8,128)(2,1)}, bf16[2,4,128,512]{3,2,1,0:T(8,128)(2,1)}, u32[]{:S(2)}, u32[]{:S(2)}) collective-permute-start(bf16[2,4,128,512]{3,2,1,0:T(8,128)(2,1)} %collective-permute-done.3), channel_id=1, source_target_pairs={{0,16},{1,113},{16,32},{17,1},{32,48},{33,17},{48,64},{49,33},{64,... | collective-permute-start | bytes 3145736 | tf_op jit(solution)/shard_map/ppermute | solution.py:206
  84.7 4.3 %broadcast_in_dim.64 = bf16[8,2,4,128,512]{4,3,2,1,0:T(8,128)(2,1)} broadcast(bf16[]{:T(256)} %constant.73.clone.1), dimensions={} | broadcast | bytes 8388610 | tf_op jit(solution)/shard_map/broadcast_in_dim | solution.py:203
  110.8 2.9 %collective-permute-done.7 = bf16[1,4,128,512]{3,2,1,0:T(8,128)(2,1)S(1)} collective-permute-done((bf16[1,4,128,512]{3,2,1,0:T(8,128)(2,1)S(1)}, bf16[1,4,128,512]{3,2,1,0:T(8,128)(2,1)S(1)}, u32[]{:S(2)}, u32[]{:S(2)}) %collective-permute-start.7) | collective-permute-done | bytes 524320 | tf_op jit(solution)/shard_map/ppermute | solution.py:211
  113.6 3.8 %collective-permute-start.8 = (bf16[1,4,128,512]{3,2,1,0:T(8,128)(2,1)S(1)}, bf16[1,4,128,512]{3,2,1,0:T(8,128)(2,1)S(1)}, u32[]{:S(2)}, u32[]{:S(2)}) collective-permute-start(bf16[1,4,128,512]{3,2,1,0:T(8,128)(2,1)S(1)} %collective-permute-done.7), channel_id=1, source_target_pairs={{0,1},{1,0},{2,3},{3,2},{4,5},{5,4},{6,7},{7,6},{8,9},{9,8},{10,11... | collective-permute-start | bytes 1572872 | tf_op jit(solution)/shard_map/ppermute | solution.py:212
  121.5 6.7 %shard_map.69 = (bf16[384,256]{1,0:T(8,128)(2,1)}, f32[128,256]{1,0:T(8,128)}, bf16[128,256]{1,0:T(8,128)(2,1)}, bf16[128,256]{1,0:T(8,128)(2,1)}) custom-call(s32[3]{0:T(128)} %pad_add_fusion.place_ref, bf16[4,2,2,2,128,256]{5,4,3,2,1,0:T(8,128)(2,1)} %bitcast.44, bf16[4,2,2,2,128,256]{5,4,3,2,1,0:T(8,128)(2,1)} %copy-done.3, ...), custom_call_target="tpu_custom_call" | custom-call | flops 1073741824 | bytes 9437184 | tf_op jit(solution)/shard_map/pallas_call | solution.py:75
  128.2 8.8 %collective-permute-start.10 = (bf16[128,256]{1,0:T(8,128)(2,1)}, bf16[128,256]{1,0:T(8,128)(2,1)S(1)}, u32[]{:S(2)}, u32[]{:S(2)}) collective-permute-start(bf16[128,256]{1,0:T(8,128)(2,1)} %get-tuple-element.17.mixed_ref), channel_id=1, source_target_pairs={{16,0},{32,16},{48,32},{64,48},{80,64},{96,80},{112,96},{128,112},... | collective-permute-start | bytes 196616 | tf_op jit(solution)/shard_map/ppermute | solution.py:242
  139.0 6.3 %collective-permute-done.9.before_ref = bf16[128,256]{1,0:T(8,128)(2,1)S(1)} collective-permute-done((bf16[128,256]{1,0:T(8,128)(2,1)}, bf16[128,256]{1,0:T(8,128)(2,1)S(1)}, u32[]{:S(2)}, u32[]{:S(2)}) %collective-permute-start.9) | collective-permute-done | bytes 65568 | tf_op jit(solution)/shard_map/ppermute | solution.py:241
  145.9 3.2 %shard_map.70.own_ref = bf16[512,256]{1,0:T(8,128)(2,1)} custom-call(s32[3]{0:T(128)} %pad_add_fusion.place_ref, bf16[256,2048]{1,0:T(8,128)(2,1)} %shard_map.68.band_ref, bf16[384,256]{1,0:T(8,128)(2,1)} %get-tuple-element.14.streams_ref, f32[128,256]{1,0:T(8,128)} %get-tuple-element.15.gate_ref, bf16[128,256]{1,0:T(8,128)(2,1)} %get-tuple-element.16.product_ref, ...), custom_call_target="tpu_custom_call" | custom-call | flops 268435456 | bytes 3145728 | tf_op jit(solution)/shard_map/pallas_call | solution.py:139
  149.1 3.3 %collective-permute-start.11 = (bf16[512,256]{1,0:T(8,128)(2,1)}, bf16[512,256]{1,0:T(8,128)(2,1)S(1)}, u32[]{:S(2)}, u32[]{:S(2)}) collective-permute-start(bf16[512,256]{1,0:T(8,128)(2,1)} %shard_map.70.own_ref), channel_id=1, source_target_pairs={{0,1},{1,0},{2,3},{3,2},{4,5},{5,4},{6,7},{7,6},{8,9},{9,8},{10,11... | collective-permute-start | bytes 786440 | tf_op jit(solution)/shard_map/ppermute | solution.py:245
  154.5 3.3 %shard_map.73 = bf16[2,2,2,256,128]{4,3,2,1,0:T(8,128)(2,1)} custom-call(s32[3]{0:T(128)} %pad_add_fusion.place_ref, bf16[512,256]{1,0:T(8,128)(2,1)} %shard_map.70.own_ref, bf16[512,256]{1,0:T(8,128)(2,1)} %copy-done.2, bf16[8,2,2,2,128,512]{5,4,3,2,1,0:T(8,128)(2,1)} %bitcast.21.weight_ref), custom_call_target="tpu_custom_call" | custom-call | flops 268435456 | bytes 3145728 | tf_op jit(solution)/shard_map/pallas_call | solution.py:175
  160.6 3.3 %shard_map.72 = bf16[2,2,2,256,128]{4,3,2,1,0:T(8,128)(2,1)} custom-call(s32[3]{0:T(128)} %pad_add_fusion.place_ref, bf16[512,256]{1,0:T(8,128)(2,1)} %shard_map.70.own_ref, bf16[512,256]{1,0:T(8,128)(2,1)} %copy-done.2, bf16[8,2,2,2,128,512]{5,4,3,2,1,0:T(8,128)(2,1)} %bitcast.21.weight_ref), custom_call_target="tpu_custom_call" | custom-call | flops 268435456 | bytes 3145728 | tf_op jit(solution)/shard_map/pallas_call | solution.py:175
  166.4 3.3 %shard_map.71 = bf16[2,2,2,256,128]{4,3,2,1,0:T(8,128)(2,1)} custom-call(s32[3]{0:T(128)} %pad_add_fusion.place_ref, bf16[512,256]{1,0:T(8,128)(2,1)} %shard_map.70.own_ref, bf16[512,256]{1,0:T(8,128)(2,1)} %copy-done.2, bf16[8,2,2,2,128,512]{5,4,3,2,1,0:T(8,128)(2,1)} %bitcast.21.weight_ref), custom_call_target="tpu_custom_call" | custom-call | flops 268435456 | bytes 3145728 | tf_op jit(solution)/shard_map/pallas_call | solution.py:175
  173.0 18.2 %collective-permute-done.13.rest_1_ = bf16[2,2,2,256,128]{4,3,2,1,0:T(8,128)(2,1)S(1)} collective-permute-done((bf16[2,2,2,256,128]{4,3,2,1,0:T(8,128)(2,1)}, bf16[2,2,2,256,128]{4,3,2,1,0:T(8,128)(2,1)S(1)}, u32[]{:S(2)}, u32[]{:S(2)}) %collective-permute-start.13) | collective-permute-done | bytes 524320 | tf_op jit(solution)/shard_map/ppermute | solution.py:249
  192.9 3.6 %shard_map.74 = bf16[2,2,2,256,128]{4,3,2,1,0:T(8,128)(2,1)} custom-call(s32[3]{0:T(128)} %pad_add_fusion.place_ref, bf16[512,256]{1,0:T(8,128)(2,1)} %shard_map.70.own_ref, bf16[512,256]{1,0:T(8,128)(2,1)} %copy-done.2, bf16[8,2,2,2,128,512]{5,4,3,2,1,0:T(8,128)(2,1)} %bitcast.21.weight_ref, bf16[2,2,2,256,128]{4,3,2,1,0:T(8,128)(2,1)} %copy-done.6, ...), custom_call_target="tpu_custom_call" | custom-call | flops 268435456 | bytes 3145728 | tf_op jit(solution)/shard_map/pallas_call | solution.py:175
  196.5 17.4 %all_to_all.26 = bf16[4,2,256,128]{3,2,1,0:T(8,128)(2,1)S(1)} all-to-all(bf16[4,2,256,128]{3,2,1,0:T(8,128)(2,1)} %bitcast.45), channel_id=1, replica_groups=mesh['h'=2,'l'=2,'z'=8,'ylo'=2,'x'=4,'core'=2] {'h','ylo'}, dimensions={0} | all-to-all | bytes 1048576 | tf_op jit(solution)/shard_map/all_to_all | solution.py:190
  (69 shorter events, 56.5 us)
Async XLA Ops:
  0.6 78.1 %copy-start = (f32[16,128]{1,0:T(8,128)S(1)}, f32[16,128]{1,0:T(8,128)}, u32[]{:S(2)}) copy-start(f32[16,128]{1,0:T(8,128)} %param.8) | copy-start | bytes 24580
  3.6 21.9 %all-to-all-start = ((bf16[4,128,512]{2,1,0:T(8,128)(2,1)}), bf16[4,128,512]{2,1,0:T(8,128)(2,1)S(1)}, u32[]{:S(2)}, u32[]{:S(2)}) async-start(bf16[4,128,512]{2,1,0:T(8,128)(2,1)} %bitcast.8), calls=%async_computation | async-start | bytes 1048576 | tf_op jit(solution)/shard_map/all_to_all | solution.py:190
  32.1 22.1 %collective-permute-start.1 = (bf16[2,4,128,512]{3,2,1,0:T(8,128)(2,1)S(1)}, bf16[2,4,128,512]{3,2,1,0:T(8,128)(2,1)}, u32[]{:S(2)}, u32[]{:S(2)}) collective-permute-start(bf16[2,4,128,512]{3,2,1,0:T(8,128)(2,1)S(1)} %all_to_all.25), channel_id=1, source_target_pairs={{0,16},{1,113},{16,32},{17,1},{32,48},{33,17},{48,64},{49,33},{64,... | collective-permute-start | bytes 3145736 | tf_op jit(solution)/shard_map/ppermute | solution.py:206
  43.4 16.1 %all-to-all-start.1 = ((bf16[4,2,128,256]{3,2,1,0:T(8,128)(2,1)}), bf16[4,2,128,256]{3,2,1,0:T(8,128)(2,1)S(1)}, u32[]{:S(2)}, u32[]{:S(2)}) async-start(bf16[4,2,128,256]{3,2,1,0:T(8,128)(2,1)} %broadcast_in_dim.61), calls=%async_computation.1 | async-start | bytes 1048576 | tf_op jit(solution)/shard_map/all_to_all | solution.py:190
  54.2 17.2 %collective-permute-start.3 = (bf16[2,4,128,512]{3,2,1,0:T(8,128)(2,1)}, bf16[2,4,128,512]{3,2,1,0:T(8,128)(2,1)}, u32[]{:S(2)}, u32[]{:S(2)}) collective-permute-start(bf16[2,4,128,512]{3,2,1,0:T(8,128)(2,1)} %collective-permute-done.1), channel_id=1, source_target_pairs={{0,16},{1,113},{16,32},{17,1},{32,48},{33,17},{48,64},{49,33},{64,... | collective-permute-start | bytes 3145736 | tf_op jit(solution)/shard_map/ppermute | solution.py:206
  61.1 29.9 %all-to-all-start.2 = ((bf16[4,4,2,128,256]{4,3,2,1,0:T(8,128)(2,1)}), bf16[4,4,2,128,256]{4,3,2,1,0:T(8,128)(2,1)S(1)}, u32[]{:S(2)}, u32[]{:S(2)}) async-start(bf16[4,4,2,128,256]{4,3,2,1,0:T(8,128)(2,1)} %broadcast_in_dim.62), calls=%async_computation.2 | async-start | bytes 4194304 | tf_op jit(solution)/shard_map/all_to_all | solution.py:190
  71.4 23.7 %collective-permute-start.5 = (bf16[2,4,128,512]{3,2,1,0:T(8,128)(2,1)}, bf16[2,4,128,512]{3,2,1,0:T(8,128)(2,1)}, u32[]{:S(2)}, u32[]{:S(2)}) collective-permute-start(bf16[2,4,128,512]{3,2,1,0:T(8,128)(2,1)} %collective-permute-done.3), channel_id=1, source_target_pairs={{0,16},{1,113},{16,32},{17,1},{32,48},{33,17},{48,64},{49,33},{64,... | collective-permute-start | bytes 3145736 | tf_op jit(solution)/shard_map/ppermute | solution.py:206
  76.6 21.0 %collective-permute-start.2 = (bf16[2,4,128,512]{3,2,1,0:T(8,128)(2,1)}, bf16[2,4,128,512]{3,2,1,0:T(8,128)(2,1)}, u32[]{:S(2)}, u32[]{:S(2)}) collective-permute-start(bf16[2,4,128,512]{3,2,1,0:T(8,128)(2,1)} %collective-permute-done.1), channel_id=1, source_target_pairs={{0,1},{1,0},{2,3},{3,2},{4,5},{5,4},{6,7},{7,6},{8,9},{9,8},{10,11... | collective-permute-start | bytes 3145736 | tf_op jit(solution)/shard_map/ppermute | solution.py:207
  82.3 24.0 %collective-permute-start.4 = (bf16[2,4,128,512]{3,2,1,0:T(8,128)(2,1)}, bf16[2,4,128,512]{3,2,1,0:T(8,128)(2,1)}, u32[]{:S(2)}, u32[]{:S(2)}) collective-permute-start(bf16[2,4,128,512]{3,2,1,0:T(8,128)(2,1)} %collective-permute-done.3), channel_id=1, source_target_pairs={{0,1},{1,0},{2,3},{3,2},{4,5},{5,4},{6,7},{7,6},{8,9},{9,8},{10,11... | collective-permute-start | bytes 3145736 | tf_op jit(solution)/shard_map/ppermute | solution.py:207
  90.9 29.3 %copy-start.1 = (bf16[4,4,2,128,256]{4,3,2,1,0:T(8,128)(2,1)}, bf16[4,4,2,128,256]{4,3,2,1,0:T(8,128)(2,1)S(1)}, u32[]{:S(2)}) copy-start(bf16[4,4,2,128,256]{4,3,2,1,0:T(8,128)(2,1)S(1)} %all-to-all-done.2) | copy-start | bytes 6291460
  90.9 29.3 %collective-permute-start = (bf16[4,2,2,2,128,256]{5,4,3,2,1,0:T(8,128)(2,1)S(1)}, bf16[4,2,2,2,128,256]{5,4,3,2,1,0:T(8,128)(2,1)S(1)}, u32[]{:S(2)}, u32[]{:S(2)}) collective-permute-start(bf16[4,2,2,2,128,256]{5,4,3,2,1,0:T(8,128)(2,1)S(1)} %bitcast.43), channel_id=1, source_target_pairs={{0,1},{1,0},{2,3},{3,2},{4,5},{5,4},{6,7},{7,6},{8,9},{9,8},{10,11... | collective-permute-start | bytes 6291464 | tf_op jit(solution)/shard_map/ppermute | solution.py:237
  95.1 22.3 %collective-permute-start.6 = (bf16[2,4,128,512]{3,2,1,0:T(8,128)(2,1)}, bf16[2,4,128,512]{3,2,1,0:T(8,128)(2,1)S(1)}, u32[]{:S(2)}, u32[]{:S(2)}) collective-permute-start(bf16[2,4,128,512]{3,2,1,0:T(8,128)(2,1)} %collective-permute-done.5), channel_id=1, source_target_pairs={{0,1},{1,0},{2,3},{3,2},{4,5},{5,4},{6,7},{7,6},{8,9},{9,8},{10,11... | collective-permute-start | bytes 3145736 | tf_op jit(solution)/shard_map/ppermute | solution.py:207
  103.4 10.2 %collective-permute-start.7 = (bf16[1,4,128,512]{3,2,1,0:T(8,128)(2,1)S(1)}, bf16[1,4,128,512]{3,2,1,0:T(8,128)(2,1)S(1)}, u32[]{:S(2)}, u32[]{:S(2)}) collective-permute-start(bf16[1,4,128,512]{3,2,1,0:T(8,128)(2,1)S(1)} %constant_dynamic-slice_fusion), channel_id=1, source_target_pairs={{0,16},{1,113},{16,32},{17,1},{32,48},{33,17},{48,64},{49,33},{64,... | collective-permute-start | bytes 1572872 | tf_op jit(solution)/shard_map/ppermute | solution.py:211
  113.6 5.7 %collective-permute-start.8 = (bf16[1,4,128,512]{3,2,1,0:T(8,128)(2,1)S(1)}, bf16[1,4,128,512]{3,2,1,0:T(8,128)(2,1)S(1)}, u32[]{:S(2)}, u32[]{:S(2)}) collective-permute-start(bf16[1,4,128,512]{3,2,1,0:T(8,128)(2,1)S(1)} %collective-permute-done.7), channel_id=1, source_target_pairs={{0,1},{1,0},{2,3},{3,2},{4,5},{5,4},{6,7},{7,6},{8,9},{9,8},{10,11... | collective-permute-start | bytes 1572872 | tf_op jit(solution)/shard_map/ppermute | solution.py:212
  120.2 1.3 copy-start.3
  128.2 10.7 %collective-permute-start.10 = (bf16[128,256]{1,0:T(8,128)(2,1)}, bf16[128,256]{1,0:T(8,128)(2,1)S(1)}, u32[]{:S(2)}, u32[]{:S(2)}) collective-permute-start(bf16[128,256]{1,0:T(8,128)(2,1)} %get-tuple-element.17.mixed_ref), channel_id=1, source_target_pairs={{16,0},{32,16},{48,32},{64,48},{80,64},{96,80},{112,96},{128,112},... | collective-permute-start | bytes 196616 | tf_op jit(solution)/shard_map/ppermute | solution.py:242
  137.0 8.2 %collective-permute-start.9 = (bf16[128,256]{1,0:T(8,128)(2,1)}, bf16[128,256]{1,0:T(8,128)(2,1)S(1)}, u32[]{:S(2)}, u32[]{:S(2)}) collective-permute-start(bf16[128,256]{1,0:T(8,128)(2,1)} %get-tuple-element.16.product_ref), channel_id=1, source_target_pairs={{0,16},{16,32},{32,48},{48,64},{64,80},{80,96},{96,112},{112,128},... | collective-permute-start | bytes 196616 | tf_op jit(solution)/shard_map/ppermute | solution.py:241
  138.9 6.3 %copy-start.7 = (bf16[128,256]{1,0:T(8,128)(2,1)}, bf16[128,256]{1,0:T(8,128)(2,1)S(1)}, u32[]{:S(2)}) copy-start(bf16[128,256]{1,0:T(8,128)(2,1)S(1)} %collective-permute-done.10.after_ref) | copy-start | bytes 196612
  149.1 4.7 %collective-permute-start.11 = (bf16[512,256]{1,0:T(8,128)(2,1)}, bf16[512,256]{1,0:T(8,128)(2,1)S(1)}, u32[]{:S(2)}, u32[]{:S(2)}) collective-permute-start(bf16[512,256]{1,0:T(8,128)(2,1)} %shard_map.70.own_ref), channel_id=1, source_target_pairs={{0,1},{1,0},{2,3},{3,2},{4,5},{5,4},{6,7},{7,6},{8,9},{9,8},{10,11... | collective-permute-start | bytes 786440 | tf_op jit(solution)/shard_map/ppermute | solution.py:245
  157.8 15.2 %collective-permute-start.14 = (bf16[2,2,2,256,128]{4,3,2,1,0:T(8,128)(2,1)}, bf16[2,2,2,256,128]{4,3,2,1,0:T(8,128)(2,1)S(1)}, u32[]{:S(2)}, u32[]{:S(2)}) collective-permute-start(bf16[2,2,2,256,128]{4,3,2,1,0:T(8,128)(2,1)} %shard_map.73), channel_id=1, source_target_pairs={{0,6},{2,0},{4,2},{6,4},{1,7},{3,1},{5,3},{7,5},{8,14},{10,8},{12,... | collective-permute-start | bytes 1572872 | tf_op jit(solution)/shard_map/ppermute | solution.py:249
  163.9 27.3 %collective-permute-start.13 = (bf16[2,2,2,256,128]{4,3,2,1,0:T(8,128)(2,1)}, bf16[2,2,2,256,128]{4,3,2,1,0:T(8,128)(2,1)S(1)}, u32[]{:S(2)}, u32[]{:S(2)}) collective-permute-start(bf16[2,2,2,256,128]{4,3,2,1,0:T(8,128)(2,1)} %shard_map.72), channel_id=1, source_target_pairs={{0,2},{2,4},{4,6},{6,0},{1,3},{3,5},{5,7},{7,1},{8,10},{10,12},{12... | collective-permute-start | bytes 1572872 | tf_op jit(solution)/shard_map/ppermute | solution.py:249
  169.8 21.5 %collective-permute-start.12 = (bf16[2,2,2,256,128]{4,3,2,1,0:T(8,128)(2,1)}, bf16[2,2,2,256,128]{4,3,2,1,0:T(8,128)(2,1)S(1)}, u32[]{:S(2)}, u32[]{:S(2)}) collective-permute-start(bf16[2,2,2,256,128]{4,3,2,1,0:T(8,128)(2,1)} %shard_map.71), channel_id=1, source_target_pairs={{0,4},{2,6},{4,0},{6,2},{1,5},{3,7},{5,1},{7,3},{8,12},{10,14},{12... | collective-permute-start | bytes 1572872 | tf_op jit(solution)/shard_map/ppermute | solution.py:249
  173.0 18.3 %copy-start.4 = (bf16[2,2,2,256,128]{4,3,2,1,0:T(8,128)(2,1)}, bf16[2,2,2,256,128]{4,3,2,1,0:T(8,128)(2,1)S(1)}, u32[]{:S(2)}) copy-start(bf16[2,2,2,256,128]{4,3,2,1,0:T(8,128)(2,1)S(1)} %collective-permute-done.14.rest_2_) | copy-start | bytes 1572868
  191.3 0.8 copy-start.5
  (3 other events, 2.1 us)

commit v5 on v3

--- a/solution.py
+++ b/solution.py
@@ -17,7 +17,7 @@
 BACK = 3 * HALF
 BF16 = jnp.bfloat16
 F32 = jnp.float32
-VMEM_FORWARD = 56 << 20
+VMEM_FORWARD = 52 << 20
 
 
 def bands_kernel(base_ref, band_ref):
@@ -132,58 +132,93 @@
         terms_ref[BACK:, lanes[s]] = (query * conv[s]).astype(BF16)
 
 
-TERMS_SPEC = pl.BlockSpec((STREAMS, 2 * ROWS), lambda j, p: (0, 0))
-
-
-def middle(place, *operands):
-    return pl.pallas_call(
-        middle_kernel,
-        out_shape=jax.ShapeDtypeStruct((STREAMS, 2 * ROWS), BF16),
-        grid_spec=pltpu.PrefetchScalarGridSpec(
-            num_scalar_prefetch=1,
-            grid=(1,),
-            in_specs=[pl.BlockSpec(value.shape, lambda j, p: (0, 0)) for value in operands],
-            out_specs=TERMS_SPEC,
-        ),
-        cost_estimate=pl.CostEstimate(flops=1 << 28, bytes_accessed=3 << 20, transcendentals=0),
-    )(place, *operands)
-
-
-def backward_kernel(place_ref, own_ref, other_ref, weight_ref, *rest):
-    *arrived, out_ref = rest
-    core = place_ref[0]
-    results = [0.0, 0.0]
-    for terms_ref, which in ((own_ref, core), (other_ref, 1 - core)):
-        weight = weight_ref[:, pl.ds(which, 1), 0, 0].reshape(FEATURES, STREAMS)
-        results[0] += jnp.dot(weight[:, BACK:], terms_ref[BACK:], preferred_element_type=F32)
-        results[1] += jnp.dot(weight[:, :BACK], terms_ref[:BACK], preferred_element_type=F32)
-    for which in range(2):
-        for h in range(2):
-            part = results[which][:, h * ROWS : (h + 1) * ROWS]
-            for ref in arrived:
-                part += ref[h, 0, which].astype(F32)
-            out_ref[h, 0, which] = part.astype(BF16)
-
-
-def backward(steps, place, own, other, weight, arrived=()):
-    spec = pl.BlockSpec((2, 1, 2, FEATURES, ROWS), lambda j, p: (0, j, 0, 0, 0))
-
-    def weight_at(j, p):
-        x = lax.rem(p[2] + steps, 4)
-        return (lax.rem(x, 2) * 2 + p[0], 0, j, x // 2, 0, 0)
-
-    return pl.pallas_call(
-        backward_kernel,
-        out_shape=jax.ShapeDtypeStruct((2, 2, 2, FEATURES, ROWS), BF16),
-        grid_spec=pltpu.PrefetchScalarGridSpec(
-            num_scalar_prefetch=1,
-            grid=(2,),
-            in_specs=[TERMS_SPEC, TERMS_SPEC, pl.BlockSpec((2, 2, 1, 1, ROWS, STREAMS), weight_at)]
-            + [spec] * len(arrived),
-            out_specs=spec,
-        ),
-        cost_estimate=pl.CostEstimate(flops=1 << 28, bytes_accessed=3 << 20, transcendentals=0),
-    )(place, own, other, weight, *arrived)
+def on_chip(kernel, out_shape, operands, flops):
+    smem, vmem = pl.BlockSpec(memory_space=pltpu.SMEM), pl.BlockSpec(memory_space=pltpu.VMEM)
+    return pl.pallas_call(
+        kernel,
+        out_shape=out_shape,
+        in_specs=[smem] + [vmem] * (len(operands) - 1),
+        out_specs=jax.tree.map(lambda _: vmem, out_shape),
+        compiler_params=pltpu.CompilerParams(vmem_limit_bytes=24 << 20),
+        cost_estimate=pl.CostEstimate(flops=flops, bytes_accessed=1 << 20, transcendentals=0),
+    )(*operands)
+
+
+def middle(*operands):
+    return on_chip(middle_kernel, jax.ShapeDtypeStruct((STREAMS, 2 * ROWS), BF16), operands, 1 << 28)
+
+
+MIXED, GRAD = 0, 1
+BLOCK = (2, 2, FEATURES, ROWS)
+
+
+def backward(steps, parts, operands, arrived=(), last=False):
+    def kernel(place_ref, own_ref, other_ref, weight_ref, *refs):
+        *arrived_refs, out_ref = refs
+        core = place_ref[0]
+        x = lax.rem(place_ref[2] + steps, 4)
+        for y in range(2):
+            for at, part in enumerate(parts):
+                rows = slice(0, BACK) if part == GRAD else slice(BACK, STREAMS)
+                result = 0.0
+                for terms_ref, which in ((own_ref, core), (other_ref, 1 - core)):
+                    weight = weight_ref[lax.rem(x, 2), :, which, y, lax.div(x, 2)].reshape(FEATURES, STREAMS)
+                    result += jnp.dot(weight[:, rows], terms_ref[rows], preferred_element_type=F32)
+                for h in range(2):
+                    total = result[:, h * ROWS : (h + 1) * ROWS]
+                    for (held, _), ref in zip(arrived, arrived_refs):
+                        if part in held:
+                            total += ref[held.index(part), h, y].astype(F32)
+                    if last:
+                        out_ref[2 * h + y, at] = total.astype(BF16)
+                    else:
+                        out_ref[at, h, y] = total.astype(BF16)
+
+    shape = (4, len(parts)) + BLOCK[2:] if last else (len(parts),) + BLOCK
+    return on_chip(
+        kernel,
+        jax.ShapeDtypeStruct(shape, BF16),
+        operands + tuple(array for _, array in arrived),
+        len(parts) << 27,
+    )
+
+
+def pack_kernel(in_ref, out_ref, packed_ref):
+    for h in range(2):
+        chans = slice(h * HALF, (h + 1) * HALF)
+        turned = out_ref[chans].astype(F32).T.astype(BF16)
+        for l in range(2):
+            for stream in range(3):
+                packed_ref[2 * h + l, :, stream * HALF : (stream + 1) * HALF] = in_ref[stream, :, chans]
+            packed_ref[2 * h + l, :, BACK:] = turned
+
+
+def packed(in_weight, out_weight):
+    vmem = pl.BlockSpec(memory_space=pltpu.VMEM)
+    return pl.pallas_call(
+        pack_kernel,
+        out_shape=jax.ShapeDtypeStruct((4, ROWS, STREAMS), BF16),
+        in_specs=[vmem] * 2,
+        out_specs=vmem,
+    )(in_weight, out_weight)
+
+
+def finish_kernel(parts_ref, mixed_ref, grad_ref):
+    for at, ref in ((MIXED, mixed_ref), (GRAD, grad_ref)):
+        total = parts_ref[0, at].astype(F32)
+        for source in range(1, 4):
+            total += parts_ref[source, at].astype(F32)
+        ref[...] = total.T.astype(BF16)
+
+
+def finish(parts):
+    vmem = pl.BlockSpec(memory_space=pltpu.VMEM)
+    return pl.pallas_call(
+        finish_kernel,
+        out_shape=(jax.ShapeDtypeStruct((ROWS, FEATURES), BF16),) * 2,
+        in_specs=[vmem],
+        out_specs=(vmem, vmem),
+    )(parts)
 
 
 def swapped(value, axes):
@@ -195,14 +230,11 @@
 
 
 def local(tokens, in_weight, out_weight, mr_filter, cotangent):
-    half = lax.axis_index("h")
+    half, core = lax.axis_index("h"), lax.axis_index("core")
     position = lax.axis_index(("l", "z"))
-    place = jnp.stack([lax.axis_index("core"), position, lax.axis_index("x")]).astype(jnp.int32)
-
-    weight = jnp.concatenate([in_weight, out_weight.T[None]], 0)
-    weight = weight.reshape(4, ROWS, 2, HALF).transpose(2, 1, 0, 3).reshape(2, 1, ROWS, STREAMS)
-    weight = jnp.broadcast_to(weight, (2, 2, ROWS, STREAMS)).reshape(4, ROWS, STREAMS)
-    weight = swapped(weight, ("h", "l"))
+    place = jnp.stack([core, position, lax.axis_index("x")]).astype(jnp.int32)
+
+    weight = swapped(packed(in_weight, out_weight), ("h", "l"))
     values = jnp.stack([tokens, cotangent], 0)
     weight, values = lax.optimization_barrier((weight, values))
     weight = lax.all_gather(weight, ("z", "core"), axis=0).reshape(8, 2, 2, 2, ROWS, STREAMS)
@@ -218,16 +250,24 @@
     ring = [(n, (n + 1) % 16) for n in range(16)]
     before = lax.ppermute(product, ("l", "z"), ring)
     after = lax.ppermute(mixed, ("l", "z"), [(b, a) for a, b in ring])
+    weight, gate = lax.optimization_barrier((weight, gate))
+    weight = lax.dynamic_index_in_dim(
+        weight.reshape(2, 2, 2, 2, 2, 2, ROWS, STREAMS), core, 1, keepdims=False
+    )
 
     terms = middle(place, band, streams, gate, product, mixed, before, after)
-    other_terms = lax.ppermute(terms, "core", cross)
-    arrived = []
-    for steps in (2, 1, 3):
-        part = backward(steps, place, terms, other_terms, weight)
-        arrived.append(lax.ppermute(part, "x", [(n, (n + steps) % 4) for n in range(4)]))
-    sums = backward(0, place, terms, other_terms, weight, arrived)
-    sums = swapped(sums.reshape(4, 2, FEATURES, ROWS), ("h", "ylo")).astype(F32).sum(0).astype(BF16)
-    return sums[0].T, sums[1].T
+    operands = (place, terms, lax.ppermute(terms, "core", cross), weight)
+
+    def sent(array, steps):
+        return lax.ppermute(array, "x", [(n, (n + steps) % 4) for n in range(4)])
+
+    both = (MIXED, GRAD)
+    relayed = sent(backward(2, (GRAD,), operands), 3)
+    direct = sent(backward(2, (MIXED,), operands), 2)
+    right = sent(backward(1, both, operands), 1)
+    left = sent(backward(3, both, operands, [((GRAD,), relayed)]), 3)
+    sums = backward(0, both, operands, [((MIXED,), direct), (both, right), (both, left)], last=True)
+    return finish(swapped(sums, ("h", "ylo")))
 
 
 def solution(mesh):

time: 191 us -> 185 us (0.969)
  the two profiles are of different devices: /device:TPU:1 before, /device:TPU:14 now
where the time goes in v5:
time: 185 us; the launch traced here: 184 us
  waiting for transfers between devices  67.3 us (36%)
  blocking collectives  42.2 us (23%)
  starting transfers between devices  35.5 us (19%)
  Pallas kernels  17.7 us (10%)
  between operations  14.2 us (8%)
  local copies, waits for them, and re-layouts  5.3 us (3%)
    all_to_all x2, blocking collectives, swapped(): return lax.all_to_all(value, axes, 0, 0, tiled=True)  42.2 us
    all_to_all x2, waiting for transfers between devices, swapped(): return lax.all_to_all(value, axes, 0, 0, tiled=True)  34.5 us
    ppermute x4, waiting for transfers between devices, sent(): return lax.ppermute(array, 'x', [(n, (n + steps) % 4) for n in range(4)])  20.2 us
    ppermute x4, starting transfers between devices, sent(): return lax.ppermute(array, 'x', [(n, (n + steps) % 4) for n in range(4)])  11.9 us
    all_to_all x2, starting transfers between devices, swapped(): return lax.all_to_all(value, axes, 0, 0, tiled=True)  11 us
    ppermute x1, starting transfers between devices, local(): after = lax.ppermute(mixed, ('l', 'z'), [(b, a) for a, b in ring])  6.93 us
    pallas_call x6, Pallas kernels, on_chip(): pl.pallas_call(kernel, out_shape=out_shape, in_specs=[smem] + [vmem] * (l...  6.1 us
    pallas_call x1, Pallas kernels, forward(): pl.pallas_call(forward_kernel, out_shape=(shape(BACK, BF16), shape(HALF,...  5.83 us
  transfers between devices with their start and end apart: 11, of which 9 were waited for; matrix products, arithmetic and copies ran while one was open for 3% of the time, Pallas kernels for 3%

profile of v5, /device:TPU:14, one launch (start us, length us, event | category | flops | bytes accessed | tf_op | source)
XLA Modules:
  0.0 183.9 jit_solution(7440455446137258506)
XLA Ops:
  7.2 1.8 %shard_map.68 = bf16[4,128,512]{2,1,0:T(8,128)(2,1)} custom-call(bf16[3,128,256]{2,1,0:T(8,128)(2,1)} %in_ref.1, bf16[256,128]{1,0:T(8,128)(2,1)} %out_ref.1), custom_call_target="tpu_custom_call" | custom-call | tf_op jit(solution)/shard_map/pallas_call | solution.py:198
  9.0 6.2 %all-to-all-start = ((bf16[4,128,512]{2,1,0:T(8,128)(2,1)}), bf16[4,128,512]{2,1,0:T(8,128)(2,1)S(1)}, u32[]{:S(2)}, u32[]{:S(2)}) async-start(bf16[4,128,512]{2,1,0:T(8,128)(2,1)} %shard_map.68), calls=%async_computation | async-start | bytes 1048576 | tf_op jit(solution)/shard_map/all_to_all | solution.py:225
  16.1 14.4 %all-to-all-done = bf16[4,128,512]{2,1,0:T(8,128)(2,1)S(1)} async-done(((bf16[4,128,512]{2,1,0:T(8,128)(2,1)}), bf16[4,128,512]{2,1,0:T(8,128)(2,1)S(1)}, u32[]{:S(2)}, u32[]{:S(2)}) %all-to-all-start) | async-done | bytes 524320 | tf_op jit(solution)/shard_map/all_to_all | solution.py:225
  31.4 21.1 %all_to_all.20 = bf16[4,2,128,256]{3,2,1,0:T(8,128)(2,1)S(1)} all-to-all(bf16[4,2,128,256]{3,2,1,0:T(8,128)(2,1)S(1)} %broadcast_in_dim.6), channel_id=1, replica_groups=mesh['h'=2,'l'=2,'z'=8,'ylo'=2,'x'=4,'core'=2] {'h','ylo'}, dimensions={0} | all-to-all | bytes 1048576 | tf_op jit(solution)/shard_map/all_to_all | solution.py:225
  54.1 4.8 %all-to-all-start.2 = ((bf16[4,4,2,128,256]{4,3,2,1,0:T(8,128)(2,1)}), bf16[4,4,2,128,256]{4,3,2,1,0:T(8,128)(2,1)S(1)}, u32[]{:S(2)}, u32[]{:S(2)}) async-start(bf16[4,4,2,128,256]{4,3,2,1,0:T(8,128)(2,1)} %broadcast_in_dim.7), calls=%async_computation.2 | async-start | bytes 4194304 | tf_op jit(solution)/shard_map/all_to_all | solution.py:225
  59.7 2.1 %shard_map.69.band_ref = bf16[256,2048]{1,0:T(8,128)(2,1)} custom-call(f32[16,256]{1,0:T(8,128)} %select_maximum_fusion.base_ref), custom_call_target="tpu_custom_call" | custom-call | tf_op jit(solution)/shard_map/pallas_call | solution.py:34
  61.8 20.1 %all-to-all-done.2 = bf16[4,4,2,128,256]{4,3,2,1,0:T(8,128)(2,1)S(1)} async-done(((bf16[4,4,2,128,256]{4,3,2,1,0:T(8,128)(2,1)}), bf16[4,4,2,128,256]{4,3,2,1,0:T(8,128)(2,1)S(1)}, u32[]{:S(2)}, u32[]{:S(2)}) %all-to-all-start.2) | async-done | bytes 2097184 | tf_op jit(solution)/shard_map/all_to_all | solution.py:225
  81.9 1.9 %collective-permute-start = (bf16[4,2,2,2,128,256]{5,4,3,2,1,0:T(8,128)(2,1)S(1)}, bf16[4,2,2,2,128,256]{5,4,3,2,1,0:T(8,128)(2,1)}, u32[]{:S(2)}, u32[]{:S(2)}) collective-permute-start(bf16[4,2,2,2,128,256]{5,4,3,2,1,0:T(8,128)(2,1)S(1)} %bitcast.15), channel_id=1, source_target_pairs={{0,1},{1,0},{2,3},{3,2},{4,5},{5,4},{6,7},{7,6},{8,9},{9,8},{10,11... | collective-permute-start | bytes 6291464 | tf_op jit(solution)/shard_map/ppermute | solution.py:247
  83.9 4.2 %collective-permute-done.other_ref = bf16[4,2,2,2,128,256]{5,4,3,2,1,0:T(8,128)(2,1)} collective-permute-done((bf16[4,2,2,2,128,256]{5,4,3,2,1,0:T(8,128)(2,1)S(1)}, bf16[4,2,2,2,128,256]{5,4,3,2,1,0:T(8,128)(2,1)}, u32[]{:S(2)}, u32[]{:S(2)}) %collective-permute-start) | collective-permute-done | bytes 2097184 | tf_op jit(solution)/shard_map/ppermute | solution.py:247
  88.1 5.1 %all-gather.3.cloned.1.call-done = bf16[64,128,512]{2,1,0:T(8,128)(2,1)} async-done(((bf16[4,128,512]{2,1,0:T(8,128)(2,1)}), bf16[64,128,512]{2,1,0:T(8,128)(2,1)}) %all-gather.3.cloned.1.call-update) | async-done | bytes 8388624 | tf_op jit(solution)/shard_map/all_gather | solution.py:240
  93.2 5.8 %shard_map.70 = (bf16[384,256]{1,0:T(8,128)(2,1)S(1)}, f32[128,256]{1,0:T(8,128)S(1)}, bf16[128,256]{1,0:T(8,128)(2,1)S(1)}, bf16[128,256]{1,0:T(8,128)(2,1)S(1)}) custom-call(s32[3]{0:T(128)S(1)} %pad_add_fusion.place_ref, bf16[4,2,2,2,128,256]{5,4,3,2,1,0:T(8,128)(2,1)} %bitcast.16, bf16[4,2,2,2,128,256]{5,4,3,2,1,0:T(8,128)(2,1)} %collective-permute-done.other_ref, ...), custom_call_target="tpu_custom_call" | custom-call | flops 1073741824 | bytes 9437184 | tf_op jit(solution)/shard_map/pallas_call | solution.py:75
  99.0 1.9 %collective-permute-start.1 = (bf16[128,256]{1,0:T(8,128)(2,1)S(1)}, bf16[128,256]{1,0:T(8,128)(2,1)S(1)}, u32[]{:S(2)}, u32[]{:S(2)}) collective-permute-start(bf16[128,256]{1,0:T(8,128)(2,1)S(1)} %get-tuple-element.19.product_ref), channel_id=1, source_target_pairs={{0,16},{16,32},{32,48},{48,64},{64,80},{80,96},{96,112},{112,128},... | collective-permute-start | bytes 196616 | tf_op jit(solution)/shard_map/ppermute | solution.py:251
  101.0 6.9 %collective-permute-start.2 = (bf16[128,256]{1,0:T(8,128)(2,1)S(1)}, bf16[128,256]{1,0:T(8,128)(2,1)S(1)}, u32[]{:S(2)}, u32[]{:S(2)}) collective-permute-start(bf16[128,256]{1,0:T(8,128)(2,1)S(1)} %get-tuple-element.20.mixed_ref), channel_id=1, source_target_pairs={{16,0},{32,16},{48,32},{64,48},{80,64},{96,80},{112,96},{128,112},... | collective-permute-start | bytes 196616 | tf_op jit(solution)/shard_map/ppermute | solution.py:252
  108.3 2.8 %collective-permute-done.2.after_ref = bf16[128,256]{1,0:T(8,128)(2,1)S(1)} collective-permute-done((bf16[128,256]{1,0:T(8,128)(2,1)S(1)}, bf16[128,256]{1,0:T(8,128)(2,1)S(1)}, u32[]{:S(2)}, u32[]{:S(2)}) %collective-permute-start.2) | collective-permute-done | bytes 65568 | tf_op jit(solution)/shard_map/ppermute | solution.py:252
  112.1 1.9 %collective-permute-start.3 = (bf16[512,256]{1,0:T(8,128)(2,1)S(1)}, bf16[512,256]{1,0:T(8,128)(2,1)S(1)}, u32[]{:S(2)}, u32[]{:S(2)}) collective-permute-start(bf16[512,256]{1,0:T(8,128)(2,1)S(1)} %shard_map.71.own_ref), channel_id=1, source_target_pairs={{0,1},{1,0},{2,3},{3,2},{4,5},{5,4},{6,7},{7,6},{8,9},{9,8},{10,11... | collective-permute-start | bytes 786440 | tf_op jit(solution)/shard_map/ppermute | solution.py:259
  114.0 2.6 %dynamic-slice_bitcast_fusion.weight_ref = bf16[2,2,2,2,2,128,512]{6,5,4,3,2,1,0:T(8,128)(2,1)S(1)} fusion(bf16[2,2,2,2,2,2,128,512]{7,6,5,4,3,2,1,0:T(8,128)(2,1)} %bitcast.14, s32[]{:T(128)S(6)} %select_n.8), kind=kLoop, calls=%fused_computation | loop fusion | bytes 8388612 | tf_op jit(solution)/shard_map/jit(dynamic_index_in_dim)/squeeze | solution.py:254
  117.7 2.5 %collective-permute-start.6 = (bf16[1,2,2,256,128]{4,3,2,1,0:T(8,128)(2,1)S(1)}, bf16[1,2,2,256,128]{4,3,2,1,0:T(8,128)(2,1)S(1)}, u32[]{:S(2)}, u32[]{:S(2)}) collective-permute-start(bf16[1,2,2,256,128]{4,3,2,1,0:T(8,128)(2,1)S(1)} %shard_map.74), channel_id=1, source_target_pairs={{0,6},{2,0},{4,2},{6,4},{1,7},{3,1},{5,3},{7,5},{8,14},{10,8},{12,... | collective-permute-start | bytes 786440 | tf_op jit(solution)/shard_map/ppermute | solution.py:262
  121.2 4.6 %collective-permute-start.5 = (bf16[2,2,2,256,128]{4,3,2,1,0:T(8,128)(2,1)S(1)}, bf16[2,2,2,256,128]{4,3,2,1,0:T(8,128)(2,1)S(1)}, u32[]{:S(2)}, u32[]{:S(2)}) collective-permute-start(bf16[2,2,2,256,128]{4,3,2,1,0:T(8,128)(2,1)S(1)} %shard_map.73), channel_id=1, source_target_pairs={{0,2},{2,4},{4,6},{6,0},{1,3},{3,5},{5,7},{7,1},{8,10},{10,12},{12... | collective-permute-start | bytes 1572872 | tf_op jit(solution)/shard_map/ppermute | solution.py:262
  125.8 3.6 %collective-permute-done.6.refs_0_ = bf16[1,2,2,256,128]{4,3,2,1,0:T(8,128)(2,1)S(1)} collective-permute-done((bf16[1,2,2,256,128]{4,3,2,1,0:T(8,128)(2,1)S(1)}, bf16[1,2,2,256,128]{4,3,2,1,0:T(8,128)(2,1)S(1)}, u32[]{:S(2)}, u32[]{:S(2)}) %collective-permute-start.6) | collective-permute-done | bytes 262176 | tf_op jit(solution)/shard_map/ppermute | solution.py:262
  130.6 1.9 %collective-permute-start.7 = (bf16[2,2,2,256,128]{4,3,2,1,0:T(8,128)(2,1)S(1)}, bf16[2,2,2,256,128]{4,3,2,1,0:T(8,128)(2,1)S(1)}, u32[]{:S(2)}, u32[]{:S(2)}) collective-permute-start(bf16[2,2,2,256,128]{4,3,2,1,0:T(8,128)(2,1)S(1)} %shard_map.75), channel_id=1, source_target_pairs={{0,6},{2,0},{4,2},{6,4},{1,7},{3,1},{5,3},{7,5},{8,14},{10,8},{12,... | collective-permute-start | bytes 1572872 | tf_op jit(solution)/shard_map/ppermute | solution.py:262
  133.3 2.9 %collective-permute-start.4 = (bf16[1,2,2,256,128]{4,3,2,1,0:T(8,128)(2,1)S(1)}, bf16[1,2,2,256,128]{4,3,2,1,0:T(8,128)(2,1)S(1)}, u32[]{:S(2)}, u32[]{:S(2)}) collective-permute-start(bf16[1,2,2,256,128]{4,3,2,1,0:T(8,128)(2,1)S(1)} %shard_map.72), channel_id=1, source_target_pairs={{0,4},{2,6},{4,0},{6,2},{1,5},{3,7},{5,1},{7,3},{8,12},{10,14},{12... | collective-permute-start | bytes 786440 | tf_op jit(solution)/shard_map/ppermute | solution.py:262
  136.2 14.5 %collective-permute-done.4.refs_0_ = bf16[1,2,2,256,128]{4,3,2,1,0:T(8,128)(2,1)S(1)} collective-permute-done((bf16[1,2,2,256,128]{4,3,2,1,0:T(8,128)(2,1)S(1)}, bf16[1,2,2,256,128]{4,3,2,1,0:T(8,128)(2,1)S(1)}, u32[]{:S(2)}, u32[]{:S(2)}) %collective-permute-start.4) | collective-permute-done | bytes 262176 | tf_op jit(solution)/shard_map/ppermute | solution.py:262
  150.7 2.1 %collective-permute-done.7.refs_2_ = bf16[2,2,2,256,128]{4,3,2,1,0:T(8,128)(2,1)S(1)} collective-permute-done((bf16[2,2,2,256,128]{4,3,2,1,0:T(8,128)(2,1)S(1)}, bf16[2,2,2,256,128]{4,3,2,1,0:T(8,128)(2,1)S(1)}, u32[]{:S(2)}, u32[]{:S(2)}) %collective-permute-start.7) | collective-permute-done | bytes 524320 | tf_op jit(solution)/shard_map/ppermute | solution.py:262
  154.0 21.2 %all_to_all.21.parts_ref = bf16[4,2,256,128]{3,2,1,0:T(8,128)(2,1)} all-to-all(bf16[4,2,256,128]{3,2,1,0:T(8,128)(2,1)S(1)} %shard_map.76), channel_id=1, replica_groups=mesh['h'=2,'l'=2,'z'=8,'ylo'=2,'x'=4,'core'=2] {'h','ylo'}, dimensions={0} | all-to-all | bytes 1048576 | tf_op jit(solution)/shard_map/all_to_all | solution.py:225
  (29 shorter events, 12.6 us)
Async XLA Ops:
  7.2 51.7 %copy-start = (f32[16,128]{1,0:T(8,128)S(1)}, f32[16,128]{1,0:T(8,128)}, u32[]{:S(2)}) copy-start(f32[16,128]{1,0:T(8,128)} %param.8) | copy-start | bytes 24580
  9.0 21.5 %all-to-all-start = ((bf16[4,128,512]{2,1,0:T(8,128)(2,1)}), bf16[4,128,512]{2,1,0:T(8,128)(2,1)S(1)}, u32[]{:S(2)}, u32[]{:S(2)}) async-start(bf16[4,128,512]{2,1,0:T(8,128)(2,1)} %shard_map.68), calls=%async_computation | async-start | bytes 1048576 | tf_op jit(solution)/shard_map/all_to_all | solution.py:225
  15.2 78.0 %all-gather.3.cloned.1.call-start = ((), (), s32[]{:S(2)}) async-start(), calls=%async_computation.4 | async-start | bytes 8912896 | tf_op jit(solution)/shard_map/all_gather | solution.py:240
  30.5 0.8 copy-start.3
  54.1 27.8 %all-to-all-start.2 = ((bf16[4,4,2,128,256]{4,3,2,1,0:T(8,128)(2,1)}), bf16[4,4,2,128,256]{4,3,2,1,0:T(8,128)(2,1)S(1)}, u32[]{:S(2)}, u32[]{:S(2)}) async-start(bf16[4,4,2,128,256]{4,3,2,1,0:T(8,128)(2,1)} %broadcast_in_dim.7), calls=%async_computation.2 | async-start | bytes 4194304 | tf_op jit(solution)/shard_map/all_to_all | solution.py:225
  81.9 11.3 %copy-start.2 = (bf16[4,4,2,128,256]{4,3,2,1,0:T(8,128)(2,1)}, bf16[4,4,2,128,256]{4,3,2,1,0:T(8,128)(2,1)S(1)}, u32[]{:S(2)}) copy-start(bf16[4,4,2,128,256]{4,3,2,1,0:T(8,128)(2,1)S(1)} %all-to-all-done.2) | copy-start | bytes 6291460
  81.9 6.2 %collective-permute-start = (bf16[4,2,2,2,128,256]{5,4,3,2,1,0:T(8,128)(2,1)S(1)}, bf16[4,2,2,2,128,256]{5,4,3,2,1,0:T(8,128)(2,1)}, u32[]{:S(2)}, u32[]{:S(2)}) collective-permute-start(bf16[4,2,2,2,128,256]{5,4,3,2,1,0:T(8,128)(2,1)S(1)} %bitcast.15), channel_id=1, source_target_pairs={{0,1},{1,0},{2,3},{3,2},{4,5},{5,4},{6,7},{7,6},{8,9},{9,8},{10,11... | collective-permute-start | bytes 6291464 | tf_op jit(solution)/shard_map/ppermute | solution.py:247
  93.2 17.9 %copy-start.1 = (bf16[256,2048]{1,0:T(8,128)(2,1)S(1)}, bf16[256,2048]{1,0:T(8,128)(2,1)}, u32[]{:S(2)}) copy-start(bf16[256,2048]{1,0:T(8,128)(2,1)} %shard_map.69.band_ref) | copy-start | bytes 3145732
  99.0 9.2 %collective-permute-start.1 = (bf16[128,256]{1,0:T(8,128)(2,1)S(1)}, bf16[128,256]{1,0:T(8,128)(2,1)S(1)}, u32[]{:S(2)}, u32[]{:S(2)}) collective-permute-start(bf16[128,256]{1,0:T(8,128)(2,1)S(1)} %get-tuple-element.19.product_ref), channel_id=1, source_target_pairs={{0,16},{16,32},{32,48},{48,64},{64,80},{80,96},{96,112},{112,128},... | collective-permute-start | bytes 196616 | tf_op jit(solution)/shard_map/ppermute | solution.py:251
  101.0 10.1 %collective-permute-start.2 = (bf16[128,256]{1,0:T(8,128)(2,1)S(1)}, bf16[128,256]{1,0:T(8,128)(2,1)S(1)}, u32[]{:S(2)}, u32[]{:S(2)}) collective-permute-start(bf16[128,256]{1,0:T(8,128)(2,1)S(1)} %get-tuple-element.20.mixed_ref), channel_id=1, source_target_pairs={{16,0},{32,16},{48,32},{64,48},{80,64},{96,80},{112,96},{128,112},... | collective-permute-start | bytes 196616 | tf_op jit(solution)/shard_map/ppermute | solution.py:252
  112.1 4.6 %collective-permute-start.3 = (bf16[512,256]{1,0:T(8,128)(2,1)S(1)}, bf16[512,256]{1,0:T(8,128)(2,1)S(1)}, u32[]{:S(2)}, u32[]{:S(2)}) collective-permute-start(bf16[512,256]{1,0:T(8,128)(2,1)S(1)} %shard_map.71.own_ref), channel_id=1, source_target_pairs={{0,1},{1,0},{2,3},{3,2},{4,5},{5,4},{6,7},{7,6},{8,9},{9,8},{10,11... | collective-permute-start | bytes 786440 | tf_op jit(solution)/shard_map/ppermute | solution.py:259
  117.7 11.8 %collective-permute-start.6 = (bf16[1,2,2,256,128]{4,3,2,1,0:T(8,128)(2,1)S(1)}, bf16[1,2,2,256,128]{4,3,2,1,0:T(8,128)(2,1)S(1)}, u32[]{:S(2)}, u32[]{:S(2)}) collective-permute-start(bf16[1,2,2,256,128]{4,3,2,1,0:T(8,128)(2,1)S(1)} %shard_map.74), channel_id=1, source_target_pairs={{0,6},{2,0},{4,2},{6,4},{1,7},{3,1},{5,3},{7,5},{8,14},{10,8},{12,... | collective-permute-start | bytes 786440 | tf_op jit(solution)/shard_map/ppermute | solution.py:262
  121.2 29.5 %collective-permute-start.5 = (bf16[2,2,2,256,128]{4,3,2,1,0:T(8,128)(2,1)S(1)}, bf16[2,2,2,256,128]{4,3,2,1,0:T(8,128)(2,1)S(1)}, u32[]{:S(2)}, u32[]{:S(2)}) collective-permute-start(bf16[2,2,2,256,128]{4,3,2,1,0:T(8,128)(2,1)S(1)} %shard_map.73), channel_id=1, source_target_pairs={{0,2},{2,4},{4,6},{6,0},{1,3},{3,5},{5,7},{7,1},{8,10},{10,12},{12... | collective-permute-start | bytes 1572872 | tf_op jit(solution)/shard_map/ppermute | solution.py:262
  130.6 22.3 %collective-permute-start.7 = (bf16[2,2,2,256,128]{4,3,2,1,0:T(8,128)(2,1)S(1)}, bf16[2,2,2,256,128]{4,3,2,1,0:T(8,128)(2,1)S(1)}, u32[]{:S(2)}, u32[]{:S(2)}) collective-permute-start(bf16[2,2,2,256,128]{4,3,2,1,0:T(8,128)(2,1)S(1)} %shard_map.75), channel_id=1, source_target_pairs={{0,6},{2,0},{4,2},{6,4},{1,7},{3,1},{5,3},{7,5},{8,14},{10,8},{12,... | collective-permute-start | bytes 1572872 | tf_op jit(solution)/shard_map/ppermute | solution.py:262
  133.3 17.4 %collective-permute-start.4 = (bf16[1,2,2,256,128]{4,3,2,1,0:T(8,128)(2,1)S(1)}, bf16[1,2,2,256,128]{4,3,2,1,0:T(8,128)(2,1)S(1)}, u32[]{:S(2)}, u32[]{:S(2)}) collective-permute-start(bf16[1,2,2,256,128]{4,3,2,1,0:T(8,128)(2,1)S(1)} %shard_map.72), channel_id=1, source_target_pairs={{0,4},{2,6},{4,0},{6,2},{1,5},{3,7},{5,1},{7,3},{8,12},{10,14},{12... | collective-permute-start | bytes 786440 | tf_op jit(solution)/shard_map/ppermute | solution.py:262
Sparse Core Ops, SparseCore 0:
  31.5 61.6 all-gather.2

commit v6 on v5

--- a/solution.py
+++ b/solution.py
@@ -255,18 +255,25 @@
         weight.reshape(2, 2, 2, 2, 2, 2, ROWS, STREAMS), core, 1, keepdims=False
     )
 
+    before, weight = lax.optimization_barrier((before, weight))
+
     terms = middle(place, band, streams, gate, product, mixed, before, after)
-    operands = (place, terms, lax.ppermute(terms, "core", cross), weight)
-
-    def sent(array, steps):
-        return lax.ppermute(array, "x", [(n, (n + steps) % 4) for n in range(4)])
+    other_terms = lax.ppermute(terms, "core", cross)
 
     both = (MIXED, GRAD)
-    relayed = sent(backward(2, (GRAD,), operands), 3)
-    direct = sent(backward(2, (MIXED,), operands), 2)
-    right = sent(backward(1, both, operands), 1)
-    left = sent(backward(3, both, operands, [((GRAD,), relayed)]), 3)
-    sums = backward(0, both, operands, [((MIXED,), direct), (both, right), (both, left)], last=True)
+
+    def sent(steps, parts, target, arrived=()):
+        nonlocal terms
+        block = backward(steps, parts, (place, terms, other_terms, weight), arrived)
+        block, terms = lax.optimization_barrier((block, terms))
+        return lax.ppermute(block, "x", [(n, (n + target) % 4) for n in range(4)])
+
+    relayed = sent(2, (GRAD,), 3)
+    direct = sent(2, (MIXED,), 2)
+    right = sent(1, both, 1)
+    left = sent(3, both, 3, [((GRAD,), relayed)])
+    arrived = [((MIXED,), direct), (both, right), (both, left)]
+    sums = backward(0, both, (place, terms, other_terms, weight), arrived, last=True)
     return finish(swapped(sums, ("h", "ylo")))
 
 

time: 185 us -> 183 us (0.989)
  waiting for transfers between devices: 67.3 us -> 65.2 us
    ppermute x1, waiting for transfers between devices: 2.82 us -> 0.44 us  [local(): after = lax.ppermute(mixed, ('l', 'z'), [(b, a) for a, b in ring])]
where the time goes in v6:
time: 183 us; the launch traced here: 182 us
  waiting for transfers between devices  65.2 us (36%)
  blocking collectives  42.4 us (23%)
  starting transfers between devices  35.5 us (19%)
  Pallas kernels  17.7 us (10%)
  between operations  14.2 us (8%)
  local copies, waits for them, and re-layouts  5.38 us (3%)
    all_to_all x2, blocking collectives, swapped(): return lax.all_to_all(value, axes, 0, 0, tiled=True)  42.4 us
    all_to_all x2, waiting for transfers between devices, swapped(): return lax.all_to_all(value, axes, 0, 0, tiled=True)  34.5 us
    ppermute x4, waiting for transfers between devices, sent(): return lax.ppermute(block, 'x', [(n, (n + target) % 4) for n in range(4)])  19.5 us
    ppermute x4, starting transfers between devices, sent(): return lax.ppermute(block, 'x', [(n, (n + target) % 4) for n in range(4)])  11.9 us
    all_to_all x2, starting transfers between devices, swapped(): return lax.all_to_all(value, axes, 0, 0, tiled=True)  11 us
    ppermute x1, starting transfers between devices, local(): after = lax.ppermute(mixed, ('l', 'z'), [(b, a) for a, b in ring])  6.93 us
    pallas_call x6, Pallas kernels, on_chip(): pl.pallas_call(kernel, out_shape=out_shape, in_specs=[smem] + [vmem] * (l...  6.09 us
    pallas_call x1, Pallas kernels, forward(): pl.pallas_call(forward_kernel, out_shape=(shape(BACK, BF16), shape(HALF,...  5.83 us
  transfers between devices with their start and end apart: 11, of which 9 were waited for; matrix products, arithmetic and copies ran while one was open for 3% of the time, Pallas kernels for 3%

profile of v6, /device:TPU:14, one launch (start us, length us, event | category | flops | bytes accessed | tf_op | source)
XLA Modules:
  0.0 182.1 jit_solution(17463290354322940956)
XLA Ops:
  7.2 1.8 %shard_map.68 = bf16[4,128,512]{2,1,0:T(8,128)(2,1)} custom-call(bf16[3,128,256]{2,1,0:T(8,128)(2,1)} %in_ref.1, bf16[256,128]{1,0:T(8,128)(2,1)} %out_ref.1), custom_call_target="tpu_custom_call" | custom-call | tf_op jit(solution)/shard_map/pallas_call | solution.py:198
  9.0 6.2 %all-to-all-start = ((bf16[4,128,512]{2,1,0:T(8,128)(2,1)}), bf16[4,128,512]{2,1,0:T(8,128)(2,1)S(1)}, u32[]{:S(2)}, u32[]{:S(2)}) async-start(bf16[4,128,512]{2,1,0:T(8,128)(2,1)} %shard_map.68), calls=%async_computation | async-start | bytes 1048576 | tf_op jit(solution)/shard_map/all_to_all | solution.py:225
  16.1 14.4 %all-to-all-done = bf16[4,128,512]{2,1,0:T(8,128)(2,1)S(1)} async-done(((bf16[4,128,512]{2,1,0:T(8,128)(2,1)}), bf16[4,128,512]{2,1,0:T(8,128)(2,1)S(1)}, u32[]{:S(2)}, u32[]{:S(2)}) %all-to-all-start) | async-done | bytes 524320 | tf_op jit(solution)/shard_map/all_to_all | solution.py:225
  31.4 21.1 %all_to_all.20 = bf16[4,2,128,256]{3,2,1,0:T(8,128)(2,1)S(1)} all-to-all(bf16[4,2,128,256]{3,2,1,0:T(8,128)(2,1)S(1)} %broadcast_in_dim.6), channel_id=1, replica_groups=mesh['h'=2,'l'=2,'z'=8,'ylo'=2,'x'=4,'core'=2] {'h','ylo'}, dimensions={0} | all-to-all | bytes 1048576 | tf_op jit(solution)/shard_map/all_to_all | solution.py:225
  54.1 4.8 %all-to-all-start.2 = ((bf16[4,4,2,128,256]{4,3,2,1,0:T(8,128)(2,1)}), bf16[4,4,2,128,256]{4,3,2,1,0:T(8,128)(2,1)S(1)}, u32[]{:S(2)}, u32[]{:S(2)}) async-start(bf16[4,4,2,128,256]{4,3,2,1,0:T(8,128)(2,1)} %broadcast_in_dim.7), calls=%async_computation.2 | async-start | bytes 4194304 | tf_op jit(solution)/shard_map/all_to_all | solution.py:225
  59.7 2.1 %shard_map.69.band_ref = bf16[256,2048]{1,0:T(8,128)(2,1)} custom-call(f32[16,256]{1,0:T(8,128)} %select_maximum_fusion.base_ref), custom_call_target="tpu_custom_call" | custom-call | tf_op jit(solution)/shard_map/pallas_call | solution.py:34
  61.8 20.1 %all-to-all-done.2 = bf16[4,4,2,128,256]{4,3,2,1,0:T(8,128)(2,1)S(1)} async-done(((bf16[4,4,2,128,256]{4,3,2,1,0:T(8,128)(2,1)}), bf16[4,4,2,128,256]{4,3,2,1,0:T(8,128)(2,1)S(1)}, u32[]{:S(2)}, u32[]{:S(2)}) %all-to-all-start.2) | async-done | bytes 2097184 | tf_op jit(solution)/shard_map/all_to_all | solution.py:225
  81.9 1.9 %collective-permute-start = (bf16[4,2,2,2,128,256]{5,4,3,2,1,0:T(8,128)(2,1)S(1)}, bf16[4,2,2,2,128,256]{5,4,3,2,1,0:T(8,128)(2,1)}, u32[]{:S(2)}, u32[]{:S(2)}) collective-permute-start(bf16[4,2,2,2,128,256]{5,4,3,2,1,0:T(8,128)(2,1)S(1)} %bitcast.15), channel_id=1, source_target_pairs={{0,1},{1,0},{2,3},{3,2},{4,5},{5,4},{6,7},{7,6},{8,9},{9,8},{10,11... | collective-permute-start | bytes 6291464 | tf_op jit(solution)/shard_map/ppermute | solution.py:247
  83.9 4.2 %collective-permute-done.other_ref = bf16[4,2,2,2,128,256]{5,4,3,2,1,0:T(8,128)(2,1)} collective-permute-done((bf16[4,2,2,2,128,256]{5,4,3,2,1,0:T(8,128)(2,1)S(1)}, bf16[4,2,2,2,128,256]{5,4,3,2,1,0:T(8,128)(2,1)}, u32[]{:S(2)}, u32[]{:S(2)}) %collective-permute-start) | collective-permute-done | bytes 2097184 | tf_op jit(solution)/shard_map/ppermute | solution.py:247
  88.1 5.1 %all-gather.3.cloned.1.call-done = bf16[64,128,512]{2,1,0:T(8,128)(2,1)} async-done(((bf16[4,128,512]{2,1,0:T(8,128)(2,1)}), bf16[64,128,512]{2,1,0:T(8,128)(2,1)}) %all-gather.3.cloned.1.call-update) | async-done | bytes 8388624 | tf_op jit(solution)/shard_map/all_gather | solution.py:240
  93.2 5.8 %shard_map.70 = (bf16[384,256]{1,0:T(8,128)(2,1)S(1)}, f32[128,256]{1,0:T(8,128)S(1)}, bf16[128,256]{1,0:T(8,128)(2,1)S(1)}, bf16[128,256]{1,0:T(8,128)(2,1)S(1)}) custom-call(s32[3]{0:T(128)S(1)} %pad_add_fusion.place_ref, bf16[4,2,2,2,128,256]{5,4,3,2,1,0:T(8,128)(2,1)} %bitcast.16, bf16[4,2,2,2,128,256]{5,4,3,2,1,0:T(8,128)(2,1)} %collective-permute-done.other_ref, ...), custom_call_target="tpu_custom_call" | custom-call | flops 1073741824 | bytes 9437184 | tf_op jit(solution)/shard_map/pallas_call | solution.py:75
  99.0 1.9 %collective-permute-start.1 = (bf16[128,256]{1,0:T(8,128)(2,1)S(1)}, bf16[128,256]{1,0:T(8,128)(2,1)S(1)}, u32[]{:S(2)}, u32[]{:S(2)}) collective-permute-start(bf16[128,256]{1,0:T(8,128)(2,1)S(1)} %get-tuple-element.29.product_ref), channel_id=1, source_target_pairs={{0,16},{16,32},{32,48},{48,64},{64,80},{80,96},{96,112},{112,128},... | collective-permute-start | bytes 196616 | tf_op jit(solution)/shard_map/ppermute | solution.py:251
  101.0 6.9 %collective-permute-start.2 = (bf16[128,256]{1,0:T(8,128)(2,1)S(1)}, bf16[128,256]{1,0:T(8,128)(2,1)S(1)}, u32[]{:S(2)}, u32[]{:S(2)}) collective-permute-start(bf16[128,256]{1,0:T(8,128)(2,1)S(1)} %get-tuple-element.30.mixed_ref), channel_id=1, source_target_pairs={{16,0},{32,16},{48,32},{64,48},{80,64},{96,80},{112,96},{128,112},... | collective-permute-start | bytes 196616 | tf_op jit(solution)/shard_map/ppermute | solution.py:252
  107.9 2.7 %dynamic-slice_bitcast_fusion.weight_ref = bf16[2,2,2,2,2,128,512]{6,5,4,3,2,1,0:T(8,128)(2,1)S(1)} fusion(bf16[2,2,2,2,2,2,128,512]{7,6,5,4,3,2,1,0:T(8,128)(2,1)} %bitcast.14, s32[]{:T(128)S(6)} %select_n.8), kind=kLoop, calls=%fused_computation | loop fusion | bytes 8388612 | tf_op jit(solution)/shard_map/jit(dynamic_index_in_dim)/squeeze | solution.py:254
  112.1 1.9 %collective-permute-start.3 = (bf16[512,256]{1,0:T(8,128)(2,1)S(1)}, bf16[512,256]{1,0:T(8,128)(2,1)S(1)}, u32[]{:S(2)}, u32[]{:S(2)}) collective-permute-start(bf16[512,256]{1,0:T(8,128)(2,1)S(1)} %shard_map.71.own_ref), channel_id=1, source_target_pairs={{0,1},{1,0},{2,3},{3,2},{4,5},{5,4},{6,7},{7,6},{8,9},{9,8},{10,11... | collective-permute-start | bytes 786440 | tf_op jit(solution)/shard_map/ppermute | solution.py:261
  116.5 2.5 %collective-permute-start.4 = (bf16[1,2,2,256,128]{4,3,2,1,0:T(8,128)(2,1)S(1)}, bf16[1,2,2,256,128]{4,3,2,1,0:T(8,128)(2,1)S(1)}, u32[]{:S(2)}, u32[]{:S(2)}) collective-permute-start(bf16[1,2,2,256,128]{4,3,2,1,0:T(8,128)(2,1)S(1)} %shard_map.72), channel_id=1, source_target_pairs={{0,6},{2,0},{4,2},{6,4},{1,7},{3,1},{5,3},{7,5},{8,14},{10,8},{12,... | collective-permute-start | bytes 786440 | tf_op jit(solution)/shard_map/ppermute | solution.py:269
  120.9 4.6 %collective-permute-start.6 = (bf16[2,2,2,256,128]{4,3,2,1,0:T(8,128)(2,1)S(1)}, bf16[2,2,2,256,128]{4,3,2,1,0:T(8,128)(2,1)S(1)}, u32[]{:S(2)}, u32[]{:S(2)}) collective-permute-start(bf16[2,2,2,256,128]{4,3,2,1,0:T(8,128)(2,1)S(1)} %shard_map.74), channel_id=1, source_target_pairs={{0,2},{2,4},{4,6},{6,0},{1,3},{3,5},{5,7},{7,1},{8,10},{10,12},{12... | collective-permute-start | bytes 1572872 | tf_op jit(solution)/shard_map/ppermute | solution.py:269
  125.5 2.5 %collective-permute-done.4.refs_0_ = bf16[1,2,2,256,128]{4,3,2,1,0:T(8,128)(2,1)S(1)} collective-permute-done((bf16[1,2,2,256,128]{4,3,2,1,0:T(8,128)(2,1)S(1)}, bf16[1,2,2,256,128]{4,3,2,1,0:T(8,128)(2,1)S(1)}, u32[]{:S(2)}, u32[]{:S(2)}) %collective-permute-start.4) | collective-permute-done | bytes 262176 | tf_op jit(solution)/shard_map/ppermute | solution.py:269
  129.0 1.9 %collective-permute-start.7 = (bf16[2,2,2,256,128]{4,3,2,1,0:T(8,128)(2,1)S(1)}, bf16[2,2,2,256,128]{4,3,2,1,0:T(8,128)(2,1)S(1)}, u32[]{:S(2)}, u32[]{:S(2)}) collective-permute-start(bf16[2,2,2,256,128]{4,3,2,1,0:T(8,128)(2,1)S(1)} %shard_map.75), channel_id=1, source_target_pairs={{0,6},{2,0},{4,2},{6,4},{1,7},{3,1},{5,3},{7,5},{8,14},{10,8},{12,... | collective-permute-start | bytes 1572872 | tf_op jit(solution)/shard_map/ppermute | solution.py:269
  131.0 2.9 %collective-permute-start.5 = (bf16[1,2,2,256,128]{4,3,2,1,0:T(8,128)(2,1)S(1)}, bf16[1,2,2,256,128]{4,3,2,1,0:T(8,128)(2,1)S(1)}, u32[]{:S(2)}, u32[]{:S(2)}) collective-permute-start(bf16[1,2,2,256,128]{4,3,2,1,0:T(8,128)(2,1)S(1)} %shard_map.73), channel_id=1, source_target_pairs={{0,4},{2,6},{4,0},{6,2},{1,5},{3,7},{5,1},{7,3},{8,12},{10,14},{12... | collective-permute-start | bytes 786440 | tf_op jit(solution)/shard_map/ppermute | solution.py:269
  133.9 14.9 %collective-permute-done.5.refs_0_ = bf16[1,2,2,256,128]{4,3,2,1,0:T(8,128)(2,1)S(1)} collective-permute-done((bf16[1,2,2,256,128]{4,3,2,1,0:T(8,128)(2,1)S(1)}, bf16[1,2,2,256,128]{4,3,2,1,0:T(8,128)(2,1)S(1)}, u32[]{:S(2)}, u32[]{:S(2)}) %collective-permute-start.5) | collective-permute-done | bytes 262176 | tf_op jit(solution)/shard_map/ppermute | solution.py:269
  148.8 2.1 %collective-permute-done.7.refs_2_ = bf16[2,2,2,256,128]{4,3,2,1,0:T(8,128)(2,1)S(1)} collective-permute-done((bf16[2,2,2,256,128]{4,3,2,1,0:T(8,128)(2,1)S(1)}, bf16[2,2,2,256,128]{4,3,2,1,0:T(8,128)(2,1)S(1)}, u32[]{:S(2)}, u32[]{:S(2)}) %collective-permute-start.7) | collective-permute-done | bytes 524320 | tf_op jit(solution)/shard_map/ppermute | solution.py:269
  152.1 21.3 %all_to_all.21.parts_ref = bf16[4,2,256,128]{3,2,1,0:T(8,128)(2,1)} all-to-all(bf16[4,2,256,128]{3,2,1,0:T(8,128)(2,1)S(1)} %shard_map.76), channel_id=1, replica_groups=mesh['h'=2,'l'=2,'z'=8,'ylo'=2,'x'=4,'core'=2] {'h','ylo'}, dimensions={0} | all-to-all | bytes 1048576 | tf_op jit(solution)/shard_map/all_to_all | solution.py:225
  173.4 1.8 %shard_map.77 = (bf16[128,256]{1,0:T(8,128)(2,1)}, bf16[128,256]{1,0:T(8,128)(2,1)}) custom-call(bf16[4,2,256,128]{3,2,1,0:T(8,128)(2,1)} %all_to_all.21.parts_ref), custom_call_target="tpu_custom_call" | custom-call | tf_op jit(solution)/shard_map/pallas_call | solution.py:216
  (29 shorter events, 12.3 us)
Async XLA Ops:
  7.2 51.7 %copy-start = (f32[16,128]{1,0:T(8,128)S(1)}, f32[16,128]{1,0:T(8,128)}, u32[]{:S(2)}) copy-start(f32[16,128]{1,0:T(8,128)} %param.8) | copy-start | bytes 24580
  9.0 21.5 %all-to-all-start = ((bf16[4,128,512]{2,1,0:T(8,128)(2,1)}), bf16[4,128,512]{2,1,0:T(8,128)(2,1)S(1)}, u32[]{:S(2)}, u32[]{:S(2)}) async-start(bf16[4,128,512]{2,1,0:T(8,128)(2,1)} %shard_map.68), calls=%async_computation | async-start | bytes 1048576 | tf_op jit(solution)/shard_map/all_to_all | solution.py:225
  15.2 78.0 %all-gather.3.cloned.1.call-start = ((), (), s32[]{:S(2)}) async-start(), calls=%async_computation.4 | async-start | bytes 8912896 | tf_op jit(solution)/shard_map/all_gather | solution.py:240
  30.5 0.8 copy-start.3
  54.1 27.8 %all-to-all-start.2 = ((bf16[4,4,2,128,256]{4,3,2,1,0:T(8,128)(2,1)}), bf16[4,4,2,128,256]{4,3,2,1,0:T(8,128)(2,1)S(1)}, u32[]{:S(2)}, u32[]{:S(2)}) async-start(bf16[4,4,2,128,256]{4,3,2,1,0:T(8,128)(2,1)} %broadcast_in_dim.7), calls=%async_computation.2 | async-start | bytes 4194304 | tf_op jit(solution)/shard_map/all_to_all | solution.py:225
  81.9 11.3 %copy-start.2 = (bf16[4,4,2,128,256]{4,3,2,1,0:T(8,128)(2,1)}, bf16[4,4,2,128,256]{4,3,2,1,0:T(8,128)(2,1)S(1)}, u32[]{:S(2)}) copy-start(bf16[4,4,2,128,256]{4,3,2,1,0:T(8,128)(2,1)S(1)} %all-to-all-done.2) | copy-start | bytes 6291460
  81.9 6.2 %collective-permute-start = (bf16[4,2,2,2,128,256]{5,4,3,2,1,0:T(8,128)(2,1)S(1)}, bf16[4,2,2,2,128,256]{5,4,3,2,1,0:T(8,128)(2,1)}, u32[]{:S(2)}, u32[]{:S(2)}) collective-permute-start(bf16[4,2,2,2,128,256]{5,4,3,2,1,0:T(8,128)(2,1)S(1)} %bitcast.15), channel_id=1, source_target_pairs={{0,1},{1,0},{2,3},{3,2},{4,5},{5,4},{6,7},{7,6},{8,9},{9,8},{10,11... | collective-permute-start | bytes 6291464 | tf_op jit(solution)/shard_map/ppermute | solution.py:247
  99.0 11.6 %collective-permute-start.1 = (bf16[128,256]{1,0:T(8,128)(2,1)S(1)}, bf16[128,256]{1,0:T(8,128)(2,1)S(1)}, u32[]{:S(2)}, u32[]{:S(2)}) collective-permute-start(bf16[128,256]{1,0:T(8,128)(2,1)S(1)} %get-tuple-element.29.product_ref), channel_id=1, source_target_pairs={{0,16},{16,32},{32,48},{48,64},{64,80},{80,96},{96,112},{112,128},... | collective-permute-start | bytes 196616 | tf_op jit(solution)/shard_map/ppermute | solution.py:251
  101.0 10.1 %collective-permute-start.2 = (bf16[128,256]{1,0:T(8,128)(2,1)S(1)}, bf16[128,256]{1,0:T(8,128)(2,1)S(1)}, u32[]{:S(2)}, u32[]{:S(2)}) collective-permute-start(bf16[128,256]{1,0:T(8,128)(2,1)S(1)} %get-tuple-element.30.mixed_ref), channel_id=1, source_target_pairs={{16,0},{32,16},{48,32},{64,48},{80,64},{96,80},{112,96},{128,112},... | collective-permute-start | bytes 196616 | tf_op jit(solution)/shard_map/ppermute | solution.py:252
  107.9 3.2 %copy-start.1 = (bf16[256,2048]{1,0:T(8,128)(2,1)S(1)}, bf16[256,2048]{1,0:T(8,128)(2,1)}, u32[]{:S(2)}) copy-start(bf16[256,2048]{1,0:T(8,128)(2,1)} %shard_map.69.band_ref) | copy-start | bytes 3145732
  112.1 3.4 %collective-permute-start.3 = (bf16[512,256]{1,0:T(8,128)(2,1)S(1)}, bf16[512,256]{1,0:T(8,128)(2,1)S(1)}, u32[]{:S(2)}, u32[]{:S(2)}) collective-permute-start(bf16[512,256]{1,0:T(8,128)(2,1)S(1)} %shard_map.71.own_ref), channel_id=1, source_target_pairs={{0,1},{1,0},{2,3},{3,2},{4,5},{5,4},{6,7},{7,6},{8,9},{9,8},{10,11... | collective-permute-start | bytes 786440 | tf_op jit(solution)/shard_map/ppermute | solution.py:261
  116.5 11.5 %collective-permute-start.4 = (bf16[1,2,2,256,128]{4,3,2,1,0:T(8,128)(2,1)S(1)}, bf16[1,2,2,256,128]{4,3,2,1,0:T(8,128)(2,1)S(1)}, u32[]{:S(2)}, u32[]{:S(2)}) collective-permute-start(bf16[1,2,2,256,128]{4,3,2,1,0:T(8,128)(2,1)S(1)} %shard_map.72), channel_id=1, source_target_pairs={{0,6},{2,0},{4,2},{6,4},{1,7},{3,1},{5,3},{7,5},{8,14},{10,8},{12,... | collective-permute-start | bytes 786440 | tf_op jit(solution)/shard_map/ppermute | solution.py:269
  120.9 27.9 %collective-permute-start.6 = (bf16[2,2,2,256,128]{4,3,2,1,0:T(8,128)(2,1)S(1)}, bf16[2,2,2,256,128]{4,3,2,1,0:T(8,128)(2,1)S(1)}, u32[]{:S(2)}, u32[]{:S(2)}) collective-permute-start(bf16[2,2,2,256,128]{4,3,2,1,0:T(8,128)(2,1)S(1)} %shard_map.74), channel_id=1, source_target_pairs={{0,2},{2,4},{4,6},{6,0},{1,3},{3,5},{5,7},{7,1},{8,10},{10,12},{12... | collective-permute-start | bytes 1572872 | tf_op jit(solution)/shard_map/ppermute | solution.py:269
  129.0 21.9 %collective-permute-start.7 = (bf16[2,2,2,256,128]{4,3,2,1,0:T(8,128)(2,1)S(1)}, bf16[2,2,2,256,128]{4,3,2,1,0:T(8,128)(2,1)S(1)}, u32[]{:S(2)}, u32[]{:S(2)}) collective-permute-start(bf16[2,2,2,256,128]{4,3,2,1,0:T(8,128)(2,1)S(1)} %shard_map.75), channel_id=1, source_target_pairs={{0,6},{2,0},{4,2},{6,4},{1,7},{3,1},{5,3},{7,5},{8,14},{10,8},{12,... | collective-permute-start | bytes 1572872 | tf_op jit(solution)/shard_map/ppermute | solution.py:269
  131.0 17.8 %collective-permute-start.5 = (bf16[1,2,2,256,128]{4,3,2,1,0:T(8,128)(2,1)S(1)}, bf16[1,2,2,256,128]{4,3,2,1,0:T(8,128)(2,1)S(1)}, u32[]{:S(2)}, u32[]{:S(2)}) collective-permute-start(bf16[1,2,2,256,128]{4,3,2,1,0:T(8,128)(2,1)S(1)} %shard_map.73), channel_id=1, source_target_pairs={{0,4},{2,6},{4,0},{6,2},{1,5},{3,7},{5,1},{7,3},{8,12},{10,14},{12... | collective-permute-start | bytes 786440 | tf_op jit(solution)/shard_map/ppermute | solution.py:269
Sparse Core Ops, SparseCore 0:
  31.5 61.6 all-gather.2

commit v7 on v5

v7 whole, which is shorter than its diff:
```python
import jax
import jax.numpy as jnp
from jax import lax
from jax.experimental import pallas as pl
from jax.experimental.pallas import tpu as pltpu
from jax.sharding import Mesh, PartitionSpec as P

AXES = ("h", "l", "z", "ylo", "x", "core")
SIZES = (2, 2, 8, 2, 4, 2)
ROWS = 128
HALF = 128
TAPS = 128
GROUP = 16
GROUPS = HALF // GROUP
FEATURES = 256
STREAMS = 4 * HALF
BACK = 3 * HALF
BF16 = jnp.bfloat16
F32 = jnp.float32
VMEM_FORWARD = 40 << 20


def bands_kernel(base_ref, band_ref):
    for row in range(2 * GROUPS):
        spread = jnp.broadcast_to(base_ref[row : row + 1, :], (2 * ROWS, 2 * ROWS))
        rolled = pltpu.roll(spread, 0, 1, stride=1, stride_axis=0)
        band_ref[:, row * ROWS : (row + 1) * ROWS] = rolled[:, :ROWS].astype(BF16)


def bands(filters):
    zeros = jnp.zeros((GROUPS, TAPS), filters.dtype)
    causal = jnp.concatenate([zeros, filters], 1)
    anticausal = jnp.concatenate([filters[:, :1], zeros, filters[:, :0:-1]], 1)
    return pl.pallas_call(
        bands_kernel,
        out_shape=jax.ShapeDtypeStruct((2 * ROWS, 2 * GROUPS * ROWS), BF16),
    )(jnp.concatenate([causal, anticausal], 0))


def forward_kernel(
    place_ref,
    own_ref,
    other_ref,
    weight_hbm,
    streams_ref,
    gate_ref,
    product_ref,
    mixed_ref,
    back_ref,
    weight_ref,
    arrived,
):
    core = place_ref[0]
    copies = [
        pltpu.make_async_copy(
            weight_hbm.at[pl.ds((x % 2) * 4, 4), core, :, x // 2], weight_ref.at[x], arrived.at[x]
        )
        for x in range(4)
    ]
    copies += [
        pltpu.make_async_copy(weight_hbm.at[pl.ds(x * 4 + 2 * core, 2)], back_ref.at[x], arrived.at[4 + x])
        for x in range(2)
    ]
    for copy in copies:
        copy.start()
    streams, grad_gate = 0.0, 0.0
    contract = (((1,), (1,)), ((), ()))
    for x in range(4):
        tokens, cotangent, weight = [], [], []
        copies[x].wait()
        for values_ref, which in ((own_ref, core), (other_ref, 1 - core)):
            for y in range(2):
                tokens.append(values_ref[x, :, y, 0].reshape(2 * ROWS, FEATURES))
                cotangent.append(values_ref[x, :, y, 1].reshape(2 * ROWS, FEATURES))
                weight += [weight_ref[x, 2 * which + z, y] for z in range(2)]
        tokens, cotangent = jnp.concatenate(tokens, 1), jnp.concatenate(cotangent, 1)
        weight = jnp.concatenate(weight, 1)
        streams += lax.dot_general(weight[:BACK], tokens, contract, preferred_element_type=F32)
        grad_gate += lax.dot_general(weight[BACK:], cotangent, contract, preferred_element_type=F32)
    streams = streams.astype(BF16)
    streams_ref[...] = streams
    gate_ref[...] = grad_gate
    query, key, value = (streams[i * HALF : (i + 1) * HALF].astype(F32) for i in range(3))
    product_ref[...] = (key * value).astype(BF16)
    mixed_ref[...] = (grad_gate * query).astype(BF16)
    copies[4].wait()
    copies[5].wait()


def forward(place, own, other, weight):
    vmem = pl.BlockSpec(memory_space=pltpu.VMEM)
    shape = lambda height, kind: jax.ShapeDtypeStruct((height, 2 * ROWS), kind)
    return pl.pallas_call(
        forward_kernel,
        out_shape=(
            shape(BACK, BF16),
            shape(HALF, F32),
            shape(HALF, BF16),
            shape(HALF, BF16),
            jax.ShapeDtypeStruct((2, 2, 2, 2, 2, STREAMS, ROWS), BF16),
        ),
        in_specs=[
            pl.BlockSpec(memory_space=pltpu.SMEM),
            vmem,
            vmem,
            pl.BlockSpec(memory_space=pl.ANY),
        ],
        out_specs=(vmem,) * 5,
        scratch_shapes=[pltpu.VMEM((4, 4, 2, STREAMS, ROWS), BF16), pltpu.SemaphoreType.DMA((6,))],
        compiler_params=pltpu.CompilerParams(vmem_limit_bytes=VMEM_FORWARD),
        cost_estimate=pl.CostEstimate(flops=1 << 30, bytes_accessed=9 << 20, transcendentals=0),
    )(place, own, other, weight)


def filtered(left, right, band):
    segments = [
        jnp.concatenate([left[s], right[s]], 1) for s in range(2)
    ]
    result = jnp.dot(jnp.concatenate(segments, 0), band, preferred_element_type=F32)
    return [
        jnp.concatenate(
            [
                result[s * HALF + g * GROUP : s * HALF + (g + 1) * GROUP, g * ROWS : (g + 1) * ROWS]
                for g in range(GROUPS)
            ],
            0,
        )
        for s in range(2)
    ]


def middle_kernel(
    place_ref, band_ref, streams_ref, gate_ref, product_ref, mixed_ref, before_ref, after_ref, terms_ref
):
    first = place_ref[1] == 0
    last = place_ref[1] == 15
    lanes = [slice(s * ROWS, (s + 1) * ROWS) for s in range(2)]
    product, mixed, before, after = (
        [ref[:, lanes[s]] for s in range(2)] for ref in (product_ref, mixed_ref, before_ref, after_ref)
    )
    zero = jnp.zeros_like(before[0])
    earlier = [jnp.where(first, zero, before[0]), jnp.where(first, before[0], before[1])]
    later = [jnp.where(last, after[1], after[0]), jnp.where(last, zero, after[1])]
    conv = filtered(earlier, product, band_ref[:, : GROUPS * ROWS])
    back = filtered(mixed, later, band_ref[:, GROUPS * ROWS :])
    for s in range(2):
        query, key, value = (
            streams_ref[i * HALF : (i + 1) * HALF, lanes[s]].astype(F32) for i in range(3)
        )
        terms = (gate_ref[:, lanes[s]] * conv[s], back[s] * value, back[s] * key, query * conv[s])
        for i in range(4):
            terms_ref[lanes[s], i * HALF : (i + 1) * HALF] = terms[i].T.astype(BF16)


def on_chip(kernel, out_shape, operands, flops):
    smem, vmem = pl.BlockSpec(memory_space=pltpu.SMEM), pl.BlockSpec(memory_space=pltpu.VMEM)
    return pl.pallas_call(
        kernel,
        out_shape=out_shape,
        in_specs=[smem] + [vmem] * (len(operands) - 1),
        out_specs=jax.tree.map(lambda _: vmem, out_shape),
        compiler_params=pltpu.CompilerParams(vmem_limit_bytes=24 << 20),
        cost_estimate=pl.CostEstimate(flops=flops, bytes_accessed=1 << 20, transcendentals=0),
    )(*operands)


def middle(*operands):
    return on_chip(middle_kernel, jax.ShapeDtypeStruct((2 * ROWS, STREAMS), BF16), operands, 1 << 28)


def backward_kernel(place_ref, own_ref, other_ref, weight_ref, out_ref):
    core = place_ref[0]
    for part, cols in enumerate((slice(BACK, STREAMS), slice(0, BACK))):
        terms = jnp.concatenate([own_ref[:, cols], other_ref[:, cols]], 1)
        for y in range(2):
            for x in range(4):
                weight = [
                    jnp.concatenate([weight_ref[x % 2, z, which, y, x // 2, cols] for z in range(2)], 1)
                    for which in (core, 1 - core)
                ]
                result = jnp.dot(terms, jnp.concatenate(weight, 0), preferred_element_type=F32)
                for h in range(2):
                    out_ref[4 * y + x, h, part] = result[h * ROWS : (h + 1) * ROWS].astype(BF16)


def backward(*operands):
    shape = (8, 2, 2, ROWS, FEATURES)
    return on_chip(backward_kernel, jax.ShapeDtypeStruct(shape, BF16), operands, 1 << 30)


def combine_kernel(place_ref, parts_ref, mine_ref, theirs_ref):
    half = place_ref[3]
    for part in range(2):
        mine, theirs = 0.0, 0.0
        for source in range(8):
            mine += parts_ref[source, half, part].astype(F32)
            theirs += parts_ref[source, 1 - half, part].astype(F32)
        mine_ref[part] = mine
        theirs_ref[part] = theirs.astype(BF16)


def combine(*operands):
    shape = (2, ROWS, FEATURES)
    out_shape = (jax.ShapeDtypeStruct(shape, F32), jax.ShapeDtypeStruct(shape, BF16))
    return on_chip(combine_kernel, out_shape, operands, 1 << 20)


def pack_kernel(in_ref, out_ref, packed_ref):
    for h in range(2):
        chans = slice(h * HALF, (h + 1) * HALF)
        streams = [in_ref[stream, :, chans].astype(F32).T.astype(BF16) for stream in range(3)]
        for l in range(2):
            for stream in range(3):
                packed_ref[2 * h + l, stream * HALF : (stream + 1) * HALF] = streams[stream]
            packed_ref[2 * h + l, BACK:] = out_ref[chans]


def packed(in_weight, out_weight):
    vmem = pl.BlockSpec(memory_space=pltpu.VMEM)
    return pl.pallas_call(
        pack_kernel,
        out_shape=jax.ShapeDtypeStruct((4, STREAMS, ROWS), BF16),
        in_specs=[vmem] * 2,
        out_specs=vmem,
    )(in_weight, out_weight)


def finish_kernel(mine_ref, theirs_ref, mixed_ref, grad_ref):
    for part, ref in enumerate((mixed_ref, grad_ref)):
        ref[...] = (mine_ref[part] + theirs_ref[part].astype(F32)).astype(BF16)


def finish(*parts):
    vmem = pl.BlockSpec(memory_space=pltpu.VMEM)
    return pl.pallas_call(
        finish_kernel,
        out_shape=(jax.ShapeDtypeStruct((ROWS, FEATURES), BF16),) * 2,
        in_specs=[vmem] * 2,
        out_specs=(vmem, vmem),
    )(*parts)


def swapped(value, axes):
    return lax.all_to_all(value, axes, 0, 0, tiled=True)


def gathered(value, axes, count):
    return swapped(jnp.broadcast_to(value[None], (count,) + value.shape), axes)


def local(tokens, in_weight, out_weight, mr_filter, cotangent):
    half, core = lax.axis_index("h"), lax.axis_index("core")
    position = lax.axis_index(("l", "z"))
    place = jnp.stack([core, position, lax.axis_index("x"), half]).astype(jnp.int32)

    weight = swapped(packed(in_weight, out_weight), ("h", "l"))
    values = jnp.stack([tokens, cotangent], 0)
    weight, values = lax.optimization_barrier((weight, values))
    weight = lax.all_gather(weight, ("z", "core"), axis=0).reshape(8, 2, 2, 2, STREAMS, ROWS)

    band = bands(lax.dynamic_slice_in_dim(mr_filter, half * GROUPS, GROUPS, 0))
    values = gathered(values, ("h", "ylo"), 4)
    values = gathered(values, "x", 4).reshape(4, 2, 2, 2, ROWS, FEATURES)
    values, band = lax.optimization_barrier((values, band))
    cross = [(0, 1), (1, 0)]
    other = lax.ppermute(values, "core", cross)

    streams, gate, product, mixed, weight = forward(place, values, other, weight)
    ring = [(n, (n + 1) % 16) for n in range(16)]
    before = lax.ppermute(product, ("l", "z"), ring)
    after = lax.ppermute(mixed, ("l", "z"), [(b, a) for a, b in ring])

    terms = middle(place, band, streams, gate, product, mixed, before, after)
    other_terms = lax.ppermute(terms, "core", cross)

    parts = swapped(backward(place, terms, other_terms, weight), ("ylo", "x"))
    mine, theirs = combine(place, parts)
    return finish(mine, lax.ppermute(theirs, "h", cross))


def solution(mesh):
    fine = Mesh(mesh.devices.reshape(SIZES), AXES)
    ctx, tp = AXES[:3], AXES[3:]
    return jax.shard_map(
        local,
        mesh=fine,
        in_specs=(P(ctx, tp), P(None, ctx, tp), P(tp, ctx), P(tp, None), P(ctx, tp)),
        out_specs=(P(ctx, tp), P(ctx, tp)),
        check_vma=False,
    )
```

time: 185 us -> 172 us (0.930)
  the two profiles are of different devices: /device:TPU:14 before, /device:TPU:1 now
where the time goes in v7:
time: 172 us; the launch traced here: 169 us
  waiting for transfers between devices  50.9 us (30%)
  blocking collectives  46.5 us (27%)
  starting transfers between devices  36.9 us (21%)
  Pallas kernels  14.5 us (8%)
  between operations  14.1 us (8%)
  local copies, waits for them, and re-layouts  3.98 us (2%)
    all_to_all x2, blocking collectives, swapped(): return lax.all_to_all(value, axes, 0, 0, tiled=True)  46.5 us
    all_to_all x2, waiting for transfers between devices, swapped(): return lax.all_to_all(value, axes, 0, 0, tiled=True)  35.2 us
    all_to_all x2, starting transfers between devices, swapped(): return lax.all_to_all(value, axes, 0, 0, tiled=True)  11.8 us
    ppermute x1, starting transfers between devices, local(): after = lax.ppermute(mixed, ('l', 'z'), [(b, a) for a, b in ring])  9.31 us
    ppermute x1, starting transfers between devices, local(): return finish(mine, lax.ppermute(theirs, 'h', cross))  6.36 us
    all_gather x1, waiting for transfers between devices, local(): lax.all_gather(weight, ('z', 'core'), axis=0)  6.02 us
    pallas_call x1, Pallas kernels, forward(): pl.pallas_call(forward_kernel, out_shape=(shape(BACK, BF16), shape(HALF,...  5.23 us
    ppermute x1, starting transfers between devices, local(): other = lax.ppermute(values, 'core', cross)  4.43 us
  transfers between devices with their start and end apart: 8, of which 8 were waited for; matrix products, arithmetic and copies ran while one was open for 2% of the time, Pallas kernels for 1%

profile of v7, /device:TPU:1, one launch (start us, length us, event | category | flops | bytes accessed | tf_op | source)
XLA Modules:
  0.0 168.5 jit_solution(602843273738004700)
XLA Ops:
  7.2 1.9 %shard_map.68 = bf16[4,512,128]{2,1,0:T(8,128)(2,1)} custom-call(bf16[3,128,256]{2,1,0:T(8,128)(2,1)} %in_ref.1, bf16[256,128]{1,0:T(8,128)(2,1)} %out_ref.1), custom_call_target="tpu_custom_call" | custom-call | tf_op jit(solution)/shard_map/pallas_call | solution.py:220
  9.1 7.6 %all-to-all-start = ((bf16[4,512,128]{2,1,0:T(8,128)(2,1)}), bf16[4,512,128]{2,1,0:T(8,128)(2,1)S(1)}, u32[]{:S(2)}, u32[]{:S(2)}) async-start(bf16[4,512,128]{2,1,0:T(8,128)(2,1)} %shard_map.68), calls=%async_computation | async-start | bytes 1048576 | tf_op jit(solution)/shard_map/all_to_all | solution.py:244
  16.7 0.9 pad_maximum_fusion
  17.6 13.3 %all-to-all-done = bf16[4,512,128]{2,1,0:T(8,128)(2,1)S(1)} async-done(((bf16[4,512,128]{2,1,0:T(8,128)(2,1)}), bf16[4,512,128]{2,1,0:T(8,128)(2,1)S(1)}, u32[]{:S(2)}, u32[]{:S(2)}) %all-to-all-start) | async-done | bytes 524320 | tf_op jit(solution)/shard_map/all_to_all | solution.py:244
  31.8 17.9 %all_to_all.20 = bf16[4,2,128,256]{3,2,1,0:T(8,128)(2,1)S(1)} all-to-all(bf16[4,2,128,256]{3,2,1,0:T(8,128)(2,1)S(1)} %broadcast_in_dim.6), channel_id=1, replica_groups=mesh['h'=2,'l'=2,'z'=8,'ylo'=2,'x'=4,'core'=2] {'h','ylo'}, dimensions={0} | all-to-all | bytes 1048576 | tf_op jit(solution)/shard_map/all_to_all | solution.py:244
  49.7 1.6 broadcast_in_dim.7
  51.3 4.1 %all-to-all-start.2 = ((bf16[4,4,2,128,256]{4,3,2,1,0:T(8,128)(2,1)}), bf16[4,4,2,128,256]{4,3,2,1,0:T(8,128)(2,1)S(1)}, u32[]{:S(2)}, u32[]{:S(2)}) async-start(bf16[4,4,2,128,256]{4,3,2,1,0:T(8,128)(2,1)} %broadcast_in_dim.7), calls=%async_computation.2 | async-start | bytes 4194304 | tf_op jit(solution)/shard_map/all_to_all | solution.py:244
  56.3 2.1 %shard_map.69.band_ref = bf16[256,2048]{1,0:T(8,128)(2,1)} custom-call(f32[16,256]{1,0:T(8,128)} %select_maximum_fusion.base_ref), custom_call_target="tpu_custom_call" | custom-call | tf_op jit(solution)/shard_map/pallas_call | solution.py:34
  58.3 21.8 %all-to-all-done.2 = bf16[4,4,2,128,256]{4,3,2,1,0:T(8,128)(2,1)S(1)} async-done(((bf16[4,4,2,128,256]{4,3,2,1,0:T(8,128)(2,1)}), bf16[4,4,2,128,256]{4,3,2,1,0:T(8,128)(2,1)S(1)}, u32[]{:S(2)}, u32[]{:S(2)}) %all-to-all-start.2) | async-done | bytes 2097184 | tf_op jit(solution)/shard_map/all_to_all | solution.py:244
  80.2 4.4 %collective-permute-start = (bf16[4,2,2,2,128,256]{5,4,3,2,1,0:T(8,128)(2,1)S(1)}, bf16[4,2,2,2,128,256]{5,4,3,2,1,0:T(8,128)(2,1)}, u32[]{:S(2)}, u32[]{:S(2)}) collective-permute-start(bf16[4,2,2,2,128,256]{5,4,3,2,1,0:T(8,128)(2,1)S(1)} %bitcast.9), channel_id=1, source_target_pairs={{0,1},{1,0},{2,3},{3,2},{4,5},{5,4},{6,7},{7,6},{8,9},{9,8},{10,11... | collective-permute-start | bytes 6291464 | tf_op jit(solution)/shard_map/ppermute | solution.py:266
  84.7 3.9 %collective-permute-done.other_ref = bf16[4,2,2,2,128,256]{5,4,3,2,1,0:T(8,128)(2,1)} collective-permute-done((bf16[4,2,2,2,128,256]{5,4,3,2,1,0:T(8,128)(2,1)S(1)}, bf16[4,2,2,2,128,256]{5,4,3,2,1,0:T(8,128)(2,1)}, u32[]{:S(2)}, u32[]{:S(2)}) %collective-permute-start) | collective-permute-done | bytes 2097184 | tf_op jit(solution)/shard_map/ppermute | solution.py:266
  88.6 6.0 %all-gather.3.cloned.1.call-done = bf16[64,512,128]{2,1,0:T(8,128)(2,1)} async-done(((bf16[4,512,128]{2,1,0:T(8,128)(2,1)}), bf16[64,512,128]{2,1,0:T(8,128)(2,1)}) %all-gather.3.cloned.1.call-update) | async-done | bytes 8388624 | tf_op jit(solution)/shard_map/all_gather | solution.py:259
  94.6 5.2 %shard_map.70 = (bf16[384,256]{1,0:T(8,128)(2,1)S(1)}, f32[128,256]{1,0:T(8,128)S(1)}, bf16[128,256]{1,0:T(8,128)(2,1)S(1)}, bf16[128,256]{1,0:T(8,128)(2,1)S(1)}, bf16[2,2,2,2,2,512,128]{6,5,4,3,2,1,0:T(8,128)(2,1)S(1)}) custom-call(s32[4]{0:T(128)S(1)} %pad_add_fusion.place_ref, bf16[4,2,2,2,128,256]{5,4,3,2,1,0:T(8,128)(2,1)S(1)} %bitcast.10, ...), custom_call_target="tpu_custom_call" | custom-call | flops 1073741824 | bytes 9437184 | tf_op jit(solution)/shard_map/pallas_call | solution.py:93
  99.9 1.9 %collective-permute-start.1 = (bf16[128,256]{1,0:T(8,128)(2,1)S(1)}, bf16[128,256]{1,0:T(8,128)(2,1)S(1)}, u32[]{:S(2)}, u32[]{:S(2)}) collective-permute-start(bf16[128,256]{1,0:T(8,128)(2,1)S(1)} %get-tuple-element.19.product_ref), channel_id=1, source_target_pairs={{0,16},{16,32},{32,48},{48,64},{64,80},{80,96},{96,112},{112,128},... | collective-permute-start | bytes 196616 | tf_op jit(solution)/shard_map/ppermute | solution.py:270
  101.8 9.3 %collective-permute-start.2 = (bf16[128,256]{1,0:T(8,128)(2,1)S(1)}, bf16[128,256]{1,0:T(8,128)(2,1)S(1)}, u32[]{:S(2)}, u32[]{:S(2)}) collective-permute-start(bf16[128,256]{1,0:T(8,128)(2,1)S(1)} %get-tuple-element.20.mixed_ref), channel_id=1, source_target_pairs={{16,0},{32,16},{48,32},{64,48},{80,64},{96,80},{112,96},{128,112},... | collective-permute-start | bytes 196616 | tf_op jit(solution)/shard_map/ppermute | solution.py:271
  111.3 1.1 collective-permute-done.2.after_ref
  112.4 1.1 shard_map.71.own_ref
  113.5 3.1 %collective-permute-start.3 = (bf16[256,512]{1,0:T(8,128)(2,1)S(1)}, bf16[256,512]{1,0:T(8,128)(2,1)S(1)}, u32[]{:S(2)}, u32[]{:S(2)}) collective-permute-start(bf16[256,512]{1,0:T(8,128)(2,1)S(1)} %shard_map.71.own_ref), channel_id=1, source_target_pairs={{0,1},{1,0},{2,3},{3,2},{4,5},{5,4},{6,7},{7,6},{8,9},{9,8},{10,11... | collective-permute-start | bytes 786440 | tf_op jit(solution)/shard_map/ppermute | solution.py:274
  116.6 1.1 collective-permute-done.3.other_ref
  117.8 1.8 %shard_map.72 = bf16[8,2,2,128,256]{4,3,2,1,0:T(8,128)(2,1)S(1)} custom-call(s32[4]{0:T(128)S(1)} %pad_add_fusion.place_ref, bf16[256,512]{1,0:T(8,128)(2,1)S(1)} %shard_map.71.own_ref, bf16[256,512]{1,0:T(8,128)(2,1)S(1)} %collective-permute-done.3.other_ref, bf16[2,2,2,2,2,512,128]{6,5,4,3,2,1,0:T(8,128)(2,1)S(1)} %get-tuple-element.21.weight_ref), custom_call_target="tpu_custom_call" | custom-call | flops 1073741824 | bytes 1048576 | tf_op jit(solution)/shard_map/pallas_call | solution.py:157
  119.6 28.6 %all_to_all.21.parts_ref = bf16[8,2,2,128,256]{4,3,2,1,0:T(8,128)(2,1)S(1)} all-to-all(bf16[8,2,2,128,256]{4,3,2,1,0:T(8,128)(2,1)S(1)} %shard_map.72), channel_id=1, replica_groups=mesh['h'=2,'l'=2,'z'=8,'ylo'=2,'x'=4,'core'=2] {'ylo','x'}, dimensions={0} | all-to-all | bytes 4194304 | tf_op jit(solution)/shard_map/all_to_all | solution.py:244
  149.7 6.4 %collective-permute-start.4 = (bf16[2,128,256]{2,1,0:T(8,128)(2,1)S(1)}, bf16[2,128,256]{2,1,0:T(8,128)(2,1)S(1)}, u32[]{:S(2)}, u32[]{:S(2)}) collective-permute-start(bf16[2,128,256]{2,1,0:T(8,128)(2,1)S(1)} %get-tuple-element.23), channel_id=1, source_target_pairs={{0,256},{256,0},{1,257},{257,1},{2,258},{258,2},{3,259},{259,3},{4... | collective-permute-start | bytes 393224 | tf_op jit(solution)/shard_map/ppermute | solution.py:278
  156.1 3.3 %collective-permute-done.4.theirs_ref = bf16[2,128,256]{2,1,0:T(8,128)(2,1)S(1)} collective-permute-done((bf16[2,128,256]{2,1,0:T(8,128)(2,1)S(1)}, bf16[2,128,256]{2,1,0:T(8,128)(2,1)S(1)}, u32[]{:S(2)}, u32[]{:S(2)}) %collective-permute-start.4) | collective-permute-done | bytes 131104 | tf_op jit(solution)/shard_map/ppermute | solution.py:278
  160.0 1.6 shard_map.74
  (21 shorter events, 4.2 us)
Async XLA Ops:
  7.2 48.3 %copy-start = (f32[16,128]{1,0:T(8,128)S(1)}, f32[16,128]{1,0:T(8,128)}, u32[]{:S(2)}) copy-start(f32[16,128]{1,0:T(8,128)} %param.8) | copy-start | bytes 24580
  9.1 21.9 %all-to-all-start = ((bf16[4,512,128]{2,1,0:T(8,128)(2,1)}), bf16[4,512,128]{2,1,0:T(8,128)(2,1)S(1)}, u32[]{:S(2)}, u32[]{:S(2)}) async-start(bf16[4,512,128]{2,1,0:T(8,128)(2,1)} %shard_map.68), calls=%async_computation | async-start | bytes 1048576 | tf_op jit(solution)/shard_map/all_to_all | solution.py:244
  16.7 77.9 %all-gather.3.cloned.1.call-start = ((), (), s32[]{:S(2)}) async-start(), calls=%async_computation.4 | async-start | bytes 8912896 | tf_op jit(solution)/shard_map/all_gather | solution.py:259
  30.9 0.8 copy-start.3
  51.3 28.9 %all-to-all-start.2 = ((bf16[4,4,2,128,256]{4,3,2,1,0:T(8,128)(2,1)}), bf16[4,4,2,128,256]{4,3,2,1,0:T(8,128)(2,1)S(1)}, u32[]{:S(2)}, u32[]{:S(2)}) async-start(bf16[4,4,2,128,256]{4,3,2,1,0:T(8,128)(2,1)} %broadcast_in_dim.7), calls=%async_computation.2 | async-start | bytes 4194304 | tf_op jit(solution)/shard_map/all_to_all | solution.py:244
  80.2 8.4 %collective-permute-start = (bf16[4,2,2,2,128,256]{5,4,3,2,1,0:T(8,128)(2,1)S(1)}, bf16[4,2,2,2,128,256]{5,4,3,2,1,0:T(8,128)(2,1)}, u32[]{:S(2)}, u32[]{:S(2)}) collective-permute-start(bf16[4,2,2,2,128,256]{5,4,3,2,1,0:T(8,128)(2,1)S(1)} %bitcast.9), channel_id=1, source_target_pairs={{0,1},{1,0},{2,3},{3,2},{4,5},{5,4},{6,7},{7,6},{8,9},{9,8},{10,11... | collective-permute-start | bytes 6291464 | tf_op jit(solution)/shard_map/ppermute | solution.py:266
  94.6 17.8 %copy-start.1 = (bf16[256,2048]{1,0:T(8,128)(2,1)S(1)}, bf16[256,2048]{1,0:T(8,128)(2,1)}, u32[]{:S(2)}) copy-start(bf16[256,2048]{1,0:T(8,128)(2,1)} %shard_map.69.band_ref) | copy-start | bytes 3145732
  99.9 11.5 %collective-permute-start.1 = (bf16[128,256]{1,0:T(8,128)(2,1)S(1)}, bf16[128,256]{1,0:T(8,128)(2,1)S(1)}, u32[]{:S(2)}, u32[]{:S(2)}) collective-permute-start(bf16[128,256]{1,0:T(8,128)(2,1)S(1)} %get-tuple-element.19.product_ref), channel_id=1, source_target_pairs={{0,16},{16,32},{32,48},{48,64},{64,80},{80,96},{96,112},{112,128},... | collective-permute-start | bytes 196616 | tf_op jit(solution)/shard_map/ppermute | solution.py:270
  101.8 10.6 %collective-permute-start.2 = (bf16[128,256]{1,0:T(8,128)(2,1)S(1)}, bf16[128,256]{1,0:T(8,128)(2,1)S(1)}, u32[]{:S(2)}, u32[]{:S(2)}) collective-permute-start(bf16[128,256]{1,0:T(8,128)(2,1)S(1)} %get-tuple-element.20.mixed_ref), channel_id=1, source_target_pairs={{16,0},{32,16},{48,32},{64,48},{80,64},{96,80},{112,96},{128,112},... | collective-permute-start | bytes 196616 | tf_op jit(solution)/shard_map/ppermute | solution.py:271
  113.5 4.3 %collective-permute-start.3 = (bf16[256,512]{1,0:T(8,128)(2,1)S(1)}, bf16[256,512]{1,0:T(8,128)(2,1)S(1)}, u32[]{:S(2)}, u32[]{:S(2)}) collective-permute-start(bf16[256,512]{1,0:T(8,128)(2,1)S(1)} %shard_map.71.own_ref), channel_id=1, source_target_pairs={{0,1},{1,0},{2,3},{3,2},{4,5},{5,4},{6,7},{7,6},{8,9},{9,8},{10,11... | collective-permute-start | bytes 786440 | tf_op jit(solution)/shard_map/ppermute | solution.py:274
  149.0 0.7 copy-start.2
  149.7 9.7 %collective-permute-start.4 = (bf16[2,128,256]{2,1,0:T(8,128)(2,1)S(1)}, bf16[2,128,256]{2,1,0:T(8,128)(2,1)S(1)}, u32[]{:S(2)}, u32[]{:S(2)}) collective-permute-start(bf16[2,128,256]{2,1,0:T(8,128)(2,1)S(1)} %get-tuple-element.23), channel_id=1, source_target_pairs={{0,256},{256,0},{1,257},{257,1},{2,258},{258,2},{3,259},{259,3},{4... | collective-permute-start | bytes 393224 | tf_op jit(solution)/shard_map/ppermute | solution.py:278
  159.4 0.6 copy-start.4
Sparse Core Ops, SparseCore 0:
  31.9 62.6 all-gather.2

commit v8 on v7

--- a/solution.py
+++ b/solution.py
@@ -61,13 +61,15 @@
         pltpu.make_async_copy(weight_hbm.at[pl.ds(x * 4 + 2 * core, 2)], back_ref.at[x], arrived.at[4 + x])
         for x in range(2)
     ]
-    for copy in copies:
+    for copy in copies[:4]:
         copy.start()
     streams, grad_gate = 0.0, 0.0
     contract = (((1,), (1,)), ((), ()))
     for x in range(4):
         tokens, cotangent, weight = [], [], []
         copies[x].wait()
+        if x < 2:
+            copies[4 + x].start()
         for values_ref, which in ((own_ref, core), (other_ref, 1 - core)):
             for y in range(2):
                 tokens.append(values_ref[x, :, y, 0].reshape(2 * ROWS, FEATURES))
@@ -168,41 +170,46 @@
     return on_chip(middle_kernel, jax.ShapeDtypeStruct((2 * ROWS, STREAMS), BF16), operands, 1 << 28)
 
 
-def backward_kernel(place_ref, own_ref, other_ref, weight_ref, out_ref):
-    core = place_ref[0]
-    for part, cols in enumerate((slice(BACK, STREAMS), slice(0, BACK))):
-        terms = jnp.concatenate([own_ref[:, cols], other_ref[:, cols]], 1)
-        for y in range(2):
-            for x in range(4):
-                weight = [
-                    jnp.concatenate([weight_ref[x % 2, z, which, y, x // 2, cols] for z in range(2)], 1)
-                    for which in (core, 1 - core)
-                ]
-                result = jnp.dot(terms, jnp.concatenate(weight, 0), preferred_element_type=F32)
-                for h in range(2):
-                    out_ref[4 * y + x, h, part] = result[h * ROWS : (h + 1) * ROWS].astype(BF16)
-
-
-def backward(*operands):
-    shape = (8, 2, 2, ROWS, FEATURES)
-    return on_chip(backward_kernel, jax.ShapeDtypeStruct(shape, BF16), operands, 1 << 30)
-
-
-def combine_kernel(place_ref, parts_ref, mine_ref, theirs_ref):
-    half = place_ref[3]
+def backward(turn, place, *operands):
+    def kernel(place_ref, own_ref, other_ref, weight_ref, out_ref):
+        core = place_ref[0]
+        block = place_ref[3] if turn == 0 else 1 - place_ref[3]
+        rows = pl.ds(pl.multiple_of(block * ROWS, ROWS), ROWS)
+        for part, cols in enumerate((slice(BACK, STREAMS), slice(0, BACK))):
+            terms = jnp.concatenate([own_ref[rows, cols], other_ref[rows, cols]], 1)
+            for y in range(2):
+                for x in range(4):
+                    weight = [
+                        jnp.concatenate([weight_ref[x % 2, z, which, y, x // 2, cols] for z in range(2)], 1)
+                        for which in (core, 1 - core)
+                    ]
+                    result = jnp.dot(terms, jnp.concatenate(weight, 0), preferred_element_type=F32)
+                    out_ref[4 * y + x, part] = result.astype(BF16)
+
+    shape = (8, 2, ROWS, FEATURES)
+    return on_chip(kernel, jax.ShapeDtypeStruct(shape, BF16), (place,) + operands, 1 << 29)
+
+
+def summed(parts_ref, part):
+    total = parts_ref[0, part].astype(F32)
+    for source in range(1, 8):
+        total += parts_ref[source, part].astype(F32)
+    return total
+
+
+def combine_kernel(parts_ref, total_ref):
     for part in range(2):
-        mine, theirs = 0.0, 0.0
-        for source in range(8):
-            mine += parts_ref[source, half, part].astype(F32)
-            theirs += parts_ref[source, 1 - half, part].astype(F32)
-        mine_ref[part] = mine
-        theirs_ref[part] = theirs.astype(BF16)
-
-
-def combine(*operands):
-    shape = (2, ROWS, FEATURES)
-    out_shape = (jax.ShapeDtypeStruct(shape, F32), jax.ShapeDtypeStruct(shape, BF16))
-    return on_chip(combine_kernel, out_shape, operands, 1 << 20)
+        total_ref[part] = summed(parts_ref, part).astype(BF16)
+
+
+def combine(parts):
+    vmem = pl.BlockSpec(memory_space=pltpu.VMEM)
+    return pl.pallas_call(
+        combine_kernel,
+        out_shape=jax.ShapeDtypeStruct((2, ROWS, FEATURES), BF16),
+        in_specs=[vmem],
+        out_specs=vmem,
+    )(parts)
 
 
 def pack_kernel(in_ref, out_ref, packed_ref):
@@ -225,9 +232,9 @@
     )(in_weight, out_weight)
 
 
-def finish_kernel(mine_ref, theirs_ref, mixed_ref, grad_ref):
+def finish_kernel(parts_ref, received_ref, mixed_ref, grad_ref):
     for part, ref in enumerate((mixed_ref, grad_ref)):
-        ref[...] = (mine_ref[part] + theirs_ref[part].astype(F32)).astype(BF16)
+        ref[...] = (summed(parts_ref, part) + received_ref[part].astype(F32)).astype(BF16)
 
 
 def finish(*parts):
@@ -273,9 +280,13 @@
     terms = middle(place, band, streams, gate, product, mixed, before, after)
     other_terms = lax.ppermute(terms, "core", cross)
 
-    parts = swapped(backward(place, terms, other_terms, weight), ("ylo", "x"))
-    mine, theirs = combine(place, parts)
-    return finish(mine, lax.ppermute(theirs, "h", cross))
+    theirs = backward(1, place, terms, other_terms, weight)
+    theirs, terms = lax.optimization_barrier((theirs, terms))
+    mine = backward(0, place, terms, other_terms, weight)
+    theirs = swapped(theirs, ("ylo", "x"))
+    theirs, mine = lax.optimization_barrier((theirs, mine))
+    mine = swapped(mine, ("ylo", "x"))
+    return finish(mine, lax.ppermute(combine(theirs), "h", cross))
 
 
 def solution(mesh):

time: 172 us -> 177 us (1.029); the launches traced: 169 us -> 176 us
  blocking collectives: 46.5 us -> 17.9 us
  waiting for transfers between devices: 50.9 us -> 70.7 us
  starting transfers between devices: 36.9 us -> 43.8 us
  Pallas kernels: 14.5 us -> 19 us
  local copies, waits for them, and re-layouts: 3.98 us -> 8.41 us
    all_to_all x2 -> x1, blocking collectives: 46.5 us -> 17.9 us  [swapped(): return lax.all_to_all(value, axes, 0, 0, tiled=True)]
    all_to_all x2 -> x4, waiting for transfers between devices: 35.2 us -> 45.6 us  [swapped(): return lax.all_to_all(value, axes, 0, 0, tiled=True)]
    ppermute x1, waiting for transfers between devices: 3.34 us -> 12.7 us  [local(): return finish(mine, lax.ppermute(combine(theirs), 'h', cross))]
    all_to_all x2 -> x4, starting transfers between devices: 11.8 us -> 18.9 us  [swapped(): return lax.all_to_all(value, axes, 0, 0, tiled=True)]
    unnamed x10 -> x16, local copies, waits for them, and re-layouts: 2.16 us -> 6.59 us
    pallas_call x0 -> x1, Pallas kernels: none -> 2.02 us  [combine(): pl.pallas_call(combine_kernel, out_shape=jax.ShapeDtypeStruct((2, ROWS, F...]
    pallas_call x3, Pallas kernels: 3.65 us -> 5.6 us  [on_chip(): pl.pallas_call(kernel, out_shape=out_shape, in_specs=[smem] + [vmem] * (l...]
  transfers between devices with their start and end apart: 8 -> 10, of which waited for: 8 -> 9; matrix products, arithmetic and copies ran while one was open for 2% -> 2% of each run, Pallas kernels for 1% -> 4%
where the time goes in v8:
time: 177 us; the launch traced here: 176 us
  waiting for transfers between devices  70.7 us (40%)
  starting transfers between devices  43.8 us (25%)
  Pallas kernels  19 us (11%)
  blocking collectives  17.9 us (10%)
  between operations  14.1 us (8%)
  local copies, waits for them, and re-layouts  8.41 us (5%)
    all_to_all x4, waiting for transfers between devices, swapped(): return lax.all_to_all(value, axes, 0, 0, tiled=True)  45.6 us
    all_to_all x4, starting transfers between devices, swapped(): return lax.all_to_all(value, axes, 0, 0, tiled=True)  18.9 us
    all_to_all x1, blocking collectives, swapped(): return lax.all_to_all(value, axes, 0, 0, tiled=True)  17.9 us
    ppermute x1, waiting for transfers between devices, local(): return finish(mine, lax.ppermute(combine(theirs), 'h', cross))  12.7 us
    ppermute x1, starting transfers between devices, local(): after = lax.ppermute(mixed, ('l', 'z'), [(b, a) for a, b in ring])  9.31 us
    unnamed x16, local copies, waits for them, and re-layouts  6.59 us
    ppermute x1, starting transfers between devices, local(): return finish(mine, lax.ppermute(combine(theirs), 'h', cross))  6.02 us
    all_gather x1, waiting for transfers between devices, local(): lax.all_gather(weight, ('z', 'core'), axis=0)  6.02 us
  transfers between devices with their start and end apart: 10, of which 9 were waited for; matrix products, arithmetic and copies ran while one was open for 2% of the time, Pallas kernels for 4%

profile of v8, /device:TPU:1, one launch (start us, length us, event | category | flops | bytes accessed | tf_op | source)
XLA Modules:
  0.0 175.6 jit_solution(16735541771112392060)
XLA Ops:
  9.1 7.6 %all-to-all-start = ((bf16[4,512,128]{2,1,0:T(8,128)(2,1)}), bf16[4,512,128]{2,1,0:T(8,128)(2,1)S(1)}, u32[]{:S(2)}, u32[]{:S(2)}) async-start(bf16[4,512,128]{2,1,0:T(8,128)(2,1)} %shard_map.68), calls=%async_computation | async-start | bytes 1048576 | tf_op jit(solution)/shard_map/all_to_all | solution.py:251
  17.6 13.3 %all-to-all-done = bf16[4,512,128]{2,1,0:T(8,128)(2,1)S(1)} async-done(((bf16[4,512,128]{2,1,0:T(8,128)(2,1)}), bf16[4,512,128]{2,1,0:T(8,128)(2,1)S(1)}, u32[]{:S(2)}, u32[]{:S(2)}) %all-to-all-start) | async-done | bytes 524320 | tf_op jit(solution)/shard_map/all_to_all | solution.py:251
  31.8 17.9 %all_to_all.25 = bf16[4,2,128,256]{3,2,1,0:T(8,128)(2,1)S(1)} all-to-all(bf16[4,2,128,256]{3,2,1,0:T(8,128)(2,1)S(1)} %broadcast_in_dim.6), channel_id=1, replica_groups=mesh['h'=2,'l'=2,'z'=8,'ylo'=2,'x'=4,'core'=2] {'h','ylo'}, dimensions={0} | all-to-all | bytes 1048576 | tf_op jit(solution)/shard_map/all_to_all | solution.py:251
  51.3 4.1 %all-to-all-start.2 = ((bf16[4,4,2,128,256]{4,3,2,1,0:T(8,128)(2,1)}), bf16[4,4,2,128,256]{4,3,2,1,0:T(8,128)(2,1)S(1)}, u32[]{:S(2)}, u32[]{:S(2)}) async-start(bf16[4,4,2,128,256]{4,3,2,1,0:T(8,128)(2,1)} %broadcast_in_dim.7), calls=%async_computation.2 | async-start | bytes 4194304 | tf_op jit(solution)/shard_map/all_to_all | solution.py:251
  56.3 2.1 %shard_map.69.band_ref = bf16[256,2048]{1,0:T(8,128)(2,1)} custom-call(f32[16,256]{1,0:T(8,128)} %select_maximum_fusion.base_ref), custom_call_target="tpu_custom_call" | custom-call | tf_op jit(solution)/shard_map/pallas_call | solution.py:34
  58.3 21.8 %all-to-all-done.2 = bf16[4,4,2,128,256]{4,3,2,1,0:T(8,128)(2,1)S(1)} async-done(((bf16[4,4,2,128,256]{4,3,2,1,0:T(8,128)(2,1)}), bf16[4,4,2,128,256]{4,3,2,1,0:T(8,128)(2,1)S(1)}, u32[]{:S(2)}, u32[]{:S(2)}) %all-to-all-start.2) | async-done | bytes 2097184 | tf_op jit(solution)/shard_map/all_to_all | solution.py:251
  80.2 4.4 %collective-permute-start = (bf16[4,2,2,2,128,256]{5,4,3,2,1,0:T(8,128)(2,1)S(1)}, bf16[4,2,2,2,128,256]{5,4,3,2,1,0:T(8,128)(2,1)}, u32[]{:S(2)}, u32[]{:S(2)}) collective-permute-start(bf16[4,2,2,2,128,256]{5,4,3,2,1,0:T(8,128)(2,1)S(1)} %bitcast.9), channel_id=1, source_target_pairs={{0,1},{1,0},{2,3},{3,2},{4,5},{5,4},{6,7},{7,6},{8,9},{9,8},{10,11... | collective-permute-start | bytes 6291464 | tf_op jit(solution)/shard_map/ppermute | solution.py:273
  84.7 3.9 %collective-permute-done.other_ref = bf16[4,2,2,2,128,256]{5,4,3,2,1,0:T(8,128)(2,1)} collective-permute-done((bf16[4,2,2,2,128,256]{5,4,3,2,1,0:T(8,128)(2,1)S(1)}, bf16[4,2,2,2,128,256]{5,4,3,2,1,0:T(8,128)(2,1)}, u32[]{:S(2)}, u32[]{:S(2)}) %collective-permute-start) | collective-permute-done | bytes 2097184 | tf_op jit(solution)/shard_map/ppermute | solution.py:273
  88.6 6.0 %all-gather.3.cloned.1.call-done = bf16[64,512,128]{2,1,0:T(8,128)(2,1)} async-done(((bf16[4,512,128]{2,1,0:T(8,128)(2,1)}), bf16[64,512,128]{2,1,0:T(8,128)(2,1)}) %all-gather.3.cloned.1.call-update) | async-done | bytes 8388624 | tf_op jit(solution)/shard_map/all_gather | solution.py:266
  94.6 5.4 %shard_map.70 = (bf16[384,256]{1,0:T(8,128)(2,1)S(1)}, f32[128,256]{1,0:T(8,128)S(1)}, bf16[128,256]{1,0:T(8,128)(2,1)S(1)}, bf16[128,256]{1,0:T(8,128)(2,1)S(1)}, bf16[2,2,2,2,2,512,128]{6,5,4,3,2,1,0:T(8,128)(2,1)S(1)}) custom-call(s32[4]{0:T(128)S(1)} %pad_add_fusion.place_ref, bf16[4,2,2,2,128,256]{5,4,3,2,1,0:T(8,128)(2,1)S(1)} %bitcast.10, ...), custom_call_target="tpu_custom_call" | custom-call | flops 1073741824 | bytes 9437184 | tf_op jit(solution)/shard_map/pallas_call | solution.py:95
  100.0 1.9 %collective-permute-start.1 = (bf16[128,256]{1,0:T(8,128)(2,1)S(1)}, bf16[128,256]{1,0:T(8,128)(2,1)S(1)}, u32[]{:S(2)}, u32[]{:S(2)}) collective-permute-start(bf16[128,256]{1,0:T(8,128)(2,1)S(1)} %get-tuple-element.21.product_ref), channel_id=1, source_target_pairs={{0,16},{16,32},{32,48},{48,64},{64,80},{80,96},{96,112},{112,128},... | collective-permute-start | bytes 196616 | tf_op jit(solution)/shard_map/ppermute | solution.py:277
  102.0 9.3 %collective-permute-start.2 = (bf16[128,256]{1,0:T(8,128)(2,1)S(1)}, bf16[128,256]{1,0:T(8,128)(2,1)S(1)}, u32[]{:S(2)}, u32[]{:S(2)}) collective-permute-start(bf16[128,256]{1,0:T(8,128)(2,1)S(1)} %get-tuple-element.22.mixed_ref), channel_id=1, source_target_pairs={{16,0},{32,16},{48,32},{64,48},{80,64},{96,80},{112,96},{128,112},... | collective-permute-start | bytes 196616 | tf_op jit(solution)/shard_map/ppermute | solution.py:278
  113.7 3.1 %collective-permute-start.3 = (bf16[256,512]{1,0:T(8,128)(2,1)S(1)}, bf16[256,512]{1,0:T(8,128)(2,1)S(1)}, u32[]{:S(2)}, u32[]{:S(2)}) collective-permute-start(bf16[256,512]{1,0:T(8,128)(2,1)S(1)} %shard_map.71.own_ref), channel_id=1, source_target_pairs={{0,1},{1,0},{2,3},{3,2},{4,5},{5,4},{6,7},{7,6},{8,9},{9,8},{10,11... | collective-permute-start | bytes 786440 | tf_op jit(solution)/shard_map/ppermute | solution.py:281
  117.9 2.3 %shard_map.72 = bf16[8,2,128,256]{3,2,1,0:T(8,128)(2,1)} custom-call(s32[4]{0:T(128)S(1)} %pad_add_fusion.place_ref, bf16[256,512]{1,0:T(8,128)(2,1)S(1)} %shard_map.71.own_ref, bf16[256,512]{1,0:T(8,128)(2,1)S(1)} %collective-permute-done.3.other_ref, bf16[2,2,2,2,2,512,128]{6,5,4,3,2,1,0:T(8,128)(2,1)S(1)} %get-tuple-element.23.weight_ref), custom_call_target="tpu_custom_call" | custom-call | flops 536870912 | bytes 1048576 | tf_op jit(solution)/shard_map/pallas_call | solution.py:159
  120.2 1.9 %copy-done.1 = bf16[2,2,2,2,2,512,128]{6,5,4,3,2,1,0:T(8,128)(2,1)} copy-done((bf16[2,2,2,2,2,512,128]{6,5,4,3,2,1,0:T(8,128)(2,1)}, bf16[2,2,2,2,2,512,128]{6,5,4,3,2,1,0:T(8,128)(2,1)S(1)}, u32[]{:S(2)}) %copy-start.1) | copy-done | bytes 4194328
  122.2 3.6 %all-to-all-start.3 = ((bf16[8,2,128,256]{3,2,1,0:T(8,128)(2,1)}), bf16[8,2,128,256]{3,2,1,0:T(8,128)(2,1)S(1)}, u32[]{:S(2)}, u32[]{:S(2)}) async-start(bf16[8,2,128,256]{3,2,1,0:T(8,128)(2,1)} %shard_map.72), calls=%async_computation.3 | async-start | bytes 2097152 | tf_op jit(solution)/shard_map/all_to_all | solution.py:251
  125.8 2.2 %copy-done.2 = bf16[2,2,2,2,2,512,128]{6,5,4,3,2,1,0:T(8,128)(2,1)S(1)} copy-done((bf16[2,2,2,2,2,512,128]{6,5,4,3,2,1,0:T(8,128)(2,1)S(1)}, bf16[2,2,2,2,2,512,128]{6,5,4,3,2,1,0:T(8,128)(2,1)}, u32[]{:S(2)}) %copy-start.2) | copy-done | bytes 4194328
  127.9 2.3 %shard_map.73 = bf16[8,2,128,256]{3,2,1,0:T(8,128)(2,1)} custom-call(s32[4]{0:T(128)S(1)} %pad_add_fusion.place_ref, bf16[256,512]{1,0:T(8,128)(2,1)S(1)} %shard_map.71.own_ref, bf16[256,512]{1,0:T(8,128)(2,1)S(1)} %collective-permute-done.3.other_ref, bf16[2,2,2,2,2,512,128]{6,5,4,3,2,1,0:T(8,128)(2,1)S(1)} %copy-done.2), custom_call_target="tpu_custom_call" | custom-call | flops 536870912 | bytes 1048576 | tf_op jit(solution)/shard_map/pallas_call | solution.py:159
  130.2 10.5 %all-to-all-done.3.parts_ref = bf16[8,2,128,256]{3,2,1,0:T(8,128)(2,1)S(1)} async-done(((bf16[8,2,128,256]{3,2,1,0:T(8,128)(2,1)}), bf16[8,2,128,256]{3,2,1,0:T(8,128)(2,1)S(1)}, u32[]{:S(2)}, u32[]{:S(2)}) %all-to-all-start.3) | async-done | bytes 1048608 | tf_op jit(solution)/shard_map/all_to_all | solution.py:251
  140.7 3.6 %all-to-all-start.4 = ((bf16[8,2,128,256]{3,2,1,0:T(8,128)(2,1)}), bf16[8,2,128,256]{3,2,1,0:T(8,128)(2,1)S(1)}, u32[]{:S(2)}, u32[]{:S(2)}) async-start(bf16[8,2,128,256]{3,2,1,0:T(8,128)(2,1)} %shard_map.73), calls=%async_computation.4 | async-start | bytes 2097152 | tf_op jit(solution)/shard_map/all_to_all | solution.py:251
  144.3 2.0 %shard_map.74 = bf16[2,128,256]{2,1,0:T(8,128)(2,1)} custom-call(bf16[8,2,128,256]{3,2,1,0:T(8,128)(2,1)} %copy-done.5), custom_call_target="tpu_custom_call" | custom-call | tf_op jit(solution)/shard_map/pallas_call | solution.py:207
  146.3 6.0 %collective-permute-start.4 = (bf16[2,128,256]{2,1,0:T(8,128)(2,1)}, bf16[2,128,256]{2,1,0:T(8,128)(2,1)S(1)}, u32[]{:S(2)}, u32[]{:S(2)}) collective-permute-start(bf16[2,128,256]{2,1,0:T(8,128)(2,1)} %shard_map.74), channel_id=1, source_target_pairs={{0,256},{256,0},{1,257},{257,1},{2,258},{258,2},{3,259},{259,3},{4... | collective-permute-start | bytes 393224 | tf_op jit(solution)/shard_map/ppermute | solution.py:289
  152.3 12.7 %collective-permute-done.4.received_ref = bf16[2,128,256]{2,1,0:T(8,128)(2,1)S(1)} collective-permute-done((bf16[2,128,256]{2,1,0:T(8,128)(2,1)}, bf16[2,128,256]{2,1,0:T(8,128)(2,1)S(1)}, u32[]{:S(2)}, u32[]{:S(2)}) %collective-permute-start.4) | collective-permute-done | bytes 131104 | tf_op jit(solution)/shard_map/ppermute | solution.py:289
  166.7 2.0 %shard_map.75 = (bf16[128,256]{1,0:T(8,128)(2,1)}, bf16[128,256]{1,0:T(8,128)(2,1)}) custom-call(bf16[8,2,128,256]{3,2,1,0:T(8,128)(2,1)} %copy-done.4, bf16[2,128,256]{2,1,0:T(8,128)(2,1)} %copy-done.7), custom_call_target="tpu_custom_call" | custom-call | tf_op jit(solution)/shard_map/pallas_call | solution.py:242
  (31 shorter events, 11.3 us)
Async XLA Ops:
  7.2 48.3 %copy-start = (f32[16,128]{1,0:T(8,128)S(1)}, f32[16,128]{1,0:T(8,128)}, u32[]{:S(2)}) copy-start(f32[16,128]{1,0:T(8,128)} %param.8) | copy-start | bytes 24580
  9.1 21.9 %all-to-all-start = ((bf16[4,512,128]{2,1,0:T(8,128)(2,1)}), bf16[4,512,128]{2,1,0:T(8,128)(2,1)S(1)}, u32[]{:S(2)}, u32[]{:S(2)}) async-start(bf16[4,512,128]{2,1,0:T(8,128)(2,1)} %shard_map.68), calls=%async_computation | async-start | bytes 1048576 | tf_op jit(solution)/shard_map/all_to_all | solution.py:251
  16.7 77.9 %all-gather.3.cloned.1.call-start = ((), (), s32[]{:S(2)}) async-start(), calls=%async_computation.5 | async-start | bytes 8912896 | tf_op jit(solution)/shard_map/all_gather | solution.py:266
  30.9 0.8 copy-start.6
  51.3 28.9 %all-to-all-start.2 = ((bf16[4,4,2,128,256]{4,3,2,1,0:T(8,128)(2,1)}), bf16[4,4,2,128,256]{4,3,2,1,0:T(8,128)(2,1)S(1)}, u32[]{:S(2)}, u32[]{:S(2)}) async-start(bf16[4,4,2,128,256]{4,3,2,1,0:T(8,128)(2,1)} %broadcast_in_dim.7), calls=%async_computation.2 | async-start | bytes 4194304 | tf_op jit(solution)/shard_map/all_to_all | solution.py:251
  80.2 8.4 %collective-permute-start = (bf16[4,2,2,2,128,256]{5,4,3,2,1,0:T(8,128)(2,1)S(1)}, bf16[4,2,2,2,128,256]{5,4,3,2,1,0:T(8,128)(2,1)}, u32[]{:S(2)}, u32[]{:S(2)}) collective-permute-start(bf16[4,2,2,2,128,256]{5,4,3,2,1,0:T(8,128)(2,1)S(1)} %bitcast.9), channel_id=1, source_target_pairs={{0,1},{1,0},{2,3},{3,2},{4,5},{5,4},{6,7},{7,6},{8,9},{9,8},{10,11... | collective-permute-start | bytes 6291464 | tf_op jit(solution)/shard_map/ppermute | solution.py:273
  94.6 18.0 %copy-start.3 = (bf16[256,2048]{1,0:T(8,128)(2,1)S(1)}, bf16[256,2048]{1,0:T(8,128)(2,1)}, u32[]{:S(2)}) copy-start(bf16[256,2048]{1,0:T(8,128)(2,1)} %shard_map.69.band_ref) | copy-start | bytes 3145732
  100.0 11.5 %collective-permute-start.1 = (bf16[128,256]{1,0:T(8,128)(2,1)S(1)}, bf16[128,256]{1,0:T(8,128)(2,1)S(1)}, u32[]{:S(2)}, u32[]{:S(2)}) collective-permute-start(bf16[128,256]{1,0:T(8,128)(2,1)S(1)} %get-tuple-element.21.product_ref), channel_id=1, source_target_pairs={{0,16},{16,32},{32,48},{48,64},{64,80},{80,96},{96,112},{112,128},... | collective-permute-start | bytes 196616 | tf_op jit(solution)/shard_map/ppermute | solution.py:277
  102.0 10.6 %collective-permute-start.2 = (bf16[128,256]{1,0:T(8,128)(2,1)S(1)}, bf16[128,256]{1,0:T(8,128)(2,1)S(1)}, u32[]{:S(2)}, u32[]{:S(2)}) collective-permute-start(bf16[128,256]{1,0:T(8,128)(2,1)S(1)} %get-tuple-element.22.mixed_ref), channel_id=1, source_target_pairs={{16,0},{32,16},{48,32},{64,48},{80,64},{96,80},{112,96},{128,112},... | collective-permute-start | bytes 196616 | tf_op jit(solution)/shard_map/ppermute | solution.py:278
  113.7 4.3 %collective-permute-start.3 = (bf16[256,512]{1,0:T(8,128)(2,1)S(1)}, bf16[256,512]{1,0:T(8,128)(2,1)S(1)}, u32[]{:S(2)}, u32[]{:S(2)}) collective-permute-start(bf16[256,512]{1,0:T(8,128)(2,1)S(1)} %shard_map.71.own_ref), channel_id=1, source_target_pairs={{0,1},{1,0},{2,3},{3,2},{4,5},{5,4},{6,7},{7,6},{8,9},{9,8},{10,11... | collective-permute-start | bytes 786440 | tf_op jit(solution)/shard_map/ppermute | solution.py:281
  120.2 1.9 %copy-start.1 = (bf16[2,2,2,2,2,512,128]{6,5,4,3,2,1,0:T(8,128)(2,1)}, bf16[2,2,2,2,2,512,128]{6,5,4,3,2,1,0:T(8,128)(2,1)S(1)}, u32[]{:S(2)}) copy-start(bf16[2,2,2,2,2,512,128]{6,5,4,3,2,1,0:T(8,128)(2,1)S(1)} %get-tuple-element.23.weight_ref) | copy-start | bytes 12582916
  122.2 18.5 %all-to-all-start.3 = ((bf16[8,2,128,256]{3,2,1,0:T(8,128)(2,1)}), bf16[8,2,128,256]{3,2,1,0:T(8,128)(2,1)S(1)}, u32[]{:S(2)}, u32[]{:S(2)}) async-start(bf16[8,2,128,256]{3,2,1,0:T(8,128)(2,1)} %shard_map.72), calls=%async_computation.3 | async-start | bytes 2097152 | tf_op jit(solution)/shard_map/all_to_all | solution.py:251
  125.7 2.2 %copy-start.2 = (bf16[2,2,2,2,2,512,128]{6,5,4,3,2,1,0:T(8,128)(2,1)S(1)}, bf16[2,2,2,2,2,512,128]{6,5,4,3,2,1,0:T(8,128)(2,1)}, u32[]{:S(2)}) copy-start(bf16[2,2,2,2,2,512,128]{6,5,4,3,2,1,0:T(8,128)(2,1)} %copy-done.1) | copy-start | bytes 12582916
  140.7 3.6 %copy-start.5 = (bf16[8,2,128,256]{3,2,1,0:T(8,128)(2,1)}, bf16[8,2,128,256]{3,2,1,0:T(8,128)(2,1)S(1)}, u32[]{:S(2)}) copy-start(bf16[8,2,128,256]{3,2,1,0:T(8,128)(2,1)S(1)} %all-to-all-done.3.parts_ref) | copy-start | bytes 3145732
  140.7 24.4 %all-to-all-start.4 = ((bf16[8,2,128,256]{3,2,1,0:T(8,128)(2,1)}), bf16[8,2,128,256]{3,2,1,0:T(8,128)(2,1)S(1)}, u32[]{:S(2)}, u32[]{:S(2)}) async-start(bf16[8,2,128,256]{3,2,1,0:T(8,128)(2,1)} %shard_map.73), calls=%async_computation.4 | async-start | bytes 2097152 | tf_op jit(solution)/shard_map/all_to_all | solution.py:251
  146.3 18.7 %collective-permute-start.4 = (bf16[2,128,256]{2,1,0:T(8,128)(2,1)}, bf16[2,128,256]{2,1,0:T(8,128)(2,1)S(1)}, u32[]{:S(2)}, u32[]{:S(2)}) collective-permute-start(bf16[2,128,256]{2,1,0:T(8,128)(2,1)} %shard_map.74), channel_id=1, source_target_pairs={{0,256},{256,0},{1,257},{257,1},{2,258},{258,2},{3,259},{259,3},{4... | collective-permute-start | bytes 393224 | tf_op jit(solution)/shard_map/ppermute | solution.py:289
  165.0 0.7 copy-start.7
  165.7 1.0 copy-start.4
Sparse Core Ops, SparseCore 0:
  31.9 62.6 all-gather.2

commit v9 on v7

--- a/solution.py
+++ b/solution.py
@@ -18,6 +18,7 @@
 BF16 = jnp.bfloat16
 F32 = jnp.float32
 VMEM_FORWARD = 40 << 20
+VMEM_SMALL = 16 << 20
 
 
 def bands_kernel(base_ref, band_ref):
@@ -34,6 +35,9 @@
     return pl.pallas_call(
         bands_kernel,
         out_shape=jax.ShapeDtypeStruct((2 * ROWS, 2 * GROUPS * ROWS), BF16),
+        in_specs=[pl.BlockSpec(memory_space=pltpu.VMEM)],
+        out_specs=pl.BlockSpec(memory_space=pltpu.VMEM),
+        compiler_params=pltpu.CompilerParams(vmem_limit_bytes=VMEM_SMALL),
     )(jnp.concatenate([causal, anticausal], 0))
 
 
@@ -51,28 +55,39 @@
     arrived,
 ):
     core = place_ref[0]
-    copies = [
-        pltpu.make_async_copy(
-            weight_hbm.at[pl.ds((x % 2) * 4, 4), core, :, x // 2], weight_ref.at[x], arrived.at[x]
-        )
-        for x in range(4)
-    ]
-    copies += [
-        pltpu.make_async_copy(weight_hbm.at[pl.ds(x * 4 + 2 * core, 2)], back_ref.at[x], arrived.at[4 + x])
-        for x in range(2)
-    ]
+    steps_to = lambda y, x: lax.rem(place_ref[4] + 4 - (2 * y + x // 2), 4)
+    copies = []
+    for x in range(4):
+        for y in range(2):
+            copies.append(
+                pltpu.make_async_copy(
+                    weight_hbm.at[pl.ds((x % 2) * 4, 4), core, steps_to(y, x)],
+                    weight_ref.at[x, y],
+                    arrived.at[2 * x + y],
+                )
+            )
+    for x in range(4):
+        for y in range(2):
+            copies.append(
+                pltpu.make_async_copy(
+                    weight_hbm.at[pl.ds((x % 2) * 4 + 2 * core, 2), :, steps_to(y, x)],
+                    back_ref.at[x % 2, y, x // 2],
+                    arrived.at[8 + 2 * x + y],
+                )
+            )
     for copy in copies:
         copy.start()
     streams, grad_gate = 0.0, 0.0
     contract = (((1,), (1,)), ((), ()))
     for x in range(4):
         tokens, cotangent, weight = [], [], []
-        copies[x].wait()
+        copies[2 * x].wait()
+        copies[2 * x + 1].wait()
         for values_ref, which in ((own_ref, core), (other_ref, 1 - core)):
             for y in range(2):
                 tokens.append(values_ref[x, :, y, 0].reshape(2 * ROWS, FEATURES))
                 cotangent.append(values_ref[x, :, y, 1].reshape(2 * ROWS, FEATURES))
-                weight += [weight_ref[x, 2 * which + z, y] for z in range(2)]
+                weight += [weight_ref[x, y, 2 * which + z] for z in range(2)]
         tokens, cotangent = jnp.concatenate(tokens, 1), jnp.concatenate(cotangent, 1)
         weight = jnp.concatenate(weight, 1)
         streams += lax.dot_general(weight[:BACK], tokens, contract, preferred_element_type=F32)
@@ -83,8 +98,8 @@
     query, key, value = (streams[i * HALF : (i + 1) * HALF].astype(F32) for i in range(3))
     product_ref[...] = (key * value).astype(BF16)
     mixed_ref[...] = (grad_gate * query).astype(BF16)
-    copies[4].wait()
-    copies[5].wait()
+    for copy in copies[8:]:
+        copy.wait()
 
 
 def forward(place, own, other, weight):
@@ -106,7 +121,7 @@
             pl.BlockSpec(memory_space=pl.ANY),
         ],
         out_specs=(vmem,) * 5,
-        scratch_shapes=[pltpu.VMEM((4, 4, 2, STREAMS, ROWS), BF16), pltpu.SemaphoreType.DMA((6,))],
+        scratch_shapes=[pltpu.VMEM((4, 2, 4, STREAMS, ROWS), BF16), pltpu.SemaphoreType.DMA((16,))],
         compiler_params=pltpu.CompilerParams(vmem_limit_bytes=VMEM_FORWARD),
         cost_estimate=pl.CostEstimate(flops=1 << 30, bytes_accessed=9 << 20, transcendentals=0),
     )(place, own, other, weight)
@@ -159,7 +174,7 @@
         out_shape=out_shape,
         in_specs=[smem] + [vmem] * (len(operands) - 1),
         out_specs=jax.tree.map(lambda _: vmem, out_shape),
-        compiler_params=pltpu.CompilerParams(vmem_limit_bytes=24 << 20),
+        compiler_params=pltpu.CompilerParams(vmem_limit_bytes=VMEM_SMALL),
         cost_estimate=pl.CostEstimate(flops=flops, bytes_accessed=1 << 20, transcendentals=0),
     )(*operands)
 
@@ -175,7 +190,7 @@
         for y in range(2):
             for x in range(4):
                 weight = [
-                    jnp.concatenate([weight_ref[x % 2, z, which, y, x // 2, cols] for z in range(2)], 1)
+                    jnp.concatenate([weight_ref[x % 2, y, x // 2, z, which, cols] for z in range(2)], 1)
                     for which in (core, 1 - core)
                 ]
                 result = jnp.dot(terms, jnp.concatenate(weight, 0), preferred_element_type=F32)
@@ -205,39 +220,27 @@
     return on_chip(combine_kernel, out_shape, operands, 1 << 20)
 
 
-def pack_kernel(in_ref, out_ref, packed_ref):
-    for h in range(2):
-        chans = slice(h * HALF, (h + 1) * HALF)
-        streams = [in_ref[stream, :, chans].astype(F32).T.astype(BF16) for stream in range(3)]
-        for l in range(2):
-            for stream in range(3):
-                packed_ref[2 * h + l, stream * HALF : (stream + 1) * HALF] = streams[stream]
-            packed_ref[2 * h + l, BACK:] = out_ref[chans]
-
-
-def packed(in_weight, out_weight):
-    vmem = pl.BlockSpec(memory_space=pltpu.VMEM)
-    return pl.pallas_call(
-        pack_kernel,
-        out_shape=jax.ShapeDtypeStruct((4, STREAMS, ROWS), BF16),
-        in_specs=[vmem] * 2,
-        out_specs=vmem,
-    )(in_weight, out_weight)
-
-
-def finish_kernel(mine_ref, theirs_ref, mixed_ref, grad_ref):
+def pack_kernel(place_ref, in_ref, out_ref, *packed_refs):
+    for steps, packed_ref in enumerate(packed_refs):
+        half = lax.div(lax.rem(place_ref[4] + steps, 4), 2)
+        chans = pl.ds(pl.multiple_of(half * HALF, HALF), HALF)
+        for stream in range(3):
+            turned = in_ref[stream, :, chans].astype(F32).T.astype(BF16)
+            packed_ref[stream * HALF : (stream + 1) * HALF] = turned
+        packed_ref[BACK:] = out_ref[chans]
+
+
+def packed(*operands):
+    return on_chip(pack_kernel, (jax.ShapeDtypeStruct((STREAMS, ROWS), BF16),) * 4, operands, 1 << 20)
+
+
+def finish_kernel(place_ref, mine_ref, theirs_ref, mixed_ref, grad_ref):
     for part, ref in enumerate((mixed_ref, grad_ref)):
         ref[...] = (mine_ref[part] + theirs_ref[part].astype(F32)).astype(BF16)
 
 
-def finish(*parts):
-    vmem = pl.BlockSpec(memory_space=pltpu.VMEM)
-    return pl.pallas_call(
-        finish_kernel,
-        out_shape=(jax.ShapeDtypeStruct((ROWS, FEATURES), BF16),) * 2,
-        in_specs=[vmem] * 2,
-        out_specs=(vmem, vmem),
-    )(*parts)
+def finish(*operands):
+    return on_chip(finish_kernel, (jax.ShapeDtypeStruct((ROWS, FEATURES), BF16),) * 2, operands, 1 << 16)
 
 
 def swapped(value, axes):
@@ -251,12 +254,16 @@
 def local(tokens, in_weight, out_weight, mr_filter, cotangent):
     half, core = lax.axis_index("h"), lax.axis_index("core")
     position = lax.axis_index(("l", "z"))
-    place = jnp.stack([core, position, lax.axis_index("x"), half]).astype(jnp.int32)
-
-    weight = swapped(packed(in_weight, out_weight), ("h", "l"))
+    along = lax.axis_index(("h", "l"))
+    place = jnp.stack([core, position, lax.axis_index("x"), half, along]).astype(jnp.int32)
+
+    pieces = list(packed(place, in_weight, out_weight))
+    for steps in (2, 1, 3):
+        pieces[steps] = lax.ppermute(pieces[steps], ("h", "l"), [(n, (n + steps) % 4) for n in range(4)])
+    weight = jnp.stack(pieces, 0)
     values = jnp.stack([tokens, cotangent], 0)
     weight, values = lax.optimization_barrier((weight, values))
-    weight = lax.all_gather(weight, ("z", "core"), axis=0).reshape(8, 2, 2, 2, STREAMS, ROWS)
+    weight = lax.all_gather(weight, ("z", "core"), axis=0).reshape(8, 2, 4, STREAMS, ROWS)
 
     band = bands(lax.dynamic_slice_in_dim(mr_filter, half * GROUPS, GROUPS, 0))
     values = gathered(values, ("h", "ylo"), 4)
@@ -275,7 +282,7 @@
 
     parts = swapped(backward(place, terms, other_terms, weight), ("ylo", "x"))
     mine, theirs = combine(place, parts)
-    return finish(mine, lax.ppermute(theirs, "h", cross))
+    return finish(place, mine, lax.ppermute(theirs, "h", cross))
 
 
 def solution(mesh):

time: 172 us -> 174 us (1.012)
  the two profiles are of different devices: /device:TPU:1 before, /device:TPU:16 now
where the time goes in v9:
time: 174 us; the launch traced here: 173 us
  blocking collectives  53.7 us (31%)
  waiting for transfers between devices  49.6 us (29%)
  starting transfers between devices  37.6 us (22%)
  between operations  14.2 us (8%)
  Pallas kernels  10 us (6%)
  local copies, waits for them, and re-layouts  6.65 us (4%)
  other arithmetic  1.83 us (1%)
    all_to_all x2, blocking collectives, swapped(): return lax.all_to_all(value, axes, 0, 0, tiled=True)  53.7 us
    all_to_all x1, waiting for transfers between devices, swapped(): return lax.all_to_all(value, axes, 0, 0, tiled=True)  24.5 us
    ppermute x3, starting transfers between devices, local(): lax.ppermute(pieces[steps], ('h', 'l'), [(n, (n + steps) % 4) for n in ra...  15 us
    ppermute x1, starting transfers between devices, local(): after = lax.ppermute(mixed, ('l', 'z'), [(b, a) for a, b in ring])  7.75 us
    ppermute x1, waiting for transfers between devices, local(): return finish(place, mine, lax.ppermute(theirs, 'h', cross))  7.63 us
    ppermute x3, waiting for transfers between devices, local(): lax.ppermute(pieces[steps], ('h', 'l'), [(n, (n + steps) % 4) for n in ra...  6.78 us
    pallas_call x5, Pallas kernels, on_chip(): pl.pallas_call(kernel, out_shape=out_shape, in_specs=[smem] + [vmem] * (l...  5.61 us
    unnamed x10, local copies, waits for them, and re-layouts  4.75 us
  transfers between devices with their start and end apart: 10, of which 9 were waited for; matrix products, arithmetic and copies ran while one was open for 2% of the time, Pallas kernels for 0%

profile of v9, /device:TPU:16, one launch (start us, length us, event | category | flops | bytes accessed | tf_op | source)
XLA Modules:
  0.0 173.5 jit_solution(1477270816180369250)
XLA Ops:
  9.8 5.7 %collective-permute-start = (bf16[512,128]{1,0:T(8,128)(2,1)S(1)}, bf16[512,128]{1,0:T(8,128)(2,1)S(1)}, u32[]{:S(2)}, u32[]{:S(2)}) collective-permute-start(bf16[512,128]{1,0:T(8,128)(2,1)S(1)} %get-tuple-element.18), channel_id=1, source_target_pairs={{0,128},{128,256},{256,384},{384,0},{1,129},{129,257},{257,385},{3... | collective-permute-start | bytes 393224 | tf_op jit(solution)/shard_map/ppermute | solution.py:262
  15.5 7.4 %collective-permute-start.1 = (bf16[512,128]{1,0:T(8,128)(2,1)S(1)}, bf16[512,128]{1,0:T(8,128)(2,1)S(1)}, u32[]{:S(2)}, u32[]{:S(2)}) collective-permute-start(bf16[512,128]{1,0:T(8,128)(2,1)S(1)} %get-tuple-element.19), channel_id=1, source_target_pairs={{0,256},{128,384},{256,0},{384,128},{1,257},{129,385},{257,1},{385... | collective-permute-start | bytes 393224 | tf_op jit(solution)/shard_map/ppermute | solution.py:262
  22.9 1.9 %collective-permute-start.2 = (bf16[512,128]{1,0:T(8,128)(2,1)S(1)}, bf16[512,128]{1,0:T(8,128)(2,1)S(1)}, u32[]{:S(2)}, u32[]{:S(2)}) collective-permute-start(bf16[512,128]{1,0:T(8,128)(2,1)S(1)} %get-tuple-element.20), channel_id=1, source_target_pairs={{0,384},{128,0},{256,128},{384,256},{1,385},{129,1},{257,129},{385... | collective-permute-start | bytes 393224 | tf_op jit(solution)/shard_map/ppermute | solution.py:262
  25.8 3.9 %collective-permute-done.1 = bf16[512,128]{1,0:T(8,128)(2,1)S(1)} collective-permute-done((bf16[512,128]{1,0:T(8,128)(2,1)S(1)}, bf16[512,128]{1,0:T(8,128)(2,1)S(1)}, u32[]{:S(2)}, u32[]{:S(2)}) %collective-permute-start.1) | collective-permute-done | bytes 131104 | tf_op jit(solution)/shard_map/ppermute | solution.py:262
  29.7 2.8 %collective-permute-done.2 = bf16[512,128]{1,0:T(8,128)(2,1)S(1)} collective-permute-done((bf16[512,128]{1,0:T(8,128)(2,1)S(1)}, bf16[512,128]{1,0:T(8,128)(2,1)S(1)}, u32[]{:S(2)}, u32[]{:S(2)}) %collective-permute-start.2) | collective-permute-done | bytes 131104 | tf_op jit(solution)/shard_map/ppermute | solution.py:262
  33.5 21.4 %all_to_all.15 = bf16[4,2,128,256]{3,2,1,0:T(8,128)(2,1)S(1)} all-to-all(bf16[4,2,128,256]{3,2,1,0:T(8,128)(2,1)S(1)} %broadcast_in_dim.6), channel_id=1, replica_groups=mesh['h'=2,'l'=2,'z'=8,'ylo'=2,'x'=4,'core'=2] {'h','ylo'}, dimensions={0} | all-to-all | bytes 1048576 | tf_op jit(solution)/shard_map/all_to_all | solution.py:247
  54.9 1.6 broadcast_in_dim.7
  56.5 4.3 %all-to-all-start.1 = ((bf16[4,4,2,128,256]{4,3,2,1,0:T(8,128)(2,1)}), bf16[4,4,2,128,256]{4,3,2,1,0:T(8,128)(2,1)S(1)}, u32[]{:S(2)}, u32[]{:S(2)}) async-start(bf16[4,4,2,128,256]{4,3,2,1,0:T(8,128)(2,1)} %broadcast_in_dim.7), calls=%async_computation.1 | async-start | bytes 4194304 | tf_op jit(solution)/shard_map/all_to_all | solution.py:247
  61.4 24.5 %all-to-all-done.1 = bf16[4,4,2,128,256]{4,3,2,1,0:T(8,128)(2,1)S(1)} async-done(((bf16[4,4,2,128,256]{4,3,2,1,0:T(8,128)(2,1)}), bf16[4,4,2,128,256]{4,3,2,1,0:T(8,128)(2,1)S(1)}, u32[]{:S(2)}, u32[]{:S(2)}) %all-to-all-start.1) | async-done | bytes 2097184 | tf_op jit(solution)/shard_map/all_to_all | solution.py:247
  85.9 1.9 %collective-permute-start.3 = (bf16[4,2,2,2,128,256]{5,4,3,2,1,0:T(8,128)(2,1)S(1)}, bf16[4,2,2,2,128,256]{5,4,3,2,1,0:T(8,128)(2,1)S(1)}, u32[]{:S(2)}, u32[]{:S(2)}) collective-permute-start(bf16[4,2,2,2,128,256]{5,4,3,2,1,0:T(8,128)(2,1)S(1)} %bitcast.14), channel_id=1, source_target_pairs={{0,1},{1,0},{2,3},{3,2},{4,5},{5,4},{6,7},{7,6},{8,9},{9,8},{10,11... | collective-permute-start | bytes 6291464 | tf_op jit(solution)/shard_map/ppermute | solution.py:273
  87.8 4.1 %collective-permute-done.3.other_ref = bf16[4,2,2,2,128,256]{5,4,3,2,1,0:T(8,128)(2,1)S(1)} collective-permute-done((bf16[4,2,2,2,128,256]{5,4,3,2,1,0:T(8,128)(2,1)S(1)}, bf16[4,2,2,2,128,256]{5,4,3,2,1,0:T(8,128)(2,1)S(1)}, u32[]{:S(2)}, u32[]{:S(2)}) %collective-permute-start.3) | collective-permute-done | bytes 2097184 | tf_op jit(solution)/shard_map/ppermute | solution.py:273
  91.9 1.4 copy-done.1
  93.3 3.1 %all-gather.3.cloned.1.call-done = bf16[64,512,128]{2,1,0:T(8,128)(2,1)} async-done(((bf16[4,512,128]{2,1,0:T(8,128)(2,1)}), bf16[64,512,128]{2,1,0:T(8,128)(2,1)}) %all-gather.3.cloned.1.call-update) | async-done | bytes 8388624 | tf_op jit(solution)/shard_map/all_gather | solution.py:266
  96.5 1.6 copy-done.2
  98.0 4.1 %shard_map.70 = (bf16[384,256]{1,0:T(8,128)(2,1)S(1)}, f32[128,256]{1,0:T(8,128)S(1)}, bf16[128,256]{1,0:T(8,128)(2,1)S(1)}, bf16[128,256]{1,0:T(8,128)(2,1)S(1)}, bf16[2,2,2,2,2,512,128]{6,5,4,3,2,1,0:T(8,128)(2,1)S(1)}) custom-call(s32[5]{0:T(128)S(1)} %stack.47.place_ref, bf16[4,2,2,2,128,256]{5,4,3,2,1,0:T(8,128)(2,1)S(1)} %bitcast.15, ...), custom_call_target="tpu_custom_call" | custom-call | flops 1073741824 | bytes 9437184 | tf_op jit(solution)/shard_map/pallas_call | solution.py:108
  102.1 1.9 %collective-permute-start.4 = (bf16[128,256]{1,0:T(8,128)(2,1)S(1)}, bf16[128,256]{1,0:T(8,128)(2,1)S(1)}, u32[]{:S(2)}, u32[]{:S(2)}) collective-permute-start(bf16[128,256]{1,0:T(8,128)(2,1)S(1)} %get-tuple-element.27.product_ref), channel_id=1, source_target_pairs={{0,16},{16,32},{32,48},{48,64},{64,80},{80,96},{96,112},{112,128},... | collective-permute-start | bytes 196616 | tf_op jit(solution)/shard_map/ppermute | solution.py:277
  104.0 7.7 %collective-permute-start.5 = (bf16[128,256]{1,0:T(8,128)(2,1)S(1)}, bf16[128,256]{1,0:T(8,128)(2,1)S(1)}, u32[]{:S(2)}, u32[]{:S(2)}) collective-permute-start(bf16[128,256]{1,0:T(8,128)(2,1)S(1)} %get-tuple-element.28.mixed_ref), channel_id=1, source_target_pairs={{16,0},{32,16},{48,32},{64,48},{80,64},{96,80},{112,96},{128,112},... | collective-permute-start | bytes 196616 | tf_op jit(solution)/shard_map/ppermute | solution.py:278
  112.3 1.4 collective-permute-done.5.after_ref
  114.7 1.9 %collective-permute-start.6 = (bf16[256,512]{1,0:T(8,128)(2,1)S(1)}, bf16[256,512]{1,0:T(8,128)(2,1)S(1)}, u32[]{:S(2)}, u32[]{:S(2)}) collective-permute-start(bf16[256,512]{1,0:T(8,128)(2,1)S(1)} %shard_map.71.own_ref), channel_id=1, source_target_pairs={{0,1},{1,0},{2,3},{3,2},{4,5},{5,4},{6,7},{7,6},{8,9},{9,8},{10,11... | collective-permute-start | bytes 786440 | tf_op jit(solution)/shard_map/ppermute | solution.py:281
  116.7 1.5 collective-permute-done.6.other_ref
  118.2 1.8 %shard_map.72 = bf16[8,2,2,128,256]{4,3,2,1,0:T(8,128)(2,1)S(1)} custom-call(s32[5]{0:T(128)S(1)} %stack.47.place_ref, bf16[256,512]{1,0:T(8,128)(2,1)S(1)} %shard_map.71.own_ref, bf16[256,512]{1,0:T(8,128)(2,1)S(1)} %collective-permute-done.6.other_ref, bf16[2,2,2,2,2,512,128]{6,5,4,3,2,1,0:T(8,128)(2,1)S(1)} %get-tuple-element.29.weight_ref), custom_call_target="tpu_custom_call" | custom-call | flops 1073741824 | bytes 1048576 | tf_op jit(solution)/shard_map/pallas_call | solution.py:172
  120.0 32.3 %all_to_all.16.parts_ref = bf16[8,2,2,128,256]{4,3,2,1,0:T(8,128)(2,1)S(1)} all-to-all(bf16[8,2,2,128,256]{4,3,2,1,0:T(8,128)(2,1)S(1)} %shard_map.72), channel_id=1, replica_groups=mesh['h'=2,'l'=2,'z'=8,'ylo'=2,'x'=4,'core'=2] {'ylo','x'}, dimensions={0} | all-to-all | bytes 4194304 | tf_op jit(solution)/shard_map/all_to_all | solution.py:247
  153.1 4.7 %collective-permute-start.7 = (bf16[2,128,256]{2,1,0:T(8,128)(2,1)S(1)}, bf16[2,128,256]{2,1,0:T(8,128)(2,1)S(1)}, u32[]{:S(2)}, u32[]{:S(2)}) collective-permute-start(bf16[2,128,256]{2,1,0:T(8,128)(2,1)S(1)} %get-tuple-element.31), channel_id=1, source_target_pairs={{0,256},{256,0},{1,257},{257,1},{2,258},{258,2},{3,259},{259,3},{4... | collective-permute-start | bytes 393224 | tf_op jit(solution)/shard_map/ppermute | solution.py:285
  157.8 7.6 %collective-permute-done.7.theirs_ref = bf16[2,128,256]{2,1,0:T(8,128)(2,1)S(1)} collective-permute-done((bf16[2,128,256]{2,1,0:T(8,128)(2,1)S(1)}, bf16[2,128,256]{2,1,0:T(8,128)(2,1)S(1)}, u32[]{:S(2)}, u32[]{:S(2)}) %collective-permute-start.7) | collective-permute-done | bytes 131104 | tf_op jit(solution)/shard_map/ppermute | solution.py:285
  (26 shorter events, 8.5 us)
Async XLA Ops:
  7.2 53.6 %copy-start = (f32[16,128]{1,0:T(8,128)S(1)}, f32[16,128]{1,0:T(8,128)}, u32[]{:S(2)}) copy-start(f32[16,128]{1,0:T(8,128)} %param.8) | copy-start | bytes 24580
  7.2 89.3 %all-gather.3.cloned.1.call-start = ((), (), s32[]{:S(2)}) async-start(), calls=%async_computation.3 | async-start | bytes 8912896 | tf_op jit(solution)/shard_map/all_gather | solution.py:266
  7.3 0.9 copy-start.3
  8.2 0.8 copy-start.4
  9.8 15.9 %collective-permute-start = (bf16[512,128]{1,0:T(8,128)(2,1)S(1)}, bf16[512,128]{1,0:T(8,128)(2,1)S(1)}, u32[]{:S(2)}, u32[]{:S(2)}) collective-permute-start(bf16[512,128]{1,0:T(8,128)(2,1)S(1)} %get-tuple-element.18), channel_id=1, source_target_pairs={{0,128},{128,256},{256,384},{384,0},{1,129},{129,257},{257,385},{3... | collective-permute-start | bytes 393224 | tf_op jit(solution)/shard_map/ppermute | solution.py:262
  15.5 14.2 %collective-permute-start.1 = (bf16[512,128]{1,0:T(8,128)(2,1)S(1)}, bf16[512,128]{1,0:T(8,128)(2,1)S(1)}, u32[]{:S(2)}, u32[]{:S(2)}) collective-permute-start(bf16[512,128]{1,0:T(8,128)(2,1)S(1)} %get-tuple-element.19), channel_id=1, source_target_pairs={{0,256},{128,384},{256,0},{384,128},{1,257},{129,385},{257,1},{385... | collective-permute-start | bytes 393224 | tf_op jit(solution)/shard_map/ppermute | solution.py:262
  22.9 9.6 %collective-permute-start.2 = (bf16[512,128]{1,0:T(8,128)(2,1)S(1)}, bf16[512,128]{1,0:T(8,128)(2,1)S(1)}, u32[]{:S(2)}, u32[]{:S(2)}) collective-permute-start(bf16[512,128]{1,0:T(8,128)(2,1)S(1)} %get-tuple-element.20), channel_id=1, source_target_pairs={{0,384},{128,0},{256,128},{384,256},{1,385},{129,1},{257,129},{385... | collective-permute-start | bytes 393224 | tf_op jit(solution)/shard_map/ppermute | solution.py:262
  56.5 29.4 %all-to-all-start.1 = ((bf16[4,4,2,128,256]{4,3,2,1,0:T(8,128)(2,1)}), bf16[4,4,2,128,256]{4,3,2,1,0:T(8,128)(2,1)S(1)}, u32[]{:S(2)}, u32[]{:S(2)}) async-start(bf16[4,4,2,128,256]{4,3,2,1,0:T(8,128)(2,1)} %broadcast_in_dim.7), calls=%async_computation.1 | async-start | bytes 4194304 | tf_op jit(solution)/shard_map/all_to_all | solution.py:247
  85.9 6.0 %collective-permute-start.3 = (bf16[4,2,2,2,128,256]{5,4,3,2,1,0:T(8,128)(2,1)S(1)}, bf16[4,2,2,2,128,256]{5,4,3,2,1,0:T(8,128)(2,1)S(1)}, u32[]{:S(2)}, u32[]{:S(2)}) collective-permute-start(bf16[4,2,2,2,128,256]{5,4,3,2,1,0:T(8,128)(2,1)S(1)} %bitcast.14), channel_id=1, source_target_pairs={{0,1},{1,0},{2,3},{3,2},{4,5},{5,4},{6,7},{7,6},{8,9},{9,8},{10,11... | collective-permute-start | bytes 6291464 | tf_op jit(solution)/shard_map/ppermute | solution.py:273
  91.9 1.4 copy-start.1
  96.5 1.6 copy-start.2
  102.1 10.1 %collective-permute-start.4 = (bf16[128,256]{1,0:T(8,128)(2,1)S(1)}, bf16[128,256]{1,0:T(8,128)(2,1)S(1)}, u32[]{:S(2)}, u32[]{:S(2)}) collective-permute-start(bf16[128,256]{1,0:T(8,128)(2,1)S(1)} %get-tuple-element.27.product_ref), channel_id=1, source_target_pairs={{0,16},{16,32},{32,48},{48,64},{64,80},{80,96},{96,112},{112,128},... | collective-permute-start | bytes 196616 | tf_op jit(solution)/shard_map/ppermute | solution.py:277
  104.0 9.6 %collective-permute-start.5 = (bf16[128,256]{1,0:T(8,128)(2,1)S(1)}, bf16[128,256]{1,0:T(8,128)(2,1)S(1)}, u32[]{:S(2)}, u32[]{:S(2)}) collective-permute-start(bf16[128,256]{1,0:T(8,128)(2,1)S(1)} %get-tuple-element.28.mixed_ref), channel_id=1, source_target_pairs={{16,0},{32,16},{48,32},{64,48},{80,64},{96,80},{112,96},{128,112},... | collective-permute-start | bytes 196616 | tf_op jit(solution)/shard_map/ppermute | solution.py:278
  114.7 3.4 %collective-permute-start.6 = (bf16[256,512]{1,0:T(8,128)(2,1)S(1)}, bf16[256,512]{1,0:T(8,128)(2,1)S(1)}, u32[]{:S(2)}, u32[]{:S(2)}) collective-permute-start(bf16[256,512]{1,0:T(8,128)(2,1)S(1)} %shard_map.71.own_ref), channel_id=1, source_target_pairs={{0,1},{1,0},{2,3},{3,2},{4,5},{5,4},{6,7},{7,6},{8,9},{9,8},{10,11... | collective-permute-start | bytes 786440 | tf_op jit(solution)/shard_map/ppermute | solution.py:281
  153.1 12.4 %collective-permute-start.7 = (bf16[2,128,256]{2,1,0:T(8,128)(2,1)S(1)}, bf16[2,128,256]{2,1,0:T(8,128)(2,1)S(1)}, u32[]{:S(2)}, u32[]{:S(2)}) collective-permute-start(bf16[2,128,256]{2,1,0:T(8,128)(2,1)S(1)} %get-tuple-element.31), channel_id=1, source_target_pairs={{0,256},{256,0},{1,257},{257,1},{2,258},{258,2},{3,259},{259,3},{4... | collective-permute-start | bytes 393224 | tf_op jit(solution)/shard_map/ppermute | solution.py:285
Sparse Core Ops, SparseCore 0:
  33.5 62.8 all-gather.2

commit v10 on v9

--- a/solution.py
+++ b/solution.py
@@ -44,7 +44,7 @@
 def forward_kernel(
     place_ref,
     own_ref,
-    other_ref,
+    other_hbm,
     weight_hbm,
     streams_ref,
     gate_ref,
@@ -52,16 +52,17 @@
     mixed_ref,
     back_ref,
     weight_ref,
+    other_ref,
     arrived,
 ):
     core = place_ref[0]
-    steps_to = lambda y, x: lax.rem(place_ref[4] + 4 - (2 * y + x // 2), 4)
     copies = []
+    others = [pltpu.make_async_copy(other_hbm.at[x], other_ref.at[x], arrived.at[16 + x]) for x in range(4)]
     for x in range(4):
         for y in range(2):
             copies.append(
                 pltpu.make_async_copy(
-                    weight_hbm.at[pl.ds((x % 2) * 4, 4), core, steps_to(y, x)],
+                    weight_hbm.at[pl.ds((x % 2) * 4, 4), core, 2 * y + x // 2],
                     weight_ref.at[x, y],
                     arrived.at[2 * x + y],
                 )
@@ -70,17 +71,22 @@
         for y in range(2):
             copies.append(
                 pltpu.make_async_copy(
-                    weight_hbm.at[pl.ds((x % 2) * 4 + 2 * core, 2), :, steps_to(y, x)],
+                    weight_hbm.at[pl.ds((x % 2) * 4 + 2 * core, 2), :, 2 * y + x // 2],
                     back_ref.at[x % 2, y, x // 2],
                     arrived.at[8 + 2 * x + y],
                 )
             )
-    for copy in copies:
+    for x in range(4):
+        others[x].start()
+        copies[2 * x].start()
+        copies[2 * x + 1].start()
+    for copy in copies[8:]:
         copy.start()
     streams, grad_gate = 0.0, 0.0
     contract = (((1,), (1,)), ((), ()))
     for x in range(4):
         tokens, cotangent, weight = [], [], []
+        others[x].wait()
         copies[2 * x].wait()
         copies[2 * x + 1].wait()
         for values_ref, which in ((own_ref, core), (other_ref, 1 - core)):
@@ -117,11 +123,15 @@
         in_specs=[
             pl.BlockSpec(memory_space=pltpu.SMEM),
             vmem,
-            vmem,
+            pl.BlockSpec(memory_space=pl.ANY),
             pl.BlockSpec(memory_space=pl.ANY),
         ],
         out_specs=(vmem,) * 5,
-        scratch_shapes=[pltpu.VMEM((4, 2, 4, STREAMS, ROWS), BF16), pltpu.SemaphoreType.DMA((16,))],
+        scratch_shapes=[
+            pltpu.VMEM((4, 2, 4, STREAMS, ROWS), BF16),
+            pltpu.VMEM((4, 2, 2, 2, ROWS, FEATURES), BF16),
+            pltpu.SemaphoreType.DMA((20,)),
+        ],
         compiler_params=pltpu.CompilerParams(vmem_limit_bytes=VMEM_FORWARD),
         cost_estimate=pl.CostEstimate(flops=1 << 30, bytes_accessed=9 << 20, transcendentals=0),
     )(place, own, other, weight)
@@ -220,18 +230,24 @@
     return on_chip(combine_kernel, out_shape, operands, 1 << 20)
 
 
-def pack_kernel(place_ref, in_ref, out_ref, *packed_refs):
-    for steps, packed_ref in enumerate(packed_refs):
-        half = lax.div(lax.rem(place_ref[4] + steps, 4), 2)
-        chans = pl.ds(pl.multiple_of(half * HALF, HALF), HALF)
-        for stream in range(3):
-            turned = in_ref[stream, :, chans].astype(F32).T.astype(BF16)
-            packed_ref[stream * HALF : (stream + 1) * HALF] = turned
-        packed_ref[BACK:] = out_ref[chans]
-
-
-def packed(*operands):
-    return on_chip(pack_kernel, (jax.ShapeDtypeStruct((STREAMS, ROWS), BF16),) * 4, operands, 1 << 20)
+def pack_kernel(in_ref, out_ref, packed_ref):
+    for h in range(2):
+        chans = slice(h * HALF, (h + 1) * HALF)
+        streams = [in_ref[stream, :, chans].astype(F32).T.astype(BF16) for stream in range(3)]
+        for l in range(2):
+            for stream in range(3):
+                packed_ref[2 * h + l, stream * HALF : (stream + 1) * HALF] = streams[stream]
+            packed_ref[2 * h + l, BACK:] = out_ref[chans]
+
+
+def packed(in_weight, out_weight):
+    vmem = pl.BlockSpec(memory_space=pltpu.VMEM)
+    return pl.pallas_call(
+        pack_kernel,
+        out_shape=jax.ShapeDtypeStruct((4, STREAMS, ROWS), BF16),
+        in_specs=[vmem] * 2,
+        out_specs=vmem,
+    )(in_weight, out_weight)
 
 
 def finish_kernel(place_ref, mine_ref, theirs_ref, mixed_ref, grad_ref):
@@ -254,13 +270,9 @@
 def local(tokens, in_weight, out_weight, mr_filter, cotangent):
     half, core = lax.axis_index("h"), lax.axis_index("core")
     position = lax.axis_index(("l", "z"))
-    along = lax.axis_index(("h", "l"))
-    place = jnp.stack([core, position, lax.axis_index("x"), half, along]).astype(jnp.int32)
-
-    pieces = list(packed(place, in_weight, out_weight))
-    for steps in (2, 1, 3):
-        pieces[steps] = lax.ppermute(pieces[steps], ("h", "l"), [(n, (n + steps) % 4) for n in range(4)])
-    weight = jnp.stack(pieces, 0)
+    place = jnp.stack([core, position, lax.axis_index("x"), half]).astype(jnp.int32)
+
+    weight = swapped(packed(in_weight, out_weight), ("h", "l"))
     values = jnp.stack([tokens, cotangent], 0)
     weight, values = lax.optimization_barrier((weight, values))
     weight = lax.all_gather(weight, ("z", "core"), axis=0).reshape(8, 2, 4, STREAMS, ROWS)

time: 174 us -> 169 us (0.971)
  the two profiles are of different devices: /device:TPU:16 before, /device:TPU:1 now
where the time goes in v10:
time: 169 us; the launch traced here: 166 us
  waiting for transfers between devices  53.2 us (31%)
  blocking collectives  46.5 us (28%)
  starting transfers between devices  36.9 us (22%)
  between operations  14.1 us (8%)
  Pallas kernels  11.8 us (7%)
  local copies, waits for them, and re-layouts  2.61 us (2%)
    all_to_all x2, blocking collectives, swapped(): return lax.all_to_all(value, axes, 0, 0, tiled=True)  46.5 us
    all_to_all x2, waiting for transfers between devices, swapped(): return lax.all_to_all(value, axes, 0, 0, tiled=True)  37.5 us
    all_to_all x2, starting transfers between devices, swapped(): return lax.all_to_all(value, axes, 0, 0, tiled=True)  11.8 us
    ppermute x1, starting transfers between devices, local(): after = lax.ppermute(mixed, ('l', 'z'), [(b, a) for a, b in ring])  9.29 us
    ppermute x1, starting transfers between devices, local(): return finish(place, mine, lax.ppermute(theirs, 'h', cross))  6.35 us
    all_gather x1, waiting for transfers between devices, local(): lax.all_gather(weight, ('z', 'core'), axis=0)  6.02 us
    pallas_call x4, Pallas kernels, on_chip(): pl.pallas_call(kernel, out_shape=out_shape, in_specs=[smem] + [vmem] * (l...  4.86 us
    pallas_call x1, Pallas kernels, forward(): pl.pallas_call(forward_kernel, out_shape=(shape(BACK, BF16), shape(HALF,...  4.69 us
  transfers between devices with their start and end apart: 8, of which 8 were waited for; matrix products, arithmetic and copies ran while one was open for 2% of the time, Pallas kernels for 0%

profile of v10, /device:TPU:1, one launch (start us, length us, event | category | flops | bytes accessed | tf_op | source)
XLA Modules:
  0.0 166.2 jit_solution(111538555188142831)
XLA Ops:
  7.2 1.9 %shard_map.68 = bf16[4,512,128]{2,1,0:T(8,128)(2,1)} custom-call(bf16[3,128,256]{2,1,0:T(8,128)(2,1)} %in_ref.1, bf16[256,128]{1,0:T(8,128)(2,1)} %out_ref.1), custom_call_target="tpu_custom_call" | custom-call | tf_op jit(solution)/shard_map/pallas_call | solution.py:245
  9.0 7.6 %all-to-all-start = ((bf16[4,512,128]{2,1,0:T(8,128)(2,1)}), bf16[4,512,128]{2,1,0:T(8,128)(2,1)S(1)}, u32[]{:S(2)}, u32[]{:S(2)}) async-start(bf16[4,512,128]{2,1,0:T(8,128)(2,1)} %shard_map.68), calls=%async_computation | async-start | bytes 1048576 | tf_op jit(solution)/shard_map/all_to_all | solution.py:263
  16.7 0.9 pad_maximum_fusion
  17.6 13.3 %all-to-all-done = bf16[4,512,128]{2,1,0:T(8,128)(2,1)S(1)} async-done(((bf16[4,512,128]{2,1,0:T(8,128)(2,1)}), bf16[4,512,128]{2,1,0:T(8,128)(2,1)S(1)}, u32[]{:S(2)}, u32[]{:S(2)}) %all-to-all-start) | async-done | bytes 524320 | tf_op jit(solution)/shard_map/all_to_all | solution.py:263
  31.8 17.9 %all_to_all.20 = bf16[4,2,128,256]{3,2,1,0:T(8,128)(2,1)S(1)} all-to-all(bf16[4,2,128,256]{3,2,1,0:T(8,128)(2,1)S(1)} %broadcast_in_dim.6), channel_id=1, replica_groups=mesh['h'=2,'l'=2,'z'=8,'ylo'=2,'x'=4,'core'=2] {'h','ylo'}, dimensions={0} | all-to-all | bytes 1048576 | tf_op jit(solution)/shard_map/all_to_all | solution.py:263
  49.7 1.6 broadcast_in_dim.7
  51.3 4.1 %all-to-all-start.2 = ((bf16[4,4,2,128,256]{4,3,2,1,0:T(8,128)(2,1)}), bf16[4,4,2,128,256]{4,3,2,1,0:T(8,128)(2,1)S(1)}, u32[]{:S(2)}, u32[]{:S(2)}) async-start(bf16[4,4,2,128,256]{4,3,2,1,0:T(8,128)(2,1)} %broadcast_in_dim.7), calls=%async_computation.2 | async-start | bytes 4194304 | tf_op jit(solution)/shard_map/all_to_all | solution.py:263
  56.0 24.1 %all-to-all-done.2 = bf16[4,4,2,128,256]{4,3,2,1,0:T(8,128)(2,1)S(1)} async-done(((bf16[4,4,2,128,256]{4,3,2,1,0:T(8,128)(2,1)}), bf16[4,4,2,128,256]{4,3,2,1,0:T(8,128)(2,1)S(1)}, u32[]{:S(2)}, u32[]{:S(2)}) %all-to-all-start.2) | async-done | bytes 2097184 | tf_op jit(solution)/shard_map/all_to_all | solution.py:263
  80.1 4.4 %collective-permute-start = (bf16[4,2,2,2,128,256]{5,4,3,2,1,0:T(8,128)(2,1)S(1)}, bf16[4,2,2,2,128,256]{5,4,3,2,1,0:T(8,128)(2,1)}, u32[]{:S(2)}, u32[]{:S(2)}) collective-permute-start(bf16[4,2,2,2,128,256]{5,4,3,2,1,0:T(8,128)(2,1)S(1)} %bitcast.9), channel_id=1, source_target_pairs={{0,1},{1,0},{2,3},{3,2},{4,5},{5,4},{6,7},{7,6},{8,9},{9,8},{10,11... | collective-permute-start | bytes 6291464 | tf_op jit(solution)/shard_map/ppermute | solution.py:285
  84.7 3.9 %collective-permute-done.other_hbm = bf16[4,2,2,2,128,256]{5,4,3,2,1,0:T(8,128)(2,1)} collective-permute-done((bf16[4,2,2,2,128,256]{5,4,3,2,1,0:T(8,128)(2,1)S(1)}, bf16[4,2,2,2,128,256]{5,4,3,2,1,0:T(8,128)(2,1)}, u32[]{:S(2)}, u32[]{:S(2)}) %collective-permute-start) | collective-permute-done | bytes 2097184 | tf_op jit(solution)/shard_map/ppermute | solution.py:285
  88.6 6.0 %all-gather.3.cloned.1.call-done = bf16[64,512,128]{2,1,0:T(8,128)(2,1)} async-done(((bf16[4,512,128]{2,1,0:T(8,128)(2,1)}), bf16[64,512,128]{2,1,0:T(8,128)(2,1)}) %all-gather.3.cloned.1.call-update) | async-done | bytes 8388624 | tf_op jit(solution)/shard_map/all_gather | solution.py:278
  94.6 4.7 %shard_map.70 = (bf16[384,256]{1,0:T(8,128)(2,1)S(1)}, f32[128,256]{1,0:T(8,128)S(1)}, bf16[128,256]{1,0:T(8,128)(2,1)S(1)}, bf16[128,256]{1,0:T(8,128)(2,1)S(1)}, bf16[2,2,2,2,2,512,128]{6,5,4,3,2,1,0:T(8,128)(2,1)S(1)}) custom-call(s32[4]{0:T(128)S(1)} %pad_add_fusion.place_ref, bf16[4,2,2,2,128,256]{5,4,3,2,1,0:T(8,128)(2,1)S(1)} %bitcast.10, ...), custom_call_target="tpu_custom_call" | custom-call | flops 1073741824 | bytes 9437184 | tf_op jit(solution)/shard_map/pallas_call | solution.py:114
  99.3 1.9 %collective-permute-start.1 = (bf16[128,256]{1,0:T(8,128)(2,1)S(1)}, bf16[128,256]{1,0:T(8,128)(2,1)S(1)}, u32[]{:S(2)}, u32[]{:S(2)}) collective-permute-start(bf16[128,256]{1,0:T(8,128)(2,1)S(1)} %get-tuple-element.19.product_ref), channel_id=1, source_target_pairs={{0,16},{16,32},{32,48},{48,64},{64,80},{80,96},{96,112},{112,128},... | collective-permute-start | bytes 196616 | tf_op jit(solution)/shard_map/ppermute | solution.py:289
  101.2 9.3 %collective-permute-start.2 = (bf16[128,256]{1,0:T(8,128)(2,1)S(1)}, bf16[128,256]{1,0:T(8,128)(2,1)S(1)}, u32[]{:S(2)}, u32[]{:S(2)}) collective-permute-start(bf16[128,256]{1,0:T(8,128)(2,1)S(1)} %get-tuple-element.20.mixed_ref), channel_id=1, source_target_pairs={{16,0},{32,16},{48,32},{64,48},{80,64},{96,80},{112,96},{128,112},... | collective-permute-start | bytes 196616 | tf_op jit(solution)/shard_map/ppermute | solution.py:290
  110.7 1.1 collective-permute-done.2.after_ref
  111.8 1.1 shard_map.71.own_ref
  112.9 3.1 %collective-permute-start.3 = (bf16[256,512]{1,0:T(8,128)(2,1)S(1)}, bf16[256,512]{1,0:T(8,128)(2,1)S(1)}, u32[]{:S(2)}, u32[]{:S(2)}) collective-permute-start(bf16[256,512]{1,0:T(8,128)(2,1)S(1)} %shard_map.71.own_ref), channel_id=1, source_target_pairs={{0,1},{1,0},{2,3},{3,2},{4,5},{5,4},{6,7},{7,6},{8,9},{9,8},{10,11... | collective-permute-start | bytes 786440 | tf_op jit(solution)/shard_map/ppermute | solution.py:293
  116.0 1.1 collective-permute-done.3.other_ref
  117.2 1.8 %shard_map.72 = bf16[8,2,2,128,256]{4,3,2,1,0:T(8,128)(2,1)S(1)} custom-call(s32[4]{0:T(128)S(1)} %pad_add_fusion.place_ref, bf16[256,512]{1,0:T(8,128)(2,1)S(1)} %shard_map.71.own_ref, bf16[256,512]{1,0:T(8,128)(2,1)S(1)} %collective-permute-done.3.other_ref, bf16[2,2,2,2,2,512,128]{6,5,4,3,2,1,0:T(8,128)(2,1)S(1)} %get-tuple-element.21.weight_ref), custom_call_target="tpu_custom_call" | custom-call | flops 1073741824 | bytes 1048576 | tf_op jit(solution)/shard_map/pallas_call | solution.py:182
  119.0 28.6 %all_to_all.21.parts_ref = bf16[8,2,2,128,256]{4,3,2,1,0:T(8,128)(2,1)S(1)} all-to-all(bf16[8,2,2,128,256]{4,3,2,1,0:T(8,128)(2,1)S(1)} %shard_map.72), channel_id=1, replica_groups=mesh['h'=2,'l'=2,'z'=8,'ylo'=2,'x'=4,'core'=2] {'ylo','x'}, dimensions={0} | all-to-all | bytes 4194304 | tf_op jit(solution)/shard_map/all_to_all | solution.py:263
  147.6 0.8 shard_map.73
  148.4 6.3 %collective-permute-start.4 = (bf16[2,128,256]{2,1,0:T(8,128)(2,1)S(1)}, bf16[2,128,256]{2,1,0:T(8,128)(2,1)S(1)}, u32[]{:S(2)}, u32[]{:S(2)}) collective-permute-start(bf16[2,128,256]{2,1,0:T(8,128)(2,1)S(1)} %get-tuple-element.23), channel_id=1, source_target_pairs={{0,256},{256,0},{1,257},{257,1},{2,258},{258,2},{3,259},{259,3},{4... | collective-permute-start | bytes 393224 | tf_op jit(solution)/shard_map/ppermute | solution.py:297
  154.8 3.4 %collective-permute-done.4.theirs_ref = bf16[2,128,256]{2,1,0:T(8,128)(2,1)S(1)} collective-permute-done((bf16[2,128,256]{2,1,0:T(8,128)(2,1)S(1)}, bf16[2,128,256]{2,1,0:T(8,128)(2,1)S(1)}, u32[]{:S(2)}, u32[]{:S(2)}) %collective-permute-start.4) | collective-permute-done | bytes 131104 | tf_op jit(solution)/shard_map/ppermute | solution.py:297
  158.2 1.2 shard_map.74
  (15 shorter events, 1.8 us)
Async XLA Ops:
  7.2 48.2 %copy-start = (f32[16,128]{1,0:T(8,128)S(1)}, f32[16,128]{1,0:T(8,128)}, u32[]{:S(2)}) copy-start(f32[16,128]{1,0:T(8,128)} %param.8) | copy-start | bytes 24580
  9.0 21.9 %all-to-all-start = ((bf16[4,512,128]{2,1,0:T(8,128)(2,1)}), bf16[4,512,128]{2,1,0:T(8,128)(2,1)S(1)}, u32[]{:S(2)}, u32[]{:S(2)}) async-start(bf16[4,512,128]{2,1,0:T(8,128)(2,1)} %shard_map.68), calls=%async_computation | async-start | bytes 1048576 | tf_op jit(solution)/shard_map/all_to_all | solution.py:263
  16.7 77.9 %all-gather.3.cloned.1.call-start = ((), (), s32[]{:S(2)}) async-start(), calls=%async_computation.4 | async-start | bytes 8912896 | tf_op jit(solution)/shard_map/all_gather | solution.py:278
  30.9 0.8 copy-start.1
  51.3 28.9 %all-to-all-start.2 = ((bf16[4,4,2,128,256]{4,3,2,1,0:T(8,128)(2,1)}), bf16[4,4,2,128,256]{4,3,2,1,0:T(8,128)(2,1)S(1)}, u32[]{:S(2)}, u32[]{:S(2)}) async-start(bf16[4,4,2,128,256]{4,3,2,1,0:T(8,128)(2,1)} %broadcast_in_dim.7), calls=%async_computation.2 | async-start | bytes 4194304 | tf_op jit(solution)/shard_map/all_to_all | solution.py:263
  80.1 8.4 %collective-permute-start = (bf16[4,2,2,2,128,256]{5,4,3,2,1,0:T(8,128)(2,1)S(1)}, bf16[4,2,2,2,128,256]{5,4,3,2,1,0:T(8,128)(2,1)}, u32[]{:S(2)}, u32[]{:S(2)}) collective-permute-start(bf16[4,2,2,2,128,256]{5,4,3,2,1,0:T(8,128)(2,1)S(1)} %bitcast.9), channel_id=1, source_target_pairs={{0,1},{1,0},{2,3},{3,2},{4,5},{5,4},{6,7},{7,6},{8,9},{9,8},{10,11... | collective-permute-start | bytes 6291464 | tf_op jit(solution)/shard_map/ppermute | solution.py:285
  99.3 11.4 %collective-permute-start.1 = (bf16[128,256]{1,0:T(8,128)(2,1)S(1)}, bf16[128,256]{1,0:T(8,128)(2,1)S(1)}, u32[]{:S(2)}, u32[]{:S(2)}) collective-permute-start(bf16[128,256]{1,0:T(8,128)(2,1)S(1)} %get-tuple-element.19.product_ref), channel_id=1, source_target_pairs={{0,16},{16,32},{32,48},{48,64},{64,80},{80,96},{96,112},{112,128},... | collective-permute-start | bytes 196616 | tf_op jit(solution)/shard_map/ppermute | solution.py:289
  101.2 10.6 %collective-permute-start.2 = (bf16[128,256]{1,0:T(8,128)(2,1)S(1)}, bf16[128,256]{1,0:T(8,128)(2,1)S(1)}, u32[]{:S(2)}, u32[]{:S(2)}) collective-permute-start(bf16[128,256]{1,0:T(8,128)(2,1)S(1)} %get-tuple-element.20.mixed_ref), channel_id=1, source_target_pairs={{16,0},{32,16},{48,32},{64,48},{80,64},{96,80},{112,96},{128,112},... | collective-permute-start | bytes 196616 | tf_op jit(solution)/shard_map/ppermute | solution.py:290
  112.9 4.3 %collective-permute-start.3 = (bf16[256,512]{1,0:T(8,128)(2,1)S(1)}, bf16[256,512]{1,0:T(8,128)(2,1)S(1)}, u32[]{:S(2)}, u32[]{:S(2)}) collective-permute-start(bf16[256,512]{1,0:T(8,128)(2,1)S(1)} %shard_map.71.own_ref), channel_id=1, source_target_pairs={{0,1},{1,0},{2,3},{3,2},{4,5},{5,4},{6,7},{7,6},{8,9},{9,8},{10,11... | collective-permute-start | bytes 786440 | tf_op jit(solution)/shard_map/ppermute | solution.py:293
  148.4 9.7 %collective-permute-start.4 = (bf16[2,128,256]{2,1,0:T(8,128)(2,1)S(1)}, bf16[2,128,256]{2,1,0:T(8,128)(2,1)S(1)}, u32[]{:S(2)}, u32[]{:S(2)}) collective-permute-start(bf16[2,128,256]{2,1,0:T(8,128)(2,1)S(1)} %get-tuple-element.23), channel_id=1, source_target_pairs={{0,256},{256,0},{1,257},{257,1},{2,258},{258,2},{3,259},{259,3},{4... | collective-permute-start | bytes 393224 | tf_op jit(solution)/shard_map/ppermute | solution.py:297
Sparse Core Ops, SparseCore 0:
  31.9 62.6 all-gather.2

commit v11 on v10

--- a/solution.py
+++ b/solution.py
@@ -5,7 +5,7 @@
 from jax.experimental.pallas import tpu as pltpu
 from jax.sharding import Mesh, PartitionSpec as P
 
-AXES = ("h", "l", "z", "ylo", "x", "core")
+AXES = ("l", "h", "z", "ylo", "x", "core")
 SIZES = (2, 2, 8, 2, 4, 2)
 ROWS = 128
 HALF = 128
@@ -50,6 +50,7 @@
     gate_ref,
     product_ref,
     mixed_ref,
+    edge_ref,
     back_ref,
     weight_ref,
     other_ref,
@@ -102,8 +103,11 @@
     streams_ref[...] = streams
     gate_ref[...] = grad_gate
     query, key, value = (streams[i * HALF : (i + 1) * HALF].astype(F32) for i in range(3))
-    product_ref[...] = (key * value).astype(BF16)
-    mixed_ref[...] = (grad_gate * query).astype(BF16)
+    product = (key * value).astype(BF16)
+    mixed = (grad_gate * query).astype(BF16)
+    product_ref[...] = product
+    mixed_ref[...] = mixed
+    edge_ref[...] = jnp.where(place_ref[1] == 7, product[:, ROWS:], mixed[:, :ROWS])
     for copy in copies[8:]:
         copy.wait()
 
@@ -118,6 +122,7 @@
             shape(HALF, F32),
             shape(HALF, BF16),
             shape(HALF, BF16),
+            jax.ShapeDtypeStruct((HALF, ROWS), BF16),
             jax.ShapeDtypeStruct((2, 2, 2, 2, 2, STREAMS, ROWS), BF16),
         ),
         in_specs=[
@@ -126,7 +131,7 @@
             pl.BlockSpec(memory_space=pl.ANY),
             pl.BlockSpec(memory_space=pl.ANY),
         ],
-        out_specs=(vmem,) * 5,
+        out_specs=(vmem,) * 6,
         scratch_shapes=[
             pltpu.VMEM((4, 2, 4, STREAMS, ROWS), BF16),
             pltpu.VMEM((4, 2, 2, 2, ROWS, FEATURES), BF16),
@@ -155,17 +160,17 @@
 
 
 def middle_kernel(
-    place_ref, band_ref, streams_ref, gate_ref, product_ref, mixed_ref, before_ref, after_ref, terms_ref
+    place_ref, band_ref, streams_ref, gate_ref, product_ref, mixed_ref, before_ref, after_ref, edge_ref, terms_ref
 ):
     first = place_ref[1] == 0
-    last = place_ref[1] == 15
+    last = place_ref[1] == 7
     lanes = [slice(s * ROWS, (s + 1) * ROWS) for s in range(2)]
     product, mixed, before, after = (
         [ref[:, lanes[s]] for s in range(2)] for ref in (product_ref, mixed_ref, before_ref, after_ref)
     )
-    zero = jnp.zeros_like(before[0])
-    earlier = [jnp.where(first, zero, before[0]), jnp.where(first, before[0], before[1])]
-    later = [jnp.where(last, after[1], after[0]), jnp.where(last, zero, after[1])]
+    edge = edge_ref[...]
+    earlier = [jnp.where(first, edge, before[0]), jnp.where(first, before[0], before[1])]
+    later = [jnp.where(last, after[1], after[0]), jnp.where(last, edge, after[1])]
     conv = filtered(earlier, product, band_ref[:, : GROUPS * ROWS])
     back = filtered(mixed, later, band_ref[:, GROUPS * ROWS :])
     for s in range(2):
@@ -236,8 +241,8 @@
         streams = [in_ref[stream, :, chans].astype(F32).T.astype(BF16) for stream in range(3)]
         for l in range(2):
             for stream in range(3):
-                packed_ref[2 * h + l, stream * HALF : (stream + 1) * HALF] = streams[stream]
-            packed_ref[2 * h + l, BACK:] = out_ref[chans]
+                packed_ref[2 * l + h, stream * HALF : (stream + 1) * HALF] = streams[stream]
+            packed_ref[2 * l + h, BACK:] = out_ref[chans]
 
 
 def packed(in_weight, out_weight):
@@ -269,10 +274,9 @@
 
 def local(tokens, in_weight, out_weight, mr_filter, cotangent):
     half, core = lax.axis_index("h"), lax.axis_index("core")
-    position = lax.axis_index(("l", "z"))
-    place = jnp.stack([core, position, lax.axis_index("x"), half]).astype(jnp.int32)
-
-    weight = swapped(packed(in_weight, out_weight), ("h", "l"))
+    place = jnp.stack([core, lax.axis_index("z"), lax.axis_index("x"), half]).astype(jnp.int32)
+
+    weight = swapped(packed(in_weight, out_weight), ("l", "h"))
     values = jnp.stack([tokens, cotangent], 0)
     weight, values = lax.optimization_barrier((weight, values))
     weight = lax.all_gather(weight, ("z", "core"), axis=0).reshape(8, 2, 4, STREAMS, ROWS)
@@ -284,12 +288,13 @@
     cross = [(0, 1), (1, 0)]
     other = lax.ppermute(values, "core", cross)
 
-    streams, gate, product, mixed, weight = forward(place, values, other, weight)
-    ring = [(n, (n + 1) % 16) for n in range(16)]
-    before = lax.ppermute(product, ("l", "z"), ring)
-    after = lax.ppermute(mixed, ("l", "z"), [(b, a) for a, b in ring])
-
-    terms = middle(place, band, streams, gate, product, mixed, before, after)
+    streams, gate, product, mixed, edge, weight = forward(place, values, other, weight)
+    ring = [(n, (n + 1) % 8) for n in range(8)]
+    before = lax.ppermute(product, "z", ring)
+    after = lax.ppermute(mixed, "z", [(b, a) for a, b in ring])
+    edge = lax.ppermute(edge, ("l", "z"), [(7, 8), (8, 7)])
+
+    terms = middle(place, band, streams, gate, product, mixed, before, after, edge)
     other_terms = lax.ppermute(terms, "core", cross)
 
     parts = swapped(backward(place, terms, other_terms, weight), ("ylo", "x"))

time: 169 us -> 173 us (1.024)
  the two profiles are of different devices: /device:TPU:1 before, /device:TPU:32 now
where the time goes in v11:
time: 173 us
  waiting for transfers between devices  63.8 us (37%)
  blocking collectives  48.7 us (28%)
  starting transfers between devices  30.6 us (18%)
  between operations  14.1 us (8%)
  Pallas kernels  11.8 us (7%)
  local copies, waits for them, and re-layouts  2.6 us (2%)
    all_to_all x2, blocking collectives, swapped(): return lax.all_to_all(value, axes, 0, 0, tiled=True)  48.7 us
    all_to_all x2, waiting for transfers between devices, swapped(): return lax.all_to_all(value, axes, 0, 0, tiled=True)  33.8 us
    all_to_all x2, starting transfers between devices, swapped(): return lax.all_to_all(value, axes, 0, 0, tiled=True)  13.3 us
    all_gather x1, waiting for transfers between devices, local(): lax.all_gather(weight, ('z', 'core'), axis=0)  9.53 us
    ppermute x1, waiting for transfers between devices, local(): edge = lax.ppermute(edge, ('l', 'z'), [(7, 8), (8, 7)])  7.65 us
    ppermute x1, waiting for transfers between devices, local(): return finish(place, mine, lax.ppermute(theirs, 'h', cross))  7.07 us
    ppermute x1, starting transfers between devices, local(): after = lax.ppermute(mixed, 'z', [(b, a) for a, b in ring])  5.13 us
    pallas_call x4, Pallas kernels, on_chip(): pl.pallas_call(kernel, out_shape=out_shape, in_specs=[smem] + [vmem] * (l...  4.86 us
  transfers between devices with their start and end apart: 9, of which 7 were waited for; matrix products, arithmetic and copies ran while one was open for 2% of the time, Pallas kernels for 0%

profile of v11, /device:TPU:32, one launch (start us, length us, event | category | flops | bytes accessed | tf_op | source)
XLA Modules:
  0.0 172.7 jit_solution(7079369870628713671)
XLA Ops:
  7.2 1.9 %shard_map.68 = bf16[4,512,128]{2,1,0:T(8,128)(2,1)} custom-call(bf16[3,128,256]{2,1,0:T(8,128)(2,1)} %in_ref.1, bf16[256,128]{1,0:T(8,128)(2,1)} %out_ref.1), custom_call_target="tpu_custom_call" | custom-call | tf_op jit(solution)/shard_map/pallas_call | solution.py:250
  9.1 8.9 %all-to-all-start = ((bf16[4,512,128]{2,1,0:T(8,128)(2,1)}), bf16[4,512,128]{2,1,0:T(8,128)(2,1)S(1)}, u32[]{:S(2)}, u32[]{:S(2)}) async-start(bf16[4,512,128]{2,1,0:T(8,128)(2,1)} %shard_map.68), calls=%async_computation | async-start | bytes 1048576 | tf_op jit(solution)/shard_map/all_to_all | solution.py:268
  18.0 0.9 pad_maximum_fusion
  18.9 9.3 %all-to-all-done = bf16[4,512,128]{2,1,0:T(8,128)(2,1)S(1)} async-done(((bf16[4,512,128]{2,1,0:T(8,128)(2,1)}), bf16[4,512,128]{2,1,0:T(8,128)(2,1)S(1)}, u32[]{:S(2)}, u32[]{:S(2)}) %all-to-all-start) | async-done | bytes 524320 | tf_op jit(solution)/shard_map/all_to_all | solution.py:268
  29.0 17.1 %all_to_all.20 = bf16[4,2,128,256]{3,2,1,0:T(8,128)(2,1)S(1)} all-to-all(bf16[4,2,128,256]{3,2,1,0:T(8,128)(2,1)S(1)} %broadcast_in_dim.6), channel_id=1, replica_groups=mesh['l'=2,'h'=2,'z'=8,'ylo'=2,'x'=4,'core'=2] {'h','ylo'}, dimensions={0} | all-to-all | bytes 1048576 | tf_op jit(solution)/shard_map/all_to_all | solution.py:268
  46.2 1.6 broadcast_in_dim.7
  47.8 4.4 %all-to-all-start.2 = ((bf16[4,4,2,128,256]{4,3,2,1,0:T(8,128)(2,1)}), bf16[4,4,2,128,256]{4,3,2,1,0:T(8,128)(2,1)S(1)}, u32[]{:S(2)}, u32[]{:S(2)}) async-start(bf16[4,4,2,128,256]{4,3,2,1,0:T(8,128)(2,1)} %broadcast_in_dim.7), calls=%async_computation.2 | async-start | bytes 4194304 | tf_op jit(solution)/shard_map/all_to_all | solution.py:268
  52.8 24.5 %all-to-all-done.2 = bf16[4,4,2,128,256]{4,3,2,1,0:T(8,128)(2,1)S(1)} async-done(((bf16[4,4,2,128,256]{4,3,2,1,0:T(8,128)(2,1)}), bf16[4,4,2,128,256]{4,3,2,1,0:T(8,128)(2,1)S(1)}, u32[]{:S(2)}, u32[]{:S(2)}) %all-to-all-start.2) | async-done | bytes 2097184 | tf_op jit(solution)/shard_map/all_to_all | solution.py:268
  77.3 1.9 %collective-permute-start = (bf16[4,2,2,2,128,256]{5,4,3,2,1,0:T(8,128)(2,1)S(1)}, bf16[4,2,2,2,128,256]{5,4,3,2,1,0:T(8,128)(2,1)}, u32[]{:S(2)}, u32[]{:S(2)}) collective-permute-start(bf16[4,2,2,2,128,256]{5,4,3,2,1,0:T(8,128)(2,1)S(1)} %bitcast.9), channel_id=1, source_target_pairs={{0,1},{1,0},{2,3},{3,2},{4,5},{5,4},{6,7},{7,6},{8,9},{9,8},{10,11... | collective-permute-start | bytes 6291464 | tf_op jit(solution)/shard_map/ppermute | solution.py:289
  79.3 4.2 %collective-permute-done.other_hbm = bf16[4,2,2,2,128,256]{5,4,3,2,1,0:T(8,128)(2,1)} collective-permute-done((bf16[4,2,2,2,128,256]{5,4,3,2,1,0:T(8,128)(2,1)S(1)}, bf16[4,2,2,2,128,256]{5,4,3,2,1,0:T(8,128)(2,1)}, u32[]{:S(2)}, u32[]{:S(2)}) %collective-permute-start) | collective-permute-done | bytes 2097184 | tf_op jit(solution)/shard_map/ppermute | solution.py:289
  83.5 9.5 %all-gather.3.cloned.1.call-done = bf16[64,512,128]{2,1,0:T(8,128)(2,1)} async-done(((bf16[4,512,128]{2,1,0:T(8,128)(2,1)}), bf16[64,512,128]{2,1,0:T(8,128)(2,1)}) %all-gather.3.cloned.1.call-update) | async-done | bytes 8388624 | tf_op jit(solution)/shard_map/all_gather | solution.py:282
  93.0 4.7 %shard_map.70 = (bf16[384,256]{1,0:T(8,128)(2,1)S(1)}, f32[128,256]{1,0:T(8,128)S(1)}, bf16[128,256]{1,0:T(8,128)(2,1)S(1)}, bf16[128,256]{1,0:T(8,128)(2,1)S(1)...) custom-call(s32[4]{0:T(128)S(1)} %pad_add_fusion.place_ref, ...), custom_call_target="tpu_custom_call" | custom-call | flops 1073741824 | bytes 9437184 | tf_op jit(solution)/shard_map/pallas_call | solution.py:118
  97.7 1.9 %collective-permute-start.1 = (bf16[128,256]{1,0:T(8,128)(2,1)S(1)}, bf16[128,256]{1,0:T(8,128)(2,1)S(1)}, u32[]{:S(2)}, u32[]{:S(2)}) collective-permute-start(bf16[128,256]{1,0:T(8,128)(2,1)S(1)} %get-tuple-element.20.product_ref), channel_id=1, source_target_pairs={{0,16},{16,32},{32,48},{48,64},{64,80},{80,96},{96,112},{112,0},{1... | collective-permute-start | bytes 196616 | tf_op jit(solution)/shard_map/ppermute | solution.py:293
  99.6 5.1 %collective-permute-start.2 = (bf16[128,256]{1,0:T(8,128)(2,1)S(1)}, bf16[128,256]{1,0:T(8,128)(2,1)S(1)}, u32[]{:S(2)}, u32[]{:S(2)}) collective-permute-start(bf16[128,256]{1,0:T(8,128)(2,1)S(1)} %get-tuple-element.21.mixed_ref), channel_id=1, source_target_pairs={{16,0},{32,16},{48,32},{64,48},{80,64},{96,80},{112,96},{0,112},{1... | collective-permute-start | bytes 196616 | tf_op jit(solution)/shard_map/ppermute | solution.py:294
  104.8 4.2 %collective-permute-start.3 = (bf16[128,128]{1,0:T(8,128)(2,1)S(1)}, bf16[128,128]{1,0:T(8,128)(2,1)S(1)}, u32[]{:S(2)}, u32[]{:S(2)}) collective-permute-start(bf16[128,128]{1,0:T(8,128)(2,1)S(1)} %get-tuple-element.22), channel_id=1, source_target_pairs={{112,256},{256,112},{113,257},{257,113},{114,258},{258,114},{115,2... | collective-permute-start | bytes 98312 | tf_op jit(solution)/shard_map/ppermute | solution.py:295
  108.9 7.6 %collective-permute-done.3.edge_ref = bf16[128,128]{1,0:T(8,128)(2,1)S(1)} collective-permute-done((bf16[128,128]{1,0:T(8,128)(2,1)S(1)}, bf16[128,128]{1,0:T(8,128)(2,1)S(1)}, u32[]{:S(2)}, u32[]{:S(2)}) %collective-permute-start.3) | collective-permute-done | bytes 32800 | tf_op jit(solution)/shard_map/ppermute | solution.py:295
  116.6 1.1 shard_map.71.own_ref
  117.7 1.9 %collective-permute-start.4 = (bf16[256,512]{1,0:T(8,128)(2,1)S(1)}, bf16[256,512]{1,0:T(8,128)(2,1)S(1)}, u32[]{:S(2)}, u32[]{:S(2)}) collective-permute-start(bf16[256,512]{1,0:T(8,128)(2,1)S(1)} %shard_map.71.own_ref), channel_id=1, source_target_pairs={{0,1},{1,0},{2,3},{3,2},{4,5},{5,4},{6,7},{7,6},{8,9},{9,8},{10,11... | collective-permute-start | bytes 786440 | tf_op jit(solution)/shard_map/ppermute | solution.py:298
  119.6 1.5 collective-permute-done.4.other_ref
  121.1 1.8 %shard_map.72 = bf16[8,2,2,128,256]{4,3,2,1,0:T(8,128)(2,1)S(1)} custom-call(s32[4]{0:T(128)S(1)} %pad_add_fusion.place_ref, bf16[256,512]{1,0:T(8,128)(2,1)S(1)} %shard_map.71.own_ref, bf16[256,512]{1,0:T(8,128)(2,1)S(1)} %collective-permute-done.4.other_ref, bf16[2,2,2,2,2,512,128]{6,5,4,3,2,1,0:T(8,128)(2,1)S(1)} %get-tuple-element.23.weight_ref), custom_call_target="tpu_custom_call" | custom-call | flops 1073741824 | bytes 1048576 | tf_op jit(solution)/shard_map/pallas_call | solution.py:187
  122.9 31.6 %all_to_all.21.parts_ref = bf16[8,2,2,128,256]{4,3,2,1,0:T(8,128)(2,1)S(1)} all-to-all(bf16[8,2,2,128,256]{4,3,2,1,0:T(8,128)(2,1)S(1)} %shard_map.72), channel_id=1, replica_groups=mesh['l'=2,'h'=2,'z'=8,'ylo'=2,'x'=4,'core'=2] {'ylo','x'}, dimensions={0} | all-to-all | bytes 4194304 | tf_op jit(solution)/shard_map/all_to_all | solution.py:268
  155.3 2.3 %collective-permute-start.5 = (bf16[2,128,256]{2,1,0:T(8,128)(2,1)S(1)}, bf16[2,128,256]{2,1,0:T(8,128)(2,1)S(1)}, u32[]{:S(2)}, u32[]{:S(2)}) collective-permute-start(bf16[2,128,256]{2,1,0:T(8,128)(2,1)S(1)} %get-tuple-element.25), channel_id=1, source_target_pairs={{0,128},{128,0},{1,129},{129,1},{2,130},{130,2},{3,131},{131,3},{4... | collective-permute-start | bytes 393224 | tf_op jit(solution)/shard_map/ppermute | solution.py:302
  157.6 7.1 %collective-permute-done.5.theirs_ref = bf16[2,128,256]{2,1,0:T(8,128)(2,1)S(1)} collective-permute-done((bf16[2,128,256]{2,1,0:T(8,128)(2,1)S(1)}, bf16[2,128,256]{2,1,0:T(8,128)(2,1)S(1)}, u32[]{:S(2)}, u32[]{:S(2)}) %collective-permute-start.5) | collective-permute-done | bytes 131104 | tf_op jit(solution)/shard_map/ppermute | solution.py:302
  164.7 1.2 shard_map.74
  (17 shorter events, 2.3 us)
Async XLA Ops:
  7.2 45.0 %copy-start = (f32[16,128]{1,0:T(8,128)S(1)}, f32[16,128]{1,0:T(8,128)}, u32[]{:S(2)}) copy-start(f32[16,128]{1,0:T(8,128)} %param.8) | copy-start | bytes 24580
  9.1 19.1 %all-to-all-start = ((bf16[4,512,128]{2,1,0:T(8,128)(2,1)}), bf16[4,512,128]{2,1,0:T(8,128)(2,1)S(1)}, u32[]{:S(2)}, u32[]{:S(2)}) async-start(bf16[4,512,128]{2,1,0:T(8,128)(2,1)} %shard_map.68), calls=%async_computation | async-start | bytes 1048576 | tf_op jit(solution)/shard_map/all_to_all | solution.py:268
  18.0 75.0 %all-gather.3.cloned.1.call-start = ((), (), s32[]{:S(2)}) async-start(), calls=%async_computation.4 | async-start | bytes 8912896 | tf_op jit(solution)/shard_map/all_gather | solution.py:282
  28.2 0.8 copy-start.1
  47.8 29.5 %all-to-all-start.2 = ((bf16[4,4,2,128,256]{4,3,2,1,0:T(8,128)(2,1)}), bf16[4,4,2,128,256]{4,3,2,1,0:T(8,128)(2,1)S(1)}, u32[]{:S(2)}, u32[]{:S(2)}) async-start(bf16[4,4,2,128,256]{4,3,2,1,0:T(8,128)(2,1)} %broadcast_in_dim.7), calls=%async_computation.2 | async-start | bytes 4194304 | tf_op jit(solution)/shard_map/all_to_all | solution.py:268
  77.3 6.2 %collective-permute-start = (bf16[4,2,2,2,128,256]{5,4,3,2,1,0:T(8,128)(2,1)S(1)}, bf16[4,2,2,2,128,256]{5,4,3,2,1,0:T(8,128)(2,1)}, u32[]{:S(2)}, u32[]{:S(2)}) collective-permute-start(bf16[4,2,2,2,128,256]{5,4,3,2,1,0:T(8,128)(2,1)S(1)} %bitcast.9), channel_id=1, source_target_pairs={{0,1},{1,0},{2,3},{3,2},{4,5},{5,4},{6,7},{7,6},{8,9},{9,8},{10,11... | collective-permute-start | bytes 6291464 | tf_op jit(solution)/shard_map/ppermute | solution.py:289
  97.7 18.9 %collective-permute-start.1 = (bf16[128,256]{1,0:T(8,128)(2,1)S(1)}, bf16[128,256]{1,0:T(8,128)(2,1)S(1)}, u32[]{:S(2)}, u32[]{:S(2)}) collective-permute-start(bf16[128,256]{1,0:T(8,128)(2,1)S(1)} %get-tuple-element.20.product_ref), channel_id=1, source_target_pairs={{0,16},{16,32},{32,48},{48,64},{64,80},{80,96},{96,112},{112,0},{1... | collective-permute-start | bytes 196616 | tf_op jit(solution)/shard_map/ppermute | solution.py:293
  99.6 17.0 %collective-permute-start.2 = (bf16[128,256]{1,0:T(8,128)(2,1)S(1)}, bf16[128,256]{1,0:T(8,128)(2,1)S(1)}, u32[]{:S(2)}, u32[]{:S(2)}) collective-permute-start(bf16[128,256]{1,0:T(8,128)(2,1)S(1)} %get-tuple-element.21.mixed_ref), channel_id=1, source_target_pairs={{16,0},{32,16},{48,32},{64,48},{80,64},{96,80},{112,96},{0,112},{1... | collective-permute-start | bytes 196616 | tf_op jit(solution)/shard_map/ppermute | solution.py:294
  104.8 11.8 %collective-permute-start.3 = (bf16[128,128]{1,0:T(8,128)(2,1)S(1)}, bf16[128,128]{1,0:T(8,128)(2,1)S(1)}, u32[]{:S(2)}, u32[]{:S(2)}) collective-permute-start(bf16[128,128]{1,0:T(8,128)(2,1)S(1)} %get-tuple-element.22), channel_id=1, source_target_pairs={{112,256},{256,112},{113,257},{257,113},{114,258},{258,114},{115,2... | collective-permute-start | bytes 98312 | tf_op jit(solution)/shard_map/ppermute | solution.py:295
  117.7 3.4 %collective-permute-start.4 = (bf16[256,512]{1,0:T(8,128)(2,1)S(1)}, bf16[256,512]{1,0:T(8,128)(2,1)S(1)}, u32[]{:S(2)}, u32[]{:S(2)}) collective-permute-start(bf16[256,512]{1,0:T(8,128)(2,1)S(1)} %shard_map.71.own_ref), channel_id=1, source_target_pairs={{0,1},{1,0},{2,3},{3,2},{4,5},{5,4},{6,7},{7,6},{8,9},{9,8},{10,11... | collective-permute-start | bytes 786440 | tf_op jit(solution)/shard_map/ppermute | solution.py:298
  155.3 9.3 %collective-permute-start.5 = (bf16[2,128,256]{2,1,0:T(8,128)(2,1)S(1)}, bf16[2,128,256]{2,1,0:T(8,128)(2,1)S(1)}, u32[]{:S(2)}, u32[]{:S(2)}) collective-permute-start(bf16[2,128,256]{2,1,0:T(8,128)(2,1)S(1)} %get-tuple-element.25), channel_id=1, source_target_pairs={{0,128},{128,0},{1,129},{129,1},{2,130},{130,2},{3,131},{131,3},{4... | collective-permute-start | bytes 393224 | tf_op jit(solution)/shard_map/ppermute | solution.py:302
Sparse Core Ops, SparseCore 0:
  29.1 63.8 all-gather.2

commit v12 on v11

--- a/solution.py
+++ b/solution.py
@@ -107,7 +107,7 @@
     mixed = (grad_gate * query).astype(BF16)
     product_ref[...] = product
     mixed_ref[...] = mixed
-    edge_ref[...] = jnp.where(place_ref[1] == 7, product[:, ROWS:], mixed[:, :ROWS])
+    edge_ref[...] = jnp.where(place_ref[1] == 7, product, mixed)
     for copy in copies[8:]:
         copy.wait()
 
@@ -122,7 +122,7 @@
             shape(HALF, F32),
             shape(HALF, BF16),
             shape(HALF, BF16),
-            jax.ShapeDtypeStruct((HALF, ROWS), BF16),
+            shape(HALF, BF16),
             jax.ShapeDtypeStruct((2, 2, 2, 2, 2, STREAMS, ROWS), BF16),
         ),
         in_specs=[
@@ -168,9 +168,9 @@
     product, mixed, before, after = (
         [ref[:, lanes[s]] for s in range(2)] for ref in (product_ref, mixed_ref, before_ref, after_ref)
     )
-    edge = edge_ref[...]
-    earlier = [jnp.where(first, edge, before[0]), jnp.where(first, before[0], before[1])]
-    later = [jnp.where(last, after[1], after[0]), jnp.where(last, edge, after[1])]
+    edge = [edge_ref[:, lanes[s]] for s in range(2)]
+    earlier = [jnp.where(first, edge[1], before[0]), jnp.where(first, before[0], before[1])]
+    later = [jnp.where(last, after[1], after[0]), jnp.where(last, edge[0], after[1])]
     conv = filtered(earlier, product, band_ref[:, : GROUPS * ROWS])
     back = filtered(mixed, later, band_ref[:, GROUPS * ROWS :])
     for s in range(2):
@@ -290,9 +290,9 @@
 
     streams, gate, product, mixed, edge, weight = forward(place, values, other, weight)
     ring = [(n, (n + 1) % 8) for n in range(8)]
+    edge = lax.ppermute(edge, ("l", "z"), [(7, 8), (8, 7)])
     before = lax.ppermute(product, "z", ring)
     after = lax.ppermute(mixed, "z", [(b, a) for a, b in ring])
-    edge = lax.ppermute(edge, ("l", "z"), [(7, 8), (8, 7)])
 
     terms = middle(place, band, streams, gate, product, mixed, before, after, edge)
     other_terms = lax.ppermute(terms, "core", cross)

time: 173 us -> 170 us (0.983)
  the two profiles are of different devices: /device:TPU:32 before, /device:TPU:1 now
where the time goes in v12:
time: 170 us; the launch traced here: 169 us
  waiting for transfers between devices  56.6 us (33%)
  blocking collectives  47.6 us (28%)
  starting transfers between devices  35.6 us (21%)
  between operations  14.2 us (8%)
  Pallas kernels  11.8 us (7%)
  local copies, waits for them, and re-layouts  2.6 us (2%)
    all_to_all x2, blocking collectives, swapped(): return lax.all_to_all(value, axes, 0, 0, tiled=True)  47.6 us
    all_to_all x2, waiting for transfers between devices, swapped(): return lax.all_to_all(value, axes, 0, 0, tiled=True)  36.9 us
    all_to_all x2, starting transfers between devices, swapped(): return lax.all_to_all(value, axes, 0, 0, tiled=True)  11.7 us
    ppermute x1, starting transfers between devices, local(): after = lax.ppermute(mixed, 'z', [(b, a) for a, b in ring])  10.7 us
    ppermute x1, waiting for transfers between devices, local(): return finish(place, mine, lax.ppermute(theirs, 'h', cross))  7.6 us
    all_gather x1, waiting for transfers between devices, local(): lax.all_gather(weight, ('z', 'core'), axis=0)  5.83 us
    ppermute x1, starting transfers between devices, local(): other = lax.ppermute(values, 'core', cross)  5.01 us
    pallas_call x4, Pallas kernels, on_chip(): pl.pallas_call(kernel, out_shape=out_shape, in_specs=[smem] + [vmem] * (l...  4.86 us
  transfers between devices with their start and end apart: 9, of which 7 were waited for; matrix products, arithmetic and copies ran while one was open for 2% of the time, Pallas kernels for 0%

profile of v12, /device:TPU:1, one launch (start us, length us, event | category | flops | bytes accessed | tf_op | source)
XLA Modules:
  0.0 169.4 jit_solution(15885103721633562454)
XLA Ops:
  7.2 1.9 %shard_map.68 = bf16[4,512,128]{2,1,0:T(8,128)(2,1)} custom-call(bf16[3,128,256]{2,1,0:T(8,128)(2,1)} %in_ref.1, bf16[256,128]{1,0:T(8,128)(2,1)} %out_ref.1), custom_call_target="tpu_custom_call" | custom-call | tf_op jit(solution)/shard_map/pallas_call | solution.py:250
  9.1 7.6 %all-to-all-start = ((bf16[4,512,128]{2,1,0:T(8,128)(2,1)}), bf16[4,512,128]{2,1,0:T(8,128)(2,1)S(1)}, u32[]{:S(2)}, u32[]{:S(2)}) async-start(bf16[4,512,128]{2,1,0:T(8,128)(2,1)} %shard_map.68), calls=%async_computation | async-start | bytes 1048576 | tf_op jit(solution)/shard_map/all_to_all | solution.py:268
  16.7 0.9 pad_maximum_fusion
  17.6 13.3 %all-to-all-done = bf16[4,512,128]{2,1,0:T(8,128)(2,1)S(1)} async-done(((bf16[4,512,128]{2,1,0:T(8,128)(2,1)}), bf16[4,512,128]{2,1,0:T(8,128)(2,1)S(1)}, u32[]{:S(2)}, u32[]{:S(2)}) %all-to-all-start) | async-done | bytes 524320 | tf_op jit(solution)/shard_map/all_to_all | solution.py:268
  31.8 18.2 %all_to_all.20 = bf16[4,2,128,256]{3,2,1,0:T(8,128)(2,1)S(1)} all-to-all(bf16[4,2,128,256]{3,2,1,0:T(8,128)(2,1)S(1)} %broadcast_in_dim.6), channel_id=1, replica_groups=mesh['l'=2,'h'=2,'z'=8,'ylo'=2,'x'=4,'core'=2] {'h','ylo'}, dimensions={0} | all-to-all | bytes 1048576 | tf_op jit(solution)/shard_map/all_to_all | solution.py:268
  50.0 1.6 broadcast_in_dim.7
  51.6 4.1 %all-to-all-start.2 = ((bf16[4,4,2,128,256]{4,3,2,1,0:T(8,128)(2,1)}), bf16[4,4,2,128,256]{4,3,2,1,0:T(8,128)(2,1)S(1)}, u32[]{:S(2)}, u32[]{:S(2)}) async-start(bf16[4,4,2,128,256]{4,3,2,1,0:T(8,128)(2,1)} %broadcast_in_dim.7), calls=%async_computation.2 | async-start | bytes 4194304 | tf_op jit(solution)/shard_map/all_to_all | solution.py:268
  56.3 23.6 %all-to-all-done.2 = bf16[4,4,2,128,256]{4,3,2,1,0:T(8,128)(2,1)S(1)} async-done(((bf16[4,4,2,128,256]{4,3,2,1,0:T(8,128)(2,1)}), bf16[4,4,2,128,256]{4,3,2,1,0:T(8,128)(2,1)S(1)}, u32[]{:S(2)}, u32[]{:S(2)}) %all-to-all-start.2) | async-done | bytes 2097184 | tf_op jit(solution)/shard_map/all_to_all | solution.py:268
  79.9 5.0 %collective-permute-start = (bf16[4,2,2,2,128,256]{5,4,3,2,1,0:T(8,128)(2,1)S(1)}, bf16[4,2,2,2,128,256]{5,4,3,2,1,0:T(8,128)(2,1)}, u32[]{:S(2)}, u32[]{:S(2)}) collective-permute-start(bf16[4,2,2,2,128,256]{5,4,3,2,1,0:T(8,128)(2,1)S(1)} %bitcast.9), channel_id=1, source_target_pairs={{0,1},{1,0},{2,3},{3,2},{4,5},{5,4},{6,7},{7,6},{8,9},{9,8},{10,11... | collective-permute-start | bytes 6291464 | tf_op jit(solution)/shard_map/ppermute | solution.py:289
  85.0 3.8 %collective-permute-done.other_hbm = bf16[4,2,2,2,128,256]{5,4,3,2,1,0:T(8,128)(2,1)} collective-permute-done((bf16[4,2,2,2,128,256]{5,4,3,2,1,0:T(8,128)(2,1)S(1)}, bf16[4,2,2,2,128,256]{5,4,3,2,1,0:T(8,128)(2,1)}, u32[]{:S(2)}, u32[]{:S(2)}) %collective-permute-start) | collective-permute-done | bytes 2097184 | tf_op jit(solution)/shard_map/ppermute | solution.py:289
  88.8 5.8 %all-gather.3.cloned.1.call-done = bf16[64,512,128]{2,1,0:T(8,128)(2,1)} async-done(((bf16[4,512,128]{2,1,0:T(8,128)(2,1)}), bf16[64,512,128]{2,1,0:T(8,128)(2,1)}) %all-gather.3.cloned.1.call-update) | async-done | bytes 8388624 | tf_op jit(solution)/shard_map/all_gather | solution.py:282
  94.6 4.7 %shard_map.70 = (bf16[384,256]{1,0:T(8,128)(2,1)S(1)}, f32[128,256]{1,0:T(8,128)S(1)}, bf16[128,256]{1,0:T(8,128)(2,1)S(1)}, bf16[128,256]{1,0:T(8,128)(2,1)S(1)...) custom-call(s32[4]{0:T(128)S(1)} %pad_add_fusion.place_ref, ...), custom_call_target="tpu_custom_call" | custom-call | flops 1073741824 | bytes 9437184 | tf_op jit(solution)/shard_map/pallas_call | solution.py:118
  100.0 1.9 %collective-permute-start.1 = (bf16[128,256]{1,0:T(8,128)(2,1)S(1)}, bf16[128,256]{1,0:T(8,128)(2,1)S(1)}, u32[]{:S(2)}, u32[]{:S(2)}) collective-permute-start(bf16[128,256]{1,0:T(8,128)(2,1)S(1)} %get-tuple-element.20.product_ref), channel_id=1, source_target_pairs={{0,16},{16,32},{32,48},{48,64},{64,80},{80,96},{96,112},{112,0},{1... | collective-permute-start | bytes 196616 | tf_op jit(solution)/shard_map/ppermute | solution.py:294
  101.9 10.7 %collective-permute-start.2 = (bf16[128,256]{1,0:T(8,128)(2,1)S(1)}, bf16[128,256]{1,0:T(8,128)(2,1)S(1)}, u32[]{:S(2)}, u32[]{:S(2)}) collective-permute-start(bf16[128,256]{1,0:T(8,128)(2,1)S(1)} %get-tuple-element.21.mixed_ref), channel_id=1, source_target_pairs={{16,0},{32,16},{48,32},{64,48},{80,64},{96,80},{112,96},{0,112},{1... | collective-permute-start | bytes 196616 | tf_op jit(solution)/shard_map/ppermute | solution.py:295
  112.7 1.3 collective-permute-done.2.after_ref
  114.0 1.0 shard_map.71.own_ref
  115.0 3.3 %collective-permute-start.4 = (bf16[256,512]{1,0:T(8,128)(2,1)S(1)}, bf16[256,512]{1,0:T(8,128)(2,1)S(1)}, u32[]{:S(2)}, u32[]{:S(2)}) collective-permute-start(bf16[256,512]{1,0:T(8,128)(2,1)S(1)} %shard_map.71.own_ref), channel_id=1, source_target_pairs={{0,1},{1,0},{2,3},{3,2},{4,5},{5,4},{6,7},{7,6},{8,9},{9,8},{10,11... | collective-permute-start | bytes 786440 | tf_op jit(solution)/shard_map/ppermute | solution.py:298
  118.3 1.1 collective-permute-done.4.other_ref
  119.5 1.8 %shard_map.72 = bf16[8,2,2,128,256]{4,3,2,1,0:T(8,128)(2,1)S(1)} custom-call(s32[4]{0:T(128)S(1)} %pad_add_fusion.place_ref, bf16[256,512]{1,0:T(8,128)(2,1)S(1)} %shard_map.71.own_ref, bf16[256,512]{1,0:T(8,128)(2,1)S(1)} %collective-permute-done.4.other_ref, bf16[2,2,2,2,2,512,128]{6,5,4,3,2,1,0:T(8,128)(2,1)S(1)} %get-tuple-element.23.weight_ref), custom_call_target="tpu_custom_call" | custom-call | flops 1073741824 | bytes 1048576 | tf_op jit(solution)/shard_map/pallas_call | solution.py:187
  121.3 29.5 %all_to_all.21.parts_ref = bf16[8,2,2,128,256]{4,3,2,1,0:T(8,128)(2,1)S(1)} all-to-all(bf16[8,2,2,128,256]{4,3,2,1,0:T(8,128)(2,1)S(1)} %shard_map.72), channel_id=1, replica_groups=mesh['l'=2,'h'=2,'z'=8,'ylo'=2,'x'=4,'core'=2] {'ylo','x'}, dimensions={0} | all-to-all | bytes 4194304 | tf_op jit(solution)/shard_map/all_to_all | solution.py:268
  150.7 0.8 shard_map.73
  151.5 2.2 %collective-permute-start.5 = (bf16[2,128,256]{2,1,0:T(8,128)(2,1)S(1)}, bf16[2,128,256]{2,1,0:T(8,128)(2,1)S(1)}, u32[]{:S(2)}, u32[]{:S(2)}) collective-permute-start(bf16[2,128,256]{2,1,0:T(8,128)(2,1)S(1)} %get-tuple-element.25), channel_id=1, source_target_pairs={{0,128},{128,0},{1,129},{129,1},{2,130},{130,2},{3,131},{131,3},{4... | collective-permute-start | bytes 393224 | tf_op jit(solution)/shard_map/ppermute | solution.py:302
  153.8 7.6 %collective-permute-done.5.theirs_ref = bf16[2,128,256]{2,1,0:T(8,128)(2,1)S(1)} collective-permute-done((bf16[2,128,256]{2,1,0:T(8,128)(2,1)S(1)}, bf16[2,128,256]{2,1,0:T(8,128)(2,1)S(1)}, u32[]{:S(2)}, u32[]{:S(2)}) %collective-permute-start.5) | collective-permute-done | bytes 131104 | tf_op jit(solution)/shard_map/ppermute | solution.py:302
  161.4 1.2 shard_map.74
  (17 shorter events, 2.2 us)
Async XLA Ops:
  7.2 48.5 %copy-start = (f32[16,128]{1,0:T(8,128)S(1)}, f32[16,128]{1,0:T(8,128)}, u32[]{:S(2)}) copy-start(f32[16,128]{1,0:T(8,128)} %param.8) | copy-start | bytes 24580
  9.1 21.9 %all-to-all-start = ((bf16[4,512,128]{2,1,0:T(8,128)(2,1)}), bf16[4,512,128]{2,1,0:T(8,128)(2,1)S(1)}, u32[]{:S(2)}, u32[]{:S(2)}) async-start(bf16[4,512,128]{2,1,0:T(8,128)(2,1)} %shard_map.68), calls=%async_computation | async-start | bytes 1048576 | tf_op jit(solution)/shard_map/all_to_all | solution.py:268
  16.7 77.9 %all-gather.3.cloned.1.call-start = ((), (), s32[]{:S(2)}) async-start(), calls=%async_computation.4 | async-start | bytes 8912896 | tf_op jit(solution)/shard_map/all_gather | solution.py:282
  30.9 0.8 copy-start.1
  51.6 28.3 %all-to-all-start.2 = ((bf16[4,4,2,128,256]{4,3,2,1,0:T(8,128)(2,1)}), bf16[4,4,2,128,256]{4,3,2,1,0:T(8,128)(2,1)S(1)}, u32[]{:S(2)}, u32[]{:S(2)}) async-start(bf16[4,4,2,128,256]{4,3,2,1,0:T(8,128)(2,1)} %broadcast_in_dim.7), calls=%async_computation.2 | async-start | bytes 4194304 | tf_op jit(solution)/shard_map/all_to_all | solution.py:268
  79.9 8.9 %collective-permute-start = (bf16[4,2,2,2,128,256]{5,4,3,2,1,0:T(8,128)(2,1)S(1)}, bf16[4,2,2,2,128,256]{5,4,3,2,1,0:T(8,128)(2,1)}, u32[]{:S(2)}, u32[]{:S(2)}) collective-permute-start(bf16[4,2,2,2,128,256]{5,4,3,2,1,0:T(8,128)(2,1)S(1)} %bitcast.9), channel_id=1, source_target_pairs={{0,1},{1,0},{2,3},{3,2},{4,5},{5,4},{6,7},{7,6},{8,9},{9,8},{10,11... | collective-permute-start | bytes 6291464 | tf_op jit(solution)/shard_map/ppermute | solution.py:289
  99.3 13.3 %collective-permute-start.3 = (bf16[128,256]{1,0:T(8,128)(2,1)S(1)}, bf16[128,256]{1,0:T(8,128)(2,1)S(1)}, u32[]{:S(2)}, u32[]{:S(2)}) collective-permute-start(bf16[128,256]{1,0:T(8,128)(2,1)S(1)} %get-tuple-element.22), channel_id=1, source_target_pairs={{112,256},{256,112},{113,257},{257,113},{114,258},{258,114},{115,2... | collective-permute-start | bytes 196616 | tf_op jit(solution)/shard_map/ppermute | solution.py:293
  100.0 12.7 %collective-permute-start.1 = (bf16[128,256]{1,0:T(8,128)(2,1)S(1)}, bf16[128,256]{1,0:T(8,128)(2,1)S(1)}, u32[]{:S(2)}, u32[]{:S(2)}) collective-permute-start(bf16[128,256]{1,0:T(8,128)(2,1)S(1)} %get-tuple-element.20.product_ref), channel_id=1, source_target_pairs={{0,16},{16,32},{32,48},{48,64},{64,80},{80,96},{96,112},{112,0},{1... | collective-permute-start | bytes 196616 | tf_op jit(solution)/shard_map/ppermute | solution.py:294
  101.9 12.0 %collective-permute-start.2 = (bf16[128,256]{1,0:T(8,128)(2,1)S(1)}, bf16[128,256]{1,0:T(8,128)(2,1)S(1)}, u32[]{:S(2)}, u32[]{:S(2)}) collective-permute-start(bf16[128,256]{1,0:T(8,128)(2,1)S(1)} %get-tuple-element.21.mixed_ref), channel_id=1, source_target_pairs={{16,0},{32,16},{48,32},{64,48},{80,64},{96,80},{112,96},{0,112},{1... | collective-permute-start | bytes 196616 | tf_op jit(solution)/shard_map/ppermute | solution.py:295
  115.0 4.4 %collective-permute-start.4 = (bf16[256,512]{1,0:T(8,128)(2,1)S(1)}, bf16[256,512]{1,0:T(8,128)(2,1)S(1)}, u32[]{:S(2)}, u32[]{:S(2)}) collective-permute-start(bf16[256,512]{1,0:T(8,128)(2,1)S(1)} %shard_map.71.own_ref), channel_id=1, source_target_pairs={{0,1},{1,0},{2,3},{3,2},{4,5},{5,4},{6,7},{7,6},{8,9},{9,8},{10,11... | collective-permute-start | bytes 786440 | tf_op jit(solution)/shard_map/ppermute | solution.py:298
  151.5 9.8 %collective-permute-start.5 = (bf16[2,128,256]{2,1,0:T(8,128)(2,1)S(1)}, bf16[2,128,256]{2,1,0:T(8,128)(2,1)S(1)}, u32[]{:S(2)}, u32[]{:S(2)}) collective-permute-start(bf16[2,128,256]{2,1,0:T(8,128)(2,1)S(1)} %get-tuple-element.25), channel_id=1, source_target_pairs={{0,128},{128,0},{1,129},{129,1},{2,130},{130,2},{3,131},{131,3},{4... | collective-permute-start | bytes 393224 | tf_op jit(solution)/shard_map/ppermute | solution.py:302
Sparse Core Ops, SparseCore 0:
  31.9 62.6 all-gather.2

commit v13 on v10

--- a/solution.py
+++ b/solution.py
@@ -50,6 +50,7 @@
     gate_ref,
     product_ref,
     mixed_ref,
+    edge_ref,
     back_ref,
     weight_ref,
     other_ref,
@@ -102,8 +103,11 @@
     streams_ref[...] = streams
     gate_ref[...] = grad_gate
     query, key, value = (streams[i * HALF : (i + 1) * HALF].astype(F32) for i in range(3))
-    product_ref[...] = (key * value).astype(BF16)
-    mixed_ref[...] = (grad_gate * query).astype(BF16)
+    product = (key * value).astype(BF16)
+    mixed = (grad_gate * query).astype(BF16)
+    product_ref[...] = product
+    mixed_ref[...] = mixed
+    edge_ref[...] = jnp.where(lax.rem(place_ref[1], 8) == 7, product, mixed)
     for copy in copies[8:]:
         copy.wait()
 
@@ -118,6 +122,7 @@
             shape(HALF, F32),
             shape(HALF, BF16),
             shape(HALF, BF16),
+            shape(HALF, BF16),
             jax.ShapeDtypeStruct((2, 2, 2, 2, 2, STREAMS, ROWS), BF16),
         ),
         in_specs=[
@@ -126,7 +131,7 @@
             pl.BlockSpec(memory_space=pl.ANY),
             pl.BlockSpec(memory_space=pl.ANY),
         ],
-        out_specs=(vmem,) * 5,
+        out_specs=(vmem,) * 6,
         scratch_shapes=[
             pltpu.VMEM((4, 2, 4, STREAMS, ROWS), BF16),
             pltpu.VMEM((4, 2, 2, 2, ROWS, FEATURES), BF16),
@@ -155,14 +160,18 @@
 
 
 def middle_kernel(
-    place_ref, band_ref, streams_ref, gate_ref, product_ref, mixed_ref, before_ref, after_ref, terms_ref
+    place_ref, band_ref, streams_ref, gate_ref, product_ref, mixed_ref, before_ref, after_ref, edge_ref, terms_ref
 ):
     first = place_ref[1] == 0
     last = place_ref[1] == 15
     lanes = [slice(s * ROWS, (s + 1) * ROWS) for s in range(2)]
-    product, mixed, before, after = (
-        [ref[:, lanes[s]] for s in range(2)] for ref in (product_ref, mixed_ref, before_ref, after_ref)
+    product, mixed, before, after, edge = (
+        [ref[:, lanes[s]] for s in range(2)]
+        for ref in (product_ref, mixed_ref, before_ref, after_ref, edge_ref)
     )
+    z = lax.rem(place_ref[1], 8)
+    before = [jnp.where(z == 0, edge[s], before[s]) for s in range(2)]
+    after = [jnp.where(z == 7, edge[s], after[s]) for s in range(2)]
     zero = jnp.zeros_like(before[0])
     earlier = [jnp.where(first, zero, before[0]), jnp.where(first, before[0], before[1])]
     later = [jnp.where(last, after[1], after[0]), jnp.where(last, zero, after[1])]
@@ -284,12 +293,12 @@
     cross = [(0, 1), (1, 0)]
     other = lax.ppermute(values, "core", cross)
 
-    streams, gate, product, mixed, weight = forward(place, values, other, weight)
-    ring = [(n, (n + 1) % 16) for n in range(16)]
-    before = lax.ppermute(product, ("l", "z"), ring)
-    after = lax.ppermute(mixed, ("l", "z"), [(b, a) for a, b in ring])
-
-    terms = middle(place, band, streams, gate, product, mixed, before, after)
+    streams, gate, product, mixed, edge, weight = forward(place, values, other, weight)
+    edge = lax.ppermute(edge, ("l", "z"), [(7, 8), (8, 7), (15, 0), (0, 15)])
+    before = lax.ppermute(product, "z", [(n, n + 1) for n in range(7)])
+    after = lax.ppermute(mixed, "z", [(n + 1, n) for n in range(7)])
+
+    terms = middle(place, band, streams, gate, product, mixed, before, after, edge)
     other_terms = lax.ppermute(terms, "core", cross)
 
     parts = swapped(backward(place, terms, other_terms, weight), ("ylo", "x"))

time: 169 us -> 173 us (1.024)
  waiting for transfers between devices: 53.2 us -> 59.3 us
  starting transfers between devices: 36.9 us -> 34.4 us
    ppermute x1, starting transfers between devices: 6.35 us -> 2.66 us  [local(): return finish(place, mine, lax.ppermute(theirs, 'h', cross))]
    ppermute x1, waiting for transfers between devices: 3.36 us -> 7.03 us  [local(): return finish(place, mine, lax.ppermute(theirs, 'h', cross))]
    ppermute x2 -> x3, waiting for transfers between devices: 1.31 us -> 3.69 us  [the longest x1 3.69 us: local(): after = lax.ppermute(mixed, 'z', [(n + 1, n) for n in range(7)])]
    ppermute x2 -> x3, starting transfers between devices: 11.2 us -> 11.9 us  [the longest x1 9.28 us: local(): edge = lax.ppermute(edge, ('l', 'z'), [(7, 8), (8, 7), (15, 0), (0, 15)])]
  transfers between devices with their start and end apart: 8 -> 9, of which waited for: 8 -> 7; matrix products, arithmetic and copies ran while one was open for 2% -> 2% of each run, Pallas kernels for 0% -> 0%
where the time goes in v13:
time: 173 us; the launch traced here: 169 us
  waiting for transfers between devices  59.3 us (34%)
  blocking collectives  46 us (27%)
  starting transfers between devices  34.4 us (20%)
  between operations  14.2 us (8%)
  Pallas kernels  11.8 us (7%)
  local copies, waits for them, and re-layouts  2.6 us (2%)
    all_to_all x2, blocking collectives, swapped(): return lax.all_to_all(value, axes, 0, 0, tiled=True)  46 us
    all_to_all x2, waiting for transfers between devices, swapped(): return lax.all_to_all(value, axes, 0, 0, tiled=True)  37.5 us
    all_to_all x2, starting transfers between devices, swapped(): return lax.all_to_all(value, axes, 0, 0, tiled=True)  11.8 us
    ppermute x1, starting transfers between devices, local(): edge = lax.ppermute(edge, ('l', 'z'), [(7, 8), (8, 7), (15, 0), (0, 15)])  9.28 us
    ppermute x1, waiting for transfers between devices, local(): return finish(place, mine, lax.ppermute(theirs, 'h', cross))  7.03 us
    all_gather x1, waiting for transfers between devices, local(): lax.all_gather(weight, ('z', 'core'), axis=0)  6.02 us
    pallas_call x4, Pallas kernels, on_chip(): pl.pallas_call(kernel, out_shape=out_shape, in_specs=[smem] + [vmem] * (l...  4.86 us
    pallas_call x1, Pallas kernels, forward(): pl.pallas_call(forward_kernel, out_shape=(shape(BACK, BF16), shape(HALF,...  4.69 us
  transfers between devices with their start and end apart: 9, of which 7 were waited for; matrix products, arithmetic and copies ran while one was open for 2% of the time, Pallas kernels for 0%

profile of v13, /device:TPU:1, one launch (start us, length us, event | category | flops | bytes accessed | tf_op | source)
XLA Modules:
  0.0 169.3 jit_solution(14962700617049782375)
XLA Ops:
  7.2 1.9 %shard_map.68 = bf16[4,512,128]{2,1,0:T(8,128)(2,1)} custom-call(bf16[3,128,256]{2,1,0:T(8,128)(2,1)} %in_ref.1, bf16[256,128]{1,0:T(8,128)(2,1)} %out_ref.1), custom_call_target="tpu_custom_call" | custom-call | tf_op jit(solution)/shard_map/pallas_call | solution.py:254
  9.1 7.6 %all-to-all-start = ((bf16[4,512,128]{2,1,0:T(8,128)(2,1)}), bf16[4,512,128]{2,1,0:T(8,128)(2,1)S(1)}, u32[]{:S(2)}, u32[]{:S(2)}) async-start(bf16[4,512,128]{2,1,0:T(8,128)(2,1)} %shard_map.68), calls=%async_computation | async-start | bytes 1048576 | tf_op jit(solution)/shard_map/all_to_all | solution.py:272
  16.7 0.9 pad_maximum_fusion
  17.6 13.3 %all-to-all-done = bf16[4,512,128]{2,1,0:T(8,128)(2,1)S(1)} async-done(((bf16[4,512,128]{2,1,0:T(8,128)(2,1)}), bf16[4,512,128]{2,1,0:T(8,128)(2,1)S(1)}, u32[]{:S(2)}, u32[]{:S(2)}) %all-to-all-start) | async-done | bytes 524320 | tf_op jit(solution)/shard_map/all_to_all | solution.py:272
  31.8 17.9 %all_to_all.20 = bf16[4,2,128,256]{3,2,1,0:T(8,128)(2,1)S(1)} all-to-all(bf16[4,2,128,256]{3,2,1,0:T(8,128)(2,1)S(1)} %broadcast_in_dim.6), channel_id=1, replica_groups=mesh['h'=2,'l'=2,'z'=8,'ylo'=2,'x'=4,'core'=2] {'h','ylo'}, dimensions={0} | all-to-all | bytes 1048576 | tf_op jit(solution)/shard_map/all_to_all | solution.py:272
  49.7 1.6 broadcast_in_dim.7
  51.3 4.1 %all-to-all-start.2 = ((bf16[4,4,2,128,256]{4,3,2,1,0:T(8,128)(2,1)}), bf16[4,4,2,128,256]{4,3,2,1,0:T(8,128)(2,1)S(1)}, u32[]{:S(2)}, u32[]{:S(2)}) async-start(bf16[4,4,2,128,256]{4,3,2,1,0:T(8,128)(2,1)} %broadcast_in_dim.7), calls=%async_computation.2 | async-start | bytes 4194304 | tf_op jit(solution)/shard_map/all_to_all | solution.py:272
  56.0 24.1 %all-to-all-done.2 = bf16[4,4,2,128,256]{4,3,2,1,0:T(8,128)(2,1)S(1)} async-done(((bf16[4,4,2,128,256]{4,3,2,1,0:T(8,128)(2,1)}), bf16[4,4,2,128,256]{4,3,2,1,0:T(8,128)(2,1)S(1)}, u32[]{:S(2)}, u32[]{:S(2)}) %all-to-all-start.2) | async-done | bytes 2097184 | tf_op jit(solution)/shard_map/all_to_all | solution.py:272
  80.1 4.4 %collective-permute-start = (bf16[4,2,2,2,128,256]{5,4,3,2,1,0:T(8,128)(2,1)S(1)}, bf16[4,2,2,2,128,256]{5,4,3,2,1,0:T(8,128)(2,1)}, u32[]{:S(2)}, u32[]{:S(2)}) collective-permute-start(bf16[4,2,2,2,128,256]{5,4,3,2,1,0:T(8,128)(2,1)S(1)} %bitcast.9), channel_id=1, source_target_pairs={{0,1},{1,0},{2,3},{3,2},{4,5},{5,4},{6,7},{7,6},{8,9},{9,8},{10,11... | collective-permute-start | bytes 6291464 | tf_op jit(solution)/shard_map/ppermute | solution.py:294
  84.7 3.9 %collective-permute-done.other_hbm = bf16[4,2,2,2,128,256]{5,4,3,2,1,0:T(8,128)(2,1)} collective-permute-done((bf16[4,2,2,2,128,256]{5,4,3,2,1,0:T(8,128)(2,1)S(1)}, bf16[4,2,2,2,128,256]{5,4,3,2,1,0:T(8,128)(2,1)}, u32[]{:S(2)}, u32[]{:S(2)}) %collective-permute-start) | collective-permute-done | bytes 2097184 | tf_op jit(solution)/shard_map/ppermute | solution.py:294
  88.6 6.0 %all-gather.3.cloned.1.call-done = bf16[64,512,128]{2,1,0:T(8,128)(2,1)} async-done(((bf16[4,512,128]{2,1,0:T(8,128)(2,1)}), bf16[64,512,128]{2,1,0:T(8,128)(2,1)}) %all-gather.3.cloned.1.call-update) | async-done | bytes 8388624 | tf_op jit(solution)/shard_map/all_gather | solution.py:287
  94.6 4.7 %shard_map.70 = (bf16[384,256]{1,0:T(8,128)(2,1)S(1)}, f32[128,256]{1,0:T(8,128)S(1)}, bf16[128,256]{1,0:T(8,128)(2,1)S(1)}, bf16[128,256]{1,0:T(8,128)(2,1)S(1)...) custom-call(s32[4]{0:T(128)S(1)} %pad_add_fusion.place_ref, ...), custom_call_target="tpu_custom_call" | custom-call | flops 1073741824 | bytes 9437184 | tf_op jit(solution)/shard_map/pallas_call | solution.py:118
  99.3 9.3 %collective-permute-start.3 = (bf16[128,256]{1,0:T(8,128)(2,1)S(1)}, bf16[128,256]{1,0:T(8,128)(2,1)S(1)}, u32[]{:S(2)}, u32[]{:S(2)}) collective-permute-start(bf16[128,256]{1,0:T(8,128)(2,1)S(1)} %get-tuple-element.22), channel_id=1, source_target_pairs={{112,128},{128,112},{240,0},{0,240},{113,129},{129,113},{241,1},{1... | collective-permute-start | bytes 196616 | tf_op jit(solution)/shard_map/ppermute | solution.py:297
  108.6 1.3 collective-permute-start.1
  109.9 1.3 collective-permute-start.2
  111.2 3.7 %collective-permute-done.2.after_ref = bf16[128,256]{1,0:T(8,128)(2,1)S(1)} collective-permute-done((bf16[128,256]{1,0:T(8,128)(2,1)S(1)}, bf16[128,256]{1,0:T(8,128)(2,1)S(1)}, u32[]{:S(2)}, u32[]{:S(2)}) %collective-permute-start.2) | collective-permute-done | bytes 65568 | tf_op jit(solution)/shard_map/ppermute | solution.py:299
  114.9 1.1 shard_map.71.own_ref
  116.0 3.7 %collective-permute-start.4 = (bf16[256,512]{1,0:T(8,128)(2,1)S(1)}, bf16[256,512]{1,0:T(8,128)(2,1)S(1)}, u32[]{:S(2)}, u32[]{:S(2)}) collective-permute-start(bf16[256,512]{1,0:T(8,128)(2,1)S(1)} %shard_map.71.own_ref), channel_id=1, source_target_pairs={{0,1},{1,0},{2,3},{3,2},{4,5},{5,4},{6,7},{7,6},{8,9},{9,8},{10,11... | collective-permute-start | bytes 786440 | tf_op jit(solution)/shard_map/ppermute | solution.py:302
  119.7 1.1 collective-permute-done.4.other_ref
  120.8 1.8 %shard_map.72 = bf16[8,2,2,128,256]{4,3,2,1,0:T(8,128)(2,1)S(1)} custom-call(s32[4]{0:T(128)S(1)} %pad_add_fusion.place_ref, bf16[256,512]{1,0:T(8,128)(2,1)S(1)} %shard_map.71.own_ref, bf16[256,512]{1,0:T(8,128)(2,1)S(1)} %collective-permute-done.4.other_ref, bf16[2,2,2,2,2,512,128]{6,5,4,3,2,1,0:T(8,128)(2,1)S(1)} %get-tuple-element.23.weight_ref), custom_call_target="tpu_custom_call" | custom-call | flops 1073741824 | bytes 1048576 | tf_op jit(solution)/shard_map/pallas_call | solution.py:191
  122.6 28.1 %all_to_all.21.parts_ref = bf16[8,2,2,128,256]{4,3,2,1,0:T(8,128)(2,1)S(1)} all-to-all(bf16[8,2,2,128,256]{4,3,2,1,0:T(8,128)(2,1)S(1)} %shard_map.72), channel_id=1, replica_groups=mesh['h'=2,'l'=2,'z'=8,'ylo'=2,'x'=4,'core'=2] {'ylo','x'}, dimensions={0} | all-to-all | bytes 4194304 | tf_op jit(solution)/shard_map/all_to_all | solution.py:272
  151.6 2.7 %collective-permute-start.5 = (bf16[2,128,256]{2,1,0:T(8,128)(2,1)S(1)}, bf16[2,128,256]{2,1,0:T(8,128)(2,1)S(1)}, u32[]{:S(2)}, u32[]{:S(2)}) collective-permute-start(bf16[2,128,256]{2,1,0:T(8,128)(2,1)S(1)} %get-tuple-element.25), channel_id=1, source_target_pairs={{0,256},{256,0},{1,257},{257,1},{2,258},{258,2},{3,259},{259,3},{4... | collective-permute-start | bytes 393224 | tf_op jit(solution)/shard_map/ppermute | solution.py:306
  154.2 7.0 %collective-permute-done.5.theirs_ref = bf16[2,128,256]{2,1,0:T(8,128)(2,1)S(1)} collective-permute-done((bf16[2,128,256]{2,1,0:T(8,128)(2,1)S(1)}, bf16[2,128,256]{2,1,0:T(8,128)(2,1)S(1)}, u32[]{:S(2)}, u32[]{:S(2)}) %collective-permute-start.5) | collective-permute-done | bytes 131104 | tf_op jit(solution)/shard_map/ppermute | solution.py:306
  161.3 1.2 shard_map.74
  (17 shorter events, 2.3 us)
Async XLA Ops:
  7.2 48.2 %copy-start = (f32[16,128]{1,0:T(8,128)S(1)}, f32[16,128]{1,0:T(8,128)}, u32[]{:S(2)}) copy-start(f32[16,128]{1,0:T(8,128)} %param.8) | copy-start | bytes 24580
  9.1 21.9 %all-to-all-start = ((bf16[4,512,128]{2,1,0:T(8,128)(2,1)}), bf16[4,512,128]{2,1,0:T(8,128)(2,1)S(1)}, u32[]{:S(2)}, u32[]{:S(2)}) async-start(bf16[4,512,128]{2,1,0:T(8,128)(2,1)} %shard_map.68), calls=%async_computation | async-start | bytes 1048576 | tf_op jit(solution)/shard_map/all_to_all | solution.py:272
  16.7 77.9 %all-gather.3.cloned.1.call-start = ((), (), s32[]{:S(2)}) async-start(), calls=%async_computation.4 | async-start | bytes 8912896 | tf_op jit(solution)/shard_map/all_gather | solution.py:287
  30.9 0.8 copy-start.1
  51.3 28.9 %all-to-all-start.2 = ((bf16[4,4,2,128,256]{4,3,2,1,0:T(8,128)(2,1)}), bf16[4,4,2,128,256]{4,3,2,1,0:T(8,128)(2,1)S(1)}, u32[]{:S(2)}, u32[]{:S(2)}) async-start(bf16[4,4,2,128,256]{4,3,2,1,0:T(8,128)(2,1)} %broadcast_in_dim.7), calls=%async_computation.2 | async-start | bytes 4194304 | tf_op jit(solution)/shard_map/all_to_all | solution.py:272
  80.1 8.4 %collective-permute-start = (bf16[4,2,2,2,128,256]{5,4,3,2,1,0:T(8,128)(2,1)S(1)}, bf16[4,2,2,2,128,256]{5,4,3,2,1,0:T(8,128)(2,1)}, u32[]{:S(2)}, u32[]{:S(2)}) collective-permute-start(bf16[4,2,2,2,128,256]{5,4,3,2,1,0:T(8,128)(2,1)S(1)} %bitcast.9), channel_id=1, source_target_pairs={{0,1},{1,0},{2,3},{3,2},{4,5},{5,4},{6,7},{7,6},{8,9},{9,8},{10,11... | collective-permute-start | bytes 6291464 | tf_op jit(solution)/shard_map/ppermute | solution.py:294
  99.3 11.9 %collective-permute-start.3 = (bf16[128,256]{1,0:T(8,128)(2,1)S(1)}, bf16[128,256]{1,0:T(8,128)(2,1)S(1)}, u32[]{:S(2)}, u32[]{:S(2)}) collective-permute-start(bf16[128,256]{1,0:T(8,128)(2,1)S(1)} %get-tuple-element.22), channel_id=1, source_target_pairs={{112,128},{128,112},{240,0},{0,240},{113,129},{129,113},{241,1},{1... | collective-permute-start | bytes 196616 | tf_op jit(solution)/shard_map/ppermute | solution.py:297
  108.6 2.6 %collective-permute-start.1 = (bf16[128,256]{1,0:T(8,128)(2,1)S(1)}, bf16[128,256]{1,0:T(8,128)(2,1)S(1)}, u32[]{:S(2)}, u32[]{:S(2)}) collective-permute-start(bf16[128,256]{1,0:T(8,128)(2,1)S(1)} %get-tuple-element.20.product_ref), channel_id=1, source_target_pairs={{0,16},{16,32},{32,48},{48,64},{64,80},{80,96},{96,112},{1,17},{17... | collective-permute-start | bytes 196616 | tf_op jit(solution)/shard_map/ppermute | solution.py:298
  109.9 5.0 %collective-permute-start.2 = (bf16[128,256]{1,0:T(8,128)(2,1)S(1)}, bf16[128,256]{1,0:T(8,128)(2,1)S(1)}, u32[]{:S(2)}, u32[]{:S(2)}) collective-permute-start(bf16[128,256]{1,0:T(8,128)(2,1)S(1)} %get-tuple-element.21.mixed_ref), channel_id=1, source_target_pairs={{16,0},{32,16},{48,32},{64,48},{80,64},{96,80},{112,96},{17,1},{33... | collective-permute-start | bytes 196616 | tf_op jit(solution)/shard_map/ppermute | solution.py:299
  116.0 4.9 %collective-permute-start.4 = (bf16[256,512]{1,0:T(8,128)(2,1)S(1)}, bf16[256,512]{1,0:T(8,128)(2,1)S(1)}, u32[]{:S(2)}, u32[]{:S(2)}) collective-permute-start(bf16[256,512]{1,0:T(8,128)(2,1)S(1)} %shard_map.71.own_ref), channel_id=1, source_target_pairs={{0,1},{1,0},{2,3},{3,2},{4,5},{5,4},{6,7},{7,6},{8,9},{9,8},{10,11... | collective-permute-start | bytes 786440 | tf_op jit(solution)/shard_map/ppermute | solution.py:302
  151.6 9.7 %collective-permute-start.5 = (bf16[2,128,256]{2,1,0:T(8,128)(2,1)S(1)}, bf16[2,128,256]{2,1,0:T(8,128)(2,1)S(1)}, u32[]{:S(2)}, u32[]{:S(2)}) collective-permute-start(bf16[2,128,256]{2,1,0:T(8,128)(2,1)S(1)} %get-tuple-element.25), channel_id=1, source_target_pairs={{0,256},{256,0},{1,257},{257,1},{2,258},{258,2},{3,259},{259,3},{4... | collective-permute-start | bytes 393224 | tf_op jit(solution)/shard_map/ppermute | solution.py:306
Sparse Core Ops, SparseCore 0:
  31.9 62.6 all-gather.2

commit v14 on v10

--- a/solution.py
+++ b/solution.py
@@ -205,7 +205,7 @@
                 ]
                 result = jnp.dot(terms, jnp.concatenate(weight, 0), preferred_element_type=F32)
                 for h in range(2):
-                    out_ref[4 * y + x, h, part] = result[h * ROWS : (h + 1) * ROWS].astype(BF16)
+                    out_ref[2 * x + y, h, part] = result[h * ROWS : (h + 1) * ROWS].astype(BF16)
 
 
 def backward(*operands):
@@ -213,21 +213,17 @@
     return on_chip(backward_kernel, jax.ShapeDtypeStruct(shape, BF16), operands, 1 << 30)
 
 
-def combine_kernel(place_ref, parts_ref, mine_ref, theirs_ref):
-    half = place_ref[3]
-    for part in range(2):
-        mine, theirs = 0.0, 0.0
-        for source in range(8):
-            mine += parts_ref[source, half, part].astype(F32)
-            theirs += parts_ref[source, 1 - half, part].astype(F32)
-        mine_ref[part] = mine
-        theirs_ref[part] = theirs.astype(BF16)
-
-
-def combine(*operands):
-    shape = (2, ROWS, FEATURES)
-    out_shape = (jax.ShapeDtypeStruct(shape, F32), jax.ShapeDtypeStruct(shape, BF16))
-    return on_chip(combine_kernel, out_shape, operands, 1 << 20)
+def combine(place, parts, turn):
+    def kernel(place_ref, parts_ref, total_ref):
+        block = place_ref[3] if turn == 0 else 1 - place_ref[3]
+        for part in range(2):
+            total = 0.0
+            for source in range(8):
+                total += parts_ref[source, block, part].astype(F32)
+            total_ref[part] = total.astype(total_ref.dtype)
+
+    out_shape = jax.ShapeDtypeStruct((2, ROWS, FEATURES), BF16 if turn else F32)
+    return on_chip(kernel, out_shape, (place, parts), 1 << 20)
 
 
 def pack_kernel(in_ref, out_ref, packed_ref):
@@ -292,9 +288,11 @@
     terms = middle(place, band, streams, gate, product, mixed, before, after)
     other_terms = lax.ppermute(terms, "core", cross)
 
-    parts = swapped(backward(place, terms, other_terms, weight), ("ylo", "x"))
-    mine, theirs = combine(place, parts)
-    return finish(place, mine, lax.ppermute(theirs, "h", cross))
+    parts = swapped(backward(place, terms, other_terms, weight), ("x", "ylo"))
+    theirs = combine(place, parts, 1)
+    theirs, parts = lax.optimization_barrier((theirs, parts))
+    theirs = lax.ppermute(theirs, "h", cross)
+    return finish(place, combine(place, parts, 0), theirs)
 
 
 def solution(mesh):

time: 169 us -> 170 us (level)
    pallas_call x4 -> x5, Pallas kernels: 4.86 us -> 5.41 us  [on_chip(): pl.pallas_call(kernel, out_shape=out_shape, in_specs=[smem] + [vmem] * (l...]
  transfers between devices with their start and end apart: 8 -> 8, of which waited for: 8 -> 8; matrix products, arithmetic and copies ran while one was open for 2% -> 2% of each run, Pallas kernels for 0% -> 1%
where the time goes in v14:
time: 170 us; the launch traced here: 166 us
  waiting for transfers between devices  52.6 us (31%)
  blocking collectives  46.9 us (28%)
  starting transfers between devices  36.9 us (22%)
  between operations  14.1 us (8%)
  Pallas kernels  12.3 us (7%)
  local copies, waits for them, and re-layouts  2.61 us (2%)
    all_to_all x2, blocking collectives, swapped(): return lax.all_to_all(value, axes, 0, 0, tiled=True)  46.9 us
    all_to_all x2, waiting for transfers between devices, swapped(): return lax.all_to_all(value, axes, 0, 0, tiled=True)  37.5 us
    all_to_all x2, starting transfers between devices, swapped(): return lax.all_to_all(value, axes, 0, 0, tiled=True)  11.8 us
    ppermute x1, starting transfers between devices, local(): after = lax.ppermute(mixed, ('l', 'z'), [(b, a) for a, b in ring])  9.29 us
    ppermute x1, starting transfers between devices, local(): theirs = lax.ppermute(theirs, 'h', cross)  6.35 us
    all_gather x1, waiting for transfers between devices, local(): lax.all_gather(weight, ('z', 'core'), axis=0)  6.02 us
    pallas_call x5, Pallas kernels, on_chip(): pl.pallas_call(kernel, out_shape=out_shape, in_specs=[smem] + [vmem] * (l...  5.41 us
    pallas_call x1, Pallas kernels, forward(): pl.pallas_call(forward_kernel, out_shape=(shape(BACK, BF16), shape(HALF,...  4.69 us
  transfers between devices with their start and end apart: 8, of which 8 were waited for; matrix products, arithmetic and copies ran while one was open for 2% of the time, Pallas kernels for 1%

profile of v14, /device:TPU:1, one launch (start us, length us, event | category | flops | bytes accessed | tf_op | source)
XLA Modules:
  0.0 166.5 jit_solution(3446960771360994011)
XLA Ops:
  7.2 1.9 %shard_map.68 = bf16[4,512,128]{2,1,0:T(8,128)(2,1)} custom-call(bf16[3,128,256]{2,1,0:T(8,128)(2,1)} %in_ref.1, bf16[256,128]{1,0:T(8,128)(2,1)} %out_ref.1), custom_call_target="tpu_custom_call" | custom-call | tf_op jit(solution)/shard_map/pallas_call | solution.py:241
  9.0 7.6 %all-to-all-start = ((bf16[4,512,128]{2,1,0:T(8,128)(2,1)}), bf16[4,512,128]{2,1,0:T(8,128)(2,1)S(1)}, u32[]{:S(2)}, u32[]{:S(2)}) async-start(bf16[4,512,128]{2,1,0:T(8,128)(2,1)} %shard_map.68), calls=%async_computation | async-start | bytes 1048576 | tf_op jit(solution)/shard_map/all_to_all | solution.py:259
  16.7 0.9 pad_maximum_fusion
  17.6 13.3 %all-to-all-done = bf16[4,512,128]{2,1,0:T(8,128)(2,1)S(1)} async-done(((bf16[4,512,128]{2,1,0:T(8,128)(2,1)}), bf16[4,512,128]{2,1,0:T(8,128)(2,1)S(1)}, u32[]{:S(2)}, u32[]{:S(2)}) %all-to-all-start) | async-done | bytes 524320 | tf_op jit(solution)/shard_map/all_to_all | solution.py:259
  30.9 0.8 copy-done.1
  31.8 17.9 %all_to_all.20 = bf16[4,2,128,256]{3,2,1,0:T(8,128)(2,1)S(1)} all-to-all(bf16[4,2,128,256]{3,2,1,0:T(8,128)(2,1)S(1)} %broadcast_in_dim.6), channel_id=1, replica_groups=mesh['h'=2,'l'=2,'z'=8,'ylo'=2,'x'=4,'core'=2] {'h','ylo'}, dimensions={0} | all-to-all | bytes 1048576 | tf_op jit(solution)/shard_map/all_to_all | solution.py:259
  49.7 1.6 broadcast_in_dim.7
  51.3 4.1 %all-to-all-start.2 = ((bf16[4,4,2,128,256]{4,3,2,1,0:T(8,128)(2,1)}), bf16[4,4,2,128,256]{4,3,2,1,0:T(8,128)(2,1)S(1)}, u32[]{:S(2)}, u32[]{:S(2)}) async-start(bf16[4,4,2,128,256]{4,3,2,1,0:T(8,128)(2,1)} %broadcast_in_dim.7), calls=%async_computation.2 | async-start | bytes 4194304 | tf_op jit(solution)/shard_map/all_to_all | solution.py:259
  56.0 24.1 %all-to-all-done.2 = bf16[4,4,2,128,256]{4,3,2,1,0:T(8,128)(2,1)S(1)} async-done(((bf16[4,4,2,128,256]{4,3,2,1,0:T(8,128)(2,1)}), bf16[4,4,2,128,256]{4,3,2,1,0:T(8,128)(2,1)S(1)}, u32[]{:S(2)}, u32[]{:S(2)}) %all-to-all-start.2) | async-done | bytes 2097184 | tf_op jit(solution)/shard_map/all_to_all | solution.py:259
  80.2 4.4 %collective-permute-start = (bf16[4,2,2,2,128,256]{5,4,3,2,1,0:T(8,128)(2,1)S(1)}, bf16[4,2,2,2,128,256]{5,4,3,2,1,0:T(8,128)(2,1)}, u32[]{:S(2)}, u32[]{:S(2)}) collective-permute-start(bf16[4,2,2,2,128,256]{5,4,3,2,1,0:T(8,128)(2,1)S(1)} %bitcast.9), channel_id=1, source_target_pairs={{0,1},{1,0},{2,3},{3,2},{4,5},{5,4},{6,7},{7,6},{8,9},{9,8},{10,11... | collective-permute-start | bytes 6291464 | tf_op jit(solution)/shard_map/ppermute | solution.py:281
  84.7 3.9 %collective-permute-done.other_hbm = bf16[4,2,2,2,128,256]{5,4,3,2,1,0:T(8,128)(2,1)} collective-permute-done((bf16[4,2,2,2,128,256]{5,4,3,2,1,0:T(8,128)(2,1)S(1)}, bf16[4,2,2,2,128,256]{5,4,3,2,1,0:T(8,128)(2,1)}, u32[]{:S(2)}, u32[]{:S(2)}) %collective-permute-start) | collective-permute-done | bytes 2097184 | tf_op jit(solution)/shard_map/ppermute | solution.py:281
  88.6 6.0 %all-gather.3.cloned.1.call-done = bf16[64,512,128]{2,1,0:T(8,128)(2,1)} async-done(((bf16[4,512,128]{2,1,0:T(8,128)(2,1)}), bf16[64,512,128]{2,1,0:T(8,128)(2,1)}) %all-gather.3.cloned.1.call-update) | async-done | bytes 8388624 | tf_op jit(solution)/shard_map/all_gather | solution.py:274
  94.6 4.7 %shard_map.70 = (bf16[384,256]{1,0:T(8,128)(2,1)S(1)}, f32[128,256]{1,0:T(8,128)S(1)}, bf16[128,256]{1,0:T(8,128)(2,1)S(1)}, bf16[128,256]{1,0:T(8,128)(2,1)S(1)}, bf16[2,2,2,2,2,512,128]{6,5,4,3,2,1,0:T(8,128)(2,1)S(1)}) custom-call(s32[4]{0:T(128)S(1)} %pad_add_fusion.place_ref, bf16[4,2,2,2,128,256]{5,4,3,2,1,0:T(8,128)(2,1)S(1)} %bitcast.10, ...), custom_call_target="tpu_custom_call" | custom-call | flops 1073741824 | bytes 9437184 | tf_op jit(solution)/shard_map/pallas_call | solution.py:114
  99.3 1.9 %collective-permute-start.1 = (bf16[128,256]{1,0:T(8,128)(2,1)S(1)}, bf16[128,256]{1,0:T(8,128)(2,1)S(1)}, u32[]{:S(2)}, u32[]{:S(2)}) collective-permute-start(bf16[128,256]{1,0:T(8,128)(2,1)S(1)} %get-tuple-element.19.product_ref), channel_id=1, source_target_pairs={{0,16},{16,32},{32,48},{48,64},{64,80},{80,96},{96,112},{112,128},... | collective-permute-start | bytes 196616 | tf_op jit(solution)/shard_map/ppermute | solution.py:285
  101.2 9.3 %collective-permute-start.2 = (bf16[128,256]{1,0:T(8,128)(2,1)S(1)}, bf16[128,256]{1,0:T(8,128)(2,1)S(1)}, u32[]{:S(2)}, u32[]{:S(2)}) collective-permute-start(bf16[128,256]{1,0:T(8,128)(2,1)S(1)} %get-tuple-element.20.mixed_ref), channel_id=1, source_target_pairs={{16,0},{32,16},{48,32},{64,48},{80,64},{96,80},{112,96},{128,112},... | collective-permute-start | bytes 196616 | tf_op jit(solution)/shard_map/ppermute | solution.py:286
  110.7 1.1 collective-permute-done.2.after_ref
  111.8 1.0 shard_map.71.own_ref
  112.9 3.1 %collective-permute-start.3 = (bf16[256,512]{1,0:T(8,128)(2,1)S(1)}, bf16[256,512]{1,0:T(8,128)(2,1)S(1)}, u32[]{:S(2)}, u32[]{:S(2)}) collective-permute-start(bf16[256,512]{1,0:T(8,128)(2,1)S(1)} %shard_map.71.own_ref), channel_id=1, source_target_pairs={{0,1},{1,0},{2,3},{3,2},{4,5},{5,4},{6,7},{7,6},{8,9},{9,8},{10,11... | collective-permute-start | bytes 786440 | tf_op jit(solution)/shard_map/ppermute | solution.py:289
  116.0 1.1 collective-permute-done.3.other_ref
  117.2 1.8 %shard_map.72 = bf16[8,2,2,128,256]{4,3,2,1,0:T(8,128)(2,1)S(1)} custom-call(s32[4]{0:T(128)S(1)} %pad_add_fusion.place_ref, bf16[256,512]{1,0:T(8,128)(2,1)S(1)} %shard_map.71.own_ref, bf16[256,512]{1,0:T(8,128)(2,1)S(1)} %collective-permute-done.3.other_ref, bf16[2,2,2,2,2,512,128]{6,5,4,3,2,1,0:T(8,128)(2,1)S(1)} %get-tuple-element.21.weight_ref), custom_call_target="tpu_custom_call" | custom-call | flops 1073741824 | bytes 1048576 | tf_op jit(solution)/shard_map/pallas_call | solution.py:182
  119.0 29.0 %all_to_all.21.parts_ref = bf16[8,2,2,128,256]{4,3,2,1,0:T(8,128)(2,1)S(1)} all-to-all(bf16[8,2,2,128,256]{4,3,2,1,0:T(8,128)(2,1)S(1)} %shard_map.72), channel_id=1, replica_groups=mesh['h'=2,'l'=2,'z'=8,'ylo'=2,'x'=4,'core'=2] {'x','ylo'}, dimensions={0} | all-to-all | bytes 4194304 | tf_op jit(solution)/shard_map/all_to_all | solution.py:259
  148.7 6.4 %collective-permute-start.4 = (bf16[2,128,256]{2,1,0:T(8,128)(2,1)S(1)}, bf16[2,128,256]{2,1,0:T(8,128)(2,1)S(1)}, u32[]{:S(2)}, u32[]{:S(2)}) collective-permute-start(bf16[2,128,256]{2,1,0:T(8,128)(2,1)S(1)} %shard_map.73), channel_id=1, source_target_pairs={{0,256},{256,0},{1,257},{257,1},{2,258},{258,2},{3,259},{259,3},{4... | collective-permute-start | bytes 393224 | tf_op jit(solution)/shard_map/ppermute | solution.py:294
  155.8 2.7 %collective-permute-done.4.theirs_ref = bf16[2,128,256]{2,1,0:T(8,128)(2,1)S(1)} collective-permute-done((bf16[2,128,256]{2,1,0:T(8,128)(2,1)S(1)}, bf16[2,128,256]{2,1,0:T(8,128)(2,1)S(1)}, u32[]{:S(2)}, u32[]{:S(2)}) %collective-permute-start.4) | collective-permute-done | bytes 131104 | tf_op jit(solution)/shard_map/ppermute | solution.py:294
  158.4 1.2 shard_map.75
  (16 shorter events, 2.3 us)
Async XLA Ops:
  7.2 48.2 %copy-start = (f32[16,128]{1,0:T(8,128)S(1)}, f32[16,128]{1,0:T(8,128)}, u32[]{:S(2)}) copy-start(f32[16,128]{1,0:T(8,128)} %param.8) | copy-start | bytes 24580
  9.0 21.9 %all-to-all-start = ((bf16[4,512,128]{2,1,0:T(8,128)(2,1)}), bf16[4,512,128]{2,1,0:T(8,128)(2,1)S(1)}, u32[]{:S(2)}, u32[]{:S(2)}) async-start(bf16[4,512,128]{2,1,0:T(8,128)(2,1)} %shard_map.68), calls=%async_computation | async-start | bytes 1048576 | tf_op jit(solution)/shard_map/all_to_all | solution.py:259
  16.7 77.9 %all-gather.3.cloned.1.call-start = ((), (), s32[]{:S(2)}) async-start(), calls=%async_computation.4 | async-start | bytes 8912896 | tf_op jit(solution)/shard_map/all_gather | solution.py:274
  30.9 0.8 copy-start.1
  51.3 28.9 %all-to-all-start.2 = ((bf16[4,4,2,128,256]{4,3,2,1,0:T(8,128)(2,1)}), bf16[4,4,2,128,256]{4,3,2,1,0:T(8,128)(2,1)S(1)}, u32[]{:S(2)}, u32[]{:S(2)}) async-start(bf16[4,4,2,128,256]{4,3,2,1,0:T(8,128)(2,1)} %broadcast_in_dim.7), calls=%async_computation.2 | async-start | bytes 4194304 | tf_op jit(solution)/shard_map/all_to_all | solution.py:259
  80.2 8.4 %collective-permute-start = (bf16[4,2,2,2,128,256]{5,4,3,2,1,0:T(8,128)(2,1)S(1)}, bf16[4,2,2,2,128,256]{5,4,3,2,1,0:T(8,128)(2,1)}, u32[]{:S(2)}, u32[]{:S(2)}) collective-permute-start(bf16[4,2,2,2,128,256]{5,4,3,2,1,0:T(8,128)(2,1)S(1)} %bitcast.9), channel_id=1, source_target_pairs={{0,1},{1,0},{2,3},{3,2},{4,5},{5,4},{6,7},{7,6},{8,9},{9,8},{10,11... | collective-permute-start | bytes 6291464 | tf_op jit(solution)/shard_map/ppermute | solution.py:281
  99.3 11.4 %collective-permute-start.1 = (bf16[128,256]{1,0:T(8,128)(2,1)S(1)}, bf16[128,256]{1,0:T(8,128)(2,1)S(1)}, u32[]{:S(2)}, u32[]{:S(2)}) collective-permute-start(bf16[128,256]{1,0:T(8,128)(2,1)S(1)} %get-tuple-element.19.product_ref), channel_id=1, source_target_pairs={{0,16},{16,32},{32,48},{48,64},{64,80},{80,96},{96,112},{112,128},... | collective-permute-start | bytes 196616 | tf_op jit(solution)/shard_map/ppermute | solution.py:285
  101.2 10.6 %collective-permute-start.2 = (bf16[128,256]{1,0:T(8,128)(2,1)S(1)}, bf16[128,256]{1,0:T(8,128)(2,1)S(1)}, u32[]{:S(2)}, u32[]{:S(2)}) collective-permute-start(bf16[128,256]{1,0:T(8,128)(2,1)S(1)} %get-tuple-element.20.mixed_ref), channel_id=1, source_target_pairs={{16,0},{32,16},{48,32},{64,48},{80,64},{96,80},{112,96},{128,112},... | collective-permute-start | bytes 196616 | tf_op jit(solution)/shard_map/ppermute | solution.py:286
  112.9 4.3 %collective-permute-start.3 = (bf16[256,512]{1,0:T(8,128)(2,1)S(1)}, bf16[256,512]{1,0:T(8,128)(2,1)S(1)}, u32[]{:S(2)}, u32[]{:S(2)}) collective-permute-start(bf16[256,512]{1,0:T(8,128)(2,1)S(1)} %shard_map.71.own_ref), channel_id=1, source_target_pairs={{0,1},{1,0},{2,3},{3,2},{4,5},{5,4},{6,7},{7,6},{8,9},{9,8},{10,11... | collective-permute-start | bytes 786440 | tf_op jit(solution)/shard_map/ppermute | solution.py:289
  148.7 9.7 %collective-permute-start.4 = (bf16[2,128,256]{2,1,0:T(8,128)(2,1)S(1)}, bf16[2,128,256]{2,1,0:T(8,128)(2,1)S(1)}, u32[]{:S(2)}, u32[]{:S(2)}) collective-permute-start(bf16[2,128,256]{2,1,0:T(8,128)(2,1)S(1)} %shard_map.73), channel_id=1, source_target_pairs={{0,256},{256,0},{1,257},{257,1},{2,258},{258,2},{3,259},{259,3},{4... | collective-permute-start | bytes 393224 | tf_op jit(solution)/shard_map/ppermute | solution.py:294
Sparse Core Ops, SparseCore 0:
  31.9 62.6 all-gather.2

commit v15 on v10

--- a/solution.py
+++ b/solution.py
@@ -19,6 +19,7 @@
 F32 = jnp.float32
 VMEM_FORWARD = 40 << 20
 VMEM_SMALL = 16 << 20
+VMEM_BANDS = 62 << 20
 
 
 def bands_kernel(base_ref, band_ref):
@@ -37,7 +38,7 @@
         out_shape=jax.ShapeDtypeStruct((2 * ROWS, 2 * GROUPS * ROWS), BF16),
         in_specs=[pl.BlockSpec(memory_space=pltpu.VMEM)],
         out_specs=pl.BlockSpec(memory_space=pltpu.VMEM),
-        compiler_params=pltpu.CompilerParams(vmem_limit_bytes=VMEM_SMALL),
+        compiler_params=pltpu.CompilerParams(vmem_limit_bytes=VMEM_BANDS),
     )(jnp.concatenate([causal, anticausal], 0))
 
 
@@ -205,7 +206,7 @@
                 ]
                 result = jnp.dot(terms, jnp.concatenate(weight, 0), preferred_element_type=F32)
                 for h in range(2):
-                    out_ref[4 * y + x, h, part] = result[h * ROWS : (h + 1) * ROWS].astype(BF16)
+                    out_ref[2 * x + y, h, part] = result[h * ROWS : (h + 1) * ROWS].astype(BF16)
 
 
 def backward(*operands):
@@ -274,13 +275,12 @@
 
     weight = swapped(packed(in_weight, out_weight), ("h", "l"))
     values = jnp.stack([tokens, cotangent], 0)
-    weight, values = lax.optimization_barrier((weight, values))
+    band = bands(lax.dynamic_slice_in_dim(mr_filter, half * GROUPS, GROUPS, 0))
+    weight, values, band = lax.optimization_barrier((weight, values, band))
     weight = lax.all_gather(weight, ("z", "core"), axis=0).reshape(8, 2, 4, STREAMS, ROWS)
 
-    band = bands(lax.dynamic_slice_in_dim(mr_filter, half * GROUPS, GROUPS, 0))
     values = gathered(values, ("h", "ylo"), 4)
     values = gathered(values, "x", 4).reshape(4, 2, 2, 2, ROWS, FEATURES)
-    values, band = lax.optimization_barrier((values, band))
     cross = [(0, 1), (1, 0)]
     other = lax.ppermute(values, "core", cross)
 
@@ -292,7 +292,7 @@
     terms = middle(place, band, streams, gate, product, mixed, before, after)
     other_terms = lax.ppermute(terms, "core", cross)
 
-    parts = swapped(backward(place, terms, other_terms, weight), ("ylo", "x"))
+    parts = swapped(backward(place, terms, other_terms, weight), ("x", "ylo"))
     mine, theirs = combine(place, parts)
     return finish(place, mine, lax.ppermute(theirs, "h", cross))
 

time: 169 us -> 171 us (1.012)
  blocking collectives: 46.5 us -> 76.9 us
  waiting for transfers between devices: 53.2 us -> 28.4 us
  starting transfers between devices: 36.9 us -> 31.6 us
  Pallas kernels: 11.8 us -> 14.7 us
    all_to_all x2 -> x3, blocking collectives: 46.5 us -> 76.9 us  [swapped(): return lax.all_to_all(value, axes, 0, 0, tiled=True)]
    all_to_all x2 -> x1, waiting for transfers between devices: 37.5 us -> 11.2 us  [swapped(): return lax.all_to_all(value, axes, 0, 0, tiled=True)]
    all_to_all x2 -> x1, starting transfers between devices: 11.8 us -> 7.64 us  [swapped(): return lax.all_to_all(value, axes, 0, 0, tiled=True)]
    pallas_call x1, Pallas kernels: 0.37 us -> 2.13 us  [bands(): pl.pallas_call(bands_kernel, out_shape=jax.ShapeDtypeStruct((2 * ROWS, 2...]
  transfers between devices with their start and end apart: 8 -> 7, of which waited for: 8 -> 6; matrix products, arithmetic and copies ran while one was open for 2% -> 1% of each run, Pallas kernels for 0% -> 1%
where the time goes in v15:
time: 171 us; the launch traced here: 168 us
  blocking collectives  76.9 us (45%)
  starting transfers between devices  31.6 us (18%)
  waiting for transfers between devices  28.4 us (17%)
  Pallas kernels  14.7 us (9%)
  between operations  14.2 us (8%)
    all_to_all x3, blocking collectives, swapped(): return lax.all_to_all(value, axes, 0, 0, tiled=True)  76.9 us
    all_to_all x1, waiting for transfers between devices, swapped(): return lax.all_to_all(value, axes, 0, 0, tiled=True)  11.2 us
    ppermute x1, starting transfers between devices, local(): after = lax.ppermute(mixed, ('l', 'z'), [(b, a) for a, b in ring])  8.04 us
    all_to_all x1, starting transfers between devices, swapped(): return lax.all_to_all(value, axes, 0, 0, tiled=True)  7.64 us
    all_gather x1, waiting for transfers between devices, local(): lax.all_gather(weight, ('z', 'core'), axis=0)  7.21 us
    ppermute x1, starting transfers between devices, local(): return finish(place, mine, lax.ppermute(theirs, 'h', cross))  6.42 us
    pallas_call x1, Pallas kernels, forward(): pl.pallas_call(forward_kernel, out_shape=(shape(BACK, BF16), shape(HALF,...  5.84 us
    pallas_call x4, Pallas kernels, on_chip(): pl.pallas_call(kernel, out_shape=out_shape, in_specs=[smem] + [vmem] * (l...  4.86 us
  transfers between devices with their start and end apart: 7, of which 6 were waited for; matrix products, arithmetic and copies ran while one was open for 1% of the time, Pallas kernels for 1%

profile of v15, /device:TPU:1, one launch (start us, length us, event | category | flops | bytes accessed | tf_op | source)
XLA Modules:
  0.0 167.8 jit_solution(14902377931039902339)
XLA Ops:
  7.2 1.9 %shard_map.68 = bf16[4,512,128]{2,1,0:T(8,128)(2,1)} custom-call(bf16[3,128,256]{2,1,0:T(8,128)(2,1)} %in_ref.1, bf16[256,128]{1,0:T(8,128)(2,1)} %out_ref.1), custom_call_target="tpu_custom_call" | custom-call | tf_op jit(solution)/shard_map/pallas_call | solution.py:246
  9.1 7.6 %all-to-all-start = ((bf16[4,512,128]{2,1,0:T(8,128)(2,1)}), bf16[4,512,128]{2,1,0:T(8,128)(2,1)S(1)}, u32[]{:S(2)}, u32[]{:S(2)}) async-start(bf16[4,512,128]{2,1,0:T(8,128)(2,1)} %shard_map.68), calls=%async_computation | async-start | bytes 1048576 | tf_op jit(solution)/shard_map/all_to_all | solution.py:264
  16.9 0.7 select_maximum_fusion.base_ref
  17.6 2.1 %shard_map.69.band_ref = bf16[256,2048]{1,0:T(8,128)(2,1)} custom-call(f32[16,256]{1,0:T(8,128)} %select_maximum_fusion.base_ref), custom_call_target="tpu_custom_call" | custom-call | tf_op jit(solution)/shard_map/pallas_call | solution.py:36
  19.7 11.2 %all-to-all-done = bf16[4,512,128]{2,1,0:T(8,128)(2,1)S(1)} async-done(((bf16[4,512,128]{2,1,0:T(8,128)(2,1)}), bf16[4,512,128]{2,1,0:T(8,128)(2,1)S(1)}, u32[]{:S(2)}, u32[]{:S(2)}) %all-to-all-start) | async-done | bytes 524320 | tf_op jit(solution)/shard_map/all_to_all | solution.py:264
  31.0 0.8 copy-done.2
  31.9 17.9 %all_to_all.20 = bf16[4,2,128,256]{3,2,1,0:T(8,128)(2,1)S(1)} all-to-all(bf16[4,2,128,256]{3,2,1,0:T(8,128)(2,1)S(1)} %broadcast_in_dim.7), channel_id=1, replica_groups=mesh['h'=2,'l'=2,'z'=8,'ylo'=2,'x'=4,'core'=2] {'h','ylo'}, dimensions={0} | all-to-all | bytes 1048576 | tf_op jit(solution)/shard_map/all_to_all | solution.py:264
  50.0 28.8 %all_to_all.21 = bf16[4,4,2,128,256]{4,3,2,1,0:T(8,128)(2,1)} all-to-all(bf16[4,4,2,128,256]{4,3,2,1,0:T(8,128)(2,1)S(1)} %broadcast_in_dim.8), channel_id=1, replica_groups=mesh['h'=2,'l'=2,'z'=8,'ylo'=2,'x'=4,'core'=2] {'x'}, dimensions={0} | all-to-all | bytes 4194304 | tf_op jit(solution)/shard_map/all_to_all | solution.py:264
  78.8 4.4 %collective-permute-start = (bf16[4,2,2,2,128,256]{5,4,3,2,1,0:T(8,128)(2,1)}, bf16[4,2,2,2,128,256]{5,4,3,2,1,0:T(8,128)(2,1)}, u32[]{:S(2)}, u32[]{:S(2)}) collective-permute-start(bf16[4,2,2,2,128,256]{5,4,3,2,1,0:T(8,128)(2,1)} %bitcast.6.own_ref), channel_id=1, source_target_pairs={{0,1},{1,0},{2,3},{3,2},{4,5},{5,4},{6,7},{7,6},{8,9},{9,8},{10,11... | collective-permute-start | bytes 6291464 | tf_op jit(solution)/shard_map/ppermute | solution.py:285
  83.3 4.2 %collective-permute-done.other_hbm = bf16[4,2,2,2,128,256]{5,4,3,2,1,0:T(8,128)(2,1)} collective-permute-done((bf16[4,2,2,2,128,256]{5,4,3,2,1,0:T(8,128)(2,1)}, bf16[4,2,2,2,128,256]{5,4,3,2,1,0:T(8,128)(2,1)}, u32[]{:S(2)}, u32[]{:S(2)}) %collective-permute-start) | collective-permute-done | bytes 2097184 | tf_op jit(solution)/shard_map/ppermute | solution.py:285
  87.5 7.2 %all-gather.3.cloned.1.call-done = bf16[64,512,128]{2,1,0:T(8,128)(2,1)} async-done(((bf16[4,512,128]{2,1,0:T(8,128)(2,1)}), bf16[64,512,128]{2,1,0:T(8,128)(2,1)}) %all-gather.3.cloned.1.call-update) | async-done | bytes 8388624 | tf_op jit(solution)/shard_map/all_gather | solution.py:280
  94.7 5.8 %shard_map.70 = (bf16[384,256]{1,0:T(8,128)(2,1)S(1)}, f32[128,256]{1,0:T(8,128)S(1)}, bf16[128,256]{1,0:T(8,128)(2,1)S(1)}, bf16[128,256]{1,0:T(8,128)(2,1)S(1)}, bf16[2,2,2,2,2,512,128]{6,5,4,3,2,1,0:T(8,128)(2,1)S(1)}) custom-call(s32[4]{0:T(128)S(1)} %pad_add_fusion.place_ref, bf16[4,2,2,2,128,256]{5,4,3,2,1,0:T(8,128)(2,1)} %bitcast.6.own_ref, ...), custom_call_target="tpu_custom_call" | custom-call | flops 1073741824 | bytes 9437184 | tf_op jit(solution)/shard_map/pallas_call | solution.py:115
  100.5 1.9 %collective-permute-start.1 = (bf16[128,256]{1,0:T(8,128)(2,1)S(1)}, bf16[128,256]{1,0:T(8,128)(2,1)S(1)}, u32[]{:S(2)}, u32[]{:S(2)}) collective-permute-start(bf16[128,256]{1,0:T(8,128)(2,1)S(1)} %get-tuple-element.17.product_ref), channel_id=1, source_target_pairs={{0,16},{16,32},{32,48},{48,64},{64,80},{80,96},{96,112},{112,128},... | collective-permute-start | bytes 196616 | tf_op jit(solution)/shard_map/ppermute | solution.py:289
  102.4 8.0 %collective-permute-start.2 = (bf16[128,256]{1,0:T(8,128)(2,1)S(1)}, bf16[128,256]{1,0:T(8,128)(2,1)S(1)}, u32[]{:S(2)}, u32[]{:S(2)}) collective-permute-start(bf16[128,256]{1,0:T(8,128)(2,1)S(1)} %get-tuple-element.18.mixed_ref), channel_id=1, source_target_pairs={{16,0},{32,16},{48,32},{64,48},{80,64},{96,80},{112,96},{128,112},... | collective-permute-start | bytes 196616 | tf_op jit(solution)/shard_map/ppermute | solution.py:290
  110.5 1.3 collective-permute-done.1.before_ref
  111.8 1.1 shard_map.71.own_ref
  112.9 3.1 %collective-permute-start.3 = (bf16[256,512]{1,0:T(8,128)(2,1)S(1)}, bf16[256,512]{1,0:T(8,128)(2,1)S(1)}, u32[]{:S(2)}, u32[]{:S(2)}) collective-permute-start(bf16[256,512]{1,0:T(8,128)(2,1)S(1)} %shard_map.71.own_ref), channel_id=1, source_target_pairs={{0,1},{1,0},{2,3},{3,2},{4,5},{5,4},{6,7},{7,6},{8,9},{9,8},{10,11... | collective-permute-start | bytes 786440 | tf_op jit(solution)/shard_map/ppermute | solution.py:293
  116.0 1.1 collective-permute-done.3.other_ref
  117.1 1.8 %shard_map.72 = bf16[8,2,2,128,256]{4,3,2,1,0:T(8,128)(2,1)S(1)} custom-call(s32[4]{0:T(128)S(1)} %pad_add_fusion.place_ref, bf16[256,512]{1,0:T(8,128)(2,1)S(1)} %shard_map.71.own_ref, bf16[256,512]{1,0:T(8,128)(2,1)S(1)} %collective-permute-done.3.other_ref, bf16[2,2,2,2,2,512,128]{6,5,4,3,2,1,0:T(8,128)(2,1)S(1)} %get-tuple-element.19.weight_ref), custom_call_target="tpu_custom_call" | custom-call | flops 1073741824 | bytes 1048576 | tf_op jit(solution)/shard_map/pallas_call | solution.py:183
  118.9 30.2 %all_to_all.22.parts_ref = bf16[8,2,2,128,256]{4,3,2,1,0:T(8,128)(2,1)S(1)} all-to-all(bf16[8,2,2,128,256]{4,3,2,1,0:T(8,128)(2,1)S(1)} %shard_map.72), channel_id=1, replica_groups=mesh['h'=2,'l'=2,'z'=8,'ylo'=2,'x'=4,'core'=2] {'x','ylo'}, dimensions={0} | all-to-all | bytes 4194304 | tf_op jit(solution)/shard_map/all_to_all | solution.py:264
  149.2 0.8 shard_map.73
  150.0 6.4 %collective-permute-start.4 = (bf16[2,128,256]{2,1,0:T(8,128)(2,1)S(1)}, bf16[2,128,256]{2,1,0:T(8,128)(2,1)S(1)}, u32[]{:S(2)}, u32[]{:S(2)}) collective-permute-start(bf16[2,128,256]{2,1,0:T(8,128)(2,1)S(1)} %get-tuple-element.21), channel_id=1, source_target_pairs={{0,256},{256,0},{1,257},{257,1},{2,258},{258,2},{3,259},{259,3},{4... | collective-permute-start | bytes 393224 | tf_op jit(solution)/shard_map/ppermute | solution.py:297
  156.4 3.3 %collective-permute-done.4.theirs_ref = bf16[2,128,256]{2,1,0:T(8,128)(2,1)S(1)} collective-permute-done((bf16[2,128,256]{2,1,0:T(8,128)(2,1)S(1)}, bf16[2,128,256]{2,1,0:T(8,128)(2,1)S(1)}, u32[]{:S(2)}, u32[]{:S(2)}) %collective-permute-start.4) | collective-permute-done | bytes 131104 | tf_op jit(solution)/shard_map/ppermute | solution.py:297
  159.7 1.2 shard_map.74
  (20 shorter events, 0.6 us)
Async XLA Ops:
  7.2 9.6 %copy-start = (f32[16,128]{1,0:T(8,128)S(1)}, f32[16,128]{1,0:T(8,128)}, u32[]{:S(2)}) copy-start(f32[16,128]{1,0:T(8,128)} %param.8) | copy-start | bytes 24580
  7.2 12.5 %copy-start.3 = (bf16[128,256]{1,0:T(8,128)(2,1)S(1)}, bf16[128,256]{1,0:T(8,128)(2,1)}, u32[]{:S(2)}) copy-start(bf16[128,256]{1,0:T(8,128)(2,1)} %param.9) | copy-start | bytes 196612
  7.2 12.5 %copy-start.4 = (bf16[128,256]{1,0:T(8,128)(2,1)S(1)}, bf16[128,256]{1,0:T(8,128)(2,1)}, u32[]{:S(2)}) copy-start(bf16[128,256]{1,0:T(8,128)(2,1)} %param.5) | copy-start | bytes 196612
  9.1 21.9 %all-to-all-start = ((bf16[4,512,128]{2,1,0:T(8,128)(2,1)}), bf16[4,512,128]{2,1,0:T(8,128)(2,1)S(1)}, u32[]{:S(2)}, u32[]{:S(2)}) async-start(bf16[4,512,128]{2,1,0:T(8,128)(2,1)} %shard_map.68), calls=%async_computation | async-start | bytes 1048576 | tf_op jit(solution)/shard_map/all_to_all | solution.py:264
  16.7 77.9 %all-gather.3.cloned.1.call-start = ((), (), s32[]{:S(2)}) async-start(), calls=%async_computation.4 | async-start | bytes 8912896 | tf_op jit(solution)/shard_map/all_gather | solution.py:280
  31.0 0.8 copy-start.2
  78.8 8.7 %collective-permute-start = (bf16[4,2,2,2,128,256]{5,4,3,2,1,0:T(8,128)(2,1)}, bf16[4,2,2,2,128,256]{5,4,3,2,1,0:T(8,128)(2,1)}, u32[]{:S(2)}, u32[]{:S(2)}) collective-permute-start(bf16[4,2,2,2,128,256]{5,4,3,2,1,0:T(8,128)(2,1)} %bitcast.6.own_ref), channel_id=1, source_target_pairs={{0,1},{1,0},{2,3},{3,2},{4,5},{5,4},{6,7},{7,6},{8,9},{9,8},{10,11... | collective-permute-start | bytes 6291464 | tf_op jit(solution)/shard_map/ppermute | solution.py:285
  94.7 17.2 %copy-start.1 = (bf16[256,2048]{1,0:T(8,128)(2,1)S(1)}, bf16[256,2048]{1,0:T(8,128)(2,1)}, u32[]{:S(2)}) copy-start(bf16[256,2048]{1,0:T(8,128)(2,1)} %shard_map.69.band_ref) | copy-start | bytes 3145732
  100.5 11.3 %collective-permute-start.1 = (bf16[128,256]{1,0:T(8,128)(2,1)S(1)}, bf16[128,256]{1,0:T(8,128)(2,1)S(1)}, u32[]{:S(2)}, u32[]{:S(2)}) collective-permute-start(bf16[128,256]{1,0:T(8,128)(2,1)S(1)} %get-tuple-element.17.product_ref), channel_id=1, source_target_pairs={{0,16},{16,32},{32,48},{48,64},{64,80},{80,96},{96,112},{112,128},... | collective-permute-start | bytes 196616 | tf_op jit(solution)/shard_map/ppermute | solution.py:289
  102.4 9.4 %collective-permute-start.2 = (bf16[128,256]{1,0:T(8,128)(2,1)S(1)}, bf16[128,256]{1,0:T(8,128)(2,1)S(1)}, u32[]{:S(2)}, u32[]{:S(2)}) collective-permute-start(bf16[128,256]{1,0:T(8,128)(2,1)S(1)} %get-tuple-element.18.mixed_ref), channel_id=1, source_target_pairs={{16,0},{32,16},{48,32},{64,48},{80,64},{96,80},{112,96},{128,112},... | collective-permute-start | bytes 196616 | tf_op jit(solution)/shard_map/ppermute | solution.py:290
  112.9 4.3 %collective-permute-start.3 = (bf16[256,512]{1,0:T(8,128)(2,1)S(1)}, bf16[256,512]{1,0:T(8,128)(2,1)S(1)}, u32[]{:S(2)}, u32[]{:S(2)}) collective-permute-start(bf16[256,512]{1,0:T(8,128)(2,1)S(1)} %shard_map.71.own_ref), channel_id=1, source_target_pairs={{0,1},{1,0},{2,3},{3,2},{4,5},{5,4},{6,7},{7,6},{8,9},{9,8},{10,11... | collective-permute-start | bytes 786440 | tf_op jit(solution)/shard_map/ppermute | solution.py:293
  150.0 9.7 %collective-permute-start.4 = (bf16[2,128,256]{2,1,0:T(8,128)(2,1)S(1)}, bf16[2,128,256]{2,1,0:T(8,128)(2,1)S(1)}, u32[]{:S(2)}, u32[]{:S(2)}) collective-permute-start(bf16[2,128,256]{2,1,0:T(8,128)(2,1)S(1)} %get-tuple-element.21), channel_id=1, source_target_pairs={{0,256},{256,0},{1,257},{257,1},{2,258},{258,2},{3,259},{259,3},{4... | collective-permute-start | bytes 393224 | tf_op jit(solution)/shard_map/ppermute | solution.py:297
Sparse Core Ops, SparseCore 0:
  31.9 62.6 all-gather.2

commit v16 on v10

--- a/solution.py
+++ b/solution.py
@@ -193,15 +193,14 @@
     return on_chip(middle_kernel, jax.ShapeDtypeStruct((2 * ROWS, STREAMS), BF16), operands, 1 << 28)
 
 
-def backward_kernel(place_ref, own_ref, other_ref, weight_ref, out_ref):
-    core = place_ref[0]
+def backward_kernel(place_ref, terms_ref, weight_ref, out_ref):
     for part, cols in enumerate((slice(BACK, STREAMS), slice(0, BACK))):
-        terms = jnp.concatenate([own_ref[:, cols], other_ref[:, cols]], 1)
+        terms = jnp.concatenate([terms_ref[core, :, cols] for core in range(2)], 1)
         for y in range(2):
             for x in range(4):
                 weight = [
-                    jnp.concatenate([weight_ref[x % 2, y, x // 2, z, which, cols] for z in range(2)], 1)
-                    for which in (core, 1 - core)
+                    jnp.concatenate([weight_ref[x % 2, y, x // 2, z, core, cols] for z in range(2)], 1)
+                    for core in range(2)
                 ]
                 result = jnp.dot(terms, jnp.concatenate(weight, 0), preferred_element_type=F32)
                 for h in range(2):
@@ -290,9 +289,9 @@
     after = lax.ppermute(mixed, ("l", "z"), [(b, a) for a, b in ring])
 
     terms = middle(place, band, streams, gate, product, mixed, before, after)
-    other_terms = lax.ppermute(terms, "core", cross)
-
-    parts = swapped(backward(place, terms, other_terms, weight), ("ylo", "x"))
+    terms = lax.all_gather(terms, "core", axis=0)
+
+    parts = swapped(backward(place, terms, weight), ("ylo", "x"))
     mine, theirs = combine(place, parts)
     return finish(place, mine, lax.ppermute(theirs, "h", cross))
 

time: 169 us -> 168 us (level)
  starting transfers between devices: 36.9 us -> 33.8 us
  blocking collectives: 46.5 us -> 49.5 us
    ppermute x1 -> x0, starting transfers between devices: 3.13 us -> none  [local(): other_terms = lax.ppermute(terms, 'core', cross)]
    all_gather x0 -> x1, blocking collectives: none -> 3.04 us  [local(): terms = lax.all_gather(terms, 'core', axis=0)]
  transfers between devices with their start and end apart: 8 -> 7, of which waited for: 8 -> 7; matrix products, arithmetic and copies ran while one was open for 2% -> 2% of each run, Pallas kernels for 0% -> 0%
where the time goes in v16:
time: 168 us; the launch traced here: 165 us
  waiting for transfers between devices  52.1 us (31%)
  blocking collectives  49.5 us (29%)
  starting transfers between devices  33.8 us (20%)
  between operations  14.1 us (8%)
  Pallas kernels  11.8 us (7%)
  local copies, waits for them, and re-layouts  2.61 us (2%)
    all_to_all x2, blocking collectives, swapped(): return lax.all_to_all(value, axes, 0, 0, tiled=True)  46.5 us
    all_to_all x2, waiting for transfers between devices, swapped(): return lax.all_to_all(value, axes, 0, 0, tiled=True)  37.5 us
    all_to_all x2, starting transfers between devices, swapped(): return lax.all_to_all(value, axes, 0, 0, tiled=True)  11.8 us
    ppermute x1, starting transfers between devices, local(): after = lax.ppermute(mixed, ('l', 'z'), [(b, a) for a, b in ring])  9.29 us
    ppermute x1, starting transfers between devices, local(): return finish(place, mine, lax.ppermute(theirs, 'h', cross))  6.36 us
    all_gather x1, waiting for transfers between devices, local(): lax.all_gather(weight, ('z', 'core'), axis=0)  6.02 us
    pallas_call x4, Pallas kernels, on_chip(): pl.pallas_call(kernel, out_shape=out_shape, in_specs=[smem] + [vmem] * (l...  4.85 us
    pallas_call x1, Pallas kernels, forward(): pl.pallas_call(forward_kernel, out_shape=(shape(BACK, BF16), shape(HALF,...  4.69 us
  transfers between devices with their start and end apart: 7, of which 7 were waited for; matrix products, arithmetic and copies ran while one was open for 2% of the time, Pallas kernels for 0%

profile of v16, /device:TPU:1, one launch (start us, length us, event | category | flops | bytes accessed | tf_op | source)
XLA Modules:
  0.0 164.9 jit_solution(16600018910830589780)
XLA Ops:
  7.2 1.9 %shard_map.68 = bf16[4,512,128]{2,1,0:T(8,128)(2,1)} custom-call(bf16[3,128,256]{2,1,0:T(8,128)(2,1)} %in_ref.1, bf16[256,128]{1,0:T(8,128)(2,1)} %out_ref.1), custom_call_target="tpu_custom_call" | custom-call | tf_op jit(solution)/shard_map/pallas_call | solution.py:244
  9.0 7.6 %all-to-all-start = ((bf16[4,512,128]{2,1,0:T(8,128)(2,1)}), bf16[4,512,128]{2,1,0:T(8,128)(2,1)S(1)}, u32[]{:S(2)}, u32[]{:S(2)}) async-start(bf16[4,512,128]{2,1,0:T(8,128)(2,1)} %shard_map.68), calls=%async_computation | async-start | bytes 1048576 | tf_op jit(solution)/shard_map/all_to_all | solution.py:262
  16.7 0.9 pad_maximum_fusion
  17.6 13.3 %all-to-all-done = bf16[4,512,128]{2,1,0:T(8,128)(2,1)S(1)} async-done(((bf16[4,512,128]{2,1,0:T(8,128)(2,1)}), bf16[4,512,128]{2,1,0:T(8,128)(2,1)S(1)}, u32[]{:S(2)}, u32[]{:S(2)}) %all-to-all-start) | async-done | bytes 524320 | tf_op jit(solution)/shard_map/all_to_all | solution.py:262
  30.9 0.8 copy-done.1
  31.8 17.9 %all_to_all.20 = bf16[4,2,128,256]{3,2,1,0:T(8,128)(2,1)S(1)} all-to-all(bf16[4,2,128,256]{3,2,1,0:T(8,128)(2,1)S(1)} %broadcast_in_dim.6), channel_id=1, replica_groups=mesh['h'=2,'l'=2,'z'=8,'ylo'=2,'x'=4,'core'=2] {'h','ylo'}, dimensions={0} | all-to-all | bytes 1048576 | tf_op jit(solution)/shard_map/all_to_all | solution.py:262
  49.7 1.6 broadcast_in_dim.7
  51.3 4.1 %all-to-all-start.2 = ((bf16[4,4,2,128,256]{4,3,2,1,0:T(8,128)(2,1)}), bf16[4,4,2,128,256]{4,3,2,1,0:T(8,128)(2,1)S(1)}, u32[]{:S(2)}, u32[]{:S(2)}) async-start(bf16[4,4,2,128,256]{4,3,2,1,0:T(8,128)(2,1)} %broadcast_in_dim.7), calls=%async_computation.2 | async-start | bytes 4194304 | tf_op jit(solution)/shard_map/all_to_all | solution.py:262
  56.0 24.1 %all-to-all-done.2 = bf16[4,4,2,128,256]{4,3,2,1,0:T(8,128)(2,1)S(1)} async-done(((bf16[4,4,2,128,256]{4,3,2,1,0:T(8,128)(2,1)}), bf16[4,4,2,128,256]{4,3,2,1,0:T(8,128)(2,1)S(1)}, u32[]{:S(2)}, u32[]{:S(2)}) %all-to-all-start.2) | async-done | bytes 2097184 | tf_op jit(solution)/shard_map/all_to_all | solution.py:262
  80.2 4.4 %collective-permute-start = (bf16[4,2,2,2,128,256]{5,4,3,2,1,0:T(8,128)(2,1)S(1)}, bf16[4,2,2,2,128,256]{5,4,3,2,1,0:T(8,128)(2,1)}, u32[]{:S(2)}, u32[]{:S(2)}) collective-permute-start(bf16[4,2,2,2,128,256]{5,4,3,2,1,0:T(8,128)(2,1)S(1)} %bitcast.10), channel_id=1, source_target_pairs={{0,1},{1,0},{2,3},{3,2},{4,5},{5,4},{6,7},{7,6},{8,9},{9,8},{10,11... | collective-permute-start | bytes 6291464 | tf_op jit(solution)/shard_map/ppermute | solution.py:284
  84.7 3.9 %collective-permute-done.other_hbm = bf16[4,2,2,2,128,256]{5,4,3,2,1,0:T(8,128)(2,1)} collective-permute-done((bf16[4,2,2,2,128,256]{5,4,3,2,1,0:T(8,128)(2,1)S(1)}, bf16[4,2,2,2,128,256]{5,4,3,2,1,0:T(8,128)(2,1)}, u32[]{:S(2)}, u32[]{:S(2)}) %collective-permute-start) | collective-permute-done | bytes 2097184 | tf_op jit(solution)/shard_map/ppermute | solution.py:284
  88.6 6.0 %all-gather.4.cloned.1.call-done = bf16[64,512,128]{2,1,0:T(8,128)(2,1)} async-done(((bf16[4,512,128]{2,1,0:T(8,128)(2,1)}), bf16[64,512,128]{2,1,0:T(8,128)(2,1)}) %all-gather.4.cloned.1.call-update) | async-done | bytes 8388624 | tf_op jit(solution)/shard_map/all_gather | solution.py:277
  94.6 4.7 %shard_map.70 = (bf16[384,256]{1,0:T(8,128)(2,1)S(1)}, f32[128,256]{1,0:T(8,128)S(1)}, bf16[128,256]{1,0:T(8,128)(2,1)S(1)}, bf16[128,256]{1,0:T(8,128)(2,1)S(1)}, bf16[2,2,2,2,2,512,128]{6,5,4,3,2,1,0:T(8,128)(2,1)S(1)}) custom-call(s32[4]{0:T(128)S(1)} %pad_add_fusion.place_ref, bf16[4,2,2,2,128,256]{5,4,3,2,1,0:T(8,128)(2,1)S(1)} %bitcast.11, ...), custom_call_target="tpu_custom_call" | custom-call | flops 1073741824 | bytes 9437184 | tf_op jit(solution)/shard_map/pallas_call | solution.py:114
  99.3 1.9 %collective-permute-start.1 = (bf16[128,256]{1,0:T(8,128)(2,1)S(1)}, bf16[128,256]{1,0:T(8,128)(2,1)S(1)}, u32[]{:S(2)}, u32[]{:S(2)}) collective-permute-start(bf16[128,256]{1,0:T(8,128)(2,1)S(1)} %get-tuple-element.19.product_ref), channel_id=1, source_target_pairs={{0,16},{16,32},{32,48},{48,64},{64,80},{80,96},{96,112},{112,128},... | collective-permute-start | bytes 196616 | tf_op jit(solution)/shard_map/ppermute | solution.py:288
  101.2 9.3 %collective-permute-start.2 = (bf16[128,256]{1,0:T(8,128)(2,1)S(1)}, bf16[128,256]{1,0:T(8,128)(2,1)S(1)}, u32[]{:S(2)}, u32[]{:S(2)}) collective-permute-start(bf16[128,256]{1,0:T(8,128)(2,1)S(1)} %get-tuple-element.20.mixed_ref), channel_id=1, source_target_pairs={{16,0},{32,16},{48,32},{64,48},{80,64},{96,80},{112,96},{128,112},... | collective-permute-start | bytes 196616 | tf_op jit(solution)/shard_map/ppermute | solution.py:289
  110.7 1.1 collective-permute-done.2.after_ref
  111.8 1.0 shard_map.71
  112.9 3.0 %all-gather.1 = bf16[512,512]{1,0:T(8,128)(2,1)S(1)} all-gather(bf16[256,512]{1,0:T(8,128)(2,1)S(1)} %shard_map.71), channel_id=3, replica_groups=mesh['h'=2,'l'=2,'z'=8,'ylo'=2,'x'=4,'core'=2] {'core'}, dimensions={0}, use_global_device_ids=true | all-gather | bytes 786432 | tf_op jit(solution)/shard_map/all_gather | solution.py:292
  115.9 1.8 %shard_map.72 = bf16[8,2,2,128,256]{4,3,2,1,0:T(8,128)(2,1)S(1)} custom-call(s32[4]{0:T(128)S(1)} %pad_add_fusion.place_ref, bf16[2,256,512]{2,1,0:T(8,128)(2,1)S(1)} %bitcast.12, bf16[2,2,2,2,2,512,128]{6,5,4,3,2,1,0:T(8,128)(2,1)S(1)} %get-tuple-element.21.weight_ref), custom_call_target="tpu_custom_call" | custom-call | flops 1073741824 | bytes 1048576 | tf_op jit(solution)/shard_map/pallas_call | solution.py:182
  117.7 28.6 %all_to_all.21.parts_ref = bf16[8,2,2,128,256]{4,3,2,1,0:T(8,128)(2,1)S(1)} all-to-all(bf16[8,2,2,128,256]{4,3,2,1,0:T(8,128)(2,1)S(1)} %shard_map.72), channel_id=1, replica_groups=mesh['h'=2,'l'=2,'z'=8,'ylo'=2,'x'=4,'core'=2] {'ylo','x'}, dimensions={0} | all-to-all | bytes 4194304 | tf_op jit(solution)/shard_map/all_to_all | solution.py:262
  146.4 0.8 shard_map.73
  147.2 6.4 %collective-permute-start.3 = (bf16[2,128,256]{2,1,0:T(8,128)(2,1)S(1)}, bf16[2,128,256]{2,1,0:T(8,128)(2,1)S(1)}, u32[]{:S(2)}, u32[]{:S(2)}) collective-permute-start(bf16[2,128,256]{2,1,0:T(8,128)(2,1)S(1)} %get-tuple-element.23), channel_id=1, source_target_pairs={{0,256},{256,0},{1,257},{257,1},{2,258},{258,2},{3,259},{259,3},{4... | collective-permute-start | bytes 393224 | tf_op jit(solution)/shard_map/ppermute | solution.py:296
  153.5 3.4 %collective-permute-done.3.theirs_ref = bf16[2,128,256]{2,1,0:T(8,128)(2,1)S(1)} collective-permute-done((bf16[2,128,256]{2,1,0:T(8,128)(2,1)S(1)}, bf16[2,128,256]{2,1,0:T(8,128)(2,1)S(1)}, u32[]{:S(2)}, u32[]{:S(2)}) %collective-permute-start.3) | collective-permute-done | bytes 131104 | tf_op jit(solution)/shard_map/ppermute | solution.py:296
  156.9 1.2 shard_map.74
  (14 shorter events, 1.0 us)
Async XLA Ops:
  7.2 48.2 %copy-start = (f32[16,128]{1,0:T(8,128)S(1)}, f32[16,128]{1,0:T(8,128)}, u32[]{:S(2)}) copy-start(f32[16,128]{1,0:T(8,128)} %param.8) | copy-start | bytes 24580
  9.0 21.9 %all-to-all-start = ((bf16[4,512,128]{2,1,0:T(8,128)(2,1)}), bf16[4,512,128]{2,1,0:T(8,128)(2,1)S(1)}, u32[]{:S(2)}, u32[]{:S(2)}) async-start(bf16[4,512,128]{2,1,0:T(8,128)(2,1)} %shard_map.68), calls=%async_computation | async-start | bytes 1048576 | tf_op jit(solution)/shard_map/all_to_all | solution.py:262
  16.7 77.9 %all-gather.4.cloned.1.call-start = ((), (), s32[]{:S(2)}) async-start(), calls=%async_computation.4 | async-start | bytes 8912896 | tf_op jit(solution)/shard_map/all_gather | solution.py:277
  30.9 0.8 copy-start.1
  51.3 28.9 %all-to-all-start.2 = ((bf16[4,4,2,128,256]{4,3,2,1,0:T(8,128)(2,1)}), bf16[4,4,2,128,256]{4,3,2,1,0:T(8,128)(2,1)S(1)}, u32[]{:S(2)}, u32[]{:S(2)}) async-start(bf16[4,4,2,128,256]{4,3,2,1,0:T(8,128)(2,1)} %broadcast_in_dim.7), calls=%async_computation.2 | async-start | bytes 4194304 | tf_op jit(solution)/shard_map/all_to_all | solution.py:262
  80.2 8.4 %collective-permute-start = (bf16[4,2,2,2,128,256]{5,4,3,2,1,0:T(8,128)(2,1)S(1)}, bf16[4,2,2,2,128,256]{5,4,3,2,1,0:T(8,128)(2,1)}, u32[]{:S(2)}, u32[]{:S(2)}) collective-permute-start(bf16[4,2,2,2,128,256]{5,4,3,2,1,0:T(8,128)(2,1)S(1)} %bitcast.10), channel_id=1, source_target_pairs={{0,1},{1,0},{2,3},{3,2},{4,5},{5,4},{6,7},{7,6},{8,9},{9,8},{10,11... | collective-permute-start | bytes 6291464 | tf_op jit(solution)/shard_map/ppermute | solution.py:284
  99.3 11.4 %collective-permute-start.1 = (bf16[128,256]{1,0:T(8,128)(2,1)S(1)}, bf16[128,256]{1,0:T(8,128)(2,1)S(1)}, u32[]{:S(2)}, u32[]{:S(2)}) collective-permute-start(bf16[128,256]{1,0:T(8,128)(2,1)S(1)} %get-tuple-element.19.product_ref), channel_id=1, source_target_pairs={{0,16},{16,32},{32,48},{48,64},{64,80},{80,96},{96,112},{112,128},... | collective-permute-start | bytes 196616 | tf_op jit(solution)/shard_map/ppermute | solution.py:288
  101.2 10.6 %collective-permute-start.2 = (bf16[128,256]{1,0:T(8,128)(2,1)S(1)}, bf16[128,256]{1,0:T(8,128)(2,1)S(1)}, u32[]{:S(2)}, u32[]{:S(2)}) collective-permute-start(bf16[128,256]{1,0:T(8,128)(2,1)S(1)} %get-tuple-element.20.mixed_ref), channel_id=1, source_target_pairs={{16,0},{32,16},{48,32},{64,48},{80,64},{96,80},{112,96},{128,112},... | collective-permute-start | bytes 196616 | tf_op jit(solution)/shard_map/ppermute | solution.py:289
  147.2 9.7 %collective-permute-start.3 = (bf16[2,128,256]{2,1,0:T(8,128)(2,1)S(1)}, bf16[2,128,256]{2,1,0:T(8,128)(2,1)S(1)}, u32[]{:S(2)}, u32[]{:S(2)}) collective-permute-start(bf16[2,128,256]{2,1,0:T(8,128)(2,1)S(1)} %get-tuple-element.23), channel_id=1, source_target_pairs={{0,256},{256,0},{1,257},{257,1},{2,258},{258,2},{3,259},{259,3},{4... | collective-permute-start | bytes 393224 | tf_op jit(solution)/shard_map/ppermute | solution.py:296
Sparse Core Ops, SparseCore 0:
  31.9 62.6 all-gather.3

commit v17 on v16

--- a/solution.py
+++ b/solution.py
@@ -50,6 +50,8 @@
     gate_ref,
     product_ref,
     mixed_ref,
+    first_ref,
+    second_ref,
     back_ref,
     weight_ref,
     other_ref,
@@ -102,8 +104,13 @@
     streams_ref[...] = streams
     gate_ref[...] = grad_gate
     query, key, value = (streams[i * HALF : (i + 1) * HALF].astype(F32) for i in range(3))
-    product_ref[...] = (key * value).astype(BF16)
-    mixed_ref[...] = (grad_gate * query).astype(BF16)
+    product = (key * value).astype(BF16)
+    mixed = (grad_gate * query).astype(BF16)
+    product_ref[...] = product
+    mixed_ref[...] = mixed
+    even = lax.rem(place_ref[1], 2) == 0
+    first_ref[...] = jnp.where(even, product, mixed)
+    second_ref[...] = jnp.where(even, mixed, product)
     for copy in copies[8:]:
         copy.wait()
 
@@ -118,6 +125,8 @@
             shape(HALF, F32),
             shape(HALF, BF16),
             shape(HALF, BF16),
+            shape(HALF, BF16),
+            shape(HALF, BF16),
             jax.ShapeDtypeStruct((2, 2, 2, 2, 2, STREAMS, ROWS), BF16),
         ),
         in_specs=[
@@ -126,7 +135,7 @@
             pl.BlockSpec(memory_space=pl.ANY),
             pl.BlockSpec(memory_space=pl.ANY),
         ],
-        out_specs=(vmem,) * 5,
+        out_specs=(vmem,) * 7,
         scratch_shapes=[
             pltpu.VMEM((4, 2, 4, STREAMS, ROWS), BF16),
             pltpu.VMEM((4, 2, 2, 2, ROWS, FEATURES), BF16),
@@ -155,14 +164,17 @@
 
 
 def middle_kernel(
-    place_ref, band_ref, streams_ref, gate_ref, product_ref, mixed_ref, before_ref, after_ref, terms_ref
+    place_ref, band_ref, streams_ref, gate_ref, product_ref, mixed_ref, first_ref, second_ref, terms_ref
 ):
     first = place_ref[1] == 0
     last = place_ref[1] == 15
     lanes = [slice(s * ROWS, (s + 1) * ROWS) for s in range(2)]
-    product, mixed, before, after = (
-        [ref[:, lanes[s]] for s in range(2)] for ref in (product_ref, mixed_ref, before_ref, after_ref)
+    even = lax.rem(place_ref[1], 2) == 0
+    product, mixed, one, two = (
+        [ref[:, lanes[s]] for s in range(2)] for ref in (product_ref, mixed_ref, first_ref, second_ref)
     )
+    before = [jnp.where(even, two[s], one[s]) for s in range(2)]
+    after = [jnp.where(even, one[s], two[s]) for s in range(2)]
     zero = jnp.zeros_like(before[0])
     earlier = [jnp.where(first, zero, before[0]), jnp.where(first, before[0], before[1])]
     later = [jnp.where(last, after[1], after[0]), jnp.where(last, zero, after[1])]
@@ -283,12 +295,11 @@
     cross = [(0, 1), (1, 0)]
     other = lax.ppermute(values, "core", cross)
 
-    streams, gate, product, mixed, weight = forward(place, values, other, weight)
-    ring = [(n, (n + 1) % 16) for n in range(16)]
-    before = lax.ppermute(product, ("l", "z"), ring)
-    after = lax.ppermute(mixed, ("l", "z"), [(b, a) for a, b in ring])
-
-    terms = middle(place, band, streams, gate, product, mixed, before, after)
+    streams, gate, product, mixed, first, second, weight = forward(place, values, other, weight)
+    first = lax.ppermute(first, ("l", "z"), [(n, n ^ 1) for n in range(16)])
+    second = lax.ppermute(second, ("l", "z"), [(n, ((n + 1) ^ 1) - 1 & 15) for n in range(16)])
+
+    terms = middle(place, band, streams, gate, product, mixed, first, second)
     terms = lax.all_gather(terms, "core", axis=0)
 
     parts = swapped(backward(place, terms, weight), ("ylo", "x"))

time: 168 us -> 169 us (level)
  the two profiles are of different devices: /device:TPU:1 before, /device:TPU:16 now
where the time goes in v17:
time: 169 us
  waiting for transfers between devices  55.8 us (33%)
  blocking collectives  55.5 us (33%)
  starting transfers between devices  27.9 us (17%)
  between operations  14.1 us (8%)
  Pallas kernels  11.8 us (7%)
  local copies, waits for them, and re-layouts  2.61 us (2%)
    all_to_all x2, blocking collectives, swapped(): return lax.all_to_all(value, axes, 0, 0, tiled=True)  53.3 us
    all_to_all x2, waiting for transfers between devices, swapped(): return lax.all_to_all(value, axes, 0, 0, tiled=True)  37.5 us
    all_to_all x2, starting transfers between devices, swapped(): return lax.all_to_all(value, axes, 0, 0, tiled=True)  13.5 us
    ppermute x1, waiting for transfers between devices, local(): return finish(place, mine, lax.ppermute(theirs, 'h', cross))  7.62 us
    ppermute x1, starting transfers between devices, local(): lax.ppermute(second, ('l', 'z'), [(n, (n + 1 ^ 1) - 1 & 15) for n in rang...  5.8 us
    pallas_call x4, Pallas kernels, on_chip(): pl.pallas_call(kernel, out_shape=out_shape, in_specs=[smem] + [vmem] * (l...  4.85 us
    ppermute x1, starting transfers between devices, local(): return finish(place, mine, lax.ppermute(theirs, 'h', cross))  4.71 us
    pallas_call x1, Pallas kernels, forward(): pl.pallas_call(forward_kernel, out_shape=(shape(BACK, BF16), shape(HALF,...  4.69 us
  transfers between devices with their start and end apart: 7, of which 6 were waited for; matrix products, arithmetic and copies ran while one was open for 2% of the time, Pallas kernels for 0%

profile of v17, /device:TPU:16, one launch (start us, length us, event | category | flops | bytes accessed | tf_op | source)
XLA Modules:
  0.0 168.7 jit_solution(13089952178171710208)
XLA Ops:
  7.2 1.9 %shard_map.68 = bf16[4,512,128]{2,1,0:T(8,128)(2,1)} custom-call(bf16[3,128,256]{2,1,0:T(8,128)(2,1)} %in_ref.1, bf16[256,128]{1,0:T(8,128)(2,1)} %out_ref.1), custom_call_target="tpu_custom_call" | custom-call | tf_op jit(solution)/shard_map/pallas_call | solution.py:256
  9.0 9.1 %all-to-all-start = ((bf16[4,512,128]{2,1,0:T(8,128)(2,1)}), bf16[4,512,128]{2,1,0:T(8,128)(2,1)S(1)}, u32[]{:S(2)}, u32[]{:S(2)}) async-start(bf16[4,512,128]{2,1,0:T(8,128)(2,1)} %shard_map.68), calls=%async_computation | async-start | bytes 1048576 | tf_op jit(solution)/shard_map/all_to_all | solution.py:274
  18.2 0.9 pad_maximum_fusion
  19.1 12.5 %all-to-all-done = bf16[4,512,128]{2,1,0:T(8,128)(2,1)S(1)} async-done(((bf16[4,512,128]{2,1,0:T(8,128)(2,1)}), bf16[4,512,128]{2,1,0:T(8,128)(2,1)S(1)}, u32[]{:S(2)}, u32[]{:S(2)}) %all-to-all-start) | async-done | bytes 524320 | tf_op jit(solution)/shard_map/all_to_all | solution.py:274
  31.6 0.8 copy-done.1
  32.4 19.8 %all_to_all.20 = bf16[4,2,128,256]{3,2,1,0:T(8,128)(2,1)S(1)} all-to-all(bf16[4,2,128,256]{3,2,1,0:T(8,128)(2,1)S(1)} %broadcast_in_dim.6), channel_id=1, replica_groups=mesh['h'=2,'l'=2,'z'=8,'ylo'=2,'x'=4,'core'=2] {'h','ylo'}, dimensions={0} | all-to-all | bytes 1048576 | tf_op jit(solution)/shard_map/all_to_all | solution.py:274
  52.3 1.6 broadcast_in_dim.7
  53.9 4.4 %all-to-all-start.2 = ((bf16[4,4,2,128,256]{4,3,2,1,0:T(8,128)(2,1)}), bf16[4,4,2,128,256]{4,3,2,1,0:T(8,128)(2,1)S(1)}, u32[]{:S(2)}, u32[]{:S(2)}) async-start(bf16[4,4,2,128,256]{4,3,2,1,0:T(8,128)(2,1)} %broadcast_in_dim.7), calls=%async_computation.2 | async-start | bytes 4194304 | tf_op jit(solution)/shard_map/all_to_all | solution.py:274
  58.9 25.0 %all-to-all-done.2 = bf16[4,4,2,128,256]{4,3,2,1,0:T(8,128)(2,1)S(1)} async-done(((bf16[4,4,2,128,256]{4,3,2,1,0:T(8,128)(2,1)}), bf16[4,4,2,128,256]{4,3,2,1,0:T(8,128)(2,1)S(1)}, u32[]{:S(2)}, u32[]{:S(2)}) %all-to-all-start.2) | async-done | bytes 2097184 | tf_op jit(solution)/shard_map/all_to_all | solution.py:274
  83.9 1.9 %collective-permute-start = (bf16[4,2,2,2,128,256]{5,4,3,2,1,0:T(8,128)(2,1)S(1)}, bf16[4,2,2,2,128,256]{5,4,3,2,1,0:T(8,128)(2,1)}, u32[]{:S(2)}, u32[]{:S(2)}) collective-permute-start(bf16[4,2,2,2,128,256]{5,4,3,2,1,0:T(8,128)(2,1)S(1)} %bitcast.10), channel_id=1, source_target_pairs={{0,1},{1,0},{2,3},{3,2},{4,5},{5,4},{6,7},{7,6},{8,9},{9,8},{10,11... | collective-permute-start | bytes 6291464 | tf_op jit(solution)/shard_map/ppermute | solution.py:296
  85.9 4.2 %collective-permute-done.other_hbm = bf16[4,2,2,2,128,256]{5,4,3,2,1,0:T(8,128)(2,1)} collective-permute-done((bf16[4,2,2,2,128,256]{5,4,3,2,1,0:T(8,128)(2,1)S(1)}, bf16[4,2,2,2,128,256]{5,4,3,2,1,0:T(8,128)(2,1)}, u32[]{:S(2)}, u32[]{:S(2)}) %collective-permute-start) | collective-permute-done | bytes 2097184 | tf_op jit(solution)/shard_map/ppermute | solution.py:296
  90.1 3.1 %all-gather.4.cloned.1.call-done = bf16[64,512,128]{2,1,0:T(8,128)(2,1)} async-done(((bf16[4,512,128]{2,1,0:T(8,128)(2,1)}), bf16[64,512,128]{2,1,0:T(8,128)(2,1)}) %all-gather.4.cloned.1.call-update) | async-done | bytes 8388624 | tf_op jit(solution)/shard_map/all_gather | solution.py:289
  93.2 4.7 %shard_map.70 = (bf16[384,256]{1,0:T(8,128)(2,1)S(1)}, f32[128,256]{1,0:T(8,128)S(1)}, bf16[128,256]{1,0:T(8,128)(2,1)S(1)}, bf16[128,256]{1,0:T(8,128)(2,1)S(1)...) custom-call(s32[4]{0:T(128)S(1)} %pad_add_fusion.place_ref, ...), custom_call_target="tpu_custom_call" | custom-call | flops 1073741824 | bytes 9437184 | tf_op jit(solution)/shard_map/pallas_call | solution.py:121
  97.9 1.9 %collective-permute-start.1 = (bf16[128,256]{1,0:T(8,128)(2,1)S(1)}, bf16[128,256]{1,0:T(8,128)(2,1)S(1)}, u32[]{:S(2)}, u32[]{:S(2)}) collective-permute-start(bf16[128,256]{1,0:T(8,128)(2,1)S(1)} %get-tuple-element.23), channel_id=1, source_target_pairs={{0,16},{16,0},{32,48},{48,32},{64,80},{80,64},{96,112},{112,96},{1... | collective-permute-start | bytes 196616 | tf_op jit(solution)/shard_map/ppermute | solution.py:299
  99.8 5.8 %collective-permute-start.2 = (bf16[128,256]{1,0:T(8,128)(2,1)S(1)}, bf16[128,256]{1,0:T(8,128)(2,1)S(1)}, u32[]{:S(2)}, u32[]{:S(2)}) collective-permute-start(bf16[128,256]{1,0:T(8,128)(2,1)S(1)} %get-tuple-element.24), channel_id=1, source_target_pairs={{0,240},{16,32},{32,16},{48,64},{64,48},{80,96},{96,80},{112,128},... | collective-permute-start | bytes 196616 | tf_op jit(solution)/shard_map/ppermute | solution.py:300
  105.6 3.4 %collective-permute-done.2.second_ref = bf16[128,256]{1,0:T(8,128)(2,1)S(1)} collective-permute-done((bf16[128,256]{1,0:T(8,128)(2,1)S(1)}, bf16[128,256]{1,0:T(8,128)(2,1)S(1)}, u32[]{:S(2)}, u32[]{:S(2)}) %collective-permute-start.2) | collective-permute-done | bytes 65568 | tf_op jit(solution)/shard_map/ppermute | solution.py:300
  109.0 1.1 shard_map.71
  110.1 2.2 %all-gather.1 = bf16[512,512]{1,0:T(8,128)(2,1)S(1)} all-gather(bf16[256,512]{1,0:T(8,128)(2,1)S(1)} %shard_map.71), channel_id=3, replica_groups=mesh['h'=2,'l'=2,'z'=8,'ylo'=2,'x'=4,'core'=2] {'core'}, dimensions={0}, use_global_device_ids=true | all-gather | bytes 786432 | tf_op jit(solution)/shard_map/all_gather | solution.py:303
  112.3 1.8 %shard_map.72 = bf16[8,2,2,128,256]{4,3,2,1,0:T(8,128)(2,1)S(1)} custom-call(s32[4]{0:T(128)S(1)} %pad_add_fusion.place_ref, bf16[2,256,512]{2,1,0:T(8,128)(2,1)S(1)} %bitcast.12, bf16[2,2,2,2,2,512,128]{6,5,4,3,2,1,0:T(8,128)(2,1)S(1)} %get-tuple-element.25.weight_ref), custom_call_target="tpu_custom_call" | custom-call | flops 1073741824 | bytes 1048576 | tf_op jit(solution)/shard_map/pallas_call | solution.py:194
  114.1 33.5 %all_to_all.21.parts_ref = bf16[8,2,2,128,256]{4,3,2,1,0:T(8,128)(2,1)S(1)} all-to-all(bf16[8,2,2,128,256]{4,3,2,1,0:T(8,128)(2,1)S(1)} %shard_map.72), channel_id=1, replica_groups=mesh['h'=2,'l'=2,'z'=8,'ylo'=2,'x'=4,'core'=2] {'ylo','x'}, dimensions={0} | all-to-all | bytes 4194304 | tf_op jit(solution)/shard_map/all_to_all | solution.py:274
  147.5 0.8 shard_map.73
  148.3 4.7 %collective-permute-start.3 = (bf16[2,128,256]{2,1,0:T(8,128)(2,1)S(1)}, bf16[2,128,256]{2,1,0:T(8,128)(2,1)S(1)}, u32[]{:S(2)}, u32[]{:S(2)}) collective-permute-start(bf16[2,128,256]{2,1,0:T(8,128)(2,1)S(1)} %get-tuple-element.27), channel_id=1, source_target_pairs={{0,256},{256,0},{1,257},{257,1},{2,258},{258,2},{3,259},{259,3},{4... | collective-permute-start | bytes 393224 | tf_op jit(solution)/shard_map/ppermute | solution.py:307
  153.1 7.6 %collective-permute-done.3.theirs_ref = bf16[2,128,256]{2,1,0:T(8,128)(2,1)S(1)} collective-permute-done((bf16[2,128,256]{2,1,0:T(8,128)(2,1)S(1)}, bf16[2,128,256]{2,1,0:T(8,128)(2,1)S(1)}, u32[]{:S(2)}, u32[]{:S(2)}) %collective-permute-start.3) | collective-permute-done | bytes 131104 | tf_op jit(solution)/shard_map/ppermute | solution.py:307
  160.7 1.2 shard_map.74
  (14 shorter events, 0.7 us)
Async XLA Ops:
  7.2 51.1 %copy-start = (f32[16,128]{1,0:T(8,128)S(1)}, f32[16,128]{1,0:T(8,128)}, u32[]{:S(2)}) copy-start(f32[16,128]{1,0:T(8,128)} %param.8) | copy-start | bytes 24580
  9.0 22.5 %all-to-all-start = ((bf16[4,512,128]{2,1,0:T(8,128)(2,1)}), bf16[4,512,128]{2,1,0:T(8,128)(2,1)S(1)}, u32[]{:S(2)}, u32[]{:S(2)}) async-start(bf16[4,512,128]{2,1,0:T(8,128)(2,1)} %shard_map.68), calls=%async_computation | async-start | bytes 1048576 | tf_op jit(solution)/shard_map/all_to_all | solution.py:274
  18.2 75.0 %all-gather.4.cloned.1.call-start = ((), (), s32[]{:S(2)}) async-start(), calls=%async_computation.4 | async-start | bytes 8912896 | tf_op jit(solution)/shard_map/all_gather | solution.py:289
  31.6 0.8 copy-start.1
  53.9 30.0 %all-to-all-start.2 = ((bf16[4,4,2,128,256]{4,3,2,1,0:T(8,128)(2,1)}), bf16[4,4,2,128,256]{4,3,2,1,0:T(8,128)(2,1)S(1)}, u32[]{:S(2)}, u32[]{:S(2)}) async-start(bf16[4,4,2,128,256]{4,3,2,1,0:T(8,128)(2,1)} %broadcast_in_dim.7), calls=%async_computation.2 | async-start | bytes 4194304 | tf_op jit(solution)/shard_map/all_to_all | solution.py:274
  83.9 6.2 %collective-permute-start = (bf16[4,2,2,2,128,256]{5,4,3,2,1,0:T(8,128)(2,1)S(1)}, bf16[4,2,2,2,128,256]{5,4,3,2,1,0:T(8,128)(2,1)}, u32[]{:S(2)}, u32[]{:S(2)}) collective-permute-start(bf16[4,2,2,2,128,256]{5,4,3,2,1,0:T(8,128)(2,1)S(1)} %bitcast.10), channel_id=1, source_target_pairs={{0,1},{1,0},{2,3},{3,2},{4,5},{5,4},{6,7},{7,6},{8,9},{9,8},{10,11... | collective-permute-start | bytes 6291464 | tf_op jit(solution)/shard_map/ppermute | solution.py:296
  97.9 7.7 %collective-permute-start.1 = (bf16[128,256]{1,0:T(8,128)(2,1)S(1)}, bf16[128,256]{1,0:T(8,128)(2,1)S(1)}, u32[]{:S(2)}, u32[]{:S(2)}) collective-permute-start(bf16[128,256]{1,0:T(8,128)(2,1)S(1)} %get-tuple-element.23), channel_id=1, source_target_pairs={{0,16},{16,0},{32,48},{48,32},{64,80},{80,64},{96,112},{112,96},{1... | collective-permute-start | bytes 196616 | tf_op jit(solution)/shard_map/ppermute | solution.py:299
  99.8 9.2 %collective-permute-start.2 = (bf16[128,256]{1,0:T(8,128)(2,1)S(1)}, bf16[128,256]{1,0:T(8,128)(2,1)S(1)}, u32[]{:S(2)}, u32[]{:S(2)}) collective-permute-start(bf16[128,256]{1,0:T(8,128)(2,1)S(1)} %get-tuple-element.24), channel_id=1, source_target_pairs={{0,240},{16,32},{32,16},{48,64},{64,48},{80,96},{96,80},{112,128},... | collective-permute-start | bytes 196616 | tf_op jit(solution)/shard_map/ppermute | solution.py:300
  148.3 12.3 %collective-permute-start.3 = (bf16[2,128,256]{2,1,0:T(8,128)(2,1)S(1)}, bf16[2,128,256]{2,1,0:T(8,128)(2,1)S(1)}, u32[]{:S(2)}, u32[]{:S(2)}) collective-permute-start(bf16[2,128,256]{2,1,0:T(8,128)(2,1)S(1)} %get-tuple-element.27), channel_id=1, source_target_pairs={{0,256},{256,0},{1,257},{257,1},{2,258},{258,2},{3,259},{259,3},{4... | collective-permute-start | bytes 393224 | tf_op jit(solution)/shard_map/ppermute | solution.py:307
Sparse Core Ops, SparseCore 0:
  32.5 60.6 all-gather.3

commit v18 on v16

--- a/solution.py
+++ b/solution.py
@@ -272,8 +272,8 @@
     place = jnp.stack([core, position, lax.axis_index("x"), half]).astype(jnp.int32)
 
     weight = swapped(packed(in_weight, out_weight), ("h", "l"))
+    weight, tokens, cotangent = lax.optimization_barrier((weight, tokens, cotangent))
     values = jnp.stack([tokens, cotangent], 0)
-    weight, values = lax.optimization_barrier((weight, values))
     weight = lax.all_gather(weight, ("z", "core"), axis=0).reshape(8, 2, 4, STREAMS, ROWS)
 
     band = bands(lax.dynamic_slice_in_dim(mr_filter, half * GROUPS, GROUPS, 0))

time: 168 us -> 168 us (level)
  blocking collectives: 49.5 us -> 71.5 us
  waiting for transfers between devices: 52.1 us -> 38.7 us
  starting transfers between devices: 33.8 us -> 26.2 us
    all_to_all x2 -> x3, blocking collectives: 46.5 us -> 68.4 us  [swapped(): return lax.all_to_all(value, axes, 0, 0, tiled=True)]
    all_to_all x2 -> x1, waiting for transfers between devices: 37.5 us -> 24.1 us  [swapped(): return lax.all_to_all(value, axes, 0, 0, tiled=True)]
    all_to_all x2 -> x1, starting transfers between devices: 11.8 us -> 4.12 us  [swapped(): return lax.all_to_all(value, axes, 0, 0, tiled=True)]
  transfers between devices with their start and end apart: 7 -> 6, of which waited for: 7 -> 6; matrix products, arithmetic and copies ran while one was open for 2% -> 1% of each run, Pallas kernels for 0% -> 0%
where the time goes in v18:
time: 168 us; the launch traced here: 164 us
  blocking collectives  71.5 us (43%)
  waiting for transfers between devices  38.7 us (23%)
  starting transfers between devices  26.2 us (16%)
  between operations  14.2 us (8%)
  Pallas kernels  11.8 us (7%)
  local copies, waits for them, and re-layouts  1.81 us (1%)
    all_to_all x3, blocking collectives, swapped(): return lax.all_to_all(value, axes, 0, 0, tiled=True)  68.4 us
    all_to_all x1, waiting for transfers between devices, swapped(): return lax.all_to_all(value, axes, 0, 0, tiled=True)  24.1 us
    ppermute x1, starting transfers between devices, local(): after = lax.ppermute(mixed, ('l', 'z'), [(b, a) for a, b in ring])  9.32 us
    ppermute x1, starting transfers between devices, local(): return finish(place, mine, lax.ppermute(theirs, 'h', cross))  6.37 us
    all_gather x1, waiting for transfers between devices, local(): lax.all_gather(weight, ('z', 'core'), axis=0)  6.02 us
    pallas_call x4, Pallas kernels, on_chip(): pl.pallas_call(kernel, out_shape=out_shape, in_specs=[smem] + [vmem] * (l...  4.85 us
    pallas_call x1, Pallas kernels, forward(): pl.pallas_call(forward_kernel, out_shape=(shape(BACK, BF16), shape(HALF,...  4.69 us
    ppermute x1, starting transfers between devices, local(): other = lax.ppermute(values, 'core', cross)  4.43 us
  transfers between devices with their start and end apart: 6, of which 6 were waited for; matrix products, arithmetic and copies ran while one was open for 1% of the time, Pallas kernels for 0%

profile of v18, /device:TPU:1, one launch (start us, length us, event | category | flops | bytes accessed | tf_op | source)
XLA Modules:
  0.0 164.3 jit_solution(5840292994032743409)
XLA Ops:
  7.2 1.9 %shard_map.68 = bf16[4,512,128]{2,1,0:T(8,128)(2,1)} custom-call(bf16[3,128,256]{2,1,0:T(8,128)(2,1)} %in_ref.1, bf16[256,128]{1,0:T(8,128)(2,1)} %out_ref.1), custom_call_target="tpu_custom_call" | custom-call | tf_op jit(solution)/shard_map/pallas_call | solution.py:244
  9.1 21.7 %all_to_all.20 = bf16[4,512,128]{2,1,0:T(8,128)(2,1)} all-to-all(bf16[4,512,128]{2,1,0:T(8,128)(2,1)} %shard_map.68), channel_id=1, replica_groups=mesh['h'=2,'l'=2,'z'=8,'ylo'=2,'x'=4,'core'=2] {'h','l'}, dimensions={0} | all-to-all | bytes 1048576 | tf_op jit(solution)/shard_map/all_to_all | solution.py:262
  31.0 18.1 %all_to_all.21 = bf16[4,2,128,256]{3,2,1,0:T(8,128)(2,1)S(1)} all-to-all(bf16[4,2,128,256]{3,2,1,0:T(8,128)(2,1)S(1)} %broadcast_in_dim.6), channel_id=1, replica_groups=mesh['h'=2,'l'=2,'z'=8,'ylo'=2,'x'=4,'core'=2] {'h','ylo'}, dimensions={0} | all-to-all | bytes 1048576 | tf_op jit(solution)/shard_map/all_to_all | solution.py:262
  49.1 1.6 broadcast_in_dim.7
  50.7 4.1 %all-to-all-start.2 = ((bf16[4,4,2,128,256]{4,3,2,1,0:T(8,128)(2,1)}), bf16[4,4,2,128,256]{4,3,2,1,0:T(8,128)(2,1)S(1)}, u32[]{:S(2)}, u32[]{:S(2)}) async-start(bf16[4,4,2,128,256]{4,3,2,1,0:T(8,128)(2,1)} %broadcast_in_dim.7), calls=%async_computation.2 | async-start | bytes 4194304 | tf_op jit(solution)/shard_map/all_to_all | solution.py:262
  55.1 0.4 shard_map.69.band_ref
  55.4 24.1 %all-to-all-done.2 = bf16[4,4,2,128,256]{4,3,2,1,0:T(8,128)(2,1)S(1)} async-done(((bf16[4,4,2,128,256]{4,3,2,1,0:T(8,128)(2,1)}), bf16[4,4,2,128,256]{4,3,2,1,0:T(8,128)(2,1)S(1)}, u32[]{:S(2)}, u32[]{:S(2)}) %all-to-all-start.2) | async-done | bytes 2097184 | tf_op jit(solution)/shard_map/all_to_all | solution.py:262
  79.6 4.4 %collective-permute-start = (bf16[4,2,2,2,128,256]{5,4,3,2,1,0:T(8,128)(2,1)S(1)}, bf16[4,2,2,2,128,256]{5,4,3,2,1,0:T(8,128)(2,1)}, u32[]{:S(2)}, u32[]{:S(2)}) collective-permute-start(bf16[4,2,2,2,128,256]{5,4,3,2,1,0:T(8,128)(2,1)S(1)} %bitcast.10), channel_id=1, source_target_pairs={{0,1},{1,0},{2,3},{3,2},{4,5},{5,4},{6,7},{7,6},{8,9},{9,8},{10,11... | collective-permute-start | bytes 6291464 | tf_op jit(solution)/shard_map/ppermute | solution.py:284
  84.0 0.1 pad_add_fusion.place_ref
  84.1 3.9 %collective-permute-done.other_hbm = bf16[4,2,2,2,128,256]{5,4,3,2,1,0:T(8,128)(2,1)} collective-permute-done((bf16[4,2,2,2,128,256]{5,4,3,2,1,0:T(8,128)(2,1)S(1)}, bf16[4,2,2,2,128,256]{5,4,3,2,1,0:T(8,128)(2,1)}, u32[]{:S(2)}, u32[]{:S(2)}) %collective-permute-start) | collective-permute-done | bytes 2097184 | tf_op jit(solution)/shard_map/ppermute | solution.py:284
  88.0 6.0 %all-gather.4.cloned.1.call-done = bf16[64,512,128]{2,1,0:T(8,128)(2,1)} async-done(((bf16[4,512,128]{2,1,0:T(8,128)(2,1)}), bf16[64,512,128]{2,1,0:T(8,128)(2,1)}) %all-gather.4.cloned.1.call-update) | async-done | bytes 8388624 | tf_op jit(solution)/shard_map/all_gather | solution.py:277
  94.0 4.7 %shard_map.70 = (bf16[384,256]{1,0:T(8,128)(2,1)S(1)}, f32[128,256]{1,0:T(8,128)S(1)}, bf16[128,256]{1,0:T(8,128)(2,1)S(1)}, bf16[128,256]{1,0:T(8,128)(2,1)S(1)}, bf16[2,2,2,2,2,512,128]{6,5,4,3,2,1,0:T(8,128)(2,1)S(1)}) custom-call(s32[4]{0:T(128)S(1)} %pad_add_fusion.place_ref, bf16[4,2,2,2,128,256]{5,4,3,2,1,0:T(8,128)(2,1)S(1)} %bitcast.11, ...), custom_call_target="tpu_custom_call" | custom-call | flops 1073741824 | bytes 9437184 | tf_op jit(solution)/shard_map/pallas_call | solution.py:114
  98.7 1.9 %collective-permute-start.1 = (bf16[128,256]{1,0:T(8,128)(2,1)S(1)}, bf16[128,256]{1,0:T(8,128)(2,1)S(1)}, u32[]{:S(2)}, u32[]{:S(2)}) collective-permute-start(bf16[128,256]{1,0:T(8,128)(2,1)S(1)} %get-tuple-element.21.product_ref), channel_id=1, source_target_pairs={{0,16},{16,32},{32,48},{48,64},{64,80},{80,96},{96,112},{112,128},... | collective-permute-start | bytes 196616 | tf_op jit(solution)/shard_map/ppermute | solution.py:288
  100.6 9.3 %collective-permute-start.2 = (bf16[128,256]{1,0:T(8,128)(2,1)S(1)}, bf16[128,256]{1,0:T(8,128)(2,1)S(1)}, u32[]{:S(2)}, u32[]{:S(2)}) collective-permute-start(bf16[128,256]{1,0:T(8,128)(2,1)S(1)} %get-tuple-element.22.mixed_ref), channel_id=1, source_target_pairs={{16,0},{32,16},{48,32},{64,48},{80,64},{96,80},{112,96},{128,112},... | collective-permute-start | bytes 196616 | tf_op jit(solution)/shard_map/ppermute | solution.py:289
  110.0 0.2 collective-permute-done.1.before_ref
  110.2 1.1 collective-permute-done.2.after_ref
  111.3 1.1 shard_map.71
  112.3 3.0 %all-gather.1 = bf16[512,512]{1,0:T(8,128)(2,1)S(1)} all-gather(bf16[256,512]{1,0:T(8,128)(2,1)S(1)} %shard_map.71), channel_id=3, replica_groups=mesh['h'=2,'l'=2,'z'=8,'ylo'=2,'x'=4,'core'=2] {'core'}, dimensions={0}, use_global_device_ids=true | all-gather | bytes 786432 | tf_op jit(solution)/shard_map/all_gather | solution.py:292
  115.4 1.8 %shard_map.72 = bf16[8,2,2,128,256]{4,3,2,1,0:T(8,128)(2,1)S(1)} custom-call(s32[4]{0:T(128)S(1)} %pad_add_fusion.place_ref, bf16[2,256,512]{2,1,0:T(8,128)(2,1)S(1)} %bitcast.12, bf16[2,2,2,2,2,512,128]{6,5,4,3,2,1,0:T(8,128)(2,1)S(1)} %get-tuple-element.23.weight_ref), custom_call_target="tpu_custom_call" | custom-call | flops 1073741824 | bytes 1048576 | tf_op jit(solution)/shard_map/pallas_call | solution.py:182
  117.2 28.6 %all_to_all.22.parts_ref = bf16[8,2,2,128,256]{4,3,2,1,0:T(8,128)(2,1)S(1)} all-to-all(bf16[8,2,2,128,256]{4,3,2,1,0:T(8,128)(2,1)S(1)} %shard_map.72), channel_id=1, replica_groups=mesh['h'=2,'l'=2,'z'=8,'ylo'=2,'x'=4,'core'=2] {'ylo','x'}, dimensions={0} | all-to-all | bytes 4194304 | tf_op jit(solution)/shard_map/all_to_all | solution.py:262
  145.8 0.8 shard_map.73
  146.6 6.4 %collective-permute-start.3 = (bf16[2,128,256]{2,1,0:T(8,128)(2,1)S(1)}, bf16[2,128,256]{2,1,0:T(8,128)(2,1)S(1)}, u32[]{:S(2)}, u32[]{:S(2)}) collective-permute-start(bf16[2,128,256]{2,1,0:T(8,128)(2,1)S(1)} %get-tuple-element.25), channel_id=1, source_target_pairs={{0,256},{256,0},{1,257},{257,1},{2,258},{258,2},{3,259},{259,3},{4... | collective-permute-start | bytes 393224 | tf_op jit(solution)/shard_map/ppermute | solution.py:296
  152.9 3.3 %collective-permute-done.3.theirs_ref = bf16[2,128,256]{2,1,0:T(8,128)(2,1)S(1)} collective-permute-done((bf16[2,128,256]{2,1,0:T(8,128)(2,1)S(1)}, bf16[2,128,256]{2,1,0:T(8,128)(2,1)S(1)}, u32[]{:S(2)}, u32[]{:S(2)}) %collective-permute-start.3) | collective-permute-done | bytes 131104 | tf_op jit(solution)/shard_map/ppermute | solution.py:296
  156.3 1.2 shard_map.74
  (15 shorter events, 0.4 us)
Async XLA Ops:
  7.2 47.7 %copy-start = (f32[16,128]{1,0:T(8,128)S(1)}, f32[16,128]{1,0:T(8,128)}, u32[]{:S(2)}) copy-start(f32[16,128]{1,0:T(8,128)} %param.8) | copy-start | bytes 24580
  7.2 23.7 %copy-start.1 = (bf16[128,256]{1,0:T(8,128)(2,1)S(1)}, bf16[128,256]{1,0:T(8,128)(2,1)}, u32[]{:S(2)}) copy-start(bf16[128,256]{1,0:T(8,128)(2,1)} %param.9) | copy-start | bytes 196612
  7.2 23.7 %copy-start.2 = (bf16[128,256]{1,0:T(8,128)(2,1)S(1)}, bf16[128,256]{1,0:T(8,128)(2,1)}, u32[]{:S(2)}) copy-start(bf16[128,256]{1,0:T(8,128)(2,1)} %param.5) | copy-start | bytes 196612
  7.2 86.8 %all-gather.4.cloned.1.call-start = ((), (), s32[]{:S(2)}) async-start(), calls=%async_computation.4 | async-start | bytes 8912896 | tf_op jit(solution)/shard_map/all_gather | solution.py:277
  50.7 28.9 %all-to-all-start.2 = ((bf16[4,4,2,128,256]{4,3,2,1,0:T(8,128)(2,1)}), bf16[4,4,2,128,256]{4,3,2,1,0:T(8,128)(2,1)S(1)}, u32[]{:S(2)}, u32[]{:S(2)}) async-start(bf16[4,4,2,128,256]{4,3,2,1,0:T(8,128)(2,1)} %broadcast_in_dim.7), calls=%async_computation.2 | async-start | bytes 4194304 | tf_op jit(solution)/shard_map/all_to_all | solution.py:262
  79.6 8.4 %collective-permute-start = (bf16[4,2,2,2,128,256]{5,4,3,2,1,0:T(8,128)(2,1)S(1)}, bf16[4,2,2,2,128,256]{5,4,3,2,1,0:T(8,128)(2,1)}, u32[]{:S(2)}, u32[]{:S(2)}) collective-permute-start(bf16[4,2,2,2,128,256]{5,4,3,2,1,0:T(8,128)(2,1)S(1)} %bitcast.10), channel_id=1, source_target_pairs={{0,1},{1,0},{2,3},{3,2},{4,5},{5,4},{6,7},{7,6},{8,9},{9,8},{10,11... | collective-permute-start | bytes 6291464 | tf_op jit(solution)/shard_map/ppermute | solution.py:284
  98.7 11.5 %collective-permute-start.1 = (bf16[128,256]{1,0:T(8,128)(2,1)S(1)}, bf16[128,256]{1,0:T(8,128)(2,1)S(1)}, u32[]{:S(2)}, u32[]{:S(2)}) collective-permute-start(bf16[128,256]{1,0:T(8,128)(2,1)S(1)} %get-tuple-element.21.product_ref), channel_id=1, source_target_pairs={{0,16},{16,32},{32,48},{48,64},{64,80},{80,96},{96,112},{112,128},... | collective-permute-start | bytes 196616 | tf_op jit(solution)/shard_map/ppermute | solution.py:288
  100.6 10.6 %collective-permute-start.2 = (bf16[128,256]{1,0:T(8,128)(2,1)S(1)}, bf16[128,256]{1,0:T(8,128)(2,1)S(1)}, u32[]{:S(2)}, u32[]{:S(2)}) collective-permute-start(bf16[128,256]{1,0:T(8,128)(2,1)S(1)} %get-tuple-element.22.mixed_ref), channel_id=1, source_target_pairs={{16,0},{32,16},{48,32},{64,48},{80,64},{96,80},{112,96},{128,112},... | collective-permute-start | bytes 196616 | tf_op jit(solution)/shard_map/ppermute | solution.py:289
  146.6 9.7 %collective-permute-start.3 = (bf16[2,128,256]{2,1,0:T(8,128)(2,1)S(1)}, bf16[2,128,256]{2,1,0:T(8,128)(2,1)S(1)}, u32[]{:S(2)}, u32[]{:S(2)}) collective-permute-start(bf16[2,128,256]{2,1,0:T(8,128)(2,1)S(1)} %get-tuple-element.25), channel_id=1, source_target_pairs={{0,256},{256,0},{1,257},{257,1},{2,258},{258,2},{3,259},{259,3},{4... | collective-permute-start | bytes 393224 | tf_op jit(solution)/shard_map/ppermute | solution.py:296
Sparse Core Ops, SparseCore 0:
  31.0 62.9 all-gather.3

commit v19 on v18

--- a/solution.py
+++ b/solution.py
@@ -62,7 +62,7 @@
         for y in range(2):
             copies.append(
                 pltpu.make_async_copy(
-                    weight_hbm.at[pl.ds((x % 2) * 4, 4), core, 2 * y + x // 2],
+                    weight_hbm.at[pl.ds((x % 2) * 4 + 2 * (1 - core), 2), core, 2 * y + x // 2],
                     weight_ref.at[x, y],
                     arrived.at[2 * x + y],
                 )
@@ -76,36 +76,38 @@
                     arrived.at[8 + 2 * x + y],
                 )
             )
+    for copy in copies[8:]:
+        copy.start()
     for x in range(4):
         others[x].start()
         copies[2 * x].start()
         copies[2 * x + 1].start()
-    for copy in copies[8:]:
-        copy.start()
     streams, grad_gate = 0.0, 0.0
     contract = (((1,), (1,)), ((), ()))
-    for x in range(4):
-        tokens, cotangent, weight = [], [], []
-        others[x].wait()
-        copies[2 * x].wait()
-        copies[2 * x + 1].wait()
-        for values_ref, which in ((own_ref, core), (other_ref, 1 - core)):
+    for values_ref in (own_ref, other_ref):
+        for x in range(4):
+            tokens, cotangent, weight = [], [], []
+            if values_ref is other_ref:
+                others[x].wait()
             for y in range(2):
+                if values_ref is own_ref:
+                    copies[8 + 2 * x + y].wait()
+                    weight += [back_ref[x % 2, y, x // 2, z, core] for z in range(2)]
+                else:
+                    copies[2 * x + y].wait()
+                    weight += [weight_ref[x, y, z] for z in range(2)]
                 tokens.append(values_ref[x, :, y, 0].reshape(2 * ROWS, FEATURES))
                 cotangent.append(values_ref[x, :, y, 1].reshape(2 * ROWS, FEATURES))
-                weight += [weight_ref[x, y, 2 * which + z] for z in range(2)]
-        tokens, cotangent = jnp.concatenate(tokens, 1), jnp.concatenate(cotangent, 1)
-        weight = jnp.concatenate(weight, 1)
-        streams += lax.dot_general(weight[:BACK], tokens, contract, preferred_element_type=F32)
-        grad_gate += lax.dot_general(weight[BACK:], cotangent, contract, preferred_element_type=F32)
+            tokens, cotangent = jnp.concatenate(tokens, 1), jnp.concatenate(cotangent, 1)
+            weight = jnp.concatenate(weight, 1)
+            streams += lax.dot_general(weight[:BACK], tokens, contract, preferred_element_type=F32)
+            grad_gate += lax.dot_general(weight[BACK:], cotangent, contract, preferred_element_type=F32)
     streams = streams.astype(BF16)
     streams_ref[...] = streams
     gate_ref[...] = grad_gate
     query, key, value = (streams[i * HALF : (i + 1) * HALF].astype(F32) for i in range(3))
     product_ref[...] = (key * value).astype(BF16)
     mixed_ref[...] = (grad_gate * query).astype(BF16)
-    for copy in copies[8:]:
-        copy.wait()
 
 
 def forward(place, own, other, weight):
@@ -128,7 +130,7 @@
         ],
         out_specs=(vmem,) * 5,
         scratch_shapes=[
-            pltpu.VMEM((4, 2, 4, STREAMS, ROWS), BF16),
+            pltpu.VMEM((4, 2, 2, STREAMS, ROWS), BF16),
             pltpu.VMEM((4, 2, 2, 2, ROWS, FEATURES), BF16),
             pltpu.SemaphoreType.DMA((20,)),
         ],

time: 168 us -> 168 us (level)
  no operation moved by 1% of the time
where the time goes in v19:
time: 168 us; the launch traced here: 164 us
  blocking collectives  71.5 us (43%)
  waiting for transfers between devices  38.7 us (23%)
  starting transfers between devices  26.2 us (16%)
  between operations  14.2 us (8%)
  Pallas kernels  11.9 us (7%)
  local copies, waits for them, and re-layouts  1.81 us (1%)
    all_to_all x3, blocking collectives, swapped(): return lax.all_to_all(value, axes, 0, 0, tiled=True)  68.4 us
    all_to_all x1, waiting for transfers between devices, swapped(): return lax.all_to_all(value, axes, 0, 0, tiled=True)  24.1 us
    ppermute x1, starting transfers between devices, local(): after = lax.ppermute(mixed, ('l', 'z'), [(b, a) for a, b in ring])  9.33 us
    ppermute x1, starting transfers between devices, local(): return finish(place, mine, lax.ppermute(theirs, 'h', cross))  6.37 us
    all_gather x1, waiting for transfers between devices, local(): lax.all_gather(weight, ('z', 'core'), axis=0)  6.02 us
    pallas_call x4, Pallas kernels, on_chip(): pl.pallas_call(kernel, out_shape=out_shape, in_specs=[smem] + [vmem] * (l...  4.85 us
    pallas_call x1, Pallas kernels, forward(): pl.pallas_call(forward_kernel, out_shape=(shape(BACK, BF16), shape(HALF,...  4.82 us
    ppermute x1, starting transfers between devices, local(): other = lax.ppermute(values, 'core', cross)  4.43 us
  transfers between devices with their start and end apart: 6, of which 6 were waited for; matrix products, arithmetic and copies ran while one was open for 1% of the time, Pallas kernels for 0%

profile of v19, /device:TPU:1, one launch (start us, length us, event | category | flops | bytes accessed | tf_op | source)
XLA Modules:
  0.0 164.5 jit_solution(7591550335029864885)
XLA Ops:
  7.2 1.9 %shard_map.68 = bf16[4,512,128]{2,1,0:T(8,128)(2,1)} custom-call(bf16[3,128,256]{2,1,0:T(8,128)(2,1)} %in_ref.1, bf16[256,128]{1,0:T(8,128)(2,1)} %out_ref.1), custom_call_target="tpu_custom_call" | custom-call | tf_op jit(solution)/shard_map/pallas_call | solution.py:246
  9.1 21.7 %all_to_all.20 = bf16[4,512,128]{2,1,0:T(8,128)(2,1)} all-to-all(bf16[4,512,128]{2,1,0:T(8,128)(2,1)} %shard_map.68), channel_id=1, replica_groups=mesh['h'=2,'l'=2,'z'=8,'ylo'=2,'x'=4,'core'=2] {'h','l'}, dimensions={0} | all-to-all | bytes 1048576 | tf_op jit(solution)/shard_map/all_to_all | solution.py:264
  31.0 18.1 %all_to_all.21 = bf16[4,2,128,256]{3,2,1,0:T(8,128)(2,1)S(1)} all-to-all(bf16[4,2,128,256]{3,2,1,0:T(8,128)(2,1)S(1)} %broadcast_in_dim.6), channel_id=1, replica_groups=mesh['h'=2,'l'=2,'z'=8,'ylo'=2,'x'=4,'core'=2] {'h','ylo'}, dimensions={0} | all-to-all | bytes 1048576 | tf_op jit(solution)/shard_map/all_to_all | solution.py:264
  49.1 1.6 broadcast_in_dim.7
  50.7 4.1 %all-to-all-start.2 = ((bf16[4,4,2,128,256]{4,3,2,1,0:T(8,128)(2,1)}), bf16[4,4,2,128,256]{4,3,2,1,0:T(8,128)(2,1)S(1)}, u32[]{:S(2)}, u32[]{:S(2)}) async-start(bf16[4,4,2,128,256]{4,3,2,1,0:T(8,128)(2,1)} %broadcast_in_dim.7), calls=%async_computation.2 | async-start | bytes 4194304 | tf_op jit(solution)/shard_map/all_to_all | solution.py:264
  55.1 0.4 shard_map.69.band_ref
  55.4 24.1 %all-to-all-done.2 = bf16[4,4,2,128,256]{4,3,2,1,0:T(8,128)(2,1)S(1)} async-done(((bf16[4,4,2,128,256]{4,3,2,1,0:T(8,128)(2,1)}), bf16[4,4,2,128,256]{4,3,2,1,0:T(8,128)(2,1)S(1)}, u32[]{:S(2)}, u32[]{:S(2)}) %all-to-all-start.2) | async-done | bytes 2097184 | tf_op jit(solution)/shard_map/all_to_all | solution.py:264
  79.6 4.4 %collective-permute-start = (bf16[4,2,2,2,128,256]{5,4,3,2,1,0:T(8,128)(2,1)S(1)}, bf16[4,2,2,2,128,256]{5,4,3,2,1,0:T(8,128)(2,1)}, u32[]{:S(2)}, u32[]{:S(2)}) collective-permute-start(bf16[4,2,2,2,128,256]{5,4,3,2,1,0:T(8,128)(2,1)S(1)} %bitcast.10), channel_id=1, source_target_pairs={{0,1},{1,0},{2,3},{3,2},{4,5},{5,4},{6,7},{7,6},{8,9},{9,8},{10,11... | collective-permute-start | bytes 6291464 | tf_op jit(solution)/shard_map/ppermute | solution.py:286
  84.0 0.1 pad_add_fusion.place_ref
  84.1 3.9 %collective-permute-done.other_hbm = bf16[4,2,2,2,128,256]{5,4,3,2,1,0:T(8,128)(2,1)} collective-permute-done((bf16[4,2,2,2,128,256]{5,4,3,2,1,0:T(8,128)(2,1)S(1)}, bf16[4,2,2,2,128,256]{5,4,3,2,1,0:T(8,128)(2,1)}, u32[]{:S(2)}, u32[]{:S(2)}) %collective-permute-start) | collective-permute-done | bytes 2097184 | tf_op jit(solution)/shard_map/ppermute | solution.py:286
  88.0 6.0 %all-gather.4.cloned.1.call-done = bf16[64,512,128]{2,1,0:T(8,128)(2,1)} async-done(((bf16[4,512,128]{2,1,0:T(8,128)(2,1)}), bf16[64,512,128]{2,1,0:T(8,128)(2,1)}) %all-gather.4.cloned.1.call-update) | async-done | bytes 8388624 | tf_op jit(solution)/shard_map/all_gather | solution.py:279
  94.0 4.8 %shard_map.70 = (bf16[384,256]{1,0:T(8,128)(2,1)S(1)}, f32[128,256]{1,0:T(8,128)S(1)}, bf16[128,256]{1,0:T(8,128)(2,1)S(1)}, bf16[128,256]{1,0:T(8,128)(2,1)S(1)}, bf16[2,2,2,2,2,512,128]{6,5,4,3,2,1,0:T(8,128)(2,1)S(1)}) custom-call(s32[4]{0:T(128)S(1)} %pad_add_fusion.place_ref, bf16[4,2,2,2,128,256]{5,4,3,2,1,0:T(8,128)(2,1)S(1)} %bitcast.11, ...), custom_call_target="tpu_custom_call" | custom-call | flops 1073741824 | bytes 9437184 | tf_op jit(solution)/shard_map/pallas_call | solution.py:116
  98.8 1.9 %collective-permute-start.1 = (bf16[128,256]{1,0:T(8,128)(2,1)S(1)}, bf16[128,256]{1,0:T(8,128)(2,1)S(1)}, u32[]{:S(2)}, u32[]{:S(2)}) collective-permute-start(bf16[128,256]{1,0:T(8,128)(2,1)S(1)} %get-tuple-element.21.product_ref), channel_id=1, source_target_pairs={{0,16},{16,32},{32,48},{48,64},{64,80},{80,96},{96,112},{112,128},... | collective-permute-start | bytes 196616 | tf_op jit(solution)/shard_map/ppermute | solution.py:290
  100.8 9.3 %collective-permute-start.2 = (bf16[128,256]{1,0:T(8,128)(2,1)S(1)}, bf16[128,256]{1,0:T(8,128)(2,1)S(1)}, u32[]{:S(2)}, u32[]{:S(2)}) collective-permute-start(bf16[128,256]{1,0:T(8,128)(2,1)S(1)} %get-tuple-element.22.mixed_ref), channel_id=1, source_target_pairs={{16,0},{32,16},{48,32},{64,48},{80,64},{96,80},{112,96},{128,112},... | collective-permute-start | bytes 196616 | tf_op jit(solution)/shard_map/ppermute | solution.py:291
  110.1 0.2 collective-permute-done.1.before_ref
  110.3 1.1 collective-permute-done.2.after_ref
  111.4 1.0 shard_map.71
  112.5 3.0 %all-gather.1 = bf16[512,512]{1,0:T(8,128)(2,1)S(1)} all-gather(bf16[256,512]{1,0:T(8,128)(2,1)S(1)} %shard_map.71), channel_id=3, replica_groups=mesh['h'=2,'l'=2,'z'=8,'ylo'=2,'x'=4,'core'=2] {'core'}, dimensions={0}, use_global_device_ids=true | all-gather | bytes 786432 | tf_op jit(solution)/shard_map/all_gather | solution.py:294
  115.5 1.8 %shard_map.72 = bf16[8,2,2,128,256]{4,3,2,1,0:T(8,128)(2,1)S(1)} custom-call(s32[4]{0:T(128)S(1)} %pad_add_fusion.place_ref, bf16[2,256,512]{2,1,0:T(8,128)(2,1)S(1)} %bitcast.12, bf16[2,2,2,2,2,512,128]{6,5,4,3,2,1,0:T(8,128)(2,1)S(1)} %get-tuple-element.23.weight_ref), custom_call_target="tpu_custom_call" | custom-call | flops 1073741824 | bytes 1048576 | tf_op jit(solution)/shard_map/pallas_call | solution.py:184
  117.3 28.6 %all_to_all.22.parts_ref = bf16[8,2,2,128,256]{4,3,2,1,0:T(8,128)(2,1)S(1)} all-to-all(bf16[8,2,2,128,256]{4,3,2,1,0:T(8,128)(2,1)S(1)} %shard_map.72), channel_id=1, replica_groups=mesh['h'=2,'l'=2,'z'=8,'ylo'=2,'x'=4,'core'=2] {'ylo','x'}, dimensions={0} | all-to-all | bytes 4194304 | tf_op jit(solution)/shard_map/all_to_all | solution.py:264
  145.9 0.8 shard_map.73
  146.7 6.4 %collective-permute-start.3 = (bf16[2,128,256]{2,1,0:T(8,128)(2,1)S(1)}, bf16[2,128,256]{2,1,0:T(8,128)(2,1)S(1)}, u32[]{:S(2)}, u32[]{:S(2)}) collective-permute-start(bf16[2,128,256]{2,1,0:T(8,128)(2,1)S(1)} %get-tuple-element.25), channel_id=1, source_target_pairs={{0,256},{256,0},{1,257},{257,1},{2,258},{258,2},{3,259},{259,3},{4... | collective-permute-start | bytes 393224 | tf_op jit(solution)/shard_map/ppermute | solution.py:298
  153.1 3.3 %collective-permute-done.3.theirs_ref = bf16[2,128,256]{2,1,0:T(8,128)(2,1)S(1)} collective-permute-done((bf16[2,128,256]{2,1,0:T(8,128)(2,1)S(1)}, bf16[2,128,256]{2,1,0:T(8,128)(2,1)S(1)}, u32[]{:S(2)}, u32[]{:S(2)}) %collective-permute-start.3) | collective-permute-done | bytes 131104 | tf_op jit(solution)/shard_map/ppermute | solution.py:298
  156.4 1.2 shard_map.74
  (15 shorter events, 0.4 us)
Async XLA Ops:
  7.2 47.7 %copy-start = (f32[16,128]{1,0:T(8,128)S(1)}, f32[16,128]{1,0:T(8,128)}, u32[]{:S(2)}) copy-start(f32[16,128]{1,0:T(8,128)} %param.8) | copy-start | bytes 24580
  7.2 23.7 %copy-start.1 = (bf16[128,256]{1,0:T(8,128)(2,1)S(1)}, bf16[128,256]{1,0:T(8,128)(2,1)}, u32[]{:S(2)}) copy-start(bf16[128,256]{1,0:T(8,128)(2,1)} %param.9) | copy-start | bytes 196612
  7.2 23.7 %copy-start.2 = (bf16[128,256]{1,0:T(8,128)(2,1)S(1)}, bf16[128,256]{1,0:T(8,128)(2,1)}, u32[]{:S(2)}) copy-start(bf16[128,256]{1,0:T(8,128)(2,1)} %param.5) | copy-start | bytes 196612
  7.2 86.8 %all-gather.4.cloned.1.call-start = ((), (), s32[]{:S(2)}) async-start(), calls=%async_computation.4 | async-start | bytes 8912896 | tf_op jit(solution)/shard_map/all_gather | solution.py:279
  50.7 28.9 %all-to-all-start.2 = ((bf16[4,4,2,128,256]{4,3,2,1,0:T(8,128)(2,1)}), bf16[4,4,2,128,256]{4,3,2,1,0:T(8,128)(2,1)S(1)}, u32[]{:S(2)}, u32[]{:S(2)}) async-start(bf16[4,4,2,128,256]{4,3,2,1,0:T(8,128)(2,1)} %broadcast_in_dim.7), calls=%async_computation.2 | async-start | bytes 4194304 | tf_op jit(solution)/shard_map/all_to_all | solution.py:264
  79.6 8.4 %collective-permute-start = (bf16[4,2,2,2,128,256]{5,4,3,2,1,0:T(8,128)(2,1)S(1)}, bf16[4,2,2,2,128,256]{5,4,3,2,1,0:T(8,128)(2,1)}, u32[]{:S(2)}, u32[]{:S(2)}) collective-permute-start(bf16[4,2,2,2,128,256]{5,4,3,2,1,0:T(8,128)(2,1)S(1)} %bitcast.10), channel_id=1, source_target_pairs={{0,1},{1,0},{2,3},{3,2},{4,5},{5,4},{6,7},{7,6},{8,9},{9,8},{10,11... | collective-permute-start | bytes 6291464 | tf_op jit(solution)/shard_map/ppermute | solution.py:286
  98.8 11.5 %collective-permute-start.1 = (bf16[128,256]{1,0:T(8,128)(2,1)S(1)}, bf16[128,256]{1,0:T(8,128)(2,1)S(1)}, u32[]{:S(2)}, u32[]{:S(2)}) collective-permute-start(bf16[128,256]{1,0:T(8,128)(2,1)S(1)} %get-tuple-element.21.product_ref), channel_id=1, source_target_pairs={{0,16},{16,32},{32,48},{48,64},{64,80},{80,96},{96,112},{112,128},... | collective-permute-start | bytes 196616 | tf_op jit(solution)/shard_map/ppermute | solution.py:290
  100.8 10.6 %collective-permute-start.2 = (bf16[128,256]{1,0:T(8,128)(2,1)S(1)}, bf16[128,256]{1,0:T(8,128)(2,1)S(1)}, u32[]{:S(2)}, u32[]{:S(2)}) collective-permute-start(bf16[128,256]{1,0:T(8,128)(2,1)S(1)} %get-tuple-element.22.mixed_ref), channel_id=1, source_target_pairs={{16,0},{32,16},{48,32},{64,48},{80,64},{96,80},{112,96},{128,112},... | collective-permute-start | bytes 196616 | tf_op jit(solution)/shard_map/ppermute | solution.py:291
  146.7 9.7 %collective-permute-start.3 = (bf16[2,128,256]{2,1,0:T(8,128)(2,1)S(1)}, bf16[2,128,256]{2,1,0:T(8,128)(2,1)S(1)}, u32[]{:S(2)}, u32[]{:S(2)}) collective-permute-start(bf16[2,128,256]{2,1,0:T(8,128)(2,1)S(1)} %get-tuple-element.25), channel_id=1, source_target_pairs={{0,256},{256,0},{1,257},{257,1},{2,258},{258,2},{3,259},{259,3},{4... | collective-permute-start | bytes 393224 | tf_op jit(solution)/shard_map/ppermute | solution.py:298
Sparse Core Ops, SparseCore 0:
  31.0 62.9 all-gather.3

commit v20 on v19

--- a/solution.py
+++ b/solution.py
@@ -231,23 +231,33 @@
     return on_chip(combine_kernel, out_shape, operands, 1 << 20)
 
 
-def pack_kernel(in_ref, out_ref, packed_ref):
-    for h in range(2):
-        chans = slice(h * HALF, (h + 1) * HALF)
-        streams = [in_ref[stream, :, chans].astype(F32).T.astype(BF16) for stream in range(3)]
-        for l in range(2):
-            for stream in range(3):
-                packed_ref[2 * h + l, stream * HALF : (stream + 1) * HALF] = streams[stream]
-            packed_ref[2 * h + l, BACK:] = out_ref[chans]
+def pack_kernel(in_hbm, out_hbm, packed_ref, in_ref, out_ref, arrived):
+    copies = [pltpu.make_async_copy(in_hbm.at[i], in_ref.at[i], arrived.at[i]) for i in range(3)]
+    copies.append(pltpu.make_async_copy(out_hbm, out_ref, arrived.at[3]))
+    for copy in copies:
+        copy.start()
+    for stream in range(4):
+        copies[stream].wait()
+        rows = slice(stream * HALF, (stream + 1) * HALF)
+        for h in range(2):
+            chans = slice(h * HALF, (h + 1) * HALF)
+            piece = out_ref[chans] if stream == 3 else in_ref[stream, :, chans].astype(F32).T.astype(BF16)
+            for l in range(2):
+                packed_ref[2 * h + l, rows] = piece
 
 
 def packed(in_weight, out_weight):
-    vmem = pl.BlockSpec(memory_space=pltpu.VMEM)
     return pl.pallas_call(
         pack_kernel,
         out_shape=jax.ShapeDtypeStruct((4, STREAMS, ROWS), BF16),
-        in_specs=[vmem] * 2,
-        out_specs=vmem,
+        in_specs=[pl.BlockSpec(memory_space=pl.ANY)] * 2,
+        out_specs=pl.BlockSpec(memory_space=pltpu.VMEM),
+        scratch_shapes=[
+            pltpu.VMEM((3, ROWS, FEATURES), BF16),
+            pltpu.VMEM((FEATURES, ROWS), BF16),
+            pltpu.SemaphoreType.DMA((4,)),
+        ],
+        compiler_params=pltpu.CompilerParams(vmem_limit_bytes=VMEM_SMALL),
     )(in_weight, out_weight)
 
 

time: 168 us -> 168 us (level)
  local copies, waits for them, and re-layouts: 1.81 us -> 3.57 us
    unnamed x6 -> x10, local copies, waits for them, and re-layouts: 0.02 us -> 1.78 us
where the time goes in v20:
time: 168 us; the launch traced here: 165 us
  blocking collectives  71.3 us (42%)
  waiting for transfers between devices  38.7 us (23%)
  starting transfers between devices  26.2 us (16%)
  between operations  14.2 us (8%)
  Pallas kernels  10.7 us (6%)
  local copies, waits for them, and re-layouts  3.57 us (2%)
    all_to_all x3, blocking collectives, swapped(): return lax.all_to_all(value, axes, 0, 0, tiled=True)  68.3 us
    all_to_all x1, waiting for transfers between devices, swapped(): return lax.all_to_all(value, axes, 0, 0, tiled=True)  24.1 us
    ppermute x1, starting transfers between devices, local(): after = lax.ppermute(mixed, ('l', 'z'), [(b, a) for a, b in ring])  9.33 us
    ppermute x1, starting transfers between devices, local(): return finish(place, mine, lax.ppermute(theirs, 'h', cross))  6.36 us
    all_gather x1, waiting for transfers between devices, local(): lax.all_gather(weight, ('z', 'core'), axis=0)  6.02 us
    pallas_call x4, Pallas kernels, on_chip(): pl.pallas_call(kernel, out_shape=out_shape, in_specs=[smem] + [vmem] * (l...  4.85 us
    pallas_call x1, Pallas kernels, forward(): pl.pallas_call(forward_kernel, out_shape=(shape(BACK, BF16), shape(HALF,...  4.82 us
    ppermute x1, starting transfers between devices, local(): other = lax.ppermute(values, 'core', cross)  4.43 us
  transfers between devices with their start and end apart: 6, of which 6 were waited for; matrix products, arithmetic and copies ran while one was open for 1% of the time, Pallas kernels for 0%

profile of v20, /device:TPU:1, one launch (start us, length us, event | category | flops | bytes accessed | tf_op | source)
XLA Modules:
  0.0 164.8 jit_solution(16442819317547555633)
XLA Ops:
  7.2 0.9 copy-done.1
  8.2 0.8 copy-done.2
  9.0 0.7 shard_map.68
  9.7 22.0 %all_to_all.20 = bf16[4,512,128]{2,1,0:T(8,128)(2,1)} all-to-all(bf16[4,512,128]{2,1,0:T(8,128)(2,1)S(1)} %shard_map.68), channel_id=1, replica_groups=mesh['h'=2,'l'=2,'z'=8,'ylo'=2,'x'=4,'core'=2] {'h','l'}, dimensions={0} | all-to-all | bytes 1048576 | tf_op jit(solution)/shard_map/all_to_all | solution.py:274
  31.8 17.6 %all_to_all.21 = bf16[4,2,128,256]{3,2,1,0:T(8,128)(2,1)S(1)} all-to-all(bf16[4,2,128,256]{3,2,1,0:T(8,128)(2,1)S(1)} %broadcast_in_dim.6), channel_id=1, replica_groups=mesh['h'=2,'l'=2,'z'=8,'ylo'=2,'x'=4,'core'=2] {'h','ylo'}, dimensions={0} | all-to-all | bytes 1048576 | tf_op jit(solution)/shard_map/all_to_all | solution.py:274
  49.5 1.6 broadcast_in_dim.7
  51.1 4.1 %all-to-all-start.2 = ((bf16[4,4,2,128,256]{4,3,2,1,0:T(8,128)(2,1)}), bf16[4,4,2,128,256]{4,3,2,1,0:T(8,128)(2,1)S(1)}, u32[]{:S(2)}, u32[]{:S(2)}) async-start(bf16[4,4,2,128,256]{4,3,2,1,0:T(8,128)(2,1)} %broadcast_in_dim.7), calls=%async_computation.2 | async-start | bytes 4194304 | tf_op jit(solution)/shard_map/all_to_all | solution.py:274
  55.4 0.4 shard_map.69.band_ref
  55.8 24.1 %all-to-all-done.2 = bf16[4,4,2,128,256]{4,3,2,1,0:T(8,128)(2,1)S(1)} async-done(((bf16[4,4,2,128,256]{4,3,2,1,0:T(8,128)(2,1)}), bf16[4,4,2,128,256]{4,3,2,1,0:T(8,128)(2,1)S(1)}, u32[]{:S(2)}, u32[]{:S(2)}) %all-to-all-start.2) | async-done | bytes 2097184 | tf_op jit(solution)/shard_map/all_to_all | solution.py:274
  79.9 4.4 %collective-permute-start = (bf16[4,2,2,2,128,256]{5,4,3,2,1,0:T(8,128)(2,1)S(1)}, bf16[4,2,2,2,128,256]{5,4,3,2,1,0:T(8,128)(2,1)}, u32[]{:S(2)}, u32[]{:S(2)}) collective-permute-start(bf16[4,2,2,2,128,256]{5,4,3,2,1,0:T(8,128)(2,1)S(1)} %bitcast.10), channel_id=1, source_target_pairs={{0,1},{1,0},{2,3},{3,2},{4,5},{5,4},{6,7},{7,6},{8,9},{9,8},{10,11... | collective-permute-start | bytes 6291464 | tf_op jit(solution)/shard_map/ppermute | solution.py:296
  84.5 3.9 %collective-permute-done.other_hbm = bf16[4,2,2,2,128,256]{5,4,3,2,1,0:T(8,128)(2,1)} collective-permute-done((bf16[4,2,2,2,128,256]{5,4,3,2,1,0:T(8,128)(2,1)S(1)}, bf16[4,2,2,2,128,256]{5,4,3,2,1,0:T(8,128)(2,1)}, u32[]{:S(2)}, u32[]{:S(2)}) %collective-permute-start) | collective-permute-done | bytes 2097184 | tf_op jit(solution)/shard_map/ppermute | solution.py:296
  88.3 6.0 %all-gather.4.cloned.1.call-done = bf16[64,512,128]{2,1,0:T(8,128)(2,1)} async-done(((bf16[4,512,128]{2,1,0:T(8,128)(2,1)}), bf16[64,512,128]{2,1,0:T(8,128)(2,1)}) %all-gather.4.cloned.1.call-update) | async-done | bytes 8388624 | tf_op jit(solution)/shard_map/all_gather | solution.py:289
  94.4 4.8 %shard_map.70 = (bf16[384,256]{1,0:T(8,128)(2,1)S(1)}, f32[128,256]{1,0:T(8,128)S(1)}, bf16[128,256]{1,0:T(8,128)(2,1)S(1)}, bf16[128,256]{1,0:T(8,128)(2,1)S(1)}, bf16[2,2,2,2,2,512,128]{6,5,4,3,2,1,0:T(8,128)(2,1)S(1)}) custom-call(s32[4]{0:T(128)S(1)} %pad_add_fusion.place_ref, bf16[4,2,2,2,128,256]{5,4,3,2,1,0:T(8,128)(2,1)S(1)} %bitcast.11, ...), custom_call_target="tpu_custom_call" | custom-call | flops 1073741824 | bytes 9437184 | tf_op jit(solution)/shard_map/pallas_call | solution.py:116
  99.2 1.9 %collective-permute-start.1 = (bf16[128,256]{1,0:T(8,128)(2,1)S(1)}, bf16[128,256]{1,0:T(8,128)(2,1)S(1)}, u32[]{:S(2)}, u32[]{:S(2)}) collective-permute-start(bf16[128,256]{1,0:T(8,128)(2,1)S(1)} %get-tuple-element.21.product_ref), channel_id=1, source_target_pairs={{0,16},{16,32},{32,48},{48,64},{64,80},{80,96},{96,112},{112,128},... | collective-permute-start | bytes 196616 | tf_op jit(solution)/shard_map/ppermute | solution.py:300
  101.1 9.3 %collective-permute-start.2 = (bf16[128,256]{1,0:T(8,128)(2,1)S(1)}, bf16[128,256]{1,0:T(8,128)(2,1)S(1)}, u32[]{:S(2)}, u32[]{:S(2)}) collective-permute-start(bf16[128,256]{1,0:T(8,128)(2,1)S(1)} %get-tuple-element.22.mixed_ref), channel_id=1, source_target_pairs={{16,0},{32,16},{48,32},{64,48},{80,64},{96,80},{112,96},{128,112},... | collective-permute-start | bytes 196616 | tf_op jit(solution)/shard_map/ppermute | solution.py:301
  110.7 1.1 collective-permute-done.2.after_ref
  111.8 1.1 shard_map.71
  112.8 3.0 %all-gather.1 = bf16[512,512]{1,0:T(8,128)(2,1)S(1)} all-gather(bf16[256,512]{1,0:T(8,128)(2,1)S(1)} %shard_map.71), channel_id=3, replica_groups=mesh['h'=2,'l'=2,'z'=8,'ylo'=2,'x'=4,'core'=2] {'core'}, dimensions={0}, use_global_device_ids=true | all-gather | bytes 786432 | tf_op jit(solution)/shard_map/all_gather | solution.py:304
  115.9 1.8 %shard_map.72 = bf16[8,2,2,128,256]{4,3,2,1,0:T(8,128)(2,1)S(1)} custom-call(s32[4]{0:T(128)S(1)} %pad_add_fusion.place_ref, bf16[2,256,512]{2,1,0:T(8,128)(2,1)S(1)} %bitcast.12, bf16[2,2,2,2,2,512,128]{6,5,4,3,2,1,0:T(8,128)(2,1)S(1)} %get-tuple-element.23.weight_ref), custom_call_target="tpu_custom_call" | custom-call | flops 1073741824 | bytes 1048576 | tf_op jit(solution)/shard_map/pallas_call | solution.py:184
  117.7 28.6 %all_to_all.22.parts_ref = bf16[8,2,2,128,256]{4,3,2,1,0:T(8,128)(2,1)S(1)} all-to-all(bf16[8,2,2,128,256]{4,3,2,1,0:T(8,128)(2,1)S(1)} %shard_map.72), channel_id=1, replica_groups=mesh['h'=2,'l'=2,'z'=8,'ylo'=2,'x'=4,'core'=2] {'ylo','x'}, dimensions={0} | all-to-all | bytes 4194304 | tf_op jit(solution)/shard_map/all_to_all | solution.py:274
  146.3 0.8 shard_map.73
  147.1 6.4 %collective-permute-start.3 = (bf16[2,128,256]{2,1,0:T(8,128)(2,1)S(1)}, bf16[2,128,256]{2,1,0:T(8,128)(2,1)S(1)}, u32[]{:S(2)}, u32[]{:S(2)}) collective-permute-start(bf16[2,128,256]{2,1,0:T(8,128)(2,1)S(1)} %get-tuple-element.25), channel_id=1, source_target_pairs={{0,256},{256,0},{1,257},{257,1},{2,258},{258,2},{3,259},{259,3},{4... | collective-permute-start | bytes 393224 | tf_op jit(solution)/shard_map/ppermute | solution.py:308
  153.4 3.4 %collective-permute-done.3.theirs_ref = bf16[2,128,256]{2,1,0:T(8,128)(2,1)S(1)} collective-permute-done((bf16[2,128,256]{2,1,0:T(8,128)(2,1)S(1)}, bf16[2,128,256]{2,1,0:T(8,128)(2,1)S(1)}, u32[]{:S(2)}, u32[]{:S(2)}) %collective-permute-start.3) | collective-permute-done | bytes 131104 | tf_op jit(solution)/shard_map/ppermute | solution.py:308
  156.8 1.2 shard_map.74
  (19 shorter events, 0.7 us)
Async XLA Ops:
  7.2 48.0 %copy-start = (f32[16,128]{1,0:T(8,128)S(1)}, f32[16,128]{1,0:T(8,128)}, u32[]{:S(2)}) copy-start(f32[16,128]{1,0:T(8,128)} %param.8) | copy-start | bytes 24580
  7.2 87.2 %all-gather.4.cloned.1.call-start = ((), (), s32[]{:S(2)}) async-start(), calls=%async_computation.4 | async-start | bytes 8912896 | tf_op jit(solution)/shard_map/all_gather | solution.py:289
  7.2 0.9 copy-start.1
  8.2 0.8 copy-start.2
  9.0 22.8 %copy-start.3 = (bf16[128,256]{1,0:T(8,128)(2,1)S(1)}, bf16[128,256]{1,0:T(8,128)(2,1)}, u32[]{:S(2)}) copy-start(bf16[128,256]{1,0:T(8,128)(2,1)} %param.9) | copy-start | bytes 196612
  9.0 22.8 %copy-start.4 = (bf16[128,256]{1,0:T(8,128)(2,1)S(1)}, bf16[128,256]{1,0:T(8,128)(2,1)}, u32[]{:S(2)}) copy-start(bf16[128,256]{1,0:T(8,128)(2,1)} %param.5) | copy-start | bytes 196612
  51.1 28.9 %all-to-all-start.2 = ((bf16[4,4,2,128,256]{4,3,2,1,0:T(8,128)(2,1)}), bf16[4,4,2,128,256]{4,3,2,1,0:T(8,128)(2,1)S(1)}, u32[]{:S(2)}, u32[]{:S(2)}) async-start(bf16[4,4,2,128,256]{4,3,2,1,0:T(8,128)(2,1)} %broadcast_in_dim.7), calls=%async_computation.2 | async-start | bytes 4194304 | tf_op jit(solution)/shard_map/all_to_all | solution.py:274
  79.9 8.4 %collective-permute-start = (bf16[4,2,2,2,128,256]{5,4,3,2,1,0:T(8,128)(2,1)S(1)}, bf16[4,2,2,2,128,256]{5,4,3,2,1,0:T(8,128)(2,1)}, u32[]{:S(2)}, u32[]{:S(2)}) collective-permute-start(bf16[4,2,2,2,128,256]{5,4,3,2,1,0:T(8,128)(2,1)S(1)} %bitcast.10), channel_id=1, source_target_pairs={{0,1},{1,0},{2,3},{3,2},{4,5},{5,4},{6,7},{7,6},{8,9},{9,8},{10,11... | collective-permute-start | bytes 6291464 | tf_op jit(solution)/shard_map/ppermute | solution.py:296
  99.2 11.5 %collective-permute-start.1 = (bf16[128,256]{1,0:T(8,128)(2,1)S(1)}, bf16[128,256]{1,0:T(8,128)(2,1)S(1)}, u32[]{:S(2)}, u32[]{:S(2)}) collective-permute-start(bf16[128,256]{1,0:T(8,128)(2,1)S(1)} %get-tuple-element.21.product_ref), channel_id=1, source_target_pairs={{0,16},{16,32},{32,48},{48,64},{64,80},{80,96},{96,112},{112,128},... | collective-permute-start | bytes 196616 | tf_op jit(solution)/shard_map/ppermute | solution.py:300
  101.1 10.7 %collective-permute-start.2 = (bf16[128,256]{1,0:T(8,128)(2,1)S(1)}, bf16[128,256]{1,0:T(8,128)(2,1)S(1)}, u32[]{:S(2)}, u32[]{:S(2)}) collective-permute-start(bf16[128,256]{1,0:T(8,128)(2,1)S(1)} %get-tuple-element.22.mixed_ref), channel_id=1, source_target_pairs={{16,0},{32,16},{48,32},{64,48},{80,64},{96,80},{112,96},{128,112},... | collective-permute-start | bytes 196616 | tf_op jit(solution)/shard_map/ppermute | solution.py:301
  147.1 9.7 %collective-permute-start.3 = (bf16[2,128,256]{2,1,0:T(8,128)(2,1)S(1)}, bf16[2,128,256]{2,1,0:T(8,128)(2,1)S(1)}, u32[]{:S(2)}, u32[]{:S(2)}) collective-permute-start(bf16[2,128,256]{2,1,0:T(8,128)(2,1)S(1)} %get-tuple-element.25), channel_id=1, source_target_pairs={{0,256},{256,0},{1,257},{257,1},{2,258},{258,2},{3,259},{259,3},{4... | collective-permute-start | bytes 393224 | tf_op jit(solution)/shard_map/ppermute | solution.py:308
Sparse Core Ops, SparseCore 0:
  31.9 62.4 all-gather.3

commit v21 on v19

--- a/solution.py
+++ b/solution.py
@@ -206,7 +206,7 @@
                 ]
                 result = jnp.dot(terms, jnp.concatenate(weight, 0), preferred_element_type=F32)
                 for h in range(2):
-                    out_ref[4 * y + x, h, part] = result[h * ROWS : (h + 1) * ROWS].astype(BF16)
+                    out_ref[2 * x + y, h, part] = result[h * ROWS : (h + 1) * ROWS].astype(BF16)
 
 
 def backward(*operands):
@@ -293,7 +293,7 @@
     terms = middle(place, band, streams, gate, product, mixed, before, after)
     terms = lax.all_gather(terms, "core", axis=0)
 
-    parts = swapped(backward(place, terms, weight), ("ylo", "x"))
+    parts = swapped(backward(place, terms, weight), ("x", "ylo"))
     mine, theirs = combine(place, parts)
     return finish(place, mine, lax.ppermute(theirs, "h", cross))
 

time: 168 us -> 168 us (level)
  no operation moved by 1% of the time
where the time goes in v21:
time: 168 us; the launch traced here: 165 us
  blocking collectives  71.9 us (43%)
  waiting for transfers between devices  38.7 us (23%)
  starting transfers between devices  26.2 us (16%)
  between operations  14.2 us (8%)
  Pallas kernels  11.9 us (7%)
  local copies, waits for them, and re-layouts  1.81 us (1%)
    all_to_all x3, blocking collectives, swapped(): return lax.all_to_all(value, axes, 0, 0, tiled=True)  68.9 us
    all_to_all x1, waiting for transfers between devices, swapped(): return lax.all_to_all(value, axes, 0, 0, tiled=True)  24.1 us
    ppermute x1, starting transfers between devices, local(): after = lax.ppermute(mixed, ('l', 'z'), [(b, a) for a, b in ring])  9.33 us
    ppermute x1, starting transfers between devices, local(): return finish(place, mine, lax.ppermute(theirs, 'h', cross))  6.37 us
    all_gather x1, waiting for transfers between devices, local(): lax.all_gather(weight, ('z', 'core'), axis=0)  6.02 us
    pallas_call x4, Pallas kernels, on_chip(): pl.pallas_call(kernel, out_shape=out_shape, in_specs=[smem] + [vmem] * (l...  4.85 us
    pallas_call x1, Pallas kernels, forward(): pl.pallas_call(forward_kernel, out_shape=(shape(BACK, BF16), shape(HALF,...  4.82 us
    ppermute x1, starting transfers between devices, local(): other = lax.ppermute(values, 'core', cross)  4.43 us
  transfers between devices with their start and end apart: 6, of which 6 were waited for; matrix products, arithmetic and copies ran while one was open for 1% of the time, Pallas kernels for 0%

profile of v21, /device:TPU:1, one launch (start us, length us, event | category | flops | bytes accessed | tf_op | source)
XLA Modules:
  0.0 164.9 jit_solution(13064223046129674177)
XLA Ops:
  7.2 1.9 %shard_map.68 = bf16[4,512,128]{2,1,0:T(8,128)(2,1)} custom-call(bf16[3,128,256]{2,1,0:T(8,128)(2,1)} %in_ref.1, bf16[256,128]{1,0:T(8,128)(2,1)} %out_ref.1), custom_call_target="tpu_custom_call" | custom-call | tf_op jit(solution)/shard_map/pallas_call | solution.py:246
  9.1 21.7 %all_to_all.20 = bf16[4,512,128]{2,1,0:T(8,128)(2,1)} all-to-all(bf16[4,512,128]{2,1,0:T(8,128)(2,1)} %shard_map.68), channel_id=1, replica_groups=mesh['h'=2,'l'=2,'z'=8,'ylo'=2,'x'=4,'core'=2] {'h','l'}, dimensions={0} | all-to-all | bytes 1048576 | tf_op jit(solution)/shard_map/all_to_all | solution.py:264
  31.0 18.1 %all_to_all.21 = bf16[4,2,128,256]{3,2,1,0:T(8,128)(2,1)S(1)} all-to-all(bf16[4,2,128,256]{3,2,1,0:T(8,128)(2,1)S(1)} %broadcast_in_dim.6), channel_id=1, replica_groups=mesh['h'=2,'l'=2,'z'=8,'ylo'=2,'x'=4,'core'=2] {'h','ylo'}, dimensions={0} | all-to-all | bytes 1048576 | tf_op jit(solution)/shard_map/all_to_all | solution.py:264
  49.1 1.6 broadcast_in_dim.7
  50.7 4.1 %all-to-all-start.2 = ((bf16[4,4,2,128,256]{4,3,2,1,0:T(8,128)(2,1)}), bf16[4,4,2,128,256]{4,3,2,1,0:T(8,128)(2,1)S(1)}, u32[]{:S(2)}, u32[]{:S(2)}) async-start(bf16[4,4,2,128,256]{4,3,2,1,0:T(8,128)(2,1)} %broadcast_in_dim.7), calls=%async_computation.2 | async-start | bytes 4194304 | tf_op jit(solution)/shard_map/all_to_all | solution.py:264
  55.1 0.4 shard_map.69.band_ref
  55.4 24.1 %all-to-all-done.2 = bf16[4,4,2,128,256]{4,3,2,1,0:T(8,128)(2,1)S(1)} async-done(((bf16[4,4,2,128,256]{4,3,2,1,0:T(8,128)(2,1)}), bf16[4,4,2,128,256]{4,3,2,1,0:T(8,128)(2,1)S(1)}, u32[]{:S(2)}, u32[]{:S(2)}) %all-to-all-start.2) | async-done | bytes 2097184 | tf_op jit(solution)/shard_map/all_to_all | solution.py:264
  79.6 4.4 %collective-permute-start = (bf16[4,2,2,2,128,256]{5,4,3,2,1,0:T(8,128)(2,1)S(1)}, bf16[4,2,2,2,128,256]{5,4,3,2,1,0:T(8,128)(2,1)}, u32[]{:S(2)}, u32[]{:S(2)}) collective-permute-start(bf16[4,2,2,2,128,256]{5,4,3,2,1,0:T(8,128)(2,1)S(1)} %bitcast.10), channel_id=1, source_target_pairs={{0,1},{1,0},{2,3},{3,2},{4,5},{5,4},{6,7},{7,6},{8,9},{9,8},{10,11... | collective-permute-start | bytes 6291464 | tf_op jit(solution)/shard_map/ppermute | solution.py:286
  84.0 0.1 pad_add_fusion.place_ref
  84.1 3.9 %collective-permute-done.other_hbm = bf16[4,2,2,2,128,256]{5,4,3,2,1,0:T(8,128)(2,1)} collective-permute-done((bf16[4,2,2,2,128,256]{5,4,3,2,1,0:T(8,128)(2,1)S(1)}, bf16[4,2,2,2,128,256]{5,4,3,2,1,0:T(8,128)(2,1)}, u32[]{:S(2)}, u32[]{:S(2)}) %collective-permute-start) | collective-permute-done | bytes 2097184 | tf_op jit(solution)/shard_map/ppermute | solution.py:286
  88.0 6.0 %all-gather.4.cloned.1.call-done = bf16[64,512,128]{2,1,0:T(8,128)(2,1)} async-done(((bf16[4,512,128]{2,1,0:T(8,128)(2,1)}), bf16[64,512,128]{2,1,0:T(8,128)(2,1)}) %all-gather.4.cloned.1.call-update) | async-done | bytes 8388624 | tf_op jit(solution)/shard_map/all_gather | solution.py:279
  94.0 4.8 %shard_map.70 = (bf16[384,256]{1,0:T(8,128)(2,1)S(1)}, f32[128,256]{1,0:T(8,128)S(1)}, bf16[128,256]{1,0:T(8,128)(2,1)S(1)}, bf16[128,256]{1,0:T(8,128)(2,1)S(1)}, bf16[2,2,2,2,2,512,128]{6,5,4,3,2,1,0:T(8,128)(2,1)S(1)}) custom-call(s32[4]{0:T(128)S(1)} %pad_add_fusion.place_ref, bf16[4,2,2,2,128,256]{5,4,3,2,1,0:T(8,128)(2,1)S(1)} %bitcast.11, ...), custom_call_target="tpu_custom_call" | custom-call | flops 1073741824 | bytes 9437184 | tf_op jit(solution)/shard_map/pallas_call | solution.py:116
  98.8 1.9 %collective-permute-start.1 = (bf16[128,256]{1,0:T(8,128)(2,1)S(1)}, bf16[128,256]{1,0:T(8,128)(2,1)S(1)}, u32[]{:S(2)}, u32[]{:S(2)}) collective-permute-start(bf16[128,256]{1,0:T(8,128)(2,1)S(1)} %get-tuple-element.21.product_ref), channel_id=1, source_target_pairs={{0,16},{16,32},{32,48},{48,64},{64,80},{80,96},{96,112},{112,128},... | collective-permute-start | bytes 196616 | tf_op jit(solution)/shard_map/ppermute | solution.py:290
  100.8 9.3 %collective-permute-start.2 = (bf16[128,256]{1,0:T(8,128)(2,1)S(1)}, bf16[128,256]{1,0:T(8,128)(2,1)S(1)}, u32[]{:S(2)}, u32[]{:S(2)}) collective-permute-start(bf16[128,256]{1,0:T(8,128)(2,1)S(1)} %get-tuple-element.22.mixed_ref), channel_id=1, source_target_pairs={{16,0},{32,16},{48,32},{64,48},{80,64},{96,80},{112,96},{128,112},... | collective-permute-start | bytes 196616 | tf_op jit(solution)/shard_map/ppermute | solution.py:291
  110.1 0.2 collective-permute-done.1.before_ref
  110.3 1.1 collective-permute-done.2.after_ref
  111.4 1.0 shard_map.71
  112.5 3.0 %all-gather.1 = bf16[512,512]{1,0:T(8,128)(2,1)S(1)} all-gather(bf16[256,512]{1,0:T(8,128)(2,1)S(1)} %shard_map.71), channel_id=3, replica_groups=mesh['h'=2,'l'=2,'z'=8,'ylo'=2,'x'=4,'core'=2] {'core'}, dimensions={0}, use_global_device_ids=true | all-gather | bytes 786432 | tf_op jit(solution)/shard_map/all_gather | solution.py:294
  115.5 1.8 %shard_map.72 = bf16[8,2,2,128,256]{4,3,2,1,0:T(8,128)(2,1)S(1)} custom-call(s32[4]{0:T(128)S(1)} %pad_add_fusion.place_ref, bf16[2,256,512]{2,1,0:T(8,128)(2,1)S(1)} %bitcast.12, bf16[2,2,2,2,2,512,128]{6,5,4,3,2,1,0:T(8,128)(2,1)S(1)} %get-tuple-element.23.weight_ref), custom_call_target="tpu_custom_call" | custom-call | flops 1073741824 | bytes 1048576 | tf_op jit(solution)/shard_map/pallas_call | solution.py:184
  117.3 29.0 %all_to_all.22.parts_ref = bf16[8,2,2,128,256]{4,3,2,1,0:T(8,128)(2,1)S(1)} all-to-all(bf16[8,2,2,128,256]{4,3,2,1,0:T(8,128)(2,1)S(1)} %shard_map.72), channel_id=1, replica_groups=mesh['h'=2,'l'=2,'z'=8,'ylo'=2,'x'=4,'core'=2] {'x','ylo'}, dimensions={0} | all-to-all | bytes 4194304 | tf_op jit(solution)/shard_map/all_to_all | solution.py:264
  146.3 0.8 shard_map.73
  147.1 6.4 %collective-permute-start.3 = (bf16[2,128,256]{2,1,0:T(8,128)(2,1)S(1)}, bf16[2,128,256]{2,1,0:T(8,128)(2,1)S(1)}, u32[]{:S(2)}, u32[]{:S(2)}) collective-permute-start(bf16[2,128,256]{2,1,0:T(8,128)(2,1)S(1)} %get-tuple-element.25), channel_id=1, source_target_pairs={{0,256},{256,0},{1,257},{257,1},{2,258},{258,2},{3,259},{259,3},{4... | collective-permute-start | bytes 393224 | tf_op jit(solution)/shard_map/ppermute | solution.py:298
  153.5 3.3 %collective-permute-done.3.theirs_ref = bf16[2,128,256]{2,1,0:T(8,128)(2,1)S(1)} collective-permute-done((bf16[2,128,256]{2,1,0:T(8,128)(2,1)S(1)}, bf16[2,128,256]{2,1,0:T(8,128)(2,1)S(1)}, u32[]{:S(2)}, u32[]{:S(2)}) %collective-permute-start.3) | collective-permute-done | bytes 131104 | tf_op jit(solution)/shard_map/ppermute | solution.py:298
  156.8 1.2 shard_map.74
  (15 shorter events, 0.4 us)
Async XLA Ops:
  7.2 47.7 %copy-start = (f32[16,128]{1,0:T(8,128)S(1)}, f32[16,128]{1,0:T(8,128)}, u32[]{:S(2)}) copy-start(f32[16,128]{1,0:T(8,128)} %param.8) | copy-start | bytes 24580
  7.2 23.7 %copy-start.1 = (bf16[128,256]{1,0:T(8,128)(2,1)S(1)}, bf16[128,256]{1,0:T(8,128)(2,1)}, u32[]{:S(2)}) copy-start(bf16[128,256]{1,0:T(8,128)(2,1)} %param.9) | copy-start | bytes 196612
  7.2 23.7 %copy-start.2 = (bf16[128,256]{1,0:T(8,128)(2,1)S(1)}, bf16[128,256]{1,0:T(8,128)(2,1)}, u32[]{:S(2)}) copy-start(bf16[128,256]{1,0:T(8,128)(2,1)} %param.5) | copy-start | bytes 196612
  7.2 86.8 %all-gather.4.cloned.1.call-start = ((), (), s32[]{:S(2)}) async-start(), calls=%async_computation.4 | async-start | bytes 8912896 | tf_op jit(solution)/shard_map/all_gather | solution.py:279
  50.7 28.9 %all-to-all-start.2 = ((bf16[4,4,2,128,256]{4,3,2,1,0:T(8,128)(2,1)}), bf16[4,4,2,128,256]{4,3,2,1,0:T(8,128)(2,1)S(1)}, u32[]{:S(2)}, u32[]{:S(2)}) async-start(bf16[4,4,2,128,256]{4,3,2,1,0:T(8,128)(2,1)} %broadcast_in_dim.7), calls=%async_computation.2 | async-start | bytes 4194304 | tf_op jit(solution)/shard_map/all_to_all | solution.py:264
  79.6 8.4 %collective-permute-start = (bf16[4,2,2,2,128,256]{5,4,3,2,1,0:T(8,128)(2,1)S(1)}, bf16[4,2,2,2,128,256]{5,4,3,2,1,0:T(8,128)(2,1)}, u32[]{:S(2)}, u32[]{:S(2)}) collective-permute-start(bf16[4,2,2,2,128,256]{5,4,3,2,1,0:T(8,128)(2,1)S(1)} %bitcast.10), channel_id=1, source_target_pairs={{0,1},{1,0},{2,3},{3,2},{4,5},{5,4},{6,7},{7,6},{8,9},{9,8},{10,11... | collective-permute-start | bytes 6291464 | tf_op jit(solution)/shard_map/ppermute | solution.py:286
  98.8 11.5 %collective-permute-start.1 = (bf16[128,256]{1,0:T(8,128)(2,1)S(1)}, bf16[128,256]{1,0:T(8,128)(2,1)S(1)}, u32[]{:S(2)}, u32[]{:S(2)}) collective-permute-start(bf16[128,256]{1,0:T(8,128)(2,1)S(1)} %get-tuple-element.21.product_ref), channel_id=1, source_target_pairs={{0,16},{16,32},{32,48},{48,64},{64,80},{80,96},{96,112},{112,128},... | collective-permute-start | bytes 196616 | tf_op jit(solution)/shard_map/ppermute | solution.py:290
  100.8 10.6 %collective-permute-start.2 = (bf16[128,256]{1,0:T(8,128)(2,1)S(1)}, bf16[128,256]{1,0:T(8,128)(2,1)S(1)}, u32[]{:S(2)}, u32[]{:S(2)}) collective-permute-start(bf16[128,256]{1,0:T(8,128)(2,1)S(1)} %get-tuple-element.22.mixed_ref), channel_id=1, source_target_pairs={{16,0},{32,16},{48,32},{64,48},{80,64},{96,80},{112,96},{128,112},... | collective-permute-start | bytes 196616 | tf_op jit(solution)/shard_map/ppermute | solution.py:291
  147.1 9.7 %collective-permute-start.3 = (bf16[2,128,256]{2,1,0:T(8,128)(2,1)S(1)}, bf16[2,128,256]{2,1,0:T(8,128)(2,1)S(1)}, u32[]{:S(2)}, u32[]{:S(2)}) collective-permute-start(bf16[2,128,256]{2,1,0:T(8,128)(2,1)S(1)} %get-tuple-element.25), channel_id=1, source_target_pairs={{0,256},{256,0},{1,257},{257,1},{2,258},{258,2},{3,259},{259,3},{4... | collective-permute-start | bytes 393224 | tf_op jit(solution)/shard_map/ppermute | solution.py:298
Sparse Core Ops, SparseCore 0:
  31.0 62.9 all-gather.3
